TPU v7x, 32 devices: a whole 2x2x4 slice. The times are simulated.
32 devices in a mesh: area: 4 (over y, core), scen: 8 (over z, x).
Axes of the slice: x: 2, y: 2, z: 4, core: 2. Of those that a mesh axis runs over, the one named last changes fastest.
Arguments:
- start_dispatch: float32 [24, 32, 35840], P(None, 'scen', 'area'), may hold values from -6 to 6
- multipliers: float32 [24, 32, 35840], P(None, 'scen', 'area'), may hold values from -6 to 6
- demand: float32 [24, 35840], P(None, 'area'), may hold values from -6 to 6
- load_factor: float32 [32], replicated, may hold values from 0.5 to 2
- node_ids: int32 [12, 32], P(None, 'scen'), may hold values from 0 to 31, as said below
- block_values: float32 [280, 2, 128, 128], P('area'), may hold values from -0.375 to 0.375
- block_cols: int32 [280, 2], P('area'), may hold values from 0 to 69, as said below
- send_block: int32 [4], P('area'), may hold values from 0 to 69
- tie_source: int32 [16], P('area'), may hold values from 0 to 3, as said below
- tie_row: int32 [16], P('area'), may hold values from 0 to 69
- tie_weight: float32 [16, 128, 128], P('area'), may hold values from -0.5 to 0.5
Outputs:
- dispatch: float32 [24, 32, 35840], P(None, 'scen', 'area')
- new_multipliers: float32 [24, 32, 35840], P(None, 'scen', 'area')
Inputs may be any that keep to these rules, and one draw needn't show every extreme that they name: `node_ids`: two scenarios s and s2 carry the same label at section k exactly when s // g == s2 // g with g = max(32 // 2^k, 1); labels of different nodes at one section differ. `block_cols`: the first stored block of block row i of an area has column i; the 2 columns of a row are distinct. `tie_source`: the boundary block feeding a tie of area a belongs to area (a + 1) mod 4 or (a - 1) mod 4; every area receives from both.
All inputs are finite; a program needn't handle non-finite values.
Results may differ from a plain program's by a relative error of at most 0.0001.
Values sent between devices are 32-bit elements; how exact they have to be, the bound alone decides.
No kernel may reach another device: no remote copies, remote signals or barrier semaphores. Data moves between devices by JAX's collectives and lax.ppermute only.
A program may use at most 128 MiB of HBM per device.

v0:
```python
import jax
import jax.numpy as jnp
from jax import lax
from jax.sharding import PartitionSpec as P

STEPS = 8


full_precision = lax.Precision.HIGHEST
step_size = 0.25
penalty = 1.0


def from_partner(block, axis, apart):
    count = lax.axis_size(axis)
    route = []
    for low in range(count):
        high = low | 1 << apart
        if high != low and high < count:
            route += [(low, high), (high, low)]
    return lax.ppermute(block, axis, route)


def from_behind(value, axis, by):
    count = lax.axis_size(axis)
    return lax.ppermute(value, axis, [(i, (i + by) % count) for i in range(count)])


def section_average(values_in, local_scenarios, all_scenarios, sections):
    per_section = values_in.shape[0] // sections
    bus_count = values_in.shape[2]
    results = []
    totals = {}
    span_devices = {}
    for which_section in range(sections):
        portion = values_in[which_section * per_section : (which_section + 1) * per_section]
        members = max(all_scenarios >> which_section, 1)
        if members <= local_scenarios:
            shaped = portion.reshape(per_section, local_scenarios // members, members, bus_count)
            averages = jnp.sum(shaped, axis=2, keepdims=True) / members
            results.append(jnp.broadcast_to(averages, shaped.shape).reshape(portion.shape))
        else:
            totals[which_section] = jnp.sum(portion, axis=1)
            span_devices[which_section] = members // local_scenarios
            results.append(None)
    for which_section in sorted(totals):
        running = totals[which_section]
        for level in range(span_devices[which_section].bit_length() - 1):
            running = running + from_partner(running, "scen", level)
        totals[which_section] = running
    for which_section in totals:
        members = span_devices[which_section] * local_scenarios
        averages = totals[which_section] / members
        results[which_section] = jnp.broadcast_to(
            averages[:, None, :], (per_section, local_scenarios, bus_count)
        )
    return jnp.concatenate(results, axis=0)


def local(
    start_dispatch,
    multipliers,
    demand,
    load_factor,
    node_ids,
    block_values,
    block_cols,
    send_block,
    tie_source,
    tie_row,
    tie_weight,
):
    periods, local_scenarios, bus_local = start_dispatch.shape
    block_width = block_values.shape[-1]
    block_count = bus_local // block_width
    row_total = periods * local_scenarios
    sections = node_ids.shape[0]
    per_section = periods // sections
    all_scenarios = local_scenarios * lax.axis_size("scen")
    labels = jnp.arange(load_factor.shape[0], dtype=jnp.int32)
    matches = node_ids[:, :, None] == labels[None, None, :]
    load_rows = jnp.sum(jnp.where(matches, load_factor[None, None, :], 0.0), axis=2)
    load_rows = jnp.repeat(load_rows, per_section, axis=0)
    target = demand[:, None, :] * load_rows[:, :, None]
    bound_count = send_block.shape[0]
    owners = tie_source // bound_count
    before = (lax.axis_index("area") - 1 + lax.axis_size("area")) % lax.axis_size("area")
    slot_index = jnp.where(owners == before, 0, bound_count) + tie_source % bound_count

    def to_blocks(field):
        return field.reshape(row_total, block_count, block_width).transpose(1, 0, 2)

    anchor = section_average(start_dispatch, local_scenarios, all_scenarios, sections)
    constant = to_blocks(multipliers - target - penalty * anchor)
    state = to_blocks(start_dispatch)
    for iteration in range(STEPS):
        pieces = state[block_cols]
        product = jnp.einsum("bjrc,bjcd->brd", pieces, block_values, precision=full_precision)
        boundary = state[send_block]
        earlier = from_behind(boundary, "area", 1)
        following = from_behind(boundary, "area", -1)
        collected = jnp.concatenate([earlier, following], axis=0)
        picked = collected[slot_index]
        coupled = jnp.einsum("mrc,mcd->mrd", picked, tie_weight, precision=full_precision)
        state = state - step_size * (product.at[tie_row].add(coupled) + constant + penalty * state)
    dispatch = state.transpose(1, 0, 2).reshape(periods, local_scenarios, bus_local)
    current = section_average(dispatch, local_scenarios, all_scenarios, sections)
    return (dispatch, multipliers + penalty * (dispatch - current))


def solution(mesh):
    in_specs = (
        P(None, "scen", "area"),
        P(None, "scen", "area"),
        P(None, "area"),
        P(),
        P(None, "scen"),
        P("area", None, None, None),
        P("area", None),
        P("area"),
        P("area"),
        P("area"),
        P("area", None, None),
    )
    out_specs = (P(None, "scen", "area"), P(None, "scen", "area"))
    return jax.shard_map(local, mesh=mesh, in_specs=in_specs, out_specs=out_specs, check_vma=False)
```

profile of v0, /device:TPU:0, one launch (start us, length us, event | category | flops | bytes accessed | tf_op | source)
XLA Modules:
  0.0 347.8 jit_solution(10732136522478588323)
XLA Ops:
  1.3 5.2 %reshape.190 = f32[96,70,128]{2,1,0:T(8,128)} reshape(f32[24,4,8960]{2,1,0:T(4,128)} %param.11) | data formatting | bytes 6881280 | tf_op jit(solution)/shard_map/reshape | solution.py:91
  8.2 2.0 collective-permute-start.7
  10.2 2.0 slice_reduce_fusion
  12.2 2.3 collective-permute-start
  14.6 1.9 collective-permute-start.5
  17.9 4.4 %copy.67 = f32[96,70,128]{2,0,1:T(8,128)} copy(f32[96,70,128]{2,1,0:T(8,128)} %reshape.190) | data formatting | bytes 6881280 | tf_op jit(solution)/shard_map/reshape | solution.py:91
  22.6 5.8 %gather_fusion = f32[140,96,128]{2,1,0:T(8,128)} fusion(f32[70,96,128]{2,1,0:T(8,128)} %bitcast.103, s32[1024]{0:T(1024)S(1)} %pad_clamp_fusion.1), kind=kCustom, calls=%fused_computation | custom fusion | bytes 13763120 | tf_op jit(solution)/shard_map/gather | solution.py:97
  29.5 1.6 collective-permute-start.1
  31.8 2.4 collective-permute-done.1
  34.2 2.7 collective-permute-start.2
  36.9 2.6 collective-permute-done.2
  40.2 3.0 subtract_subtract_fusion
  43.2 5.3 %reshape.194 = f32[96,70,128]{2,1,0:T(8,128)} reshape(f32[24,4,8960]{2,1,0:T(4,128)} %subtract_subtract_fusion) | data formatting | bytes 6881280 | tf_op jit(solution)/shard_map/reshape | solution.py:91
  48.5 17.1 %fusion.7 = f32[70,96,128]{2,1,0:T(8,128)} fusion(f32[70,96,128]{2,1,0:T(8,128)} %bitcast.104, f32[70,2,96,128]{3,2,1,0:T(8,128)} %bitcast.105, f32[70,2,128,128]{3,2,1,0:T(8,128)} %param.16, f32[96,70,128]{2,1,0:T(8,128)} %reshape.194), kind=kOutput, calls=%fused_computation.39 | convolution fusion | flops 2644131840 | bytes 26378240 | tf_op jit(solution)/shard_map/bjrc,bjcd->brd/dot_general | solution.py:98
  65.7 2.2 scatter_fusion
  67.8 4.0 %multiply_subtract_fusion.6 = f32[70,96,128]{2,1,0:T(8,128)S(1)} fusion(f32[70,96,128]{2,1,0:T(8,128)} %scatter_fusion, f32[96,70,128]{2,1,0:T(8,128)} %reshape.190), kind=kLoop, calls=%fused_computation.49 | loop fusion | flops 1720320 | bytes 10321920 | tf_op jit(solution)/shard_map/sub | solution.py:105
  71.9 1.8 copy-done.2
  73.6 1.9 collective-permute-start.9
  75.6 5.8 %gather_fusion.2 = f32[140,96,128]{2,1,0:T(8,128)} fusion(f32[70,96,128]{2,1,0:T(8,128)} %copy-done.2, s32[1024]{0:T(1024)S(1)} %pad_clamp_fusion.1), kind=kCustom, calls=%fused_computation.2 | custom fusion | bytes 13763120 | tf_op jit(solution)/shard_map/gather | solution.py:97
  81.3 17.1 %fusion.6 = f32[70,96,128]{2,1,0:T(8,128)} fusion(f32[70,96,128]{2,1,0:T(8,128)} %copy-done.2, f32[70,2,96,128]{3,2,1,0:T(8,128)} %bitcast.107, f32[70,2,128,128]{3,2,1,0:T(8,128)} %param.16, f32[96,70,128]{2,1,0:T(8,128)} %reshape.194), kind=kOutput, calls=%fused_computation.37 | convolution fusion | flops 2644131840 | bytes 26378240 | tf_op jit(solution)/shard_map/bjrc,bjcd->brd/dot_general | solution.py:98
  99.6 2.2 scatter_fusion.1
  101.8 3.7 %multiply_subtract_fusion.5 = f32[70,96,128]{2,1,0:T(8,128)S(1)} fusion(f32[70,96,128]{2,1,0:T(8,128)} %copy-done.2, f32[70,96,128]{2,1,0:T(8,128)} %scatter_fusion.1), kind=kLoop, calls=%fused_computation.48 | loop fusion | flops 1720320 | bytes 10321920 | tf_op jit(solution)/shard_map/sub | solution.py:105
  105.5 1.8 copy-done.3
  107.2 2.1 collective-permute-start.11
  109.4 5.8 %gather_fusion.4 = f32[140,96,128]{2,1,0:T(8,128)} fusion(f32[70,96,128]{2,1,0:T(8,128)} %copy-done.3, s32[1024]{0:T(1024)S(1)} %pad_clamp_fusion.1), kind=kCustom, calls=%fused_computation.4 | custom fusion | bytes 13763120 | tf_op jit(solution)/shard_map/gather | solution.py:97
  115.2 17.1 %fusion.5 = f32[70,96,128]{2,1,0:T(8,128)} fusion(f32[70,96,128]{2,1,0:T(8,128)} %copy-done.3, f32[70,2,96,128]{3,2,1,0:T(8,128)} %bitcast.108, f32[70,2,128,128]{3,2,1,0:T(8,128)} %param.16, f32[96,70,128]{2,1,0:T(8,128)} %reshape.194), kind=kOutput, calls=%fused_computation.35 | convolution fusion | flops 2644131840 | bytes 26378240 | tf_op jit(solution)/shard_map/bjrc,bjcd->brd/dot_general | solution.py:98
  133.4 2.2 scatter_fusion.2
  135.6 3.7 %multiply_subtract_fusion.4 = f32[70,96,128]{2,1,0:T(8,128)S(1)} fusion(f32[70,96,128]{2,1,0:T(8,128)} %copy-done.3, f32[70,96,128]{2,1,0:T(8,128)} %scatter_fusion.2), kind=kLoop, calls=%fused_computation.47 | loop fusion | flops 1720320 | bytes 10321920 | tf_op jit(solution)/shard_map/sub | solution.py:105
  139.3 1.8 copy-done.4
  141.0 1.9 collective-permute-start.13
  142.9 5.8 %gather_fusion.6 = f32[140,96,128]{2,1,0:T(8,128)} fusion(f32[70,96,128]{2,1,0:T(8,128)} %copy-done.4, s32[1024]{0:T(1024)S(1)} %pad_clamp_fusion.1), kind=kCustom, calls=%fused_computation.6 | custom fusion | bytes 13763120 | tf_op jit(solution)/shard_map/gather | solution.py:97
  148.7 17.1 %fusion.4 = f32[70,96,128]{2,1,0:T(8,128)} fusion(f32[70,96,128]{2,1,0:T(8,128)} %copy-done.4, f32[70,2,96,128]{3,2,1,0:T(8,128)} %bitcast.109, f32[70,2,128,128]{3,2,1,0:T(8,128)} %param.16, f32[96,70,128]{2,1,0:T(8,128)} %reshape.194), kind=kOutput, calls=%fused_computation.33 | convolution fusion | flops 2644131840 | bytes 26378240 | tf_op jit(solution)/shard_map/bjrc,bjcd->brd/dot_general | solution.py:98
  166.9 2.2 scatter_fusion.3
  169.1 3.7 %multiply_subtract_fusion.3 = f32[70,96,128]{2,1,0:T(8,128)S(1)} fusion(f32[70,96,128]{2,1,0:T(8,128)} %copy-done.4, f32[70,96,128]{2,1,0:T(8,128)} %scatter_fusion.3), kind=kLoop, calls=%fused_computation.46 | loop fusion | flops 1720320 | bytes 10321920 | tf_op jit(solution)/shard_map/sub | solution.py:105
  172.9 1.8 copy-done.5
  174.6 1.9 collective-permute-start.15
  176.6 5.8 %gather_fusion.8 = f32[140,96,128]{2,1,0:T(8,128)} fusion(f32[70,96,128]{2,1,0:T(8,128)} %copy-done.5, s32[1024]{0:T(1024)S(1)} %pad_clamp_fusion.1), kind=kCustom, calls=%fused_computation.8 | custom fusion | bytes 13763120 | tf_op jit(solution)/shard_map/gather | solution.py:97
  182.3 17.1 %fusion.3 = f32[70,96,128]{2,1,0:T(8,128)} fusion(f32[70,96,128]{2,1,0:T(8,128)} %copy-done.5, f32[70,2,96,128]{3,2,1,0:T(8,128)} %bitcast.110, f32[70,2,128,128]{3,2,1,0:T(8,128)} %param.16, f32[96,70,128]{2,1,0:T(8,128)} %reshape.194), kind=kOutput, calls=%fused_computation.31 | convolution fusion | flops 2644131840 | bytes 26378240 | tf_op jit(solution)/shard_map/bjrc,bjcd->brd/dot_general | solution.py:98
  200.6 2.2 scatter_fusion.4
  202.7 3.7 %multiply_subtract_fusion.2 = f32[70,96,128]{2,1,0:T(8,128)S(1)} fusion(f32[70,96,128]{2,1,0:T(8,128)} %copy-done.5, f32[70,96,128]{2,1,0:T(8,128)} %scatter_fusion.4), kind=kLoop, calls=%fused_computation.45 | loop fusion | flops 1720320 | bytes 10321920 | tf_op jit(solution)/shard_map/sub | solution.py:105
  206.5 1.8 copy-done.6
  208.2 2.1 collective-permute-start.17
  210.4 5.8 %gather_fusion.10 = f32[140,96,128]{2,1,0:T(8,128)} fusion(f32[70,96,128]{2,1,0:T(8,128)} %copy-done.6, s32[1024]{0:T(1024)S(1)} %pad_clamp_fusion.1), kind=kCustom, calls=%fused_computation.10 | custom fusion | bytes 13763120 | tf_op jit(solution)/shard_map/gather | solution.py:97
  216.1 17.1 %fusion.2 = f32[70,96,128]{2,1,0:T(8,128)} fusion(f32[70,96,128]{2,1,0:T(8,128)} %copy-done.6, f32[70,2,96,128]{3,2,1,0:T(8,128)} %bitcast.111, f32[70,2,128,128]{3,2,1,0:T(8,128)} %param.16, f32[96,70,128]{2,1,0:T(8,128)} %reshape.194), kind=kOutput, calls=%fused_computation.29 | convolution fusion | flops 2644131840 | bytes 26378240 | tf_op jit(solution)/shard_map/bjrc,bjcd->brd/dot_general | solution.py:98
  234.4 2.2 scatter_fusion.5
  236.5 3.7 %multiply_subtract_fusion.1 = f32[70,96,128]{2,1,0:T(8,128)S(1)} fusion(f32[70,96,128]{2,1,0:T(8,128)} %copy-done.6, f32[70,96,128]{2,1,0:T(8,128)} %scatter_fusion.5), kind=kLoop, calls=%fused_computation.44 | loop fusion | flops 1720320 | bytes 10321920 | tf_op jit(solution)/shard_map/sub | solution.py:105
  240.3 1.8 copy-done.7
  242.0 1.9 collective-permute-start.19
  243.9 5.8 %gather_fusion.12 = f32[140,96,128]{2,1,0:T(8,128)} fusion(f32[70,96,128]{2,1,0:T(8,128)} %copy-done.7, s32[1024]{0:T(1024)S(1)} %pad_clamp_fusion.1), kind=kCustom, calls=%fused_computation.12 | custom fusion | bytes 13763120 | tf_op jit(solution)/shard_map/gather | solution.py:97
  249.7 17.1 %fusion.1 = f32[70,96,128]{2,1,0:T(8,128)} fusion(f32[70,96,128]{2,1,0:T(8,128)} %copy-done.7, f32[70,2,96,128]{3,2,1,0:T(8,128)} %bitcast.112, f32[70,2,128,128]{3,2,1,0:T(8,128)} %param.16, f32[96,70,128]{2,1,0:T(8,128)} %reshape.194), kind=kOutput, calls=%fused_computation.27 | convolution fusion | flops 2644131840 | bytes 26378240 | tf_op jit(solution)/shard_map/bjrc,bjcd->brd/dot_general | solution.py:98
  267.9 2.2 scatter_fusion.6
  270.1 3.7 %multiply_subtract_fusion = f32[70,96,128]{2,1,0:T(8,128)S(1)} fusion(f32[70,96,128]{2,1,0:T(8,128)} %copy-done.7, f32[70,96,128]{2,1,0:T(8,128)} %scatter_fusion.6), kind=kLoop, calls=%fused_computation.43 | loop fusion | flops 1720320 | bytes 10321920 | tf_op jit(solution)/shard_map/sub | solution.py:105
  273.8 1.8 copy-done.1
  275.6 1.9 collective-permute-start.21
  277.5 5.8 %gather_fusion.14 = f32[140,96,128]{2,1,0:T(8,128)} fusion(f32[70,96,128]{2,1,0:T(8,128)} %copy-done.1, s32[1024]{0:T(1024)S(1)} %pad_clamp_fusion.1), kind=kCustom, calls=%fused_computation.14 | custom fusion | bytes 13763120 | tf_op jit(solution)/shard_map/gather | solution.py:97
  283.3 17.1 %fusion = f32[70,96,128]{2,1,0:T(8,128)} fusion(f32[70,96,128]{2,1,0:T(8,128)} %copy-done.1, f32[70,2,96,128]{3,2,1,0:T(8,128)} %bitcast.106, f32[70,2,128,128]{3,2,1,0:T(8,128)} %param.16, f32[96,70,128]{2,1,0:T(8,128)} %reshape.194), kind=kOutput, calls=%fused_computation.25 | convolution fusion | flops 2644131840 | bytes 26378240 | tf_op jit(solution)/shard_map/bjrc,bjcd->brd/dot_general | solution.py:98
  301.5 2.4 scatter_fusion.7
  304.0 3.7 %subtract_bitcast_fusion = f32[96,70,128]{2,0,1:T(8,128)S(1)} fusion(f32[70,96,128]{2,1,0:T(8,128)} %copy-done.1, f32[70,96,128]{2,1,0:T(8,128)} %scatter_fusion.7), kind=kLoop, calls=%fused_computation.42 | loop fusion | flops 1720320 | bytes 10321920 | tf_op jit(solution)/shard_map/transpose | solution.py:106
  317.8 5.7 %copy.35 = f32[96,70,128]{2,1,0:T(8,128)} copy(f32[96,70,128]{2,0,1:T(8,128)} %copy-done.8) | data formatting | bytes 6881280 | tf_op jit(solution)/shard_map/transpose | solution.py:106
  325.2 5.1 %reshape.195 = f32[24,4,8960]{2,1,0:T(4,128)} reshape(f32[96,70,128]{2,1,0:T(8,128)} %copy.35) | data formatting | bytes 6881280 | tf_op jit(solution)/shard_map/reshape | solution.py:106
  335.7 2.3 collective-permute-done.23
  338.1 4.1 %collective-permute-start.24 = (f32[2,8960]{1,0:T(2,128)S(1)}, f32[2,8960]{1,0:T(2,128)S(1)}, u32[]{:S(2)}, u32[]{:S(2)}) collective-permute-start(f32[2,8960]{1,0:T(2,128)S(1)} %add.201), channel_id=1, source_target_pairs={{0,4},{4,0},{1,5},{5,1},{2,6},{6,2},{3,7},{7,3},{8,12},{12,8},{9,1... | collective-permute-start | bytes 215048 | tf_op jit(solution)/shard_map/ppermute | solution.py:21
  342.2 2.3 collective-permute-done.24
  345.2 2.2 subtract_add_fusion
  (184 shorter events, 30.9 us)
Async XLA Ops:
  0.6 28.4 %copy-start = (f32[4,128,128]{2,1,0:T(8,128)S(1)}, f32[4,128,128]{2,1,0:T(8,128)}, u32[]{:S(2)}) copy-start(f32[4,128,128]{2,1,0:T(8,128)} %param.21) | copy-start | bytes 786436
  1.3 15.2 %copy-start.18 = (s32[4]{0:T(128)S(1)}, s32[4]{0:T(128)}, u32[]{:S(2)}) copy-start(s32[4]{0:T(128)} %param.19) | copy-start | bytes 52
  6.6 10.7 %copy-start.15 = (s32[12,4]{0,1:T(4,128)S(1)}, s32[12,4]{0,1:T(4,128)}, u32[]{:S(2)}) copy-start(s32[12,4]{0,1:T(4,128)} %param.15) | copy-start | bytes 580
  6.6 10.8 %copy-start.16 = (s32[70,2]{0,1:T(2,128)S(1)}, s32[70,2]{0,1:T(2,128)}, u32[]{:S(2)}) copy-start(s32[70,2]{0,1:T(2,128)} %param.17) | copy-start | bytes 1684
  6.6 11.1 %copy-start.19 = (s32[4]{0:T(128)S(1)}, s32[4]{0:T(128)}, u32[]{:S(2)}) copy-start(s32[4]{0:T(128)} %param.20) | copy-start | bytes 52
  6.6 11.1 %copy-start.17 = (f32[32]{0:T(128)S(1)}, f32[32]{0:T(128)}, u32[]{:S(2)}) copy-start(f32[32]{0:T(128)} %param.14) | copy-start | bytes 388
  7.7 20.8 %collective-permute-start.6 = (f32[1,96,128]{2,1,0:T(8,128)S(1)}, f32[1,96,128]{2,1,0:T(8,128)S(1)}, u32[]{:S(2)}, u32[]{:S(2)}) collective-permute-start(f32[1,96,128]{2,1,0:T(8,128)S(1)} %bitcast.118), channel_id=1, source_target_pairs={{0,8},{8,16},{16,24},{24,0},{1,9},{9,17},{17,25},{25,1},{2,10},{10... | collective-permute-start | bytes 147464 | tf_op jit(solution)/shard_map/ppermute | solution.py:26
  8.2 20.3 %collective-permute-start.7 = (f32[1,96,128]{2,1,0:T(8,128)S(1)}, f32[1,96,128]{2,1,0:T(8,128)S(1)}, u32[]{:S(2)}, u32[]{:S(2)}) collective-permute-start(f32[1,96,128]{2,1,0:T(8,128)S(1)} %bitcast.119), channel_id=1, source_target_pairs={{0,24},{8,0},{16,8},{24,16},{1,25},{9,1},{17,9},{25,17},{2,26},{10... | collective-permute-start | bytes 147464 | tf_op jit(solution)/shard_map/ppermute | solution.py:26
  12.2 17.2 %collective-permute-start = (f32[2,8960]{1,0:T(2,128)S(1)}, f32[2,8960]{1,0:T(2,128)S(1)}, u32[]{:S(2)}, u32[]{:S(2)}) collective-permute-start(f32[2,8960]{1,0:T(2,128)S(1)} %get-tuple-element.93), channel_id=1, source_target_pairs={{0,1},{1,0},{2,3},{3,2},{4,5},{5,4},{6,7},{7,6},{8,9},{9,8},{10,11... | collective-permute-start | bytes 215048 | tf_op jit(solution)/shard_map/ppermute | solution.py:21
  14.5 16.7 %collective-permute-start.3 = (f32[2,8960]{1,0:T(2,128)S(1)}, f32[2,8960]{1,0:T(2,128)S(1)}, u32[]{:S(2)}, u32[]{:S(2)}) collective-permute-start(f32[2,8960]{1,0:T(2,128)S(1)} %get-tuple-element.92), channel_id=1, source_target_pairs={{0,1},{1,0},{2,3},{3,2},{4,5},{5,4},{6,7},{7,6},{8,9},{9,8},{10,11... | collective-permute-start | bytes 215048 | tf_op jit(solution)/shard_map/ppermute | solution.py:21
  14.6 17.2 %collective-permute-start.5 = (f32[2,8960]{1,0:T(2,128)S(1)}, f32[2,8960]{1,0:T(2,128)S(1)}, u32[]{:S(2)}, u32[]{:S(2)}) collective-permute-start(f32[2,8960]{1,0:T(2,128)S(1)} %get-tuple-element.91), channel_id=1, source_target_pairs={{0,1},{1,0},{2,3},{3,2},{4,5},{5,4},{6,7},{7,6},{8,9},{9,8},{10,11... | collective-permute-start | bytes 215048 | tf_op jit(solution)/shard_map/ppermute | solution.py:21
  16.5 11.9 %copy-start.14 = (s32[1024]{0:T(1024)}, s32[1024]{0:T(1024)S(1)}, u32[]{:S(2)}) copy-start(s32[1024]{0:T(1024)S(1)} %pad_clamp_fusion) | copy-start | bytes 12292
  29.0 10.9 %copy-start.9 = (f32[24,4,8960]{2,1,0:T(4,128)S(1)}, f32[24,4,8960]{2,1,0:T(4,128)}, u32[]{:S(2)}) copy-start(f32[24,4,8960]{2,1,0:T(4,128)} %param.11) | copy-start | bytes 10321924
  29.5 4.7 %collective-permute-start.1 = (f32[2,8960]{1,0:T(2,128)S(1)}, f32[2,8960]{1,0:T(2,128)S(1)}, u32[]{:S(2)}, u32[]{:S(2)}) collective-permute-start(f32[2,8960]{1,0:T(2,128)S(1)} %add.174), channel_id=1, source_target_pairs={{0,2},{2,0},{1,3},{3,1},{4,6},{6,4},{5,7},{7,5},{8,10},{10,8},{9,1... | collective-permute-start | bytes 215048 | tf_op jit(solution)/shard_map/ppermute | solution.py:21
  31.2 9.0 %copy-start.10 = (f32[24,4,8960]{2,1,0:T(4,128)S(1)}, f32[24,4,8960]{2,1,0:T(4,128)}, u32[]{:S(2)}) copy-start(f32[24,4,8960]{2,1,0:T(4,128)} %param.12) | copy-start | bytes 10321924
  31.2 9.0 %copy-start.13 = (f32[24,8960]{1,0:T(8,128)S(1)}, f32[24,8960]{1,0:T(8,128)}, u32[]{:S(2)}) copy-start(f32[24,8960]{1,0:T(8,128)} %param.13) | copy-start | bytes 2580484
  31.2 5.7 %collective-permute-start.4 = (f32[2,8960]{1,0:T(2,128)S(1)}, f32[2,8960]{1,0:T(2,128)S(1)}, u32[]{:S(2)}, u32[]{:S(2)}) collective-permute-start(f32[2,8960]{1,0:T(2,128)S(1)} %add.177), channel_id=1, source_target_pairs={{0,2},{2,0},{1,3},{3,1},{4,6},{6,4},{5,7},{7,5},{8,10},{10,8},{9,1... | collective-permute-start | bytes 215048 | tf_op jit(solution)/shard_map/ppermute | solution.py:21
  34.2 5.3 %collective-permute-start.2 = (f32[2,8960]{1,0:T(2,128)S(1)}, f32[2,8960]{1,0:T(2,128)S(1)}, u32[]{:S(2)}, u32[]{:S(2)}) collective-permute-start(f32[2,8960]{1,0:T(2,128)S(1)} %add.175), channel_id=1, source_target_pairs={{0,4},{4,0},{1,5},{5,1},{2,6},{6,2},{3,7},{7,3},{8,12},{12,8},{9,1... | collective-permute-start | bytes 215048 | tf_op jit(solution)/shard_map/ppermute | solution.py:21
  71.9 1.8 copy-start.2
  73.6 24.8 %collective-permute-start.8 = (f32[1,96,128]{2,1,0:T(8,128)S(1)}, f32[1,96,128]{2,1,0:T(8,128)S(1)}, u32[]{:S(2)}, u32[]{:S(2)}) collective-permute-start(f32[1,96,128]{2,1,0:T(8,128)S(1)} %constant_dynamic-slice_fusion.6), channel_id=1, source_target_pairs={{0,8},{8,16},{16,24},{24,0},{1,9},{9,17},{17,25},{25,1},{2,10},{10... | collective-permute-start | bytes 147464 | tf_op jit(solution)/shard_map/ppermute | solution.py:26
  73.6 24.8 %collective-permute-start.9 = (f32[1,96,128]{2,1,0:T(8,128)S(1)}, f32[1,96,128]{2,1,0:T(8,128)S(1)}, u32[]{:S(2)}, u32[]{:S(2)}) collective-permute-start(f32[1,96,128]{2,1,0:T(8,128)S(1)} %constant_dynamic-slice_fusion.6), channel_id=1, source_target_pairs={{0,24},{8,0},{16,8},{24,16},{1,25},{9,1},{17,9},{25,17},{2,26},{10... | collective-permute-start | bytes 147464 | tf_op jit(solution)/shard_map/ppermute | solution.py:26
  105.5 1.8 copy-start.3
  107.2 25.0 %collective-permute-start.10 = (f32[1,96,128]{2,1,0:T(8,128)S(1)}, f32[1,96,128]{2,1,0:T(8,128)S(1)}, u32[]{:S(2)}, u32[]{:S(2)}) collective-permute-start(f32[1,96,128]{2,1,0:T(8,128)S(1)} %constant_dynamic-slice_fusion.5), channel_id=1, source_target_pairs={{0,8},{8,16},{16,24},{24,0},{1,9},{9,17},{17,25},{25,1},{2,10},{10... | collective-permute-start | bytes 147464 | tf_op jit(solution)/shard_map/ppermute | solution.py:26
  107.2 25.0 %collective-permute-start.11 = (f32[1,96,128]{2,1,0:T(8,128)S(1)}, f32[1,96,128]{2,1,0:T(8,128)S(1)}, u32[]{:S(2)}, u32[]{:S(2)}) collective-permute-start(f32[1,96,128]{2,1,0:T(8,128)S(1)} %constant_dynamic-slice_fusion.5), channel_id=1, source_target_pairs={{0,24},{8,0},{16,8},{24,16},{1,25},{9,1},{17,9},{25,17},{2,26},{10... | collective-permute-start | bytes 147464 | tf_op jit(solution)/shard_map/ppermute | solution.py:26
  139.3 1.8 copy-start.4
  141.0 24.8 %collective-permute-start.12 = (f32[1,96,128]{2,1,0:T(8,128)S(1)}, f32[1,96,128]{2,1,0:T(8,128)S(1)}, u32[]{:S(2)}, u32[]{:S(2)}) collective-permute-start(f32[1,96,128]{2,1,0:T(8,128)S(1)} %constant_dynamic-slice_fusion.4), channel_id=1, source_target_pairs={{0,8},{8,16},{16,24},{24,0},{1,9},{9,17},{17,25},{25,1},{2,10},{10... | collective-permute-start | bytes 147464 | tf_op jit(solution)/shard_map/ppermute | solution.py:26
  141.0 24.8 %collective-permute-start.13 = (f32[1,96,128]{2,1,0:T(8,128)S(1)}, f32[1,96,128]{2,1,0:T(8,128)S(1)}, u32[]{:S(2)}, u32[]{:S(2)}) collective-permute-start(f32[1,96,128]{2,1,0:T(8,128)S(1)} %constant_dynamic-slice_fusion.4), channel_id=1, source_target_pairs={{0,24},{8,0},{16,8},{24,16},{1,25},{9,1},{17,9},{25,17},{2,26},{10... | collective-permute-start | bytes 147464 | tf_op jit(solution)/shard_map/ppermute | solution.py:26
  172.8 1.8 copy-start.5
  174.6 24.8 %collective-permute-start.14 = (f32[1,96,128]{2,1,0:T(8,128)S(1)}, f32[1,96,128]{2,1,0:T(8,128)S(1)}, u32[]{:S(2)}, u32[]{:S(2)}) collective-permute-start(f32[1,96,128]{2,1,0:T(8,128)S(1)} %constant_dynamic-slice_fusion.3), channel_id=1, source_target_pairs={{0,8},{8,16},{16,24},{24,0},{1,9},{9,17},{17,25},{25,1},{2,10},{10... | collective-permute-start | bytes 147464 | tf_op jit(solution)/shard_map/ppermute | solution.py:26
  174.6 24.8 %collective-permute-start.15 = (f32[1,96,128]{2,1,0:T(8,128)S(1)}, f32[1,96,128]{2,1,0:T(8,128)S(1)}, u32[]{:S(2)}, u32[]{:S(2)}) collective-permute-start(f32[1,96,128]{2,1,0:T(8,128)S(1)} %constant_dynamic-slice_fusion.3), channel_id=1, source_target_pairs={{0,24},{8,0},{16,8},{24,16},{1,25},{9,1},{17,9},{25,17},{2,26},{10... | collective-permute-start | bytes 147464 | tf_op jit(solution)/shard_map/ppermute | solution.py:26
  206.5 1.8 copy-start.6
  208.2 25.0 %collective-permute-start.16 = (f32[1,96,128]{2,1,0:T(8,128)S(1)}, f32[1,96,128]{2,1,0:T(8,128)S(1)}, u32[]{:S(2)}, u32[]{:S(2)}) collective-permute-start(f32[1,96,128]{2,1,0:T(8,128)S(1)} %constant_dynamic-slice_fusion.2), channel_id=1, source_target_pairs={{0,8},{8,16},{16,24},{24,0},{1,9},{9,17},{17,25},{25,1},{2,10},{10... | collective-permute-start | bytes 147464 | tf_op jit(solution)/shard_map/ppermute | solution.py:26
  208.2 25.0 %collective-permute-start.17 = (f32[1,96,128]{2,1,0:T(8,128)S(1)}, f32[1,96,128]{2,1,0:T(8,128)S(1)}, u32[]{:S(2)}, u32[]{:S(2)}) collective-permute-start(f32[1,96,128]{2,1,0:T(8,128)S(1)} %constant_dynamic-slice_fusion.2), channel_id=1, source_target_pairs={{0,24},{8,0},{16,8},{24,16},{1,25},{9,1},{17,9},{25,17},{2,26},{10... | collective-permute-start | bytes 147464 | tf_op jit(solution)/shard_map/ppermute | solution.py:26
  240.3 1.8 copy-start.7
  242.0 24.8 %collective-permute-start.18 = (f32[1,96,128]{2,1,0:T(8,128)S(1)}, f32[1,96,128]{2,1,0:T(8,128)S(1)}, u32[]{:S(2)}, u32[]{:S(2)}) collective-permute-start(f32[1,96,128]{2,1,0:T(8,128)S(1)} %constant_dynamic-slice_fusion.1), channel_id=1, source_target_pairs={{0,8},{8,16},{16,24},{24,0},{1,9},{9,17},{17,25},{25,1},{2,10},{10... | collective-permute-start | bytes 147464 | tf_op jit(solution)/shard_map/ppermute | solution.py:26
  242.0 24.8 %collective-permute-start.19 = (f32[1,96,128]{2,1,0:T(8,128)S(1)}, f32[1,96,128]{2,1,0:T(8,128)S(1)}, u32[]{:S(2)}, u32[]{:S(2)}) collective-permute-start(f32[1,96,128]{2,1,0:T(8,128)S(1)} %constant_dynamic-slice_fusion.1), channel_id=1, source_target_pairs={{0,24},{8,0},{16,8},{24,16},{1,25},{9,1},{17,9},{25,17},{2,26},{10... | collective-permute-start | bytes 147464 | tf_op jit(solution)/shard_map/ppermute | solution.py:26
  273.8 1.8 copy-start.1
  275.6 24.8 %collective-permute-start.20 = (f32[1,96,128]{2,1,0:T(8,128)S(1)}, f32[1,96,128]{2,1,0:T(8,128)S(1)}, u32[]{:S(2)}, u32[]{:S(2)}) collective-permute-start(f32[1,96,128]{2,1,0:T(8,128)S(1)} %constant_dynamic-slice_fusion), channel_id=1, source_target_pairs={{0,8},{8,16},{16,24},{24,0},{1,9},{9,17},{17,25},{25,1},{2,10},{10... | collective-permute-start | bytes 147464 | tf_op jit(solution)/shard_map/ppermute | solution.py:26
  275.6 24.8 %collective-permute-start.21 = (f32[1,96,128]{2,1,0:T(8,128)S(1)}, f32[1,96,128]{2,1,0:T(8,128)S(1)}, u32[]{:S(2)}, u32[]{:S(2)}) collective-permute-start(f32[1,96,128]{2,1,0:T(8,128)S(1)} %constant_dynamic-slice_fusion), channel_id=1, source_target_pairs={{0,24},{8,0},{16,8},{24,16},{1,25},{9,1},{17,9},{25,17},{2,26},{10... | collective-permute-start | bytes 147464 | tf_op jit(solution)/shard_map/ppermute | solution.py:26
  307.7 2.0 copy-start.8
  310.0 24.4 %collective-permute-start.27 = (f32[2,8960]{1,0:T(2,128)S(1)}, f32[2,8960]{1,0:T(2,128)}, u32[]{:S(2)}, u32[]{:S(2)}) collective-permute-start(f32[2,8960]{1,0:T(2,128)S(1)} %reduce_sum.111), channel_id=1, source_target_pairs={{0,1},{1,0},{2,3},{3,2},{4,5},{5,4},{6,7},{7,6},{8,9},{9,8},{10,11... | collective-permute-start | bytes 215048 | tf_op jit(solution)/shard_map/ppermute | solution.py:21
  312.6 17.7 %collective-permute-start.25 = (f32[2,8960]{1,0:T(2,128)}, f32[2,8960]{1,0:T(2,128)}, u32[]{:S(2)}, u32[]{:S(2)}) collective-permute-start(f32[2,8960]{1,0:T(2,128)} %reduce_sum.107), channel_id=1, source_target_pairs={{0,1},{1,0},{2,3},{3,2},{4,5},{5,4},{6,7},{7,6},{8,9},{9,8},{10,11... | collective-permute-start | bytes 215048 | tf_op jit(solution)/shard_map/ppermute | solution.py:21
  316.1 16.6 %collective-permute-start.22 = (f32[2,8960]{1,0:T(2,128)}, f32[2,8960]{1,0:T(2,128)}, u32[]{:S(2)}, u32[]{:S(2)}) collective-permute-start(f32[2,8960]{1,0:T(2,128)} %reduce_sum.106), channel_id=1, source_target_pairs={{0,1},{1,0},{2,3},{3,2},{4,5},{5,4},{6,7},{7,6},{8,9},{9,8},{10,11... | collective-permute-start | bytes 215048 | tf_op jit(solution)/shard_map/ppermute | solution.py:21
  331.3 10.9 %collective-permute-start.26 = (f32[2,8960]{1,0:T(2,128)S(1)}, f32[2,8960]{1,0:T(2,128)S(1)}, u32[]{:S(2)}, u32[]{:S(2)}) collective-permute-start(f32[2,8960]{1,0:T(2,128)S(1)} %add.203), channel_id=1, source_target_pairs={{0,2},{2,0},{1,3},{3,1},{4,6},{6,4},{5,7},{7,5},{8,10},{10,8},{9,1... | collective-permute-start | bytes 215048 | tf_op jit(solution)/shard_map/ppermute | solution.py:21
  333.6 11.6 %copy-start.11 = (f32[24,4,8960]{2,1,0:T(4,128)S(1)}, f32[24,4,8960]{2,1,0:T(4,128)}, u32[]{:S(2)}) copy-start(f32[24,4,8960]{2,1,0:T(4,128)} %param.12) | copy-start | bytes 10321924
  333.6 11.6 %copy-start.12 = (f32[24,4,8960]{2,1,0:T(4,128)S(1)}, f32[24,4,8960]{2,1,0:T(4,128)}, u32[]{:S(2)}) copy-start(f32[24,4,8960]{2,1,0:T(4,128)} %reshape.195) | copy-start | bytes 10321924
  333.6 4.4 %collective-permute-start.23 = (f32[2,8960]{1,0:T(2,128)S(1)}, f32[2,8960]{1,0:T(2,128)S(1)}, u32[]{:S(2)}, u32[]{:S(2)}) collective-permute-start(f32[2,8960]{1,0:T(2,128)S(1)} %add.200), channel_id=1, source_target_pairs={{0,2},{2,0},{1,3},{3,1},{4,6},{6,4},{5,7},{7,5},{8,10},{10,8},{9,1... | collective-permute-start | bytes 215048 | tf_op jit(solution)/shard_map/ppermute | solution.py:21
  338.1 6.4 %collective-permute-start.24 = (f32[2,8960]{1,0:T(2,128)S(1)}, f32[2,8960]{1,0:T(2,128)S(1)}, u32[]{:S(2)}, u32[]{:S(2)}) collective-permute-start(f32[2,8960]{1,0:T(2,128)S(1)} %add.201), channel_id=1, source_target_pairs={{0,4},{4,0},{1,5},{5,1},{2,6},{6,2},{3,7},{7,3},{8,12},{12,8},{9,1... | collective-permute-start | bytes 215048 | tf_op jit(solution)/shard_map/ppermute | solution.py:21
where the time goes:
time: 355 us; the launch traced here: 348 us
  matrix products  140 us (39%)
  local copies, waits for them, and re-layouts  99.2 us (28%)
  other arithmetic  62 us (17%)
  starting transfers between devices  34.3 us (10%)
  waiting for transfers between devices  9.61 us (3%)
    dot_general x8, matrix products, local(): jnp.einsum('bjrc,bjcd->brd', pieces, block_values, precision=full_precision)  137 us
    gather x8, local copies, waits for them, and re-layouts, local(): pieces = state[block_cols]  46.2 us
    sub x7, other arithmetic, local(): state - step_size * (product.at[tie_row].add(coupled) + constant + penalt...  26.4 us
    ppermute x12, starting transfers between devices, from_partner(): return lax.ppermute(block, axis, route)  17.9 us
    scatter-add x8, other arithmetic, local(): product.at[tie_row].add(coupled) + constant + penalty * state  17.6 us
    ppermute x16, starting transfers between devices, from_behind(): lax.ppermute(value, axis, [(i, (i + by) % count) for i in range(count)])  16.4 us
    unnamed x58, local copies, waits for them, and re-layouts  15.1 us
    reshape x3, local copies, waits for them, and re-layouts, to_blocks(): return field.reshape(row_total, block_count, block_width).transpose(1, 0, 2)  14.9 us
  transfers between devices with their start and end apart: 28, of which 4 were waited for; matrix products, arithmetic and copies ran while one was open for 56% of the time, Pallas kernels for 0%

commit v1 on v0

v1 whole, which is shorter than its diff:
```python
import functools

import jax
import jax.numpy as jnp
from jax import lax
from jax.experimental import pallas as pl
from jax.experimental.pallas import tpu as pltpu
from jax.sharding import PartitionSpec as P

STEPS = 8
step_size = 0.25
penalty = 1.0
keep = 1.0 - step_size * penalty

f32 = jnp.float32
bf16 = jnp.bfloat16
VMEM = pltpu.VMEM
SMEM = pltpu.SMEM
MIB = 1 << 20


def in_vmem(array):
    return pltpu.with_memory_space_constraint(array, VMEM)


def in_smem(array):
    return pltpu.with_memory_space_constraint(array, SMEM)


def in_hbm(array):
    return pltpu.with_memory_space_constraint(array, pltpu.HBM)


vmem_spec = pl.BlockSpec(memory_space=VMEM)
smem_spec = pl.BlockSpec(memory_space=SMEM)
any_spec = pl.BlockSpec(memory_space=pl.ANY)


def params(mib):
    return pltpu.CompilerParams(vmem_limit_bytes=mib * MIB)


def cost(flops, moved):
    return pl.CostEstimate(flops=flops, bytes_accessed=moved, transcendentals=0)


def split(value):
    high = value.astype(bf16)
    return high, (value - high.astype(f32)).astype(bf16)


def store_split(ref, index, value):
    rows = value.shape[0]
    high, low = split(value)
    ref[index, 0:rows] = high
    ref[index, rows : 2 * rows] = low


def fold(product, rows):
    return (product[:rows, :128] + product[:rows, 128:]) + (product[rows:, :128] + product[rows:, 128:])


def lanes(block):
    return pl.ds(pl.multiple_of(block * 128, 128), 128)


def partner(value, apart):
    rows = value.shape[0]
    up = pltpu.roll(value, rows - apart, 0)
    down = pltpu.roll(value, apart, 0)
    place = lax.broadcasted_iota(jnp.int32, value.shape, 0)
    return jnp.where((place & apart) == 0, up, down)


def local_mean(value, members):
    total, apart = value, 1
    while apart < members:
        total = total + partner(total, apart)
        apart *= 2
    return total / members


def spread(pair, scenarios):
    count, width = pair.shape
    wide = jnp.broadcast_to(pair[:, None, :], (count, scenarios, width))
    return wide.reshape(count * scenarios, width)


def first_kernel(shared, per, cols, send, tie_row, start, *refs):
    sums, boundary = refs[:shared], refs[shared]
    cols_out, send_out, row_out = refs[shared + 1 : shared + 4]
    head, block, sems = refs[shared + 4 :]
    copy_head = pltpu.make_async_copy(start.at[0 : shared * per], head, sems.at[0])
    copy_block = pltpu.make_async_copy(start.at[:, :, lanes(send[0])], block, sems.at[1])
    copy_head.start()
    copy_block.start()

    def move(i, carry):
        cols_out[i] = cols[i]
        return carry

    lax.fori_loop(0, cols.shape[0], move, 0)
    send_out[0] = send[0]
    for m in range(tie_row.shape[0]):
        row_out[m] = tie_row[m]
    copy_block.wait()
    boundary[...] = block[...].reshape(boundary.shape)
    copy_head.wait()
    for k in range(shared):
        sums[k][...] = jnp.sum(head[k * per : (k + 1) * per], axis=1)


def add_kernel(count, *refs):
    for k in range(count):
        refs[2 * count + k][...] = refs[k][...] + refs[count + k][...]


def node_totals(sums):
    shared = len(sums)
    totals = list(sums)
    for turn in range(shared):
        active = [k for k in range(shared) if shared - k - 1 - turn >= 0]
        received = [swap(totals[k], "scen", shared - k - 1 - turn) for k in active]
        added = pl.pallas_call(
            functools.partial(add_kernel, len(active)),
            in_specs=[vmem_spec] * (2 * len(active)),
            out_specs=[vmem_spec] * len(active),
            out_shape=[VMEM(totals[k].shape, f32) for k in active],
            compiler_params=params(2),
            name=f"node_add_{turn}",
        )(*[in_vmem(totals[k]) for k in active], *[in_vmem(r) for r in received])
        for k, value in zip(active, added):
            totals[k] = value
    return totals


def swap(block, axis, level):
    count = lax.axis_size(axis)
    return lax.ppermute(block, axis, [(i, i ^ (1 << level)) for i in range(count)])


def from_behind(value, axis, by):
    count = lax.axis_size(axis)
    return lax.ppermute(value, axis, [(i, (i + by) % count) for i in range(count)])


def prepare_kernel(shared, per, scen_all, chunk, side, values, start, mult, demand, load, tie_weight,
                   weights, ties, state, parts, constant):
    step = pl.program_id(0)
    rows = state.shape[1]
    scenarios = start.shape[1]
    group = per * scenarios

    def one(b, carry):
        i = step * chunk + b
        for j in range(2):
            high, low = split(values[b, j] * -step_size)
            weights[i, j * 128 : (j + 1) * 128, 0:128] = high
            weights[i, j * 128 : (j + 1) * 128, 128:256] = low
        x = start[:, :, lanes(b)].reshape(rows, 128)
        m = mult[:, :, lanes(b)].reshape(rows, 128)
        target = spread(demand[:, lanes(b)], scenarios) * load[...]
        state[i] = x
        store_split(parts, i, x)
        rest = m - target
        for k in range(rows // group):
            cut = slice(k * group, (k + 1) * group)
            piece = rest[cut]
            members = max(scen_all >> k, 1)
            if k >= shared:
                piece = piece - penalty * local_mean(x[cut], members)
            constant[i, cut] = -step_size * piece
        return carry

    lax.fori_loop(0, chunk, one, 0, unroll=True)

    @pl.when(step == 0)
    def _():
        for m in range(tie_weight.shape[0]):
            high, low = split(tie_weight[m] * -step_size)
            below = jnp.full((128, 128), side[m], jnp.int32) == 0
            zero = jnp.zeros((128, 128), f32)
            for n, part in enumerate((high.astype(f32), low.astype(f32))):
                cut = slice(n * 128, (n + 1) * 128)
                ties[m, 0:128, cut] = jnp.where(below, part, zero).astype(bf16)
                ties[m, 128:256, cut] = jnp.where(below, zero, part).astype(bf16)


def step_kernel(cols, weights, state, parts, constant, new_state, new_parts):
    rows = state.shape[1]
    for i in range(state.shape[0]):
        other = cols[2 * i + 1]
        left = jnp.concatenate([parts[i], parts[other]], axis=1)
        product = jnp.dot(left, weights[i], preferred_element_type=f32)
        value = (keep * state[i] + constant[i]) + fold(product, rows)
        new_state[i] = value
        store_split(new_parts, i, value)


def add_ties(tie_row, low, high, ties, state, parts):
    rows = state.shape[1]
    both = jnp.concatenate([low[...], high[...]], axis=1)
    left = jnp.concatenate(split(both), axis=0)
    for m in range(ties.shape[0]):
        added = fold(jnp.dot(left, ties[m], preferred_element_type=f32), rows)
        row = tie_row[m]
        state[row] = state[row] + added
    for m in range(ties.shape[0]):
        row = tie_row[m]
        store_split(parts, row, state[row])


def tie_kernel(tie_row, send, low, high, ties, state_in, parts_in, state, parts, boundary):
    add_ties(tie_row, low, high, ties, state, parts)
    boundary[...] = state[send[0]]


def anchor_kernel(shared, scen_all, scenarios, tie_row, send, low, high, ties, *refs):
    totals = refs[:shared]
    state, parts, constant, boundary = refs[shared + 3 :]
    rows = state.shape[1]
    group = totals[0].shape[0] * scenarios
    span = min(-(-shared * group // 16) * 16, rows)

    def one(i, carry):
        for k in range(shared):
            cut = slice(k * group, (k + 1) * group)
            mean = spread(totals[k][:, lanes(i)], scenarios) / (scen_all >> k)
            mean = (step_size * penalty) * mean
            constant[i, cut] = constant[i, cut] + mean
            state[i, cut] = state[i, cut] + mean
        high_part, low_part = split(state[i, 0:span])
        parts[i, 0:span] = high_part
        parts[i, rows : rows + span] = low_part
        return carry

    lax.fori_loop(0, state.shape[0], one, 0, unroll=7)
    add_ties(tie_row, low, high, ties, state, parts)
    boundary[...] = state[send[0]]


def last_tie_kernel(shared, per, scenarios, tie_row, low, high, ties, state_in, parts_in, state, *refs):
    sums, parts = refs[:shared], refs[shared]
    add_ties(tie_row, low, high, ties, state, parts)
    group = per * scenarios

    def one(i, carry):
        for k in range(shared):
            piece = state[i, k * group : (k + 1) * group].reshape(per, scenarios, 128)
            sums[k][:, lanes(i)] = jnp.sum(piece, axis=1)
        return carry

    lax.fori_loop(0, state.shape[0], one, 0, unroll=7)


def output_kernel(shared, per, scen_all, chunk, state, mult, dispatch, new_mult):
    step = pl.program_id(0)
    rows = state.shape[1]
    periods, scenarios = mult.shape[:2]
    group = per * scenarios

    def one(b, carry):
        value = state[step * chunk + b]
        dispatch[:, :, lanes(b)] = value.reshape(periods, scenarios, 128)
        m = mult[:, :, lanes(b)].reshape(rows, 128)
        for k in range(rows // group):
            cut = slice(k * group, (k + 1) * group)
            members = max(scen_all >> k, 1)
            piece = m[cut]
            if k >= shared:
                piece = piece + penalty * (value[cut] - local_mean(value[cut], members))
            new_mult[k * per : (k + 1) * per, :, lanes(b)] = piece.reshape(per, scenarios, 128)
        return carry

    lax.fori_loop(0, chunk, one, 0, unroll=True)


def finish_kernel(shared, per, scen_all, state, *refs):
    totals = refs[:shared]
    new_in, new_mult, buffer, sems = refs[shared:]
    periods, scenarios = buffer.shape[:2]
    group = per * scenarios
    fetch = pltpu.make_async_copy(new_mult.at[0:periods], buffer, sems.at[0])
    fetch.start()
    fetch.wait()

    def one(i, carry):
        for k in range(shared):
            value = state[i, k * group : (k + 1) * group]
            mean = spread(totals[k][:, lanes(i)], scenarios) / (scen_all >> k)
            gap = penalty * (value - mean)
            cut = slice(k * per, (k + 1) * per)
            buffer[cut, :, lanes(i)] = buffer[cut, :, lanes(i)] + gap.reshape(per, scenarios, 128)
        return carry

    lax.fori_loop(0, state.shape[0], one, 0, unroll=7)
    back = pltpu.make_async_copy(buffer, new_mult.at[0:periods], sems.at[0])
    back.start()
    back.wait()


def largest_divisor(count, most):
    return max(d for d in range(1, most + 1) if count % d == 0)


def local(
    start_dispatch,
    multipliers,
    demand,
    load_factor,
    node_ids,
    block_values,
    block_cols,
    send_block,
    tie_source,
    tie_row,
    tie_weight,
):
    periods, scenarios, buses = start_dispatch.shape
    blocks = buses // 128
    rows = periods * scenarios
    sections = node_ids.shape[0]
    per = periods // sections
    devices = lax.axis_size("scen")
    scen_all = scenarios * devices
    shared = devices.bit_length() - 1
    tie_count = tie_row.shape[0]
    chunk = largest_divisor(blocks, 7)

    labels = jnp.arange(load_factor.shape[0], dtype=jnp.int32)
    matches = node_ids[:, :, None] == labels[None, None, :]
    load_rows = jnp.sum(jnp.where(matches, load_factor[None, None, :], 0.0), axis=2)
    load_rows = jnp.repeat(load_rows, per, axis=0).reshape(rows, 1)
    load_wide = jnp.broadcast_to(load_rows, (rows, 128))
    before = (lax.axis_index("area") - 1 + lax.axis_size("area")) % lax.axis_size("area")
    side = jnp.where(tie_source // send_block.shape[0] == before, 0, 1)

    first = pl.pallas_call(
        functools.partial(first_kernel, shared, per),
        in_specs=[smem_spec] * 3 + [any_spec],
        out_specs=[vmem_spec] * (shared + 1) + [smem_spec] * 3,
        out_shape=[VMEM((per, buses), f32)] * shared
        + [VMEM((rows, 128), f32), SMEM((2 * blocks,), jnp.int32), SMEM((1,), jnp.int32), SMEM((tie_count,), jnp.int32)],
        scratch_shapes=[
            VMEM((shared * per, scenarios, buses), f32),
            VMEM((periods, scenarios, 128), f32),
            pltpu.SemaphoreType.DMA((2,)),
        ],
        compiler_params=params(6),
        name="first_sums",
    )(block_cols.reshape(-1), send_block, tie_row, in_hbm(start_dispatch))
    sums, boundary = list(first[:shared]), first[shared]
    cols, send, row_of_tie = first[shared + 1 :]

    weights, ties, state, parts, constant = pl.pallas_call(
        functools.partial(prepare_kernel, shared, per, scen_all, chunk),
        grid=(blocks // chunk,),
        in_specs=[
            smem_spec,
            pl.BlockSpec((chunk, 2, 128, 128), lambda i: (i, 0, 0, 0)),
            pl.BlockSpec((periods, scenarios, chunk * 128), lambda i: (0, 0, i)),
            pl.BlockSpec((periods, scenarios, chunk * 128), lambda i: (0, 0, i)),
            pl.BlockSpec((periods, chunk * 128), lambda i: (0, i)),
            vmem_spec,
            vmem_spec,
        ],
        out_specs=[vmem_spec] * 5,
        out_shape=[
            VMEM((blocks, 256, 256), bf16),
            VMEM((tie_count, 256, 256), bf16),
            VMEM((blocks, rows, 128), f32),
            VMEM((blocks, 2 * rows, 128), bf16),
            VMEM((blocks, rows, 128), f32),
        ],
        compiler_params=params(10),
        cost_estimate=cost(10**9, 20 * 10**6),
        name="prepare",
    )(side, in_hbm(block_values), in_hbm(start_dispatch), in_hbm(multipliers), in_hbm(demand), load_wide, tie_weight)

    state_shape = VMEM((blocks, rows, 128), f32)
    parts_shape = VMEM((blocks, 2 * rows, 128), bf16)

    totals = node_totals(sums)
    for iteration in range(STEPS):
        low = from_behind(boundary, "area", 1)
        high = from_behind(boundary, "area", -1)
        state, parts = pl.pallas_call(
            step_kernel,
            in_specs=[smem_spec] + [vmem_spec] * 4,
            out_specs=[vmem_spec] * 2,
            out_shape=[state_shape, parts_shape],
            compiler_params=params(2),
            cost_estimate=cost(blocks * 2 * rows * 256 * 256 * 2, 12 * 10**6),
            name=f"step_{iteration}",
        )(in_smem(cols), in_vmem(weights), in_vmem(state), in_vmem(parts), in_vmem(constant))
        tie_args = [in_vmem(low), in_vmem(high), in_vmem(ties)]
        if iteration == 0:
            state, parts, constant, boundary = pl.pallas_call(
                functools.partial(anchor_kernel, shared, scen_all, scenarios),
                in_specs=[smem_spec] * 2 + [vmem_spec] * (6 + shared),
                out_specs=[vmem_spec] * 4,
                out_shape=[state_shape, parts_shape, state_shape, VMEM((rows, 128), f32)],
                input_output_aliases={5 + shared: 0, 6 + shared: 1, 7 + shared: 2},
                compiler_params=params(2),
                name="anchor",
            )(in_smem(row_of_tie), in_smem(send), *tie_args, *[in_vmem(t) for t in totals],
              in_vmem(state), in_vmem(parts), in_vmem(constant))
        elif iteration < STEPS - 1:
            state, parts, boundary = pl.pallas_call(
                tie_kernel,
                in_specs=[smem_spec] * 2 + [vmem_spec] * 5,
                out_specs=[vmem_spec] * 3,
                out_shape=[state_shape, parts_shape, VMEM((rows, 128), f32)],
                input_output_aliases={5: 0, 6: 1},
                compiler_params=params(2),
                name=f"ties_{iteration}",
            )(in_smem(row_of_tie), in_smem(send), *tie_args, in_vmem(state), in_vmem(parts))
        else:
            last = pl.pallas_call(
                functools.partial(last_tie_kernel, shared, per, scenarios),
                in_specs=[smem_spec] + [vmem_spec] * 5,
                out_specs=[vmem_spec] * (2 + shared),
                out_shape=[state_shape] + [VMEM((per, buses), f32)] * shared + [parts_shape],
                input_output_aliases={4: 0, 5: 1 + shared},
                compiler_params=params(2),
                name=f"ties_{iteration}",
            )(in_smem(row_of_tie), *tie_args, in_vmem(state), in_vmem(parts))
            state, sums = last[0], list(last[1 : 1 + shared])

    totals = node_totals(sums)
    block = pl.BlockSpec((periods, scenarios, chunk * 128), lambda i: (0, 0, i))
    whole = jax.ShapeDtypeStruct((periods, scenarios, buses), f32)
    dispatch, new_mult = pl.pallas_call(
        functools.partial(output_kernel, shared, per, scen_all, chunk),
        grid=(blocks // chunk,),
        in_specs=[vmem_spec, block],
        out_specs=[block, block],
        out_shape=[whole, whole],
        compiler_params=params(10),
        cost_estimate=cost(10**9, 12 * 10**6),
        name="outputs",
    )(in_vmem(state), in_hbm(multipliers))
    new_mult = pl.pallas_call(
        functools.partial(finish_kernel, shared, per, scen_all),
        in_specs=[vmem_spec] * (1 + shared) + [any_spec],
        out_specs=any_spec,
        out_shape=whole,
        input_output_aliases={1 + shared: 0},
        scratch_shapes=[VMEM((shared * per, scenarios, buses), f32), pltpu.SemaphoreType.DMA((1,))],
        compiler_params=params(6),
        name="finish",
    )(in_vmem(state), *[in_vmem(t) for t in totals], in_hbm(new_mult))
    return dispatch, new_mult


def solution(mesh):
    in_specs = (
        P(None, "scen", "area"),
        P(None, "scen", "area"),
        P(None, "area"),
        P(),
        P(None, "scen"),
        P("area", None, None, None),
        P("area", None),
        P("area"),
        P("area"),
        P("area"),
        P("area", None, None),
    )
    out_specs = (P(None, "scen", "area"), P(None, "scen", "area"))
    return jax.shard_map(local, mesh=mesh, in_specs=in_specs, out_specs=out_specs, check_vma=False)
```

time: 355 us -> 91 us (0.26); the launches traced: 348 us -> 90.4 us
  matrix products: 140 us -> 0 us
  local copies, waits for them, and re-layouts: 99.2 us -> 1.85 us
  other arithmetic: 62 us -> 0.16 us
  Pallas kernels: 0 us -> 45.2 us
  starting transfers between devices: 34.3 us -> 21 us
  waiting for transfers between devices: 9.61 us -> 20.4 us
    dot_general x16 -> x0, matrix products: 140 us -> none  [the longest x8 137 us: local(): jnp.einsum('bjrc,bjcd->brd', pieces, block_values, precision=full_precision)]
    gather x23 -> x0, local copies, waits for them, and re-layouts: 51.6 us -> none  [the longest x8 46.2 us: local(): pieces = state[block_cols]]
    pallas_call x0 -> x26, Pallas kernels: none -> 45.2 us  [the longest x8 18.8 us: local(): pl.pallas_call(step_kernel, in_specs=[smem_spec] + [vmem_spec] * 4, out_s...]
    sub x8 -> x0, other arithmetic: 29.4 us -> none  [the longest x7 26.4 us: local(): state - step_size * (product.at[tie_row].add(coupled) + constant + penalt...]
    reshape x16 -> x1, local copies, waits for them, and re-layouts: 21.8 us -> 0.13 us  [local(): block_cols.reshape(-1)]
    scatter-add x8 -> x0, other arithmetic: 17.6 us -> none  [local(): product.at[tie_row].add(coupled) + constant + penalty * state]
    unnamed x58 -> x12, local copies, waits for them, and re-layouts: 15.1 us -> 1.54 us
    ppermute x16, starting transfers between devices: 16.4 us -> 6.45 us  [from_behind(): lax.ppermute(value, axis, [(i, (i + by) % count) for i in range(count)])]
  transfers between devices with their start and end apart: 28 -> 28, of which waited for: 4 -> 15; matrix products, arithmetic and copies ran while one was open for 56% -> 0% of each run, Pallas kernels for 0% -> 41%
where the time goes in v1:
time: 91 us; the launch traced here: 90.4 us
  Pallas kernels  45.2 us (50%)
  starting transfers between devices  21 us (23%)
  waiting for transfers between devices  20.4 us (22%)
  local copies, waits for them, and re-layouts  1.85 us (2%)
  between operations  1.83 us (2%)
    pallas_call x8, Pallas kernels, local(): pl.pallas_call(step_kernel, in_specs=[smem_spec] + [vmem_spec] * 4, out_s...  18.8 us
    ppermute x12, starting transfers between devices, swap(): lax.ppermute(block, axis, [(i, i ^ 1 << level) for i in range(count)])  14.5 us
    ppermute x12, waiting for transfers between devices, swap(): lax.ppermute(block, axis, [(i, i ^ 1 << level) for i in range(count)])  11.9 us
    pallas_call x1, Pallas kernels, local(): pl.pallas_call(functools.partial(prepare_kernel, shared, per, scen_all, c...  10.3 us
    ppermute x16, waiting for transfers between devices, from_behind(): lax.ppermute(value, axis, [(i, (i + by) % count) for i in range(count)])  8.49 us
    pallas_call x1, Pallas kernels, local(): pl.pallas_call(functools.partial(output_kernel, shared, per, scen_all, ch...  7.89 us
    ppermute x16, starting transfers between devices, from_behind(): lax.ppermute(value, axis, [(i, (i + by) % count) for i in range(count)])  6.45 us
    pallas_call x1, Pallas kernels, local(): pl.pallas_call(functools.partial(finish_kernel, shared, per, scen_all), i...  2.52 us
  transfers between devices with their start and end apart: 28, of which 15 were waited for; matrix products, arithmetic and copies ran while one was open for 0% of the time, Pallas kernels for 41%

profile of v1, /device:TPU:0, one launch (start us, length us, event | category | flops | bytes accessed | tf_op | source)
XLA Modules:
  0.0 90.4 jit_solution(12706857816915315780)
XLA Ops:
  1.3 0.8 copy.34
  2.1 0.1 reshape.10.cols
  2.3 0.6 copy-done.1
  2.9 2.3 %first_sums.1 = (f32[2,8960]{1,0:T(2,128)S(1)}, f32[2,8960]{1,0:T(2,128)S(1)}, f32[2,8960]{1,0:T(2,128)S(1)}, f32[96,128]{1,0:T(8,128)S(1)}, s32[140]{0:T(256)S(4)}, /*index=5*/s32[1]{0:T(128)S(4)}, s32[4]{0:T(128)S(4)}) custom-call(s32[140]{0:T(256)S(1)} %reshape.10.cols, s32[1]{0:T(128)S(6)} %copy.54.send, s32[4]{0:T(128)S(1)} %copy-done.1, ...), custom_call_target="tpu_custom_call" | custom-call | tf_op jit(solution)/shard_map/first_sums/pallas_call | solution.py:338
  5.2 2.5 %collective-permute-start.1 = (f32[96,128]{1,0:T(8,128)S(1)}, f32[96,128]{1,0:T(8,128)S(1)}, u32[]{:S(2)}, u32[]{:S(2)}) collective-permute-start(f32[96,128]{1,0:T(8,128)S(1)} %get-tuple-element.70), channel_id=1, source_target_pairs={{0,24},{8,0},{16,8},{24,16},{1,25},{9,1},{17,9},{25,17},{2,26},{10... | collective-permute-start | bytes 147464 | tf_op jit(solution)/shard_map/ppermute | solution.py:144
  7.6 2.6 %collective-permute-start.2 = (f32[2,8960]{1,0:T(2,128)S(1)}, f32[2,8960]{1,0:T(2,128)S(1)}, u32[]{:S(2)}, u32[]{:S(2)}) collective-permute-start(f32[2,8960]{1,0:T(2,128)S(1)} %get-tuple-element.72.refs_0_), channel_id=1, source_target_pairs={{0,4},{1,5},{2,6},{3,7},{4,0},{5,1},{6,2},{7,3},{8,12},{9,13},{10,... | collective-permute-start | bytes 215048 | tf_op jit(solution)/shard_map/ppermute | solution.py:139
  10.2 1.6 %collective-permute-start.3 = (f32[2,8960]{1,0:T(2,128)S(1)}, f32[2,8960]{1,0:T(2,128)S(1)}, u32[]{:S(2)}, u32[]{:S(2)}) collective-permute-start(f32[2,8960]{1,0:T(2,128)S(1)} %get-tuple-element.73.refs_1_), channel_id=1, source_target_pairs={{0,2},{1,3},{2,0},{3,1},{4,6},{5,7},{6,4},{7,5},{8,10},{9,11},{10,... | collective-permute-start | bytes 215048 | tf_op jit(solution)/shard_map/ppermute | solution.py:139
  11.8 1.5 %collective-permute-start.4 = (f32[2,8960]{1,0:T(2,128)S(1)}, f32[2,8960]{1,0:T(2,128)S(1)}, u32[]{:S(2)}, u32[]{:S(2)}) collective-permute-start(f32[2,8960]{1,0:T(2,128)S(1)} %get-tuple-element.74.refs_2_), channel_id=1, source_target_pairs={{0,1},{1,0},{2,3},{3,2},{4,5},{5,4},{6,7},{7,6},{8,9},{9,8},{10,11... | collective-permute-start | bytes 215048 | tf_op jit(solution)/shard_map/ppermute | solution.py:139
  13.4 0.2 select_reduce_fusion
  13.7 1.4 %collective-permute-done.2.refs_3_ = f32[2,8960]{1,0:T(2,128)S(1)} collective-permute-done((f32[2,8960]{1,0:T(2,128)S(1)}, f32[2,8960]{1,0:T(2,128)S(1)}, u32[]{:S(2)}, u32[]{:S(2)}) %collective-permute-start.2) | collective-permute-done | bytes 71712 | tf_op jit(solution)/shard_map/ppermute | solution.py:139
  15.0 0.2 collective-permute-done.3.refs_4_
  15.2 0.9 collective-permute-done.4.refs_5_
  16.2 0.6 collective-permute-start.5
  16.7 1.5 %collective-permute-start.6 = (f32[2,8960]{1,0:T(2,128)S(1)}, f32[2,8960]{1,0:T(2,128)S(1)}, u32[]{:S(2)}, u32[]{:S(2)}) collective-permute-start(f32[2,8960]{1,0:T(2,128)S(1)} %get-tuple-element.76.refs_1_), channel_id=1, source_target_pairs={{0,1},{1,0},{2,3},{3,2},{4,5},{5,4},{6,7},{7,6},{8,9},{9,8},{10,11... | collective-permute-start | bytes 215048 | tf_op jit(solution)/shard_map/ppermute | solution.py:139
  18.3 10.3 %prepare.1 = (bf16[70,256,256]{2,1,0:T(8,128)(2,1)S(1)}, bf16[4,256,256]{2,1,0:T(8,128)(2,1)S(1)}, f32[70,96,128]{2,1,0:T(8,128)S(1)}, bf16[70,192,128]{2,1,0:T(8,128)(2,1)S(1)}, f32[70,96,128]{2,1,0:T(8,128)S(1)}) custom-call(s32[4]{0:T(128)S(1)} %compare_select_fusion.side, f32[70,2,128,128]{3,2,1,0:T(8,128)} %values.1, f32[24,4,8960]{2,1,0:T(4,128)} %start.3, ...), custom_call_target="tpu_custom_call" | custom-call | flops 1000000000 | bytes 20000000 | tf_op jit(solution)/shard_map/prepare/pallas_call | solution.py:355
  28.7 0.6 collective-permute-start.7
  29.3 2.1 %step_0.1 = (f32[70,96,128]{2,1,0:T(8,128)S(1)}, bf16[70,192,128]{2,1,0:T(8,128)(2,1)S(1)}) custom-call(s32[140]{0:T(256)S(4)} %get-tuple-element.80.cols, bf16[70,256,256]{2,1,0:T(8,128)(2,1)S(1)} %get-tuple-element.81.weights, f32[70,96,128]{2,1,0:T(8,128)S(1)} %get-tuple-element.82.state, bf16[70,192,128]{2,1,0:T(8,128)(2,1)S(1)} %get-tuple-element.83.parts, ...), custom_call_target="tpu_custom_call" | custom-call | flops 1761607680 | bytes 12000000 | tf_op jit(solution)/shard_map/step_0/pallas_call | solution.py:387
  31.4 1.7 %collective-permute-done.7.refs_1_ = f32[2,8960]{1,0:T(2,128)S(1)} collective-permute-done((f32[2,8960]{1,0:T(2,128)S(1)}, f32[2,8960]{1,0:T(2,128)S(1)}, u32[]{:S(2)}, u32[]{:S(2)}) %collective-permute-start.7) | collective-permute-done | bytes 71712 | tf_op jit(solution)/shard_map/ppermute | solution.py:139
  33.1 0.8 anchor.1
  33.9 0.5 collective-permute-start.8
  34.4 2.3 %step_1.1 = (f32[70,96,128]{2,1,0:T(8,128)S(1)}, bf16[70,192,128]{2,1,0:T(8,128)(2,1)S(1)}) custom-call(s32[140]{0:T(256)S(4)} %get-tuple-element.80.cols, bf16[70,256,256]{2,1,0:T(8,128)(2,1)S(1)} %get-tuple-element.81.weights, f32[70,96,128]{2,1,0:T(8,128)S(1)} %get-tuple-element.88.state, bf16[70,192,128]{2,1,0:T(8,128)(2,1)S(1)} %get-tuple-element.89.parts, ...), custom_call_target="tpu_custom_call" | custom-call | flops 1761607680 | bytes 12000000 | tf_op jit(solution)/shard_map/step_1/pallas_call | solution.py:387
  36.8 1.1 %collective-permute-done.8.low = f32[96,128]{1,0:T(8,128)S(1)} collective-permute-done((f32[96,128]{1,0:T(8,128)S(1)}, f32[96,128]{1,0:T(8,128)S(1)}, u32[]{:S(2)}, u32[]{:S(2)}) %collective-permute-start.8) | collective-permute-done | bytes 49184 | tf_op jit(solution)/shard_map/ppermute | solution.py:144
  37.9 0.3 ties_1.1
  38.2 0.3 collective-permute-start.11
  38.5 0.3 collective-permute-start.10
  38.7 2.3 %step_2.1 = (f32[70,96,128]{2,1,0:T(8,128)S(1)}, bf16[70,192,128]{2,1,0:T(8,128)(2,1)S(1)}) custom-call(s32[140]{0:T(256)S(4)} %get-tuple-element.80.cols, bf16[70,256,256]{2,1,0:T(8,128)(2,1)S(1)} %get-tuple-element.81.weights, f32[70,96,128]{2,1,0:T(8,128)S(1)} %get-tuple-element.94.state, bf16[70,192,128]{2,1,0:T(8,128)(2,1)S(1)} %get-tuple-element.95.parts, ...), custom_call_target="tpu_custom_call" | custom-call | flops 1761607680 | bytes 12000000 | tf_op jit(solution)/shard_map/step_2/pallas_call | solution.py:387
  41.1 1.3 %collective-permute-done.10.low = f32[96,128]{1,0:T(8,128)S(1)} collective-permute-done((f32[96,128]{1,0:T(8,128)S(1)}, f32[96,128]{1,0:T(8,128)S(1)}, u32[]{:S(2)}, u32[]{:S(2)}) %collective-permute-start.10) | collective-permute-done | bytes 49184 | tf_op jit(solution)/shard_map/ppermute | solution.py:144
  42.4 0.3 ties_2.1
  42.7 0.3 collective-permute-start.13
  42.9 0.3 collective-permute-start.12
  43.3 2.4 %step_3.1 = (f32[70,96,128]{2,1,0:T(8,128)S(1)}, bf16[70,192,128]{2,1,0:T(8,128)(2,1)S(1)}) custom-call(s32[140]{0:T(256)S(4)} %get-tuple-element.80.cols, bf16[70,256,256]{2,1,0:T(8,128)(2,1)S(1)} %get-tuple-element.81.weights, f32[70,96,128]{2,1,0:T(8,128)S(1)} %get-tuple-element.99.state, bf16[70,192,128]{2,1,0:T(8,128)(2,1)S(1)} %get-tuple-element.100.parts, ...), custom_call_target="tpu_custom_call" | custom-call | flops 1761607680 | bytes 12000000 | tf_op jit(solution)/shard_map/step_3/pallas_call | solution.py:387
  45.7 1.3 %collective-permute-done.12.low = f32[96,128]{1,0:T(8,128)S(1)} collective-permute-done((f32[96,128]{1,0:T(8,128)S(1)}, f32[96,128]{1,0:T(8,128)S(1)}, u32[]{:S(2)}, u32[]{:S(2)}) %collective-permute-start.12) | collective-permute-done | bytes 49184 | tf_op jit(solution)/shard_map/ppermute | solution.py:144
  46.9 0.3 ties_3.1
  47.3 0.3 collective-permute-start.15
  47.5 0.3 collective-permute-start.14
  47.8 2.4 %step_4.1 = (f32[70,96,128]{2,1,0:T(8,128)S(1)}, bf16[70,192,128]{2,1,0:T(8,128)(2,1)S(1)}) custom-call(s32[140]{0:T(256)S(4)} %get-tuple-element.80.cols, bf16[70,256,256]{2,1,0:T(8,128)(2,1)S(1)} %get-tuple-element.81.weights, f32[70,96,128]{2,1,0:T(8,128)S(1)} %get-tuple-element.104.state, bf16[70,192,128]{2,1,0:T(8,128)(2,1)S(1)} %get-tuple-element.105.parts, ...), custom_call_target="tpu_custom_call" | custom-call | flops 1761607680 | bytes 12000000 | tf_op jit(solution)/shard_map/step_4/pallas_call | solution.py:387
  50.2 1.3 %collective-permute-done.14.low = f32[96,128]{1,0:T(8,128)S(1)} collective-permute-done((f32[96,128]{1,0:T(8,128)S(1)}, f32[96,128]{1,0:T(8,128)S(1)}, u32[]{:S(2)}, u32[]{:S(2)}) %collective-permute-start.14) | collective-permute-done | bytes 49184 | tf_op jit(solution)/shard_map/ppermute | solution.py:144
  51.6 0.3 ties_4.1
  51.9 0.2 collective-permute-start.17
  52.1 0.4 collective-permute-start.16
  52.4 2.4 %step_5.1 = (f32[70,96,128]{2,1,0:T(8,128)S(1)}, bf16[70,192,128]{2,1,0:T(8,128)(2,1)S(1)}) custom-call(s32[140]{0:T(256)S(4)} %get-tuple-element.80.cols, bf16[70,256,256]{2,1,0:T(8,128)(2,1)S(1)} %get-tuple-element.81.weights, f32[70,96,128]{2,1,0:T(8,128)S(1)} %get-tuple-element.109.state, bf16[70,192,128]{2,1,0:T(8,128)(2,1)S(1)} %get-tuple-element.110.parts, ...), custom_call_target="tpu_custom_call" | custom-call | flops 1761607680 | bytes 12000000 | tf_op jit(solution)/shard_map/step_5/pallas_call | solution.py:387
  54.9 1.1 %collective-permute-done.16.low = f32[96,128]{1,0:T(8,128)S(1)} collective-permute-done((f32[96,128]{1,0:T(8,128)S(1)}, f32[96,128]{1,0:T(8,128)S(1)}, u32[]{:S(2)}, u32[]{:S(2)}) %collective-permute-start.16) | collective-permute-done | bytes 49184 | tf_op jit(solution)/shard_map/ppermute | solution.py:144
  55.9 0.3 ties_5.1
  56.2 0.3 collective-permute-start.19
  56.6 0.2 collective-permute-start.18
  56.8 2.4 %step_6.1 = (f32[70,96,128]{2,1,0:T(8,128)S(1)}, bf16[70,192,128]{2,1,0:T(8,128)(2,1)S(1)}) custom-call(s32[140]{0:T(256)S(4)} %get-tuple-element.80.cols, bf16[70,256,256]{2,1,0:T(8,128)(2,1)S(1)} %get-tuple-element.81.weights, f32[70,96,128]{2,1,0:T(8,128)S(1)} %get-tuple-element.114.state, bf16[70,192,128]{2,1,0:T(8,128)(2,1)S(1)} %get-tuple-element.115.parts, ...), custom_call_target="tpu_custom_call" | custom-call | flops 1761607680 | bytes 12000000 | tf_op jit(solution)/shard_map/step_6/pallas_call | solution.py:387
  59.2 1.2 %collective-permute-done.18.low = f32[96,128]{1,0:T(8,128)S(1)} collective-permute-done((f32[96,128]{1,0:T(8,128)S(1)}, f32[96,128]{1,0:T(8,128)S(1)}, u32[]{:S(2)}, u32[]{:S(2)}) %collective-permute-start.18) | collective-permute-done | bytes 49184 | tf_op jit(solution)/shard_map/ppermute | solution.py:144
  60.5 0.3 ties_6.1
  60.8 0.4 collective-permute-start.21
  61.1 0.3 collective-permute-start.20
  61.4 2.4 %step_7.1 = (f32[70,96,128]{2,1,0:T(8,128)S(1)}, bf16[70,192,128]{2,1,0:T(8,128)(2,1)S(1)}) custom-call(s32[140]{0:T(256)S(4)} %get-tuple-element.80.cols, bf16[70,256,256]{2,1,0:T(8,128)(2,1)S(1)} %get-tuple-element.81.weights, f32[70,96,128]{2,1,0:T(8,128)S(1)} %get-tuple-element.119.state, bf16[70,192,128]{2,1,0:T(8,128)(2,1)S(1)} %get-tuple-element.120.parts, ...), custom_call_target="tpu_custom_call" | custom-call | flops 1761607680 | bytes 12000000 | tf_op jit(solution)/shard_map/step_7/pallas_call | solution.py:387
  63.8 1.2 %collective-permute-done.20.low = f32[96,128]{1,0:T(8,128)S(1)} collective-permute-done((f32[96,128]{1,0:T(8,128)S(1)}, f32[96,128]{1,0:T(8,128)S(1)}, u32[]{:S(2)}, u32[]{:S(2)}) %collective-permute-start.20) | collective-permute-done | bytes 49184 | tf_op jit(solution)/shard_map/ppermute | solution.py:144
  65.0 0.8 ties_7.1
  65.8 2.5 %collective-permute-start.22 = (f32[2,8960]{1,0:T(2,128)S(1)}, f32[2,8960]{1,0:T(2,128)S(1)}, u32[]{:S(2)}, u32[]{:S(2)}) collective-permute-start(f32[2,8960]{1,0:T(2,128)S(1)} %get-tuple-element.125.refs_0_), channel_id=1, source_target_pairs={{0,4},{1,5},{2,6},{3,7},{4,0},{5,1},{6,2},{7,3},{8,12},{9,13},{10,... | collective-permute-start | bytes 215048 | tf_op jit(solution)/shard_map/ppermute | solution.py:139
  68.4 0.6 collective-permute-start.24
  69.0 3.6 %collective-permute-done.22.refs_3_ = f32[2,8960]{1,0:T(2,128)S(1)} collective-permute-done((f32[2,8960]{1,0:T(2,128)S(1)}, f32[2,8960]{1,0:T(2,128)S(1)}, u32[]{:S(2)}, u32[]{:S(2)}) %collective-permute-start.22) | collective-permute-done | bytes 71712 | tf_op jit(solution)/shard_map/ppermute | solution.py:139
  72.6 0.4 collective-permute-done.23.refs_4_
  73.0 1.8 %collective-permute-start.25 = (f32[2,8960]{1,0:T(2,128)S(1)}, f32[2,8960]{1,0:T(2,128)S(1)}, u32[]{:S(2)}, u32[]{:S(2)}) collective-permute-start(f32[2,8960]{1,0:T(2,128)S(1)} %get-tuple-element.128.refs_0_), channel_id=1, source_target_pairs={{0,2},{1,3},{2,0},{3,1},{4,6},{5,7},{6,4},{7,5},{8,10},{9,11},{10,... | collective-permute-start | bytes 215048 | tf_op jit(solution)/shard_map/ppermute | solution.py:139
  74.8 0.6 collective-permute-start.26
  75.3 2.1 %collective-permute-done.25.refs_2_ = f32[2,8960]{1,0:T(2,128)S(1)} collective-permute-done((f32[2,8960]{1,0:T(2,128)S(1)}, f32[2,8960]{1,0:T(2,128)S(1)}, u32[]{:S(2)}, u32[]{:S(2)}) %collective-permute-start.25) | collective-permute-done | bytes 71712 | tf_op jit(solution)/shard_map/ppermute | solution.py:139
  77.4 1.7 %collective-permute-done.26.refs_3_ = f32[2,8960]{1,0:T(2,128)S(1)} collective-permute-done((f32[2,8960]{1,0:T(2,128)S(1)}, f32[2,8960]{1,0:T(2,128)S(1)}, u32[]{:S(2)}, u32[]{:S(2)}) %collective-permute-start.26) | collective-permute-done | bytes 71712 | tf_op jit(solution)/shard_map/ppermute | solution.py:139
  79.1 0.7 collective-permute-start.27
  79.8 7.9 %outputs.1 = (f32[24,4,8960]{2,1,0:T(4,128)}, f32[24,4,8960]{2,1,0:T(4,128)}) custom-call(f32[70,96,128]{2,1,0:T(8,128)S(1)} %get-tuple-element.123.state, f32[24,4,8960]{2,1,0:T(4,128)} %mult.3), custom_call_target="tpu_custom_call" | custom-call | flops 1000000000 | bytes 12000000 | tf_op jit(solution)/shard_map/outputs/pallas_call | solution.py:433
  87.7 2.5 %finish.1 = f32[24,4,8960]{2,1,0:T(4,128)} custom-call(f32[70,96,128]{2,1,0:T(8,128)S(1)} %get-tuple-element.123.state, f32[2,8960]{1,0:T(2,128)S(1)} %node_add_2.3.refs_0_, f32[2,8960]{1,0:T(2,128)S(1)} %get-tuple-element.131.refs_1_, f32[2,8960]{1,0:T(2,128)S(1)} %get-tuple-element.132.refs_2_, ...), custom_call_target="tpu_custom_call", output_to_operand_aliasing={{}: (4, {})} | custom-call | tf_op jit(solution)/shard_map/finish/pallas_call | solution.py:443
  (36 shorter events, 0.6 us)
Async XLA Ops:
  0.6 17.7 %copy-start = (f32[4,128,128]{2,1,0:T(8,128)S(1)}, f32[4,128,128]{2,1,0:T(8,128)}, u32[]{:S(2)}) copy-start(f32[4,128,128]{2,1,0:T(8,128)} %tie_weight.1) | copy-start | bytes 786436
  2.2 0.7 copy-start.1
  2.9 10.4 %copy-start.2 = (s32[12,4]{0,1:T(4,128)S(1)}, s32[12,4]{0,1:T(4,128)}, u32[]{:S(2)}) copy-start(s32[12,4]{0,1:T(4,128)} %param.15) | copy-start | bytes 580
  2.9 10.5 %copy-start.4 = (s32[4]{0:T(128)S(1)}, s32[4]{0:T(128)}, u32[]{:S(2)}) copy-start(s32[4]{0:T(128)} %param.19) | copy-start | bytes 52
  2.9 10.5 %copy-start.3 = (f32[32]{0:T(128)S(1)}, f32[32]{0:T(128)}, u32[]{:S(2)}) copy-start(f32[32]{0:T(128)} %param.14) | copy-start | bytes 388
  5.2 27.9 %collective-permute-start.1 = (f32[96,128]{1,0:T(8,128)S(1)}, f32[96,128]{1,0:T(8,128)S(1)}, u32[]{:S(2)}, u32[]{:S(2)}) collective-permute-start(f32[96,128]{1,0:T(8,128)S(1)} %get-tuple-element.70), channel_id=1, source_target_pairs={{0,24},{8,0},{16,8},{24,16},{1,25},{9,1},{17,9},{25,17},{2,26},{10... | collective-permute-start | bytes 147464 | tf_op jit(solution)/shard_map/ppermute | solution.py:144
  7.6 25.5 %collective-permute-start = (f32[96,128]{1,0:T(8,128)S(1)}, f32[96,128]{1,0:T(8,128)S(1)}, u32[]{:S(2)}, u32[]{:S(2)}) collective-permute-start(f32[96,128]{1,0:T(8,128)S(1)} %get-tuple-element.70), channel_id=1, source_target_pairs={{0,8},{8,16},{16,24},{24,0},{1,9},{9,17},{17,25},{25,1},{2,10},{10... | collective-permute-start | bytes 147464 | tf_op jit(solution)/shard_map/ppermute | solution.py:144
  7.6 7.4 %collective-permute-start.2 = (f32[2,8960]{1,0:T(2,128)S(1)}, f32[2,8960]{1,0:T(2,128)S(1)}, u32[]{:S(2)}, u32[]{:S(2)}) collective-permute-start(f32[2,8960]{1,0:T(2,128)S(1)} %get-tuple-element.72.refs_0_), channel_id=1, source_target_pairs={{0,4},{1,5},{2,6},{3,7},{4,0},{5,1},{6,2},{7,3},{8,12},{9,13},{10,... | collective-permute-start | bytes 215048 | tf_op jit(solution)/shard_map/ppermute | solution.py:139
  10.2 5.0 %collective-permute-start.3 = (f32[2,8960]{1,0:T(2,128)S(1)}, f32[2,8960]{1,0:T(2,128)S(1)}, u32[]{:S(2)}, u32[]{:S(2)}) collective-permute-start(f32[2,8960]{1,0:T(2,128)S(1)} %get-tuple-element.73.refs_1_), channel_id=1, source_target_pairs={{0,2},{1,3},{2,0},{3,1},{4,6},{5,7},{6,4},{7,5},{8,10},{9,11},{10,... | collective-permute-start | bytes 215048 | tf_op jit(solution)/shard_map/ppermute | solution.py:139
  11.8 4.3 %collective-permute-start.4 = (f32[2,8960]{1,0:T(2,128)S(1)}, f32[2,8960]{1,0:T(2,128)S(1)}, u32[]{:S(2)}, u32[]{:S(2)}) collective-permute-start(f32[2,8960]{1,0:T(2,128)S(1)} %get-tuple-element.74.refs_2_), channel_id=1, source_target_pairs={{0,1},{1,0},{2,3},{3,2},{4,5},{5,4},{6,7},{7,6},{8,9},{9,8},{10,11... | collective-permute-start | bytes 215048 | tf_op jit(solution)/shard_map/ppermute | solution.py:139
  16.2 12.4 %collective-permute-start.5 = (f32[2,8960]{1,0:T(2,128)S(1)}, f32[2,8960]{1,0:T(2,128)S(1)}, u32[]{:S(2)}, u32[]{:S(2)}) collective-permute-start(f32[2,8960]{1,0:T(2,128)S(1)} %get-tuple-element.75.refs_0_), channel_id=1, source_target_pairs={{0,2},{1,3},{2,0},{3,1},{4,6},{5,7},{6,4},{7,5},{8,10},{9,11},{10,... | collective-permute-start | bytes 215048 | tf_op jit(solution)/shard_map/ppermute | solution.py:139
  16.7 11.9 %collective-permute-start.6 = (f32[2,8960]{1,0:T(2,128)S(1)}, f32[2,8960]{1,0:T(2,128)S(1)}, u32[]{:S(2)}, u32[]{:S(2)}) collective-permute-start(f32[2,8960]{1,0:T(2,128)S(1)} %get-tuple-element.76.refs_1_), channel_id=1, source_target_pairs={{0,1},{1,0},{2,3},{3,2},{4,5},{5,4},{6,7},{7,6},{8,9},{9,8},{10,11... | collective-permute-start | bytes 215048 | tf_op jit(solution)/shard_map/ppermute | solution.py:139
  28.7 4.4 %collective-permute-start.7 = (f32[2,8960]{1,0:T(2,128)S(1)}, f32[2,8960]{1,0:T(2,128)S(1)}, u32[]{:S(2)}, u32[]{:S(2)}) collective-permute-start(f32[2,8960]{1,0:T(2,128)S(1)} %get-tuple-element.77.refs_0_), channel_id=1, source_target_pairs={{0,1},{1,0},{2,3},{3,2},{4,5},{5,4},{6,7},{7,6},{8,9},{9,8},{10,11... | collective-permute-start | bytes 215048 | tf_op jit(solution)/shard_map/ppermute | solution.py:139
  33.9 2.9 %collective-permute-start.9 = (f32[96,128]{1,0:T(8,128)S(1)}, f32[96,128]{1,0:T(8,128)S(1)}, u32[]{:S(2)}, u32[]{:S(2)}) collective-permute-start(f32[96,128]{1,0:T(8,128)S(1)} %get-tuple-element.87), channel_id=1, source_target_pairs={{0,24},{8,0},{16,8},{24,16},{1,25},{9,1},{17,9},{25,17},{2,26},{10... | collective-permute-start | bytes 147464 | tf_op jit(solution)/shard_map/ppermute | solution.py:144
  33.9 3.9 %collective-permute-start.8 = (f32[96,128]{1,0:T(8,128)S(1)}, f32[96,128]{1,0:T(8,128)S(1)}, u32[]{:S(2)}, u32[]{:S(2)}) collective-permute-start(f32[96,128]{1,0:T(8,128)S(1)} %get-tuple-element.87), channel_id=1, source_target_pairs={{0,8},{8,16},{16,24},{24,0},{1,9},{9,17},{17,25},{25,1},{2,10},{10... | collective-permute-start | bytes 147464 | tf_op jit(solution)/shard_map/ppermute | solution.py:144
  38.2 2.9 %collective-permute-start.11 = (f32[96,128]{1,0:T(8,128)S(1)}, f32[96,128]{1,0:T(8,128)S(1)}, u32[]{:S(2)}, u32[]{:S(2)}) collective-permute-start(f32[96,128]{1,0:T(8,128)S(1)} %get-tuple-element.93), channel_id=1, source_target_pairs={{0,24},{8,0},{16,8},{24,16},{1,25},{9,1},{17,9},{25,17},{2,26},{10... | collective-permute-start | bytes 147464 | tf_op jit(solution)/shard_map/ppermute | solution.py:144
  38.5 3.9 %collective-permute-start.10 = (f32[96,128]{1,0:T(8,128)S(1)}, f32[96,128]{1,0:T(8,128)S(1)}, u32[]{:S(2)}, u32[]{:S(2)}) collective-permute-start(f32[96,128]{1,0:T(8,128)S(1)} %get-tuple-element.93), channel_id=1, source_target_pairs={{0,8},{8,16},{16,24},{24,0},{1,9},{9,17},{17,25},{25,1},{2,10},{10... | collective-permute-start | bytes 147464 | tf_op jit(solution)/shard_map/ppermute | solution.py:144
  42.7 3.0 %collective-permute-start.13 = (f32[96,128]{1,0:T(8,128)S(1)}, f32[96,128]{1,0:T(8,128)S(1)}, u32[]{:S(2)}, u32[]{:S(2)}) collective-permute-start(f32[96,128]{1,0:T(8,128)S(1)} %get-tuple-element.98), channel_id=1, source_target_pairs={{0,24},{8,0},{16,8},{24,16},{1,25},{9,1},{17,9},{25,17},{2,26},{10... | collective-permute-start | bytes 147464 | tf_op jit(solution)/shard_map/ppermute | solution.py:144
  42.9 4.0 %collective-permute-start.12 = (f32[96,128]{1,0:T(8,128)S(1)}, f32[96,128]{1,0:T(8,128)S(1)}, u32[]{:S(2)}, u32[]{:S(2)}) collective-permute-start(f32[96,128]{1,0:T(8,128)S(1)} %get-tuple-element.98), channel_id=1, source_target_pairs={{0,8},{8,16},{16,24},{24,0},{1,9},{9,17},{17,25},{25,1},{2,10},{10... | collective-permute-start | bytes 147464 | tf_op jit(solution)/shard_map/ppermute | solution.py:144
  47.3 3.0 %collective-permute-start.15 = (f32[96,128]{1,0:T(8,128)S(1)}, f32[96,128]{1,0:T(8,128)S(1)}, u32[]{:S(2)}, u32[]{:S(2)}) collective-permute-start(f32[96,128]{1,0:T(8,128)S(1)} %get-tuple-element.103), channel_id=1, source_target_pairs={{0,24},{8,0},{16,8},{24,16},{1,25},{9,1},{17,9},{25,17},{2,26},{10... | collective-permute-start | bytes 147464 | tf_op jit(solution)/shard_map/ppermute | solution.py:144
  47.5 4.0 %collective-permute-start.14 = (f32[96,128]{1,0:T(8,128)S(1)}, f32[96,128]{1,0:T(8,128)S(1)}, u32[]{:S(2)}, u32[]{:S(2)}) collective-permute-start(f32[96,128]{1,0:T(8,128)S(1)} %get-tuple-element.103), channel_id=1, source_target_pairs={{0,8},{8,16},{16,24},{24,0},{1,9},{9,17},{17,25},{25,1},{2,10},{10... | collective-permute-start | bytes 147464 | tf_op jit(solution)/shard_map/ppermute | solution.py:144
  51.9 3.0 %collective-permute-start.17 = (f32[96,128]{1,0:T(8,128)S(1)}, f32[96,128]{1,0:T(8,128)S(1)}, u32[]{:S(2)}, u32[]{:S(2)}) collective-permute-start(f32[96,128]{1,0:T(8,128)S(1)} %get-tuple-element.108), channel_id=1, source_target_pairs={{0,24},{8,0},{16,8},{24,16},{1,25},{9,1},{17,9},{25,17},{2,26},{10... | collective-permute-start | bytes 147464 | tf_op jit(solution)/shard_map/ppermute | solution.py:144
  52.1 3.9 %collective-permute-start.16 = (f32[96,128]{1,0:T(8,128)S(1)}, f32[96,128]{1,0:T(8,128)S(1)}, u32[]{:S(2)}, u32[]{:S(2)}) collective-permute-start(f32[96,128]{1,0:T(8,128)S(1)} %get-tuple-element.108), channel_id=1, source_target_pairs={{0,8},{8,16},{16,24},{24,0},{1,9},{9,17},{17,25},{25,1},{2,10},{10... | collective-permute-start | bytes 147464 | tf_op jit(solution)/shard_map/ppermute | solution.py:144
  56.2 3.0 %collective-permute-start.19 = (f32[96,128]{1,0:T(8,128)S(1)}, f32[96,128]{1,0:T(8,128)S(1)}, u32[]{:S(2)}, u32[]{:S(2)}) collective-permute-start(f32[96,128]{1,0:T(8,128)S(1)} %get-tuple-element.113), channel_id=1, source_target_pairs={{0,24},{8,0},{16,8},{24,16},{1,25},{9,1},{17,9},{25,17},{2,26},{10... | collective-permute-start | bytes 147464 | tf_op jit(solution)/shard_map/ppermute | solution.py:144
  56.6 3.9 %collective-permute-start.18 = (f32[96,128]{1,0:T(8,128)S(1)}, f32[96,128]{1,0:T(8,128)S(1)}, u32[]{:S(2)}, u32[]{:S(2)}) collective-permute-start(f32[96,128]{1,0:T(8,128)S(1)} %get-tuple-element.113), channel_id=1, source_target_pairs={{0,8},{8,16},{16,24},{24,0},{1,9},{9,17},{17,25},{25,1},{2,10},{10... | collective-permute-start | bytes 147464 | tf_op jit(solution)/shard_map/ppermute | solution.py:144
  60.8 3.0 %collective-permute-start.21 = (f32[96,128]{1,0:T(8,128)S(1)}, f32[96,128]{1,0:T(8,128)S(1)}, u32[]{:S(2)}, u32[]{:S(2)}) collective-permute-start(f32[96,128]{1,0:T(8,128)S(1)} %get-tuple-element.118), channel_id=1, source_target_pairs={{0,24},{8,0},{16,8},{24,16},{1,25},{9,1},{17,9},{25,17},{2,26},{10... | collective-permute-start | bytes 147464 | tf_op jit(solution)/shard_map/ppermute | solution.py:144
  61.1 3.9 %collective-permute-start.20 = (f32[96,128]{1,0:T(8,128)S(1)}, f32[96,128]{1,0:T(8,128)S(1)}, u32[]{:S(2)}, u32[]{:S(2)}) collective-permute-start(f32[96,128]{1,0:T(8,128)S(1)} %get-tuple-element.118), channel_id=1, source_target_pairs={{0,8},{8,16},{16,24},{24,0},{1,9},{9,17},{17,25},{25,1},{2,10},{10... | collective-permute-start | bytes 147464 | tf_op jit(solution)/shard_map/ppermute | solution.py:144
  65.8 6.8 %collective-permute-start.22 = (f32[2,8960]{1,0:T(2,128)S(1)}, f32[2,8960]{1,0:T(2,128)S(1)}, u32[]{:S(2)}, u32[]{:S(2)}) collective-permute-start(f32[2,8960]{1,0:T(2,128)S(1)} %get-tuple-element.125.refs_0_), channel_id=1, source_target_pairs={{0,4},{1,5},{2,6},{3,7},{4,0},{5,1},{6,2},{7,3},{8,12},{9,13},{10,... | collective-permute-start | bytes 215048 | tf_op jit(solution)/shard_map/ppermute | solution.py:139
  68.3 4.7 %collective-permute-start.23 = (f32[2,8960]{1,0:T(2,128)S(1)}, f32[2,8960]{1,0:T(2,128)S(1)}, u32[]{:S(2)}, u32[]{:S(2)}) collective-permute-start(f32[2,8960]{1,0:T(2,128)S(1)} %get-tuple-element.126.refs_1_), channel_id=1, source_target_pairs={{0,2},{1,3},{2,0},{3,1},{4,6},{5,7},{6,4},{7,5},{8,10},{9,11},{10,... | collective-permute-start | bytes 215048 | tf_op jit(solution)/shard_map/ppermute | solution.py:139
  68.4 4.6 %collective-permute-start.24 = (f32[2,8960]{1,0:T(2,128)S(1)}, f32[2,8960]{1,0:T(2,128)S(1)}, u32[]{:S(2)}, u32[]{:S(2)}) collective-permute-start(f32[2,8960]{1,0:T(2,128)S(1)} %get-tuple-element.127.refs_2_), channel_id=1, source_target_pairs={{0,1},{1,0},{2,3},{3,2},{4,5},{5,4},{6,7},{7,6},{8,9},{9,8},{10,11... | collective-permute-start | bytes 215048 | tf_op jit(solution)/shard_map/ppermute | solution.py:139
  73.0 4.4 %collective-permute-start.25 = (f32[2,8960]{1,0:T(2,128)S(1)}, f32[2,8960]{1,0:T(2,128)S(1)}, u32[]{:S(2)}, u32[]{:S(2)}) collective-permute-start(f32[2,8960]{1,0:T(2,128)S(1)} %get-tuple-element.128.refs_0_), channel_id=1, source_target_pairs={{0,2},{1,3},{2,0},{3,1},{4,6},{5,7},{6,4},{7,5},{8,10},{9,11},{10,... | collective-permute-start | bytes 215048 | tf_op jit(solution)/shard_map/ppermute | solution.py:139
  74.8 4.3 %collective-permute-start.26 = (f32[2,8960]{1,0:T(2,128)S(1)}, f32[2,8960]{1,0:T(2,128)S(1)}, u32[]{:S(2)}, u32[]{:S(2)}) collective-permute-start(f32[2,8960]{1,0:T(2,128)S(1)} %get-tuple-element.129.refs_1_), channel_id=1, source_target_pairs={{0,1},{1,0},{2,3},{3,2},{4,5},{5,4},{6,7},{7,6},{8,9},{9,8},{10,11... | collective-permute-start | bytes 215048 | tf_op jit(solution)/shard_map/ppermute | solution.py:139
  79.1 8.6 %collective-permute-start.27 = (f32[2,8960]{1,0:T(2,128)S(1)}, f32[2,8960]{1,0:T(2,128)S(1)}, u32[]{:S(2)}, u32[]{:S(2)}) collective-permute-start(f32[2,8960]{1,0:T(2,128)S(1)} %get-tuple-element.130.refs_0_), channel_id=1, source_target_pairs={{0,1},{1,0},{2,3},{3,2},{4,5},{5,4},{6,7},{7,6},{8,9},{9,8},{10,11... | collective-permute-start | bytes 215048 | tf_op jit(solution)/shard_map/ppermute | solution.py:139

commit v2 on v1

v2 whole, which is shorter than its diff:
```python
import functools

import jax
import jax.numpy as jnp
from jax import lax
from jax.experimental import pallas as pl
from jax.experimental.pallas import tpu as pltpu
from jax.sharding import PartitionSpec as P

STEPS = 8
step_size = 0.25
penalty = 1.0
keep = 1.0 - step_size * penalty

f32 = jnp.float32
bf16 = jnp.bfloat16
VMEM = pltpu.VMEM
SMEM = pltpu.SMEM
MIB = 1 << 20


def in_vmem(array):
    return pltpu.with_memory_space_constraint(array, VMEM)


def in_smem(array):
    return pltpu.with_memory_space_constraint(array, SMEM)


def in_hbm(array):
    return pltpu.with_memory_space_constraint(array, pltpu.HBM)


vmem_spec = pl.BlockSpec(memory_space=VMEM)
smem_spec = pl.BlockSpec(memory_space=SMEM)
any_spec = pl.BlockSpec(memory_space=pl.ANY)


def params(mib):
    return pltpu.CompilerParams(vmem_limit_bytes=mib * MIB)


def cost(flops, moved):
    return pl.CostEstimate(flops=flops, bytes_accessed=moved, transcendentals=0)


def split(value):
    high = value.astype(bf16)
    return high, (value - high.astype(f32)).astype(bf16)


def store_split(ref, index, value):
    rows = value.shape[0]
    high, low = split(value)
    ref[index, 0:rows] = high
    ref[index, rows : 2 * rows] = low


def fold(product, rows):
    return (product[:rows, :128] + product[:rows, 128:]) + (product[rows:, :128] + product[rows:, 128:])


def lanes(block):
    return pl.ds(pl.multiple_of(block * 128, 128), 128)


def partner(value, apart):
    rows = value.shape[0]
    up = pltpu.roll(value, rows - apart, 0)
    down = pltpu.roll(value, apart, 0)
    place = lax.broadcasted_iota(jnp.int32, value.shape, 0)
    return jnp.where((place & apart) == 0, up, down)


def local_mean(value, members):
    total, apart = value, 1
    while apart < members:
        total = total + partner(total, apart)
        apart *= 2
    return total / members


def spread(pair, scenarios):
    count, width = pair.shape
    wide = jnp.broadcast_to(pair[:, None, :], (count, scenarios, width))
    return wide.reshape(count * scenarios, width)


def copies_of(pairs, sems):
    copies = [pltpu.make_async_copy(source, target, sems.at[n]) for n, (source, target) in enumerate(pairs)]
    for copy in copies:
        copy.start()
    return copies


def first_kernel(shared, per, small, send, start, *refs):
    sources, refs = refs[:small], refs[small:]
    sums, targets = refs[:shared], refs[shared : shared + small]
    send_out, head, sems = refs[shared + small :]
    cuts = [pl.ds(k * per, per) for k in range(shared)]
    pairs = [(start.at[cut], head.at[cut]) for cut in cuts] + list(zip(sources, targets))
    copies = copies_of(pairs, sems)
    for k in range(shared):
        copies[k].wait()
        sums[k][...] = jnp.sum(head[k * per : (k + 1) * per], axis=1)
    send_out[0] = send[0]
    for copy in copies[shared:]:
        copy.wait()


def add_kernel(count, *refs):
    for k in range(count):
        refs[-count + k][...] = refs[k][...] + refs[count + k][...]


def node_totals(sums, beside):
    shared = len(sums)
    totals = list(sums)
    done = sums[0]
    for turn in range(shared):
        active = [k for k in range(shared) if shared - k - 1 - turn >= 0]
        received = [swap(totals[k], "scen", shared - k - 1 - turn) for k in active]
        after = beside(turn, done)
        added = pl.pallas_call(
            functools.partial(add_kernel, len(active)),
            in_specs=[vmem_spec] * (2 * len(active)) + [any_spec] * len(after),
            out_specs=[vmem_spec] * len(active),
            out_shape=[VMEM(totals[k].shape, f32) for k in active],
            compiler_params=params(2),
            name=f"node_add_{turn}",
        )(*[in_vmem(totals[k]) for k in active], *[in_vmem(r) for r in received], *after)
        for k, value in zip(active, added):
            totals[k] = value
        done = added[0]
    return totals


def swap(block, axis, level):
    count = lax.axis_size(axis)
    return lax.ppermute(block, axis, [(i, i ^ (1 << level)) for i in range(count)])


def from_pair(value, axis):
    count = lax.axis_size(axis)
    return lax.ppermute(value, axis, [(i, i ^ 1) for i in range(count)])


def from_other(value, axis):
    count = lax.axis_size(axis)
    return lax.ppermute(value, axis, [(i, (i + 1 if i % 2 else i - 1) % count) for i in range(count)])


def lay_out(shared, per, scen_all, first, count, chunk, inputs, load, arrays, buffers, sems, between=None):
    weights, state, parts, constant = arrays
    values, start, mult, demand = buffers
    rows = state.shape[1]
    scenarios = start.shape[1]
    group = per * scenarios
    pairs = []
    for c in range(0, count, chunk):
        span = pl.ds(first + c, chunk)
        wide = pl.ds((first + c) * 128, chunk * 128)
        here = pl.ds(c * 128, chunk * 128)
        pairs += [
            (inputs[0].at[span], values.at[pl.ds(c, chunk)]),
            (inputs[1].at[:, :, wide], start.at[:, :, here]),
            (inputs[2].at[:, :, wide], mult.at[:, :, here]),
            (inputs[3].at[:, wide], demand.at[:, here]),
        ]
    copies = copies_of(pairs, sems)
    if between is not None:
        between()

    def one(b, carry):
        i = first + b
        for j in range(2):
            high, low = split(values[b, j] * -step_size)
            weights[i, j * 128 : (j + 1) * 128, 0:128] = high
            weights[i, j * 128 : (j + 1) * 128, 128:256] = low
        for k in range(rows // group):
            cut = slice(k * group, (k + 1) * group)
            span = slice(k * per, (k + 1) * per)
            x = start[span, :, lanes(b)].reshape(group, 128)
            m = mult[span, :, lanes(b)].reshape(group, 128)
            rest = m - spread(demand[span, lanes(b)], scenarios) * load[cut]
            if k >= shared:
                rest = rest - penalty * local_mean(x, max(scen_all >> k, 1))
            constant[i, cut] = -step_size * rest
            state[i, cut] = x
        store_split(parts, i, state[i])
        return carry

    for n, c in enumerate(range(0, count, chunk)):
        for copy in copies[4 * n : 4 * n + 4]:
            copy.wait()
        lax.fori_loop(c, c + chunk, one, 0, unroll=chunk)


def prepare_kernel(shared, per, scen_all, count, chunk, send, tie_source, node_ids, load_factor,
                   values, start, mult, demand, tie_weight,
                   weights, state, parts, constant, ties, load, boundary, *scratch):
    buffers, tie_buffer, block, sems = scratch[:4], scratch[4], scratch[5], scratch[6]
    scenarios = start.shape[1]
    extra = sems.shape[0] - 2
    copy_block = pltpu.make_async_copy(start.at[:, :, lanes(send[0])], block, sems.at[extra])
    copy_ties = pltpu.make_async_copy(tie_weight, tie_buffer, sems.at[extra + 1])
    copy_block.start()
    copy_ties.start()

    def between():
        for k in range(node_ids.shape[1]):
            for s in range(scenarios):
                row = jnp.full((1, 128), load_factor[node_ids[s, k]], f32)
                for t in range(per):
                    at = (k * per + t) * scenarios + s
                    load[at : at + 1] = row
        copy_block.wait()
        boundary[...] = block[...].reshape(boundary.shape)
        copy_ties.wait()
        mine = lax.axis_index("area")
        zero = jnp.zeros((128, 128), f32)
        for m in range(tie_weight.shape[0]):
            high, low = split(tie_buffer[m] * -step_size)
            from_partner = jnp.full((128, 128), tie_source[m] // send.shape[0], jnp.int32) == (mine ^ 1)
            for n, part in enumerate((high.astype(f32), low.astype(f32))):
                cut = slice(n * 128, (n + 1) * 128)
                ties[m, 0:128, cut] = jnp.where(from_partner, part, zero).astype(bf16)
                ties[m, 128:256, cut] = jnp.where(from_partner, zero, part).astype(bf16)

    lay_out(shared, per, scen_all, 0, count, chunk, (values, start, mult, demand), load,
            (weights, state, parts, constant), buffers, sems, between)


def prepare_more(shared, per, scen_all, first, count, chunk, values, start, mult, demand, load, after,
                 w_in, s_in, p_in, c_in, weights, state, parts, constant, *scratch):
    lay_out(shared, per, scen_all, first, count, chunk, (values, start, mult, demand), load,
            (weights, state, parts, constant), scratch[:4], scratch[4])


def step_kernel(cols, weights, state, parts, constant, new_state, new_parts):
    rows = state.shape[1]
    for i in range(state.shape[0]):
        other = cols[1, i]
        left = jnp.concatenate([parts[i], parts[other]], axis=1)
        product = jnp.dot(left, weights[i], preferred_element_type=f32)
        value = (keep * state[i] + constant[i]) + fold(product, rows)
        new_state[i] = value
        store_split(new_parts, i, value)


def add_ties(tie_row, low, high, ties, state, parts):
    rows = state.shape[1]
    both = jnp.concatenate([low[...], high[...]], axis=1)
    left = jnp.concatenate(split(both), axis=0)
    for m in range(ties.shape[0]):
        added = fold(jnp.dot(left, ties[m], preferred_element_type=f32), rows)
        row = tie_row[m]
        state[row] = state[row] + added
    for m in range(ties.shape[0]):
        row = tie_row[m]
        store_split(parts, row, state[row])


def tie_kernel(tie_row, send, low, high, ties, state_in, parts_in, state, parts, boundary):
    add_ties(tie_row, low, high, ties, state, parts)
    boundary[...] = state[send[0]]


def anchor_kernel(shared, scen_all, scenarios, tie_row, send, low, high, ties, *refs):
    totals = refs[:shared]
    state, parts, constant, boundary = refs[shared + 3 :]
    rows = state.shape[1]
    group = totals[0].shape[0] * scenarios
    span = min(-(-shared * group // 16) * 16, rows)

    def one(i, carry):
        for k in range(shared):
            cut = slice(k * group, (k + 1) * group)
            mean = spread(totals[k][:, lanes(i)], scenarios) / (scen_all >> k)
            mean = (step_size * penalty) * mean
            constant[i, cut] = constant[i, cut] + mean
            state[i, cut] = state[i, cut] + mean
        high_part, low_part = split(state[i, 0:span])
        parts[i, 0:span] = high_part
        parts[i, rows : rows + span] = low_part
        return carry

    lax.fori_loop(0, state.shape[0], one, 0, unroll=7)
    add_ties(tie_row, low, high, ties, state, parts)
    boundary[...] = state[send[0]]


def last_tie_kernel(shared, per, scenarios, tie_row, low, high, ties, state_in, parts_in, state, *refs):
    sums, parts = refs[:shared], refs[shared]
    add_ties(tie_row, low, high, ties, state, parts)
    group = per * scenarios

    def one(i, carry):
        for k in range(shared):
            piece = state[i, k * group : (k + 1) * group].reshape(per, scenarios, 128)
            sums[k][:, lanes(i)] = jnp.sum(piece, axis=1)
        return carry

    lax.fori_loop(0, state.shape[0], one, 0, unroll=7)


def write_blocks(pieces, blocks, one, buffer, out, sems, reads=None):
    width = blocks // pieces
    copies = []
    for piece in range(pieces):
        if reads is not None:
            reads[piece].wait()
        lax.fori_loop(piece * width, (piece + 1) * width, one, 0, unroll=largest_divisor(width, 7))
        cut = pl.ds(piece * width * 128, width * 128)
        copies.append(pltpu.make_async_copy(buffer.at[:, :, cut], out.at[:, :, cut], sems.at[piece]))
        copies[-1].start()
    for copy in copies:
        copy.wait()


def dispatch_kernel(pieces, state, mult, dispatch, mult_head, buffer, sems):
    head = pltpu.make_async_copy(mult.at[0 : mult_head.shape[0]], mult_head, sems.at[pieces])
    head.start()

    def one(i, carry):
        buffer[:, :, lanes(i)] = state[i].reshape(buffer.shape[0], buffer.shape[1], 128)
        return carry

    write_blocks(pieces, state.shape[0], one, buffer, dispatch, sems)
    head.wait()


def own_kernel(shared, per, scen_all, pieces, state, mult, after, new_mult, buffer, old_buffer, sems):
    scenarios = buffer.shape[1]
    blocks = state.shape[0]
    width = blocks // pieces
    cuts = [pl.ds(piece * width * 128, width * 128) for piece in range(pieces)]
    tail = mult.at[shared * per :]
    reads = [
        pltpu.make_async_copy(tail.at[:, :, cut], old_buffer.at[:, :, cut], sems.at[pieces + n])
        for n, cut in enumerate(cuts)
    ]
    for read in reads:
        read.start()
    group = per * scenarios

    def one(i, carry):
        for k in range(shared, state.shape[1] // group):
            value = state[i, k * group : (k + 1) * group]
            gap = penalty * (value - local_mean(value, max(scen_all >> k, 1)))
            cut = slice((k - shared) * per, (k - shared + 1) * per)
            buffer[cut, :, lanes(i)] = old_buffer[cut, :, lanes(i)] + gap.reshape(per, scenarios, 128)
        return carry

    write_blocks(pieces, blocks, one, buffer, new_mult.at[shared * per :], sems, reads)


def finish_kernel(shared, per, scen_all, pieces, state, mult, *refs):
    totals = refs[:shared]
    new_in, new_mult, buffer, sems = refs[shared:]
    scenarios = buffer.shape[1]
    group = per * scenarios

    def one(i, carry):
        for k in range(shared):
            value = state[i, k * group : (k + 1) * group]
            mean = spread(totals[k][:, lanes(i)], scenarios) / (scen_all >> k)
            gap = penalty * (value - mean)
            cut = slice(k * per, (k + 1) * per)
            buffer[cut, :, lanes(i)] = mult[cut, :, lanes(i)] + gap.reshape(per, scenarios, 128)
        return carry

    write_blocks(pieces, state.shape[0], one, buffer, new_mult.at[0 : shared * per], sems)


def largest_divisor(count, most):
    return max(d for d in range(1, most + 1) if count % d == 0)


def local(
    start_dispatch,
    multipliers,
    demand,
    load_factor,
    node_ids,
    block_values,
    block_cols,
    send_block,
    tie_source,
    tie_row,
    tie_weight,
):
    periods, scenarios, buses = start_dispatch.shape
    blocks = buses // 128
    rows = periods * scenarios
    sections = node_ids.shape[0]
    per = periods // sections
    devices = lax.axis_size("scen")
    scen_all = scenarios * devices
    shared = devices.bit_length() - 1
    tie_count = tie_row.shape[0]

    small = [block_cols.T, tie_row, tie_source, node_ids.T, load_factor]
    first = pl.pallas_call(
        functools.partial(first_kernel, shared, per, len(small)),
        in_specs=[smem_spec] + [any_spec] * (1 + len(small)),
        out_specs=[vmem_spec] * shared + [smem_spec] * (len(small) + 1),
        out_shape=[VMEM((per, buses), f32)] * shared + [SMEM(a.shape, a.dtype) for a in small + [send_block]],
        scratch_shapes=[
            VMEM((shared * per, scenarios, buses), f32),
            pltpu.SemaphoreType.DMA((shared + len(small),)),
        ],
        compiler_params=params(4),
        name="first_sums",
    )(send_block, in_hbm(start_dispatch), *[in_hbm(a) for a in small])
    sums = list(first[:shared])
    cols, row_of_tie, source_of_tie, labels, factors, send = first[shared:]
    inputs = [in_hbm(a) for a in (block_values, start_dispatch, multipliers, demand)]

    state_shape = VMEM((blocks, rows, 128), f32)
    parts_shape = VMEM((blocks, 2 * rows, 128), bf16)

    laid_shapes = [VMEM((blocks, 256, 256), bf16), state_shape, parts_shape, state_shape]
    chunk = largest_divisor(blocks, 7)
    parts_of = blocks // chunk
    ends = [0, 2 * parts_of // 5 * chunk, 7 * parts_of // 10 * chunk, blocks]
    laid = {}

    def buffers(count):
        return [
            VMEM((count, 2, 128, 128), f32),
            VMEM((periods, scenarios, count * 128), f32),
            VMEM((periods, scenarios, count * 128), f32),
            VMEM((periods, count * 128), f32),
        ]

    def prepare(turn, after):
        if turn >= len(ends) - 1:
            return []
        count = ends[turn + 1] - ends[turn]
        copies = 4 * (count // chunk)
        if turn == 0:
            made = pl.pallas_call(
                functools.partial(prepare_kernel, shared, per, scen_all, count, chunk),
                in_specs=[smem_spec] * 4 + [any_spec] * 5,
                out_specs=[vmem_spec] * 7,
                out_shape=laid_shapes
                + [VMEM((tie_count, 256, 256), bf16), VMEM((rows, 128), f32), VMEM((rows, 128), f32)],
                scratch_shapes=buffers(count)
                + [
                    VMEM((tie_count, 128, 128), f32),
                    VMEM((periods, scenarios, 128), f32),
                    pltpu.SemaphoreType.DMA((copies + 2,)),
                ],
                compiler_params=params(9),
                cost_estimate=cost(10**9, 10**6),
                name="prepare_0",
            )(in_smem(send), in_smem(source_of_tie), in_smem(labels), in_smem(factors), *inputs, in_hbm(tie_weight))
            laid["arrays"], laid["small"] = made[:4], made[4:]
            return [in_vmem(made[5])]
        laid["arrays"] = pl.pallas_call(
            functools.partial(prepare_more, shared, per, scen_all, ends[turn], count, chunk),
            in_specs=[any_spec] * 4 + [vmem_spec] * 6,
            out_specs=[vmem_spec] * 4,
            out_shape=laid_shapes,
            input_output_aliases={6: 0, 7: 1, 8: 2, 9: 3},
            scratch_shapes=buffers(count) + [pltpu.SemaphoreType.DMA((copies,))],
            compiler_params=params(9),
            cost_estimate=cost(10**9, 10**6),
            name=f"prepare_{turn}",
        )(*inputs, in_vmem(laid["small"][1]), in_vmem(after), *[in_vmem(a) for a in laid["arrays"]])
        return [in_vmem(laid["arrays"][1])] if turn < len(ends) - 2 else []

    totals = node_totals(sums, prepare)
    for turn in range(shared, len(ends) - 1):
        prepare(turn, totals[0])
    weights, state, parts, constant = laid["arrays"]
    ties, load, boundary = laid["small"]
    for iteration in range(STEPS):
        low = from_pair(boundary, "area")
        high = from_other(boundary, "area")
        state, parts = pl.pallas_call(
            step_kernel,
            in_specs=[smem_spec] + [vmem_spec] * 4,
            out_specs=[vmem_spec] * 2,
            out_shape=[state_shape, parts_shape],
            compiler_params=params(2),
            cost_estimate=cost(blocks * 2 * rows * 256 * 256 * 2, 12 * 10**6),
            name=f"step_{iteration}",
        )(in_smem(cols), in_vmem(weights), in_vmem(state), in_vmem(parts), in_vmem(constant))
        tie_args = [in_vmem(low), in_vmem(high), in_vmem(ties)]
        if iteration == 0:
            state, parts, constant, boundary = pl.pallas_call(
                functools.partial(anchor_kernel, shared, scen_all, scenarios),
                in_specs=[smem_spec] * 2 + [vmem_spec] * (6 + shared),
                out_specs=[vmem_spec] * 4,
                out_shape=[state_shape, parts_shape, state_shape, VMEM((rows, 128), f32)],
                input_output_aliases={5 + shared: 0, 6 + shared: 1, 7 + shared: 2},
                compiler_params=params(2),
                name="anchor",
            )(in_smem(row_of_tie), in_smem(send), *tie_args, *[in_vmem(t) for t in totals],
              in_vmem(state), in_vmem(parts), in_vmem(constant))
        elif iteration < STEPS - 1:
            state, parts, boundary = pl.pallas_call(
                tie_kernel,
                in_specs=[smem_spec] * 2 + [vmem_spec] * 5,
                out_specs=[vmem_spec] * 3,
                out_shape=[state_shape, parts_shape, VMEM((rows, 128), f32)],
                input_output_aliases={5: 0, 6: 1},
                compiler_params=params(2),
                name=f"ties_{iteration}",
            )(in_smem(row_of_tie), in_smem(send), *tie_args, in_vmem(state), in_vmem(parts))
        else:
            last = pl.pallas_call(
                functools.partial(last_tie_kernel, shared, per, scenarios),
                in_specs=[smem_spec] + [vmem_spec] * 5,
                out_specs=[vmem_spec] * (2 + shared),
                out_shape=[state_shape] + [VMEM((per, buses), f32)] * shared + [parts_shape],
                input_output_aliases={4: 0, 5: 1 + shared},
                compiler_params=params(2),
                name=f"ties_{iteration}",
            )(in_smem(row_of_tie), *tie_args, in_vmem(state), in_vmem(parts))
            state, sums = last[0], list(last[1 : 1 + shared])

    state = in_vmem(state)
    pieces = largest_divisor(blocks, 7)
    written = {}

    def write(turn, after):
        if turn == 0:
            written["dispatch"], written["head"] = pl.pallas_call(
                functools.partial(dispatch_kernel, pieces),
                in_specs=[vmem_spec, any_spec],
                out_specs=[any_spec, vmem_spec],
                out_shape=[
                    pltpu.HBM((periods, scenarios, buses), f32),
                    VMEM((shared * per, scenarios, buses), f32),
                ],
                scratch_shapes=[VMEM((periods, scenarios, buses), f32), pltpu.SemaphoreType.DMA((pieces + 1,))],
                compiler_params=params(6),
                cost_estimate=cost(10**9, 10**6),
                name="dispatch",
            )(state, in_hbm(multipliers))
            return [in_hbm(written["dispatch"])]
        if turn == 1:
            tail = VMEM((periods - shared * per, scenarios, buses), f32)
            written["mult"] = pl.pallas_call(
                functools.partial(own_kernel, shared, per, scen_all, pieces),
                in_specs=[vmem_spec, any_spec, vmem_spec],
                out_specs=any_spec,
                out_shape=pltpu.HBM((periods, scenarios, buses), f32),
                scratch_shapes=[tail, tail, pltpu.SemaphoreType.DMA((2 * pieces,))],
                compiler_params=params(8),
                cost_estimate=cost(10**9, 10**6),
                name="own_multipliers",
            )(state, in_hbm(multipliers), in_vmem(after))
            return [in_hbm(written["mult"])]
        return []

    totals = node_totals(sums, write)
    dispatch = written["dispatch"]
    new_mult = pl.pallas_call(
        functools.partial(finish_kernel, shared, per, scen_all, pieces),
        in_specs=[vmem_spec] * (2 + shared) + [any_spec],
        out_specs=any_spec,
        out_shape=pltpu.HBM((periods, scenarios, buses), f32),
        input_output_aliases={2 + shared: 0},
        scratch_shapes=[VMEM((shared * per, scenarios, buses), f32), pltpu.SemaphoreType.DMA((pieces,))],
        compiler_params=params(6),
        name="finish",
    )(state, in_vmem(written["head"]), *[in_vmem(t) for t in totals], in_hbm(written["mult"]))
    return dispatch, new_mult


def solution(mesh):
    in_specs = (
        P(None, "scen", "area"),
        P(None, "scen", "area"),
        P(None, "area"),
        P(),
        P(None, "scen"),
        P("area", None, None, None),
        P("area", None),
        P("area"),
        P("area"),
        P("area"),
        P("area", None, None),
    )
    out_specs = (P(None, "scen", "area"), P(None, "scen", "area"))
    return jax.shard_map(local, mesh=mesh, in_specs=in_specs, out_specs=out_specs, check_vma=False)
```

time: 91 us -> 75.2 us (0.83)
  waiting for transfers between devices: 20.4 us -> 10.4 us
  Pallas kernels: 45.2 us -> 38.9 us
  starting transfers between devices: 21 us -> 23.8 us
  local copies, waits for them, and re-layouts: 1.85 us -> 0 us
    ppermute x12, waiting for transfers between devices: 11.9 us -> 5.63 us  [swap(): lax.ppermute(block, axis, [(i, i ^ 1 << level) for i in range(count)])]
    pallas_call x4 -> x7, Pallas kernels: 23 us -> 16.8 us  [the longest x2 5.86 us: prepare(): pl.pallas_call(functools.partial(prepare_more, shared, per, scen_all, end...]
    ppermute x16, waiting for transfers between devices: 8.49 us -> 4.81 us  [the longest x8 4.78 us: from_other(): lax.ppermute(value, axis, [(i, (i + 1 if i % 2 else i - 1) % count) for i...]
    ppermute x16, starting transfers between devices: 6.45 us -> 8 us  [the longest x8 5.85 us: from_other(): lax.ppermute(value, axis, [(i, (i + 1 if i % 2 else i - 1) % count) for i...]
    unnamed x12 -> x0, local copies, waits for them, and re-layouts: 1.54 us -> none
    ppermute x12, starting transfers between devices: 14.5 us -> 15.8 us  [swap(): lax.ppermute(block, axis, [(i, i ^ 1 << level) for i in range(count)])]
  transfers between devices with their start and end apart: 28 -> 28, of which waited for: 15 -> 12; matrix products, arithmetic and copies ran while one was open for 0% -> 0% of each run, Pallas kernels for 41% -> 43%
where the time goes in v2:
time: 75.2 us; the launch traced here: 75 us
  Pallas kernels  38.9 us (52%)
  starting transfers between devices  23.8 us (32%)
  waiting for transfers between devices  10.4 us (14%)
  between operations  1.78 us (2%)
    pallas_call x8, Pallas kernels, local(): pl.pallas_call(step_kernel, in_specs=[smem_spec] + [vmem_spec] * 4, out_s...  18.4 us
    ppermute x12, starting transfers between devices, swap(): lax.ppermute(block, axis, [(i, i ^ 1 << level) for i in range(count)])  15.8 us
    pallas_call x2, Pallas kernels, prepare(): pl.pallas_call(functools.partial(prepare_more, shared, per, scen_all, end...  5.86 us
    ppermute x8, starting transfers between devices, from_other(): lax.ppermute(value, axis, [(i, (i + 1 if i % 2 else i - 1) % count) for i...  5.85 us
    ppermute x12, waiting for transfers between devices, swap(): lax.ppermute(block, axis, [(i, i ^ 1 << level) for i in range(count)])  5.63 us
    ppermute x8, waiting for transfers between devices, from_other(): lax.ppermute(value, axis, [(i, (i + 1 if i % 2 else i - 1) % count) for i...  4.78 us
    pallas_call x1, Pallas kernels, prepare(): pl.pallas_call(functools.partial(prepare_kernel, shared, per, scen_all, c...  3.58 us
    pallas_call x1, Pallas kernels, write(): pl.pallas_call(functools.partial(own_kernel, shared, per, scen_all, piece...  2.72 us
  transfers between devices with their start and end apart: 28, of which 12 were waited for; matrix products, arithmetic and copies ran while one was open for 0% of the time, Pallas kernels for 43%

profile of v2, /device:TPU:0, one launch (start us, length us, event | category | flops | bytes accessed | tf_op | source)
XLA Modules:
  0.0 75.0 jit_solution(10674506349919445399)
XLA Ops:
  1.3 1.6 %first_sums.1 = (f32[2,8960]{1,0:T(2,128)S(1)}, f32[2,8960]{1,0:T(2,128)S(1)}, f32[2,8960]{1,0:T(2,128)S(1)}, s32[2,70]{1,0:T(2,128)S(4)}, s32[4]{0:T(128)S(4)},...) custom-call(s32[1]{0:T(128)S(6)} %copy.65.send, f32[24,4,8960]{2,1,0:T(4,128)} %start.7, ...), custom_call_target="tpu_custom_call" | custom-call | tf_op jit(solution)/shard_map/first_sums/pallas_call | solution.py:404
  2.9 4.1 %collective-permute-start.2 = (f32[2,8960]{1,0:T(2,128)S(1)}, f32[2,8960]{1,0:T(2,128)S(1)}, u32[]{:S(2)}, u32[]{:S(2)}) collective-permute-start(f32[2,8960]{1,0:T(2,128)S(1)} %get-tuple-element.87.refs_0_), channel_id=1, source_target_pairs={{0,4},{1,5},{2,6},{3,7},{4,0},{5,1},{6,2},{7,3},{8,12},{9,13},{10,... | collective-permute-start | bytes 215048 | tf_op jit(solution)/shard_map/ppermute | solution.py:140
  7.0 1.6 %collective-permute-start.3 = (f32[2,8960]{1,0:T(2,128)S(1)}, f32[2,8960]{1,0:T(2,128)S(1)}, u32[]{:S(2)}, u32[]{:S(2)}) collective-permute-start(f32[2,8960]{1,0:T(2,128)S(1)} %get-tuple-element.88.refs_1_), channel_id=1, source_target_pairs={{0,2},{1,3},{2,0},{3,1},{4,6},{5,7},{6,4},{7,5},{8,10},{9,11},{10,... | collective-permute-start | bytes 215048 | tf_op jit(solution)/shard_map/ppermute | solution.py:140
  8.6 1.5 %collective-permute-start.4 = (f32[2,8960]{1,0:T(2,128)S(1)}, f32[2,8960]{1,0:T(2,128)S(1)}, u32[]{:S(2)}, u32[]{:S(2)}) collective-permute-start(f32[2,8960]{1,0:T(2,128)S(1)} %get-tuple-element.89.refs_2_), channel_id=1, source_target_pairs={{0,1},{1,0},{2,3},{3,2},{4,5},{5,4},{6,7},{7,6},{8,9},{9,8},{10,11... | collective-permute-start | bytes 215048 | tf_op jit(solution)/shard_map/ppermute | solution.py:140
  10.1 3.6 %prepare_0.1 = (bf16[70,256,256]{2,1,0:T(8,128)(2,1)S(1)}, f32[70,96,128]{2,1,0:T(8,128)S(1)}, bf16[70,192,128]{2,1,0:T(8,128)(2,1)S(1)}, f32[70,96,128]{2,1,0:T...) custom-call(s32[1]{0:T(128)S(4)} %get-tuple-element.81.send, ...), custom_call_target="tpu_custom_call" | custom-call | flops 1000000000 | bytes 1000000 | tf_op jit(solution)/shard_map/prepare_0/pallas_call | solution.py:443
  13.7 0.1 collective-permute-start
  13.7 1.6 %collective-permute-start.1 = (f32[96,128]{1,0:T(8,128)S(1)}, f32[96,128]{1,0:T(8,128)S(1)}, u32[]{:S(2)}, u32[]{:S(2)}) collective-permute-start(f32[96,128]{1,0:T(8,128)S(1)} %get-tuple-element.85), channel_id=1, source_target_pairs={{0,24},{8,16},{16,8},{24,0},{1,25},{9,17},{17,9},{25,1},{2,26},{10... | collective-permute-start | bytes 147464 | tf_op jit(solution)/shard_map/ppermute | solution.py:150
  15.4 0.5 collective-permute-start.5
  15.9 0.5 collective-permute-start.6
  16.5 2.9 %prepare_1.1 = (bf16[70,256,256]{2,1,0:T(8,128)(2,1)S(1)}, f32[70,96,128]{2,1,0:T(8,128)S(1)}, bf16[70,192,128]{2,1,0:T(8,128)(2,1)S(1)}, f32[70,96,128]{2,1,0:T(8,128)S(1)}) custom-call(f32[70,2,128,128]{3,2,1,0:T(8,128)} %values.5, f32[24,4,8960]{2,1,0:T(4,128)} %start.7, ...), custom_call_target="tpu_custom_call", output_to_operand_aliasing={{0}: (6, {}), {1}: (7, {}), {2}: (8, {}), {3}: (9, {})} | custom-call | flops 1000000000 | bytes 1000000 | tf_op jit(solution)/shard_map/prepare_1/pallas_call | solution.py:461
  19.4 0.4 collective-permute-done.5.refs_2_
  19.8 0.4 collective-permute-done.6.refs_3_
  20.3 0.7 collective-permute-start.7
  21.0 2.9 %prepare_2.1 = (bf16[70,256,256]{2,1,0:T(8,128)(2,1)S(1)}, f32[70,96,128]{2,1,0:T(8,128)S(1)}, bf16[70,192,128]{2,1,0:T(8,128)(2,1)S(1)}, f32[70,96,128]{2,1,0:T(8,128)S(1)}) custom-call(f32[70,2,128,128]{3,2,1,0:T(8,128)} %values.5, f32[24,4,8960]{2,1,0:T(4,128)} %start.7, ...), custom_call_target="tpu_custom_call", output_to_operand_aliasing={{0}: (6, {}), {1}: (7, {}), {2}: (8, {}), {3}: (9, {})} | custom-call | flops 1000000000 | bytes 1000000 | tf_op jit(solution)/shard_map/prepare_2/pallas_call | solution.py:461
  24.0 2.1 %step_0.1 = (f32[70,96,128]{2,1,0:T(8,128)S(1)}, bf16[70,192,128]{2,1,0:T(8,128)(2,1)S(1)}) custom-call(s32[2,70]{1,0:T(2,128)S(4)} %get-tuple-element.101.cols, bf16[70,256,256]{2,1,0:T(8,128)(2,1)S(1)} %get-tuple-element.105.weights, f32[70,96,128]{2,1,0:T(8,128)S(1)} %get-tuple-element.106.state, bf16[70,192,128]{2,1,0:T(8,128)(2,1)S(1)} %get-tuple-element.107.parts, ...), custom_call_target="tpu_custom_call" | custom-call | flops 1761607680 | bytes 12000000 | tf_op jit(solution)/shard_map/step_0/pallas_call | solution.py:482
  26.1 0.0 collective-permute-done.low
  26.1 1.0 %anchor.1 = (f32[70,96,128]{2,1,0:T(8,128)S(1)}, bf16[70,192,128]{2,1,0:T(8,128)(2,1)S(1)}, f32[70,96,128]{2,1,0:T(8,128)S(1)}, f32[96,128]{1,0:T(8,128)S(1)}) custom-call(s32[4]{0:T(128)S(4)} %get-tuple-element.80.tie_row, s32[1]{0:T(128)S(4)} %get-tuple-element.81.send, ...), custom_call_target="tpu_custom_call", output_to_operand_aliasing={{0}: (8, {}), {1}: (9, {}), {2}: (10, {})} | custom-call | tf_op jit(solution)/shard_map/anchor/pallas_call | solution.py:493
  27.1 0.1 collective-permute-start.8
  27.2 0.6 collective-permute-start.9
  27.8 2.5 %step_1.1 = (f32[70,96,128]{2,1,0:T(8,128)S(1)}, bf16[70,192,128]{2,1,0:T(8,128)(2,1)S(1)}) custom-call(s32[2,70]{1,0:T(2,128)S(4)} %get-tuple-element.101.cols, bf16[70,256,256]{2,1,0:T(8,128)(2,1)S(1)} %get-tuple-element.105.weights, f32[70,96,128]{2,1,0:T(8,128)S(1)} %get-tuple-element.112.state, bf16[70,192,128]{2,1,0:T(8,128)(2,1)S(1)} %get-tuple-element.113.parts, ...), custom_call_target="tpu_custom_call" | custom-call | flops 1761607680 | bytes 12000000 | tf_op jit(solution)/shard_map/step_1/pallas_call | solution.py:482
  30.3 0.5 collective-permute-done.9.high
  30.7 0.3 ties_1.1
  31.0 0.5 collective-permute-start.10
  31.6 0.8 %collective-permute-start.11 = (f32[96,128]{1,0:T(8,128)S(1)}, f32[96,128]{1,0:T(8,128)S(1)}, u32[]{:S(2)}, u32[]{:S(2)}) collective-permute-start(f32[96,128]{1,0:T(8,128)S(1)} %get-tuple-element.117), channel_id=1, source_target_pairs={{0,24},{8,16},{16,8},{24,0},{1,25},{9,17},{17,9},{25,1},{2,26},{10... | collective-permute-start | bytes 147464 | tf_op jit(solution)/shard_map/ppermute | solution.py:150
  32.3 2.4 %step_2.1 = (f32[70,96,128]{2,1,0:T(8,128)S(1)}, bf16[70,192,128]{2,1,0:T(8,128)(2,1)S(1)}) custom-call(s32[2,70]{1,0:T(2,128)S(4)} %get-tuple-element.101.cols, bf16[70,256,256]{2,1,0:T(8,128)(2,1)S(1)} %get-tuple-element.105.weights, f32[70,96,128]{2,1,0:T(8,128)S(1)} %get-tuple-element.118.state, bf16[70,192,128]{2,1,0:T(8,128)(2,1)S(1)} %get-tuple-element.119.parts, ...), custom_call_target="tpu_custom_call" | custom-call | flops 1761607680 | bytes 12000000 | tf_op jit(solution)/shard_map/step_2/pallas_call | solution.py:482
  34.8 0.6 collective-permute-done.11.high
  35.3 0.3 ties_2.1
  35.6 0.2 collective-permute-start.12
  35.8 0.5 collective-permute-start.13
  36.3 2.1 %step_3.1 = (f32[70,96,128]{2,1,0:T(8,128)S(1)}, bf16[70,192,128]{2,1,0:T(8,128)(2,1)S(1)}) custom-call(s32[2,70]{1,0:T(2,128)S(4)} %get-tuple-element.101.cols, bf16[70,256,256]{2,1,0:T(8,128)(2,1)S(1)} %get-tuple-element.105.weights, f32[70,96,128]{2,1,0:T(8,128)S(1)} %get-tuple-element.123.state, bf16[70,192,128]{2,1,0:T(8,128)(2,1)S(1)} %get-tuple-element.124.parts, ...), custom_call_target="tpu_custom_call" | custom-call | flops 1761607680 | bytes 12000000 | tf_op jit(solution)/shard_map/step_3/pallas_call | solution.py:482
  38.4 0.9 %collective-permute-done.13.high = f32[96,128]{1,0:T(8,128)S(1)} collective-permute-done((f32[96,128]{1,0:T(8,128)S(1)}, f32[96,128]{1,0:T(8,128)S(1)}, u32[]{:S(2)}, u32[]{:S(2)}) %collective-permute-start.13) | collective-permute-done | bytes 49184 | tf_op jit(solution)/shard_map/ppermute | solution.py:150
  39.3 0.3 ties_3.1
  39.6 0.5 collective-permute-start.14
  40.1 0.7 collective-permute-start.15
  40.9 2.4 %step_4.1 = (f32[70,96,128]{2,1,0:T(8,128)S(1)}, bf16[70,192,128]{2,1,0:T(8,128)(2,1)S(1)}) custom-call(s32[2,70]{1,0:T(2,128)S(4)} %get-tuple-element.101.cols, bf16[70,256,256]{2,1,0:T(8,128)(2,1)S(1)} %get-tuple-element.105.weights, f32[70,96,128]{2,1,0:T(8,128)S(1)} %get-tuple-element.128.state, bf16[70,192,128]{2,1,0:T(8,128)(2,1)S(1)} %get-tuple-element.129.parts, ...), custom_call_target="tpu_custom_call" | custom-call | flops 1761607680 | bytes 12000000 | tf_op jit(solution)/shard_map/step_4/pallas_call | solution.py:482
  43.3 0.6 collective-permute-done.15.high
  43.9 0.3 ties_4.1
  44.2 0.2 collective-permute-start.16
  44.4 0.5 collective-permute-start.17
  44.9 2.3 %step_5.1 = (f32[70,96,128]{2,1,0:T(8,128)S(1)}, bf16[70,192,128]{2,1,0:T(8,128)(2,1)S(1)}) custom-call(s32[2,70]{1,0:T(2,128)S(4)} %get-tuple-element.101.cols, bf16[70,256,256]{2,1,0:T(8,128)(2,1)S(1)} %get-tuple-element.105.weights, f32[70,96,128]{2,1,0:T(8,128)S(1)} %get-tuple-element.133.state, bf16[70,192,128]{2,1,0:T(8,128)(2,1)S(1)} %get-tuple-element.134.parts, ...), custom_call_target="tpu_custom_call" | custom-call | flops 1761607680 | bytes 12000000 | tf_op jit(solution)/shard_map/step_5/pallas_call | solution.py:482
  47.3 0.7 collective-permute-done.17.high
  48.0 0.3 ties_5.1
  48.3 0.4 collective-permute-start.18
  48.7 0.7 collective-permute-start.19
  49.3 2.4 %step_6.1 = (f32[70,96,128]{2,1,0:T(8,128)S(1)}, bf16[70,192,128]{2,1,0:T(8,128)(2,1)S(1)}) custom-call(s32[2,70]{1,0:T(2,128)S(4)} %get-tuple-element.101.cols, bf16[70,256,256]{2,1,0:T(8,128)(2,1)S(1)} %get-tuple-element.105.weights, f32[70,96,128]{2,1,0:T(8,128)S(1)} %get-tuple-element.138.state, bf16[70,192,128]{2,1,0:T(8,128)(2,1)S(1)} %get-tuple-element.139.parts, ...), custom_call_target="tpu_custom_call" | custom-call | flops 1761607680 | bytes 12000000 | tf_op jit(solution)/shard_map/step_6/pallas_call | solution.py:482
  51.8 0.6 collective-permute-done.19.high
  52.4 0.3 ties_6.1
  52.7 0.2 collective-permute-start.20
  52.9 0.5 collective-permute-start.21
  53.4 2.1 %step_7.1 = (f32[70,96,128]{2,1,0:T(8,128)S(1)}, bf16[70,192,128]{2,1,0:T(8,128)(2,1)S(1)}) custom-call(s32[2,70]{1,0:T(2,128)S(4)} %get-tuple-element.101.cols, bf16[70,256,256]{2,1,0:T(8,128)(2,1)S(1)} %get-tuple-element.105.weights, f32[70,96,128]{2,1,0:T(8,128)S(1)} %get-tuple-element.143.state, bf16[70,192,128]{2,1,0:T(8,128)(2,1)S(1)} %get-tuple-element.144.parts, ...), custom_call_target="tpu_custom_call" | custom-call | flops 1761607680 | bytes 12000000 | tf_op jit(solution)/shard_map/step_7/pallas_call | solution.py:482
  55.5 0.9 %collective-permute-done.21.high = f32[96,128]{1,0:T(8,128)S(1)} collective-permute-done((f32[96,128]{1,0:T(8,128)S(1)}, f32[96,128]{1,0:T(8,128)S(1)}, u32[]{:S(2)}, u32[]{:S(2)}) %collective-permute-start.21) | collective-permute-done | bytes 49184 | tf_op jit(solution)/shard_map/ppermute | solution.py:150
  56.5 0.8 %ties_7.1 = (f32[70,96,128]{2,1,0:T(8,128)S(1)}, f32[2,8960]{1,0:T(2,128)S(1)}, f32[2,8960]{1,0:T(2,128)S(1)}, f32[2,8960]{1,0:T(2,128)S(1)}, bf16[70,192,128]{2,1,0:T(8,128)(2,1)S(1)}) custom-call(s32[4]{0:T(128)S(4)} %get-tuple-element.80.tie_row, f32[96,128]{1,0:T(8,128)S(1)} %collective-permute-done.20.low, ...), custom_call_target="tpu_custom_call", output_to_operand_aliasing={{0}: (4, {}), {4}: (5, {})} | custom-call | tf_op jit(solution)/shard_map/ties_7/pallas_call | solution.py:514
  57.3 0.3 collective-permute-start.22
  57.6 1.7 %collective-permute-start.23 = (f32[2,8960]{1,0:T(2,128)S(1)}, f32[2,8960]{1,0:T(2,128)S(1)}, u32[]{:S(2)}, u32[]{:S(2)}) collective-permute-start(f32[2,8960]{1,0:T(2,128)S(1)} %get-tuple-element.151.refs_1_), channel_id=1, source_target_pairs={{0,2},{1,3},{2,0},{3,1},{4,6},{5,7},{6,4},{7,5},{8,10},{9,11},{10,... | collective-permute-start | bytes 215048 | tf_op jit(solution)/shard_map/ppermute | solution.py:140
  59.3 1.2 %collective-permute-start.24 = (f32[2,8960]{1,0:T(2,128)S(1)}, f32[2,8960]{1,0:T(2,128)S(1)}, u32[]{:S(2)}, u32[]{:S(2)}) collective-permute-start(f32[2,8960]{1,0:T(2,128)S(1)} %get-tuple-element.152.refs_2_), channel_id=1, source_target_pairs={{0,1},{1,0},{2,3},{3,2},{4,5},{5,4},{6,7},{7,6},{8,9},{9,8},{10,11... | collective-permute-start | bytes 215048 | tf_op jit(solution)/shard_map/ppermute | solution.py:140
  60.5 1.9 %dispatch.1 = (f32[24,4,8960]{2,1,0:T(4,128)}, f32[6,4,8960]{2,1,0:T(4,128)S(1)}) custom-call(f32[70,96,128]{2,1,0:T(8,128)S(1)} %get-tuple-element.147.state, f32[24,4,8960]{2,1,0:T(4,128)} %mult.9), custom_call_target="tpu_custom_call" | custom-call | flops 1000000000 | bytes 1000000 | tf_op jit(solution)/shard_map/dispatch/pallas_call | solution.py:531
  62.4 1.9 %collective-permute-done.22.refs_3_ = f32[2,8960]{1,0:T(2,128)S(1)} collective-permute-done((f32[2,8960]{1,0:T(2,128)S(1)}, f32[2,8960]{1,0:T(2,128)S(1)}, u32[]{:S(2)}, u32[]{:S(2)}) %collective-permute-start.22) | collective-permute-done | bytes 71712 | tf_op jit(solution)/shard_map/ppermute | solution.py:140
  64.3 0.6 collective-permute-start.25
  64.9 1.5 %collective-permute-start.26 = (f32[2,8960]{1,0:T(2,128)S(1)}, f32[2,8960]{1,0:T(2,128)S(1)}, u32[]{:S(2)}, u32[]{:S(2)}) collective-permute-start(f32[2,8960]{1,0:T(2,128)S(1)} %get-tuple-element.154.refs_1_), channel_id=1, source_target_pairs={{0,1},{1,0},{2,3},{3,2},{4,5},{5,4},{6,7},{7,6},{8,9},{9,8},{10,11... | collective-permute-start | bytes 215048 | tf_op jit(solution)/shard_map/ppermute | solution.py:140
  66.4 2.7 %own_multipliers.1.refs_4_.refs_3_ = f32[24,4,8960]{2,1,0:T(4,128)} custom-call(f32[70,96,128]{2,1,0:T(8,128)S(1)} %get-tuple-element.147.state, f32[24,4,8960]{2,1,0:T(4,128)} %mult.9, f32[2,8960]{1,0:T(2,128)S(1)} %get-tuple-element.153.after.refs_0_), custom_call_target="tpu_custom_call" | custom-call | flops 1000000000 | bytes 1000000 | tf_op jit(solution)/shard_map/own_multipliers/pallas_call | solution.py:547
  69.1 0.1 collective-permute-done.26.refs_3_
  69.2 1.6 %collective-permute-start.27 = (f32[2,8960]{1,0:T(2,128)S(1)}, f32[2,8960]{1,0:T(2,128)S(1)}, u32[]{:S(2)}, u32[]{:S(2)}) collective-permute-start(f32[2,8960]{1,0:T(2,128)S(1)} %get-tuple-element.155.refs_0_), channel_id=1, source_target_pairs={{0,1},{1,0},{2,3},{3,2},{4,5},{5,4},{6,7},{7,6},{8,9},{9,8},{10,11... | collective-permute-start | bytes 215048 | tf_op jit(solution)/shard_map/ppermute | solution.py:140
  70.8 2.8 %collective-permute-done.27.refs_1_ = f32[2,8960]{1,0:T(2,128)S(1)} collective-permute-done((f32[2,8960]{1,0:T(2,128)S(1)}, f32[2,8960]{1,0:T(2,128)S(1)}, u32[]{:S(2)}, u32[]{:S(2)}) %collective-permute-start.27) | collective-permute-done | bytes 71712 | tf_op jit(solution)/shard_map/ppermute | solution.py:140
  73.6 1.2 %finish.1 = f32[24,4,8960]{2,1,0:T(4,128)} custom-call(f32[70,96,128]{2,1,0:T(8,128)S(1)} %get-tuple-element.147.state, f32[6,4,8960]{2,1,0:T(4,128)S(1)} %get-tuple-element.149.mult, f32[2,8960]{1,0:T(2,128)S(1)} %node_add_2.3.refs_0_, f32[2,8960]{1,0:T(2,128)S(1)} %get-tuple-element.156.refs_1_, ...), custom_call_target="tpu_custom_call", output_to_operand_aliasing={{}: (5, {})} | custom-call | tf_op jit(solution)/shard_map/finish/pallas_call | solution.py:562
  (21 shorter events, 0.2 us)
Async XLA Ops:
  2.9 12.5 %collective-permute-start.2 = (f32[2,8960]{1,0:T(2,128)S(1)}, f32[2,8960]{1,0:T(2,128)S(1)}, u32[]{:S(2)}, u32[]{:S(2)}) collective-permute-start(f32[2,8960]{1,0:T(2,128)S(1)} %get-tuple-element.87.refs_0_), channel_id=1, source_target_pairs={{0,4},{1,5},{2,6},{3,7},{4,0},{5,1},{6,2},{7,3},{8,12},{9,13},{10,... | collective-permute-start | bytes 215048 | tf_op jit(solution)/shard_map/ppermute | solution.py:140
  7.0 8.4 %collective-permute-start.3 = (f32[2,8960]{1,0:T(2,128)S(1)}, f32[2,8960]{1,0:T(2,128)S(1)}, u32[]{:S(2)}, u32[]{:S(2)}) collective-permute-start(f32[2,8960]{1,0:T(2,128)S(1)} %get-tuple-element.88.refs_1_), channel_id=1, source_target_pairs={{0,2},{1,3},{2,0},{3,1},{4,6},{5,7},{6,4},{7,5},{8,10},{9,11},{10,... | collective-permute-start | bytes 215048 | tf_op jit(solution)/shard_map/ppermute | solution.py:140
  8.6 6.8 %collective-permute-start.4 = (f32[2,8960]{1,0:T(2,128)S(1)}, f32[2,8960]{1,0:T(2,128)S(1)}, u32[]{:S(2)}, u32[]{:S(2)}) collective-permute-start(f32[2,8960]{1,0:T(2,128)S(1)} %get-tuple-element.89.refs_2_), channel_id=1, source_target_pairs={{0,1},{1,0},{2,3},{3,2},{4,5},{5,4},{6,7},{7,6},{8,9},{9,8},{10,11... | collective-permute-start | bytes 215048 | tf_op jit(solution)/shard_map/ppermute | solution.py:140
  13.7 12.4 %collective-permute-start = (f32[96,128]{1,0:T(8,128)S(1)}, f32[96,128]{1,0:T(8,128)S(1)}, u32[]{:S(2)}, u32[]{:S(2)}) collective-permute-start(f32[96,128]{1,0:T(8,128)S(1)} %get-tuple-element.85), channel_id=1, source_target_pairs={{0,8},{8,0},{16,24},{24,16},{1,9},{9,1},{17,25},{25,17},{2,10},{10... | collective-permute-start | bytes 147464 | tf_op jit(solution)/shard_map/ppermute | solution.py:145
  13.7 12.4 %collective-permute-start.1 = (f32[96,128]{1,0:T(8,128)S(1)}, f32[96,128]{1,0:T(8,128)S(1)}, u32[]{:S(2)}, u32[]{:S(2)}) collective-permute-start(f32[96,128]{1,0:T(8,128)S(1)} %get-tuple-element.85), channel_id=1, source_target_pairs={{0,24},{8,16},{16,8},{24,0},{1,25},{9,17},{17,9},{25,1},{2,26},{10... | collective-permute-start | bytes 147464 | tf_op jit(solution)/shard_map/ppermute | solution.py:150
  15.4 4.4 %collective-permute-start.5 = (f32[2,8960]{1,0:T(2,128)S(1)}, f32[2,8960]{1,0:T(2,128)S(1)}, u32[]{:S(2)}, u32[]{:S(2)}) collective-permute-start(f32[2,8960]{1,0:T(2,128)S(1)} %get-tuple-element.91.after.refs_0_), channel_id=1, source_target_pairs={{0,2},{1,3},{2,0},{3,1},{4,6},{5,7},{6,4},{7,5},{8,10},{9,11},{10,... | collective-permute-start | bytes 215048 | tf_op jit(solution)/shard_map/ppermute | solution.py:140
  15.9 4.3 %collective-permute-start.6 = (f32[2,8960]{1,0:T(2,128)S(1)}, f32[2,8960]{1,0:T(2,128)S(1)}, u32[]{:S(2)}, u32[]{:S(2)}) collective-permute-start(f32[2,8960]{1,0:T(2,128)S(1)} %get-tuple-element.92.refs_1_), channel_id=1, source_target_pairs={{0,1},{1,0},{2,3},{3,2},{4,5},{5,4},{6,7},{7,6},{8,9},{9,8},{10,11... | collective-permute-start | bytes 215048 | tf_op jit(solution)/shard_map/ppermute | solution.py:140
  20.3 5.8 %collective-permute-start.7 = (f32[2,8960]{1,0:T(2,128)S(1)}, f32[2,8960]{1,0:T(2,128)S(1)}, u32[]{:S(2)}, u32[]{:S(2)}) collective-permute-start(f32[2,8960]{1,0:T(2,128)S(1)} %get-tuple-element.98.refs_0_.after), channel_id=1, source_target_pairs={{0,1},{1,0},{2,3},{3,2},{4,5},{5,4},{6,7},{7,6},{8,9},{9,8},{10,11... | collective-permute-start | bytes 215048 | tf_op jit(solution)/shard_map/ppermute | solution.py:140
  27.1 3.2 %collective-permute-start.8 = (f32[96,128]{1,0:T(8,128)S(1)}, f32[96,128]{1,0:T(8,128)S(1)}, u32[]{:S(2)}, u32[]{:S(2)}) collective-permute-start(f32[96,128]{1,0:T(8,128)S(1)} %get-tuple-element.111), channel_id=1, source_target_pairs={{0,8},{8,0},{16,24},{24,16},{1,9},{9,1},{17,25},{25,17},{2,10},{10... | collective-permute-start | bytes 147464 | tf_op jit(solution)/shard_map/ppermute | solution.py:145
  27.2 3.6 %collective-permute-start.9 = (f32[96,128]{1,0:T(8,128)S(1)}, f32[96,128]{1,0:T(8,128)S(1)}, u32[]{:S(2)}, u32[]{:S(2)}) collective-permute-start(f32[96,128]{1,0:T(8,128)S(1)} %get-tuple-element.111), channel_id=1, source_target_pairs={{0,24},{8,16},{16,8},{24,0},{1,25},{9,17},{17,9},{25,1},{2,26},{10... | collective-permute-start | bytes 147464 | tf_op jit(solution)/shard_map/ppermute | solution.py:150
  31.0 3.7 %collective-permute-start.10 = (f32[96,128]{1,0:T(8,128)S(1)}, f32[96,128]{1,0:T(8,128)S(1)}, u32[]{:S(2)}, u32[]{:S(2)}) collective-permute-start(f32[96,128]{1,0:T(8,128)S(1)} %get-tuple-element.117), channel_id=1, source_target_pairs={{0,8},{8,0},{16,24},{24,16},{1,9},{9,1},{17,25},{25,17},{2,10},{10... | collective-permute-start | bytes 147464 | tf_op jit(solution)/shard_map/ppermute | solution.py:145
  31.6 3.8 %collective-permute-start.11 = (f32[96,128]{1,0:T(8,128)S(1)}, f32[96,128]{1,0:T(8,128)S(1)}, u32[]{:S(2)}, u32[]{:S(2)}) collective-permute-start(f32[96,128]{1,0:T(8,128)S(1)} %get-tuple-element.117), channel_id=1, source_target_pairs={{0,24},{8,16},{16,8},{24,0},{1,25},{9,17},{17,9},{25,1},{2,26},{10... | collective-permute-start | bytes 147464 | tf_op jit(solution)/shard_map/ppermute | solution.py:150
  35.6 2.7 %collective-permute-start.12 = (f32[96,128]{1,0:T(8,128)S(1)}, f32[96,128]{1,0:T(8,128)S(1)}, u32[]{:S(2)}, u32[]{:S(2)}) collective-permute-start(f32[96,128]{1,0:T(8,128)S(1)} %get-tuple-element.122), channel_id=1, source_target_pairs={{0,8},{8,0},{16,24},{24,16},{1,9},{9,1},{17,25},{25,17},{2,10},{10... | collective-permute-start | bytes 147464 | tf_op jit(solution)/shard_map/ppermute | solution.py:145
  35.8 3.5 %collective-permute-start.13 = (f32[96,128]{1,0:T(8,128)S(1)}, f32[96,128]{1,0:T(8,128)S(1)}, u32[]{:S(2)}, u32[]{:S(2)}) collective-permute-start(f32[96,128]{1,0:T(8,128)S(1)} %get-tuple-element.122), channel_id=1, source_target_pairs={{0,24},{8,16},{16,8},{24,0},{1,25},{9,17},{17,9},{25,1},{2,26},{10... | collective-permute-start | bytes 147464 | tf_op jit(solution)/shard_map/ppermute | solution.py:150
  39.6 3.7 %collective-permute-start.14 = (f32[96,128]{1,0:T(8,128)S(1)}, f32[96,128]{1,0:T(8,128)S(1)}, u32[]{:S(2)}, u32[]{:S(2)}) collective-permute-start(f32[96,128]{1,0:T(8,128)S(1)} %get-tuple-element.127), channel_id=1, source_target_pairs={{0,8},{8,0},{16,24},{24,16},{1,9},{9,1},{17,25},{25,17},{2,10},{10... | collective-permute-start | bytes 147464 | tf_op jit(solution)/shard_map/ppermute | solution.py:145
  40.1 3.8 %collective-permute-start.15 = (f32[96,128]{1,0:T(8,128)S(1)}, f32[96,128]{1,0:T(8,128)S(1)}, u32[]{:S(2)}, u32[]{:S(2)}) collective-permute-start(f32[96,128]{1,0:T(8,128)S(1)} %get-tuple-element.127), channel_id=1, source_target_pairs={{0,24},{8,16},{16,8},{24,0},{1,25},{9,17},{17,9},{25,1},{2,26},{10... | collective-permute-start | bytes 147464 | tf_op jit(solution)/shard_map/ppermute | solution.py:150
  44.2 3.0 %collective-permute-start.16 = (f32[96,128]{1,0:T(8,128)S(1)}, f32[96,128]{1,0:T(8,128)S(1)}, u32[]{:S(2)}, u32[]{:S(2)}) collective-permute-start(f32[96,128]{1,0:T(8,128)S(1)} %get-tuple-element.132), channel_id=1, source_target_pairs={{0,8},{8,0},{16,24},{24,16},{1,9},{9,1},{17,25},{25,17},{2,10},{10... | collective-permute-start | bytes 147464 | tf_op jit(solution)/shard_map/ppermute | solution.py:145
  44.4 3.5 %collective-permute-start.17 = (f32[96,128]{1,0:T(8,128)S(1)}, f32[96,128]{1,0:T(8,128)S(1)}, u32[]{:S(2)}, u32[]{:S(2)}) collective-permute-start(f32[96,128]{1,0:T(8,128)S(1)} %get-tuple-element.132), channel_id=1, source_target_pairs={{0,24},{8,16},{16,8},{24,0},{1,25},{9,17},{17,9},{25,1},{2,26},{10... | collective-permute-start | bytes 147464 | tf_op jit(solution)/shard_map/ppermute | solution.py:150
  48.3 3.5 %collective-permute-start.18 = (f32[96,128]{1,0:T(8,128)S(1)}, f32[96,128]{1,0:T(8,128)S(1)}, u32[]{:S(2)}, u32[]{:S(2)}) collective-permute-start(f32[96,128]{1,0:T(8,128)S(1)} %get-tuple-element.137), channel_id=1, source_target_pairs={{0,8},{8,0},{16,24},{24,16},{1,9},{9,1},{17,25},{25,17},{2,10},{10... | collective-permute-start | bytes 147464 | tf_op jit(solution)/shard_map/ppermute | solution.py:145
  48.7 3.7 %collective-permute-start.19 = (f32[96,128]{1,0:T(8,128)S(1)}, f32[96,128]{1,0:T(8,128)S(1)}, u32[]{:S(2)}, u32[]{:S(2)}) collective-permute-start(f32[96,128]{1,0:T(8,128)S(1)} %get-tuple-element.137), channel_id=1, source_target_pairs={{0,24},{8,16},{16,8},{24,0},{1,25},{9,17},{17,9},{25,1},{2,26},{10... | collective-permute-start | bytes 147464 | tf_op jit(solution)/shard_map/ppermute | solution.py:150
  52.7 2.8 %collective-permute-start.20 = (f32[96,128]{1,0:T(8,128)S(1)}, f32[96,128]{1,0:T(8,128)S(1)}, u32[]{:S(2)}, u32[]{:S(2)}) collective-permute-start(f32[96,128]{1,0:T(8,128)S(1)} %get-tuple-element.142), channel_id=1, source_target_pairs={{0,8},{8,0},{16,24},{24,16},{1,9},{9,1},{17,25},{25,17},{2,10},{10... | collective-permute-start | bytes 147464 | tf_op jit(solution)/shard_map/ppermute | solution.py:145
  52.9 3.5 %collective-permute-start.21 = (f32[96,128]{1,0:T(8,128)S(1)}, f32[96,128]{1,0:T(8,128)S(1)}, u32[]{:S(2)}, u32[]{:S(2)}) collective-permute-start(f32[96,128]{1,0:T(8,128)S(1)} %get-tuple-element.142), channel_id=1, source_target_pairs={{0,24},{8,16},{16,8},{24,0},{1,25},{9,17},{17,9},{25,1},{2,26},{10... | collective-permute-start | bytes 147464 | tf_op jit(solution)/shard_map/ppermute | solution.py:150
  57.3 7.0 %collective-permute-start.22 = (f32[2,8960]{1,0:T(2,128)S(1)}, f32[2,8960]{1,0:T(2,128)S(1)}, u32[]{:S(2)}, u32[]{:S(2)}) collective-permute-start(f32[2,8960]{1,0:T(2,128)S(1)} %get-tuple-element.150.refs_0_), channel_id=1, source_target_pairs={{0,4},{1,5},{2,6},{3,7},{4,0},{5,1},{6,2},{7,3},{8,12},{9,13},{10,... | collective-permute-start | bytes 215048 | tf_op jit(solution)/shard_map/ppermute | solution.py:140
  57.6 6.7 %collective-permute-start.23 = (f32[2,8960]{1,0:T(2,128)S(1)}, f32[2,8960]{1,0:T(2,128)S(1)}, u32[]{:S(2)}, u32[]{:S(2)}) collective-permute-start(f32[2,8960]{1,0:T(2,128)S(1)} %get-tuple-element.151.refs_1_), channel_id=1, source_target_pairs={{0,2},{1,3},{2,0},{3,1},{4,6},{5,7},{6,4},{7,5},{8,10},{9,11},{10,... | collective-permute-start | bytes 215048 | tf_op jit(solution)/shard_map/ppermute | solution.py:140
  59.3 5.0 %collective-permute-start.24 = (f32[2,8960]{1,0:T(2,128)S(1)}, f32[2,8960]{1,0:T(2,128)S(1)}, u32[]{:S(2)}, u32[]{:S(2)}) collective-permute-start(f32[2,8960]{1,0:T(2,128)S(1)} %get-tuple-element.152.refs_2_), channel_id=1, source_target_pairs={{0,1},{1,0},{2,3},{3,2},{4,5},{5,4},{6,7},{7,6},{8,9},{9,8},{10,11... | collective-permute-start | bytes 215048 | tf_op jit(solution)/shard_map/ppermute | solution.py:140
  64.3 4.8 %collective-permute-start.25 = (f32[2,8960]{1,0:T(2,128)S(1)}, f32[2,8960]{1,0:T(2,128)S(1)}, u32[]{:S(2)}, u32[]{:S(2)}) collective-permute-start(f32[2,8960]{1,0:T(2,128)S(1)} %get-tuple-element.153.after.refs_0_), channel_id=1, source_target_pairs={{0,2},{1,3},{2,0},{3,1},{4,6},{5,7},{6,4},{7,5},{8,10},{9,11},{10,... | collective-permute-start | bytes 215048 | tf_op jit(solution)/shard_map/ppermute | solution.py:140
  64.9 4.3 %collective-permute-start.26 = (f32[2,8960]{1,0:T(2,128)S(1)}, f32[2,8960]{1,0:T(2,128)S(1)}, u32[]{:S(2)}, u32[]{:S(2)}) collective-permute-start(f32[2,8960]{1,0:T(2,128)S(1)} %get-tuple-element.154.refs_1_), channel_id=1, source_target_pairs={{0,1},{1,0},{2,3},{3,2},{4,5},{5,4},{6,7},{7,6},{8,9},{9,8},{10,11... | collective-permute-start | bytes 215048 | tf_op jit(solution)/shard_map/ppermute | solution.py:140
  69.2 4.4 %collective-permute-start.27 = (f32[2,8960]{1,0:T(2,128)S(1)}, f32[2,8960]{1,0:T(2,128)S(1)}, u32[]{:S(2)}, u32[]{:S(2)}) collective-permute-start(f32[2,8960]{1,0:T(2,128)S(1)} %get-tuple-element.155.refs_0_), channel_id=1, source_target_pairs={{0,1},{1,0},{2,3},{3,2},{4,5},{5,4},{6,7},{7,6},{8,9},{9,8},{10,11... | collective-permute-start | bytes 215048 | tf_op jit(solution)/shard_map/ppermute | solution.py:140

commit v3 on v2

v3 whole, which is shorter than its diff:
```python
import functools

import jax
import jax.numpy as jnp
from jax import lax
from jax.experimental import pallas as pl
from jax.experimental.pallas import tpu as pltpu
from jax.sharding import PartitionSpec as P

STEPS = 8
step_size = 0.25
penalty = 1.0
keep = 1.0 - step_size * penalty

f32 = jnp.float32
bf16 = jnp.bfloat16
VMEM = pltpu.VMEM
SMEM = pltpu.SMEM
MIB = 1 << 20


def in_vmem(array):
    return pltpu.with_memory_space_constraint(array, VMEM)


def in_smem(array):
    return pltpu.with_memory_space_constraint(array, SMEM)


def in_hbm(array):
    return pltpu.with_memory_space_constraint(array, pltpu.HBM)


vmem_spec = pl.BlockSpec(memory_space=VMEM)
smem_spec = pl.BlockSpec(memory_space=SMEM)
any_spec = pl.BlockSpec(memory_space=pl.ANY)


def params(mib):
    return pltpu.CompilerParams(vmem_limit_bytes=mib * MIB)


def cost(flops, moved):
    return pl.CostEstimate(flops=flops, bytes_accessed=moved, transcendentals=0)


def split(value):
    high = value.astype(bf16)
    return high, (value - high.astype(f32)).astype(bf16)


def store_split(ref, index, value):
    rows = value.shape[0]
    high, low = split(value)
    ref[index, 0:rows] = high
    ref[index, rows : 2 * rows] = low


def fold(product, rows):
    return (product[:rows, :128] + product[:rows, 128:]) + (product[rows:, :128] + product[rows:, 128:])


def lanes(block):
    return pl.ds(pl.multiple_of(block * 128, 128), 128)


def partner(value, apart):
    rows = value.shape[0]
    up = pltpu.roll(value, rows - apart, 0)
    down = pltpu.roll(value, apart, 0)
    place = lax.broadcasted_iota(jnp.int32, value.shape, 0)
    return jnp.where((place & apart) == 0, up, down)


def local_mean(value, members):
    total, apart = value, 1
    while apart < members:
        total = total + partner(total, apart)
        apart *= 2
    return total * (1.0 / members)


def spread(pair, scenarios):
    count, width = pair.shape
    wide = jnp.broadcast_to(pair[:, None, :], (count, scenarios, width))
    return wide.reshape(count * scenarios, width)


def copies_of(pairs, sems):
    copies = [pltpu.make_async_copy(source, target, sems.at[n]) for n, (source, target) in enumerate(pairs)]
    for copy in copies:
        copy.start()
    return copies


def first_kernel(shared, per, small, send, start, *refs):
    sources, refs = refs[:small], refs[small:]
    sums, targets = refs[:shared], refs[shared : shared + small]
    send_out, head, sems = refs[shared + small :]
    cuts = [pl.ds(k * per, per) for k in range(shared)]
    pairs = [(start.at[cut], head.at[cut]) for cut in cuts] + list(zip(sources, targets))
    copies = copies_of(pairs, sems)
    for k in range(shared):
        copies[k].wait()
        sums[k][...] = jnp.sum(head[k * per : (k + 1) * per], axis=1)
    send_out[0] = send[0]
    for copy in copies[shared:]:
        copy.wait()


def add_kernel(count, *refs):
    for k in range(count):
        refs[-count + k][...] = refs[k][...] + refs[count + k][...]


def node_totals(sums, beside):
    shared = len(sums)
    totals = list(sums)
    for turn in range(shared):
        active = [k for k in range(shared) if shared - k - 1 - turn >= 0]
        received = [swap(totals[k], "scen", shared - k - 1 - turn) for k in active]
        after = beside(turn, totals)
        added = pl.pallas_call(
            functools.partial(add_kernel, len(active)),
            in_specs=[vmem_spec] * (2 * len(active)) + [any_spec] * len(after),
            out_specs=[vmem_spec] * len(active),
            out_shape=[VMEM(totals[k].shape, f32) for k in active],
            compiler_params=params(2),
            name=f"node_add_{turn}",
        )(*[in_vmem(totals[k]) for k in active], *[in_vmem(r) for r in received], *after)
        for k, value in zip(active, added):
            totals[k] = value
    return totals


def swap(block, axis, level):
    count = lax.axis_size(axis)
    apart = 6 if level == 2 else 1 << level
    return lax.ppermute(block, axis, [(i, i ^ apart) for i in range(count)])


def from_pair(value, axis):
    count = lax.axis_size(axis)
    return lax.ppermute(value, axis, [(i, i ^ 1) for i in range(count)])


def from_other(value, axis):
    count = lax.axis_size(axis)
    return lax.ppermute(value, axis, [(i, (i + 1 if i % 2 else i - 1) % count) for i in range(count)])


def prepare_kernel(shared, per, scen_all, send, tie_source, node_ids, load_factor,
                   start, mult, demand, tie_weight, state, parts, constant, ties, load, boundary):
    rows = state.shape[1]
    scenarios = start.shape[1]
    group = per * scenarios
    for k in range(node_ids.shape[1]):
        for s in range(scenarios):
            row = jnp.full((1, 128), load_factor[node_ids[s, k]], f32)
            for t in range(per):
                at = (k * per + t) * scenarios + s
                load[at : at + 1] = row
    boundary[...] = start[:, :, lanes(send[0])].reshape(boundary.shape)
    mine = lax.axis_index("area")
    zero = jnp.zeros((128, 128), f32)
    for m in range(tie_weight.shape[0]):
        high, low = split(tie_weight[m] * -step_size)
        from_partner = jnp.full((128, 128), tie_source[m] // send.shape[0], jnp.int32) == (mine ^ 1)
        for n, part in enumerate((high.astype(f32), low.astype(f32))):
            cut = slice(n * 128, (n + 1) * 128)
            ties[m, 0:128, cut] = jnp.where(from_partner, zero, part).astype(bf16)
            ties[m, 128:256, cut] = jnp.where(from_partner, part, zero).astype(bf16)

    def one(i, carry):
        for k in range(rows // group):
            cut = slice(k * group, (k + 1) * group)
            span = slice(k * per, (k + 1) * per)
            x = start[span, :, lanes(i)].reshape(group, 128)
            m = mult[span, :, lanes(i)].reshape(group, 128)
            rest = m - spread(demand[span, lanes(i)], scenarios) * load[cut]
            if k >= shared:
                rest = rest - penalty * local_mean(x, max(scen_all >> k, 1))
            constant[i, cut] = -step_size * rest
            state[i, cut] = x
        store_split(parts, i, state[i])
        return carry

    lax.fori_loop(0, state.shape[0], one, 0, unroll=largest_divisor(state.shape[0], 7))


def advance(i, other, weight, state, parts, constant, new_state, new_parts):
    left = jnp.concatenate([parts[i], parts[other]], axis=1)
    product = jnp.dot(left, weight, preferred_element_type=f32)
    value = (keep * state[i] + constant[i]) + fold(product, state.shape[1])
    new_state[i] = value
    store_split(new_parts, i, value)
    return value


def first_step(first, count, cols, values, state, parts, constant, weights, new_state, new_parts):
    for i in range(first, first + count):
        for j in range(2):
            high, low = split(values[i, j] * -step_size)
            weights[i, j * 128 : (j + 1) * 128, 0:128] = high
            weights[i, j * 128 : (j + 1) * 128, 128:256] = low
        advance(i, cols[1, i], weights[i], state, parts, constant, new_state, new_parts)


def first_step_begin(first, count, cols, values, state, parts, constant, after, *refs):
    first_step(first, count, cols, values, state, parts, constant, *refs)


def first_step_end(first, count, cols, values, state, parts, constant, after, w_in, s_in, p_in, *refs):
    first_step(first, count, cols, values, state, parts, constant, *refs)


def step_kernel(cols, weights, state, parts, constant, spare_state, spare_parts, new_state, new_parts):
    for i in range(state.shape[0]):
        advance(i, cols[1, i], weights[i], state, parts, constant, new_state, new_parts)


def add_sums(shared, per, scenarios, i, value, sums):
    group = per * scenarios
    for k in range(shared):
        piece = value[k * group : (k + 1) * group].reshape(per, scenarios, 128)
        sums[k][:, lanes(i)] = jnp.sum(piece, axis=1)


def last_step_kernel(shared, per, scenarios, cols, weights, state, parts, constant, spare_state, spare_parts,
                     new_state, new_parts, *sums):
    for i in range(state.shape[0]):
        value = advance(i, cols[1, i], weights[i], state, parts, constant, new_state, new_parts)
        add_sums(shared, per, scenarios, i, value, sums)


def add_ties(tie_row, low, high, ties, state):
    rows = state.shape[1]
    both = jnp.concatenate([low[...], high[...]], axis=1)
    left = jnp.concatenate(split(both), axis=0)
    count = ties.shape[0]
    added = [fold(jnp.dot(left, ties[m], preferred_element_type=f32), rows) for m in range(count)]
    values = []
    for m in range(count):
        total = state[tie_row[m]]
        for n in range(count):
            same = jnp.where(tie_row[n] == tie_row[m], 1.0, 0.0)
            total = total + (added[n] if n == m else same * added[n])
        values.append(total)
    for m in range(count):
        state[tie_row[m]] = values[m]
    return values


def put_parts(tie_row, values, parts):
    for m, value in enumerate(values):
        store_split(parts, tie_row[m], value)


def tie_kernel(tie_row, send, low, high, ties, state_in, parts_in, state, parts, boundary):
    put_parts(tie_row, add_ties(tie_row, low, high, ties, state), parts)
    boundary[...] = state[send[0]]


def anchor_kernel(shared, scen_all, scenarios, tie_row, send, low, high, ties, *refs):
    totals = refs[:shared]
    state, parts, constant, boundary = refs[shared + 3 :]
    rows = state.shape[1]
    group = totals[0].shape[0] * scenarios
    span = min(-(-shared * group // 16) * 16, rows)

    def one(i, carry):
        for k in range(shared):
            cut = slice(k * group, (k + 1) * group)
            mean = spread(totals[k][:, lanes(i)], scenarios) * (1.0 / (scen_all >> k))
            mean = (step_size * penalty) * mean
            constant[i, cut] = constant[i, cut] + mean
            state[i, cut] = state[i, cut] + mean
        high_part, low_part = split(state[i, 0:span])
        parts[i, 0:span] = high_part
        parts[i, rows : rows + span] = low_part
        return carry

    lax.fori_loop(0, state.shape[0], one, 0, unroll=largest_divisor(state.shape[0], 14))
    put_parts(tie_row, add_ties(tie_row, low, high, ties, state), parts)
    boundary[...] = state[send[0]]


def last_tie_kernel(shared, per, scenarios, tie_row, low, high, ties, *refs):
    state, sums = refs[shared + 1], refs[shared + 2 :]
    values = add_ties(tie_row, low, high, ties, state)
    for m, value in enumerate(values):
        add_sums(shared, per, scenarios, tie_row[m], value, sums)


def write_blocks(pieces, blocks, one, buffer, out, sems):
    width = blocks // pieces
    copies = []
    for piece in range(pieces):
        lax.fori_loop(piece * width, (piece + 1) * width, one, 0, unroll=largest_divisor(width, 7))
        cut = pl.ds(piece * width * 128, width * 128)
        copies.append(pltpu.make_async_copy(buffer.at[:, :, cut], out.at[:, :, cut], sems.at[piece]))
        copies[-1].start()
    for copy in copies:
        copy.wait()


def dispatch_kernel(pieces, state, dispatch, buffer, sems):
    def one(i, carry):
        buffer[:, :, lanes(i)] = state[i].reshape(buffer.shape[0], buffer.shape[1], 128)
        return carry

    write_blocks(pieces, state.shape[0], one, buffer, dispatch, sems)


def multiplier_kernel(sections, scen_all, pieces, state, mult, *refs):
    new_mult, buffer, sems = refs[-3:]
    totals = dict(zip(sections, refs[: -3]))
    per, scenarios = buffer.shape[0] // len(sections), buffer.shape[1]
    group = per * scenarios

    def one(i, carry):
        for n, k in enumerate(sections):
            value = state[i, k * group : (k + 1) * group]
            if scen_all >> k > scenarios:
                mean = spread(totals[k][:, lanes(i)], scenarios) * (1.0 / (scen_all >> k))
            else:
                mean = local_mean(value, max(scen_all >> k, 1))
            gap = penalty * (value - mean)
            old = mult[k * per : (k + 1) * per, :, lanes(i)]
            buffer[n * per : (n + 1) * per, :, lanes(i)] = old + gap.reshape(per, scenarios, 128)
        return carry

    rows = pl.ds(sections[0] * per, len(sections) * per)
    write_blocks(pieces, state.shape[0], one, buffer, new_mult.at[rows], sems)


def largest_divisor(count, most):
    return max(d for d in range(1, most + 1) if count % d == 0)


def local(
    start_dispatch,
    multipliers,
    demand,
    load_factor,
    node_ids,
    block_values,
    block_cols,
    send_block,
    tie_source,
    tie_row,
    tie_weight,
):
    periods, scenarios, buses = start_dispatch.shape
    blocks = buses // 128
    rows = periods * scenarios
    sections = node_ids.shape[0]
    per = periods // sections
    devices = lax.axis_size("scen")
    scen_all = scenarios * devices
    shared = devices.bit_length() - 1
    tie_count = tie_row.shape[0]

    small = [block_cols.T, tie_row, tie_source, node_ids.T, load_factor]
    first = pl.pallas_call(
        functools.partial(first_kernel, shared, per, len(small)),
        in_specs=[smem_spec] + [any_spec] * (1 + len(small)),
        out_specs=[vmem_spec] * shared + [smem_spec] * (len(small) + 1),
        out_shape=[VMEM((per, buses), f32)] * shared + [SMEM(a.shape, a.dtype) for a in small + [send_block]],
        scratch_shapes=[
            VMEM((shared * per, scenarios, buses), f32),
            pltpu.SemaphoreType.DMA((shared + len(small),)),
        ],
        compiler_params=params(4),
        cost_estimate=cost(2 * 10**10, 10**6),
        name="first_sums",
    )(send_block, in_hbm(start_dispatch), *[in_hbm(a) for a in small])
    sums = list(first[:shared])
    cols, row_of_tie, source_of_tie, labels, factors, send = first[shared:]

    state_shape = VMEM((blocks, rows, 128), f32)
    parts_shape = VMEM((blocks, 2 * rows, 128), bf16)

    weights_shape = VMEM((blocks, 256, 256), bf16)
    half = blocks // 2
    laid = {}

    def prepare(turn, totals):
        after = totals[0]
        if turn == 0:
            laid["start"] = pl.pallas_call(
                functools.partial(prepare_kernel, shared, per, scen_all),
                in_specs=[smem_spec] * 4 + [vmem_spec] * 4,
                out_specs=[vmem_spec] * 6,
                out_shape=[state_shape, parts_shape, state_shape]
                + [VMEM((tie_count, 256, 256), bf16), VMEM((rows, 128), f32), VMEM((rows, 128), f32)],
                compiler_params=params(2),
                cost_estimate=cost(10**9, 10**6),
                name="prepare",
            )(in_smem(send), in_smem(source_of_tie), in_smem(labels), in_smem(factors),
              *[in_vmem(a) for a in (start_dispatch, multipliers, demand, tie_weight)])
            return [in_vmem(laid["start"][5])]
        if turn > 2:
            return []
        first, count = (0, half) if turn == 1 else (half, blocks - half)
        held = [in_vmem(a) for a in laid["start"][:3]]
        made = [] if turn == 1 else [in_vmem(a) for a in laid["made"]]
        laid["made"] = pl.pallas_call(
            functools.partial(first_step_begin if turn == 1 else first_step_end, first, count),
            in_specs=[smem_spec] + [vmem_spec] * (5 + len(made)),
            out_specs=[vmem_spec] * 3,
            out_shape=[weights_shape, state_shape, parts_shape],
            input_output_aliases={} if turn == 1 else {6: 0, 7: 1, 8: 2},
            compiler_params=params(2),
            cost_estimate=cost(10**9, 10**6),
            name=f"step_0_{turn}",
        )(in_smem(cols), in_vmem(block_values), *held, in_vmem(after), *made)
        return [in_vmem(laid["made"][1])] if turn == 1 else []

    totals = node_totals(sums, prepare)
    for turn in range(shared, 3):
        prepare(turn, totals)
    spare_state, spare_parts, constant, ties, load, boundary = laid["start"]
    weights, state, parts = laid["made"]
    for iteration in range(STEPS):
        low = from_other(boundary, "area")
        high = from_pair(boundary, "area")
        tie_args = [in_vmem(low), in_vmem(high), in_vmem(ties)]
        if iteration == 0:
            state, parts, constant, boundary = pl.pallas_call(
                functools.partial(anchor_kernel, shared, scen_all, scenarios),
                in_specs=[smem_spec] * 2 + [vmem_spec] * (6 + shared),
                out_specs=[vmem_spec] * 4,
                out_shape=[state_shape, parts_shape, state_shape, VMEM((rows, 128), f32)],
                input_output_aliases={5 + shared: 0, 6 + shared: 1, 7 + shared: 2},
                compiler_params=params(2),
                name="anchor",
            )(in_smem(row_of_tie), in_smem(send), *tie_args, *[in_vmem(t) for t in totals],
              in_vmem(state), in_vmem(parts), in_vmem(constant))
            continue
        last = iteration == STEPS - 1
        used = (state, parts)
        made = pl.pallas_call(
            functools.partial(last_step_kernel, shared, per, scenarios) if last else step_kernel,
            in_specs=[smem_spec] + [vmem_spec] * 6,
            out_specs=[vmem_spec] * (2 + shared * last),
            out_shape=[state_shape, parts_shape] + [VMEM((per, buses), f32)] * (shared * last),
            input_output_aliases={5: 0, 6: 1},
            compiler_params=params(2),
            cost_estimate=cost(blocks * 2 * rows * 256 * 256 * 2, 12 * 10**6),
            name=f"step_{iteration}",
        )(in_smem(cols), *[in_vmem(a) for a in (weights, state, parts, constant, spare_state, spare_parts)])
        state, parts = made[:2]
        spare_state, spare_parts = used
        if last:
            made = pl.pallas_call(
                functools.partial(last_tie_kernel, shared, per, scenarios),
                in_specs=[smem_spec] + [vmem_spec] * (4 + shared),
                out_specs=[vmem_spec] * (1 + shared),
                out_shape=[state_shape] + [VMEM((per, buses), f32)] * shared,
                input_output_aliases={4 + k: k for k in range(1 + shared)},
                compiler_params=params(2),
                name=f"ties_{iteration}",
            )(in_smem(row_of_tie), *tie_args, in_vmem(state), *[in_vmem(a) for a in made[2:]])
            state, sums = made[0], list(made[1:])
        else:
            state, parts, boundary = pl.pallas_call(
                tie_kernel,
                in_specs=[smem_spec] * 2 + [vmem_spec] * 5,
                out_specs=[vmem_spec] * 3,
                out_shape=[state_shape, parts_shape, VMEM((rows, 128), f32)],
                input_output_aliases={5: 0, 6: 1},
                compiler_params=params(2),
                name=f"ties_{iteration}",
            )(in_smem(row_of_tie), in_smem(send), *tie_args, in_vmem(state), in_vmem(parts))

    state = in_vmem(state)
    pieces = largest_divisor(blocks, 7)
    written = {}

    def multiply(chosen, totals, after):
        old = [in_hbm(written["mult"])] if "mult" in written else []
        extra = [in_vmem(t) for t in totals] + ([in_vmem(after)] if after is not None else [])
        written["mult"] = pl.pallas_call(
            functools.partial(multiplier_kernel, chosen, scen_all, pieces),
            in_specs=[vmem_spec] * (2 + len(extra)) + [any_spec] * len(old),
            out_specs=any_spec,
            out_shape=pltpu.HBM((periods, scenarios, buses), f32),
            input_output_aliases={2 + len(extra): 0} if old else {},
            scratch_shapes=[
                VMEM((len(chosen) * per, scenarios, buses), f32),
                pltpu.SemaphoreType.DMA((pieces,)),
            ],
            compiler_params=params(5),
            cost_estimate=cost(10**9, 10**6),
            name=f"multipliers_{chosen[0]}",
        )(state, in_vmem(multipliers), *extra, *old)
        return [in_hbm(written["mult"])]

    def write(turn, totals):
        if turn == 0:
            written["dispatch"] = pl.pallas_call(
                functools.partial(dispatch_kernel, pieces),
                in_specs=[vmem_spec],
                out_specs=any_spec,
                out_shape=pltpu.HBM((periods, scenarios, buses), f32),
                scratch_shapes=[VMEM((periods, scenarios, buses), f32), pltpu.SemaphoreType.DMA((pieces,))],
                compiler_params=params(5),
                cost_estimate=cost(10**9, 10**6),
                name="dispatch",
            )(state)
            return [in_hbm(written["dispatch"])]
        done = shared - turn
        chosen = list(range(done, sections if turn == 1 else done + 1))
        return multiply(chosen, [totals[done]], None)

    totals = node_totals(sums, write)
    dispatch = written["dispatch"]
    new_mult = multiply([0], [totals[0]], None)[0]
    return dispatch, new_mult


def solution(mesh):
    in_specs = (
        P(None, "scen", "area"),
        P(None, "scen", "area"),
        P(None, "area"),
        P(),
        P(None, "scen"),
        P("area", None, None, None),
        P("area", None),
        P("area"),
        P("area"),
        P("area"),
        P("area", None, None),
    )
    out_specs = (P(None, "scen", "area"), P(None, "scen", "area"))
    return jax.shard_map(local, mesh=mesh, in_specs=in_specs, out_specs=out_specs, check_vma=False)
```

time: 75.2 us -> 72.6 us (0.965)
  Pallas kernels: 38.9 us -> 32.9 us
  waiting for transfers between devices: 10.4 us -> 16.4 us
  starting transfers between devices: 23.8 us -> 21.3 us
    ppermute x12, waiting for transfers between devices: 5.63 us -> 12.2 us  [swap(): return lax.ppermute(block, axis, [(i, i ^ apart) for i in range(count)])]
    pallas_call x13, Pallas kernels: 31.7 us -> 26.1 us  [the longest x7 15 us: local(): pl.pallas_call(functools.partial(last_step_kernel, shared, per, scenarios...]
    ppermute x12, starting transfers between devices: 15.8 us -> 12.4 us  [swap(): return lax.ppermute(block, axis, [(i, i ^ apart) for i in range(count)])]
    ppermute x8, starting transfers between devices: 2.15 us -> 4.18 us  [from_pair(): return lax.ppermute(value, axis, [(i, i ^ 1) for i in range(count)])]
    ppermute x8, starting transfers between devices: 5.85 us -> 4.74 us  [from_other(): lax.ppermute(value, axis, [(i, (i + 1 if i % 2 else i - 1) % count) for i...]
  transfers between devices with their start and end apart: 28 -> 28, of which waited for: 12 -> 13; matrix products, arithmetic and copies ran while one was open for 0% -> 0% of each run, Pallas kernels for 43% -> 37%
where the time goes in v3:
time: 72.6 us; the launch traced here: 72.4 us
  Pallas kernels  32.9 us (45%)
  starting transfers between devices  21.3 us (29%)
  waiting for transfers between devices  16.4 us (23%)
  between operations  1.77 us (2%)
    pallas_call x7, Pallas kernels, local(): pl.pallas_call(functools.partial(last_step_kernel, shared, per, scenarios...  15 us
    ppermute x12, starting transfers between devices, swap(): return lax.ppermute(block, axis, [(i, i ^ apart) for i in range(count)])  12.4 us
    ppermute x12, waiting for transfers between devices, swap(): return lax.ppermute(block, axis, [(i, i ^ apart) for i in range(count)])  12.2 us
    ppermute x8, starting transfers between devices, from_other(): lax.ppermute(value, axis, [(i, (i + 1 if i % 2 else i - 1) % count) for i...  4.74 us
    pallas_call x2, Pallas kernels, prepare(): pl.pallas_call(functools.partial(first_step_begin if turn == 1 else first...  4.2 us
    ppermute x8, starting transfers between devices, from_pair(): return lax.ppermute(value, axis, [(i, i ^ 1) for i in range(count)])  4.18 us
    ppermute x8, waiting for transfers between devices, from_other(): lax.ppermute(value, axis, [(i, (i + 1 if i % 2 else i - 1) % count) for i...  4.18 us
    pallas_call x3, Pallas kernels, multiply(): pl.pallas_call(functools.partial(multiplier_kernel, chosen, scen_all, pie...  3.62 us
  transfers between devices with their start and end apart: 28, of which 13 were waited for; matrix products, arithmetic and copies ran while one was open for 0% of the time, Pallas kernels for 37%

profile of v3, /device:TPU:0, one launch (start us, length us, event | category | flops | bytes accessed | tf_op | source)
XLA Modules:
  0.0 72.4 jit_solution(9990860327937290206)
XLA Ops:
  1.3 0.0 slice-start
  1.4 1.8 %first_sums.1 = (f32[2,8960]{1,0:T(2,128)S(1)}, f32[2,8960]{1,0:T(2,128)S(1)}, f32[2,8960]{1,0:T(2,128)S(1)}, s32[2,70]{1,0:T(2,128)S(4)}, s32[4]{0:T(128)S(4)},...) custom-call(s32[1]{0:T(128)S(6)} %copy.89.send, f32[24,4,8960]{2,1,0:T(4,128)} %start.3, ...), custom_call_target="tpu_custom_call" | custom-call | flops 20000000000 | bytes 1000000 | tf_op jit(solution)/shard_map/first_sums/pallas_call | solution.py:365
  3.1 5.1 %collective-permute-start.2 = (f32[2,8960]{1,0:T(2,128)S(1)}, f32[2,8960]{1,0:T(2,128)S(1)}, u32[]{:S(2)}, u32[]{:S(2)}) collective-permute-start(f32[2,8960]{1,0:T(2,128)S(1)} %get-tuple-element.81.refs_0_), channel_id=1, source_target_pairs={{0,6},{1,7},{2,4},{3,5},{4,2},{5,3},{6,0},{7,1},{8,14},{9,15},{10,... | collective-permute-start | bytes 215048 | tf_op jit(solution)/shard_map/ppermute | solution.py:139
  8.2 1.5 %collective-permute-start.4 = (f32[2,8960]{1,0:T(2,128)S(1)}, f32[2,8960]{1,0:T(2,128)S(1)}, u32[]{:S(2)}, u32[]{:S(2)}) collective-permute-start(f32[2,8960]{1,0:T(2,128)S(1)} %get-tuple-element.83.refs_2_), channel_id=1, source_target_pairs={{0,1},{1,0},{2,3},{3,2},{4,5},{5,4},{6,7},{7,6},{8,9},{9,8},{10,11... | collective-permute-start | bytes 215048 | tf_op jit(solution)/shard_map/ppermute | solution.py:139
  9.7 3.2 %prepare.1 = (f32[70,96,128]{2,1,0:T(8,128)S(1)}, bf16[70,192,128]{2,1,0:T(8,128)(2,1)S(1)}, f32[70,96,128]{2,1,0:T(8,128)S(1)}, bf16[4,256,256]{2,1,0:T(8,128)(...) custom-call(s32[1]{0:T(128)S(4)} %get-tuple-element.75.send, s32[4]{0:T(128)S(4)} %get-tuple-element.76.tie_source, ...), custom_call_target="tpu_custom_call" | custom-call | flops 1000000000 | bytes 1000000 | tf_op jit(solution)/shard_map/prepare/pallas_call | solution.py:391
  13.0 0.4 collective-permute-start
  13.4 1.2 %collective-permute-start.1 = (f32[96,128]{1,0:T(8,128)S(1)}, f32[96,128]{1,0:T(8,128)S(1)}, u32[]{:S(2)}, u32[]{:S(2)}) collective-permute-start(f32[96,128]{1,0:T(8,128)S(1)} %get-tuple-element.79.refs_6_), channel_id=1, source_target_pairs={{0,8},{8,0},{16,24},{24,16},{1,9},{9,1},{17,25},{25,17},{2,10},{10... | collective-permute-start | bytes 147464 | tf_op jit(solution)/shard_map/ppermute | solution.py:144
  14.6 0.0 collective-permute-done.2.refs_3_
  14.7 2.1 %collective-permute-start.5 = (f32[2,8960]{1,0:T(2,128)S(1)}, f32[2,8960]{1,0:T(2,128)S(1)}, u32[]{:S(2)}, u32[]{:S(2)}) collective-permute-start(f32[2,8960]{1,0:T(2,128)S(1)} %get-tuple-element.84.after.refs_0_), channel_id=1, source_target_pairs={{0,2},{1,3},{2,0},{3,1},{4,6},{5,7},{6,4},{7,5},{8,10},{9,11},{10,... | collective-permute-start | bytes 215048 | tf_op jit(solution)/shard_map/ppermute | solution.py:139
  16.8 0.5 collective-permute-start.6
  17.3 2.1 %step_0_1.1 = (bf16[70,256,256]{2,1,0:T(8,128)(2,1)S(1)}, f32[70,96,128]{2,1,0:T(8,128)S(1)}, bf16[70,192,128]{2,1,0:T(8,128)(2,1)S(1)}) custom-call(s32[2,70]{1,0:T(2,128)S(4)} %get-tuple-element.86.cols, f32[70,2,128,128]{3,2,1,0:T(8,128)S(1)} %bitcast.3, f32[70,96,128]{2,1,0:T(8,128)S(1)} %get-tuple-element.87.state.spare_state, ...), custom_call_target="tpu_custom_call" | custom-call | flops 1000000000 | bytes 1000000 | tf_op jit(solution)/shard_map/step_0_1/pallas_call | solution.py:408
  19.4 1.7 %collective-permute-done.6.refs_3_ = f32[2,8960]{1,0:T(2,128)S(1)} collective-permute-done((f32[2,8960]{1,0:T(2,128)S(1)}, f32[2,8960]{1,0:T(2,128)S(1)}, u32[]{:S(2)}, u32[]{:S(2)}) %collective-permute-start.6) | collective-permute-done | bytes 71712 | tf_op jit(solution)/shard_map/ppermute | solution.py:139
  21.1 0.6 collective-permute-start.7
  21.7 2.1 %step_0_2.1 = (bf16[70,256,256]{2,1,0:T(8,128)(2,1)S(1)}, f32[70,96,128]{2,1,0:T(8,128)S(1)}, bf16[70,192,128]{2,1,0:T(8,128)(2,1)S(1)}) custom-call(s32[2,70]{1,0:T(2,128)S(4)} %get-tuple-element.86.cols, f32[70,2,128,128]{3,2,1,0:T(8,128)S(1)} %bitcast.3, ...), custom_call_target="tpu_custom_call", output_to_operand_aliasing={{0}: (6, {}), {1}: (7, {}), {2}: (8, {})} | custom-call | flops 1000000000 | bytes 1000000 | tf_op jit(solution)/shard_map/step_0_2/pallas_call | solution.py:408
  23.8 1.7 %collective-permute-done.7.refs_1_ = f32[2,8960]{1,0:T(2,128)S(1)} collective-permute-done((f32[2,8960]{1,0:T(2,128)S(1)}, f32[2,8960]{1,0:T(2,128)S(1)}, u32[]{:S(2)}, u32[]{:S(2)}) %collective-permute-start.7) | collective-permute-done | bytes 71712 | tf_op jit(solution)/shard_map/ppermute | solution.py:139
  25.5 0.9 %anchor.1 = (f32[70,96,128]{2,1,0:T(8,128)S(1)}, bf16[70,192,128]{2,1,0:T(8,128)(2,1)S(1)}, f32[70,96,128]{2,1,0:T(8,128)S(1)}, f32[96,128]{1,0:T(8,128)S(1)}) custom-call(s32[4]{0:T(128)S(4)} %get-tuple-element.74.tie_row, s32[1]{0:T(128)S(4)} %get-tuple-element.75.send, ...), custom_call_target="tpu_custom_call", output_to_operand_aliasing={{0}: (8, {}), {1}: (9, {}), {2}: (10, {})} | custom-call | tf_op jit(solution)/shard_map/anchor/pallas_call | solution.py:430
  26.5 0.1 collective-permute-start.8
  26.6 0.6 collective-permute-start.9
  27.2 2.1 %step_1.1 = (f32[70,96,128]{2,1,0:T(8,128)S(1)}, bf16[70,192,128]{2,1,0:T(8,128)(2,1)S(1)}) custom-call(s32[2,70]{1,0:T(2,128)S(4)} %get-tuple-element.86.cols, bf16[70,256,256]{2,1,0:T(8,128)(2,1)S(1)} %get-tuple-element.99.weights, f32[70,96,128]{2,1,0:T(8,128)S(1)} %get-tuple-element.100.state.spare_state, ...), custom_call_target="tpu_custom_call", output_to_operand_aliasing={{0}: (5, {}), {1}: (6, {})} | custom-call | flops 1761607680 | bytes 12000000 | tf_op jit(solution)/shard_map/step_1/pallas_call | solution.py:443
  29.3 0.8 %collective-permute-done.8.low = f32[96,128]{1,0:T(8,128)S(1)} collective-permute-done((f32[96,128]{1,0:T(8,128)S(1)}, f32[96,128]{1,0:T(8,128)S(1)}, u32[]{:S(2)}, u32[]{:S(2)}) %collective-permute-start.8) | collective-permute-done | bytes 49184 | tf_op jit(solution)/shard_map/ppermute | solution.py:149
  30.1 0.3 ties_1.1
  30.4 0.7 %collective-permute-start.10 = (f32[96,128]{1,0:T(8,128)S(1)}, f32[96,128]{1,0:T(8,128)S(1)}, u32[]{:S(2)}, u32[]{:S(2)}) collective-permute-start(f32[96,128]{1,0:T(8,128)S(1)} %get-tuple-element.105), channel_id=1, source_target_pairs={{0,24},{8,16},{16,8},{24,0},{1,25},{9,17},{17,9},{25,1},{2,26},{10... | collective-permute-start | bytes 147464 | tf_op jit(solution)/shard_map/ppermute | solution.py:149
  31.1 0.4 collective-permute-start.11
  31.5 2.1 %step_2.1 = (f32[70,96,128]{2,1,0:T(8,128)S(1)}, bf16[70,192,128]{2,1,0:T(8,128)(2,1)S(1)}) custom-call(s32[2,70]{1,0:T(2,128)S(4)} %get-tuple-element.86.cols, bf16[70,256,256]{2,1,0:T(8,128)(2,1)S(1)} %get-tuple-element.99.weights, f32[70,96,128]{2,1,0:T(8,128)S(1)} %get-tuple-element.106.state.spare_state, ...), custom_call_target="tpu_custom_call", output_to_operand_aliasing={{0}: (5, {}), {1}: (6, {})} | custom-call | flops 1761607680 | bytes 12000000 | tf_op jit(solution)/shard_map/step_2/pallas_call | solution.py:443
  33.6 0.4 collective-permute-done.10.low
  34.0 0.3 ties_2.1
  34.3 0.9 %collective-permute-start.12 = (f32[96,128]{1,0:T(8,128)S(1)}, f32[96,128]{1,0:T(8,128)S(1)}, u32[]{:S(2)}, u32[]{:S(2)}) collective-permute-start(f32[96,128]{1,0:T(8,128)S(1)} %get-tuple-element.110), channel_id=1, source_target_pairs={{0,24},{8,16},{16,8},{24,0},{1,25},{9,17},{17,9},{25,1},{2,26},{10... | collective-permute-start | bytes 147464 | tf_op jit(solution)/shard_map/ppermute | solution.py:149
  35.3 0.4 collective-permute-start.13
  35.7 2.1 %step_3.1 = (f32[70,96,128]{2,1,0:T(8,128)S(1)}, bf16[70,192,128]{2,1,0:T(8,128)(2,1)S(1)}) custom-call(s32[2,70]{1,0:T(2,128)S(4)} %get-tuple-element.86.cols, bf16[70,256,256]{2,1,0:T(8,128)(2,1)S(1)} %get-tuple-element.99.weights, f32[70,96,128]{2,1,0:T(8,128)S(1)} %get-tuple-element.111.state.spare_state, ...), custom_call_target="tpu_custom_call", output_to_operand_aliasing={{0}: (5, {}), {1}: (6, {})} | custom-call | flops 1761607680 | bytes 12000000 | tf_op jit(solution)/shard_map/step_3/pallas_call | solution.py:443
  37.8 0.6 collective-permute-done.12.low
  38.4 0.3 ties_3.1
  38.7 0.7 collective-permute-start.14
  39.4 0.4 collective-permute-start.15
  39.8 2.1 %step_4.1 = (f32[70,96,128]{2,1,0:T(8,128)S(1)}, bf16[70,192,128]{2,1,0:T(8,128)(2,1)S(1)}) custom-call(s32[2,70]{1,0:T(2,128)S(4)} %get-tuple-element.86.cols, bf16[70,256,256]{2,1,0:T(8,128)(2,1)S(1)} %get-tuple-element.99.weights, f32[70,96,128]{2,1,0:T(8,128)S(1)} %get-tuple-element.116.state.spare_state, ...), custom_call_target="tpu_custom_call", output_to_operand_aliasing={{0}: (5, {}), {1}: (6, {})} | custom-call | flops 1761607680 | bytes 12000000 | tf_op jit(solution)/shard_map/step_4/pallas_call | solution.py:443
  41.9 0.7 collective-permute-done.14.low
  42.6 0.3 ties_4.1
  42.9 0.6 collective-permute-start.16
  43.5 0.4 collective-permute-start.17
  43.9 2.3 %step_5.1 = (f32[70,96,128]{2,1,0:T(8,128)S(1)}, bf16[70,192,128]{2,1,0:T(8,128)(2,1)S(1)}) custom-call(s32[2,70]{1,0:T(2,128)S(4)} %get-tuple-element.86.cols, bf16[70,256,256]{2,1,0:T(8,128)(2,1)S(1)} %get-tuple-element.99.weights, f32[70,96,128]{2,1,0:T(8,128)S(1)} %get-tuple-element.121.state.spare_state, ...), custom_call_target="tpu_custom_call", output_to_operand_aliasing={{0}: (5, {}), {1}: (6, {})} | custom-call | flops 1761607680 | bytes 12000000 | tf_op jit(solution)/shard_map/step_5/pallas_call | solution.py:443
  46.3 0.5 collective-permute-done.16.low
  46.7 0.3 ties_5.1
  47.0 0.6 collective-permute-start.18
  47.7 0.4 collective-permute-start.19
  48.1 2.1 %step_6.1 = (f32[70,96,128]{2,1,0:T(8,128)S(1)}, bf16[70,192,128]{2,1,0:T(8,128)(2,1)S(1)}) custom-call(s32[2,70]{1,0:T(2,128)S(4)} %get-tuple-element.86.cols, bf16[70,256,256]{2,1,0:T(8,128)(2,1)S(1)} %get-tuple-element.99.weights, f32[70,96,128]{2,1,0:T(8,128)S(1)} %get-tuple-element.126.state.spare_state, ...), custom_call_target="tpu_custom_call", output_to_operand_aliasing={{0}: (5, {}), {1}: (6, {})} | custom-call | flops 1761607680 | bytes 12000000 | tf_op jit(solution)/shard_map/step_6/pallas_call | solution.py:443
  50.2 0.7 collective-permute-done.18.low
  50.8 0.3 ties_6.1
  51.2 0.6 collective-permute-start.20
  51.8 0.4 collective-permute-start.21
  52.2 2.2 %step_7.1 = (f32[70,96,128]{2,1,0:T(8,128)S(1)}, bf16[70,192,128]{2,1,0:T(8,128)(2,1)S(1)}, f32[2,8960]{1,0:T(2,128)S(1)}, f32[2,8960]{1,0:T(2,128)S(1)}, f32[2,8960]{1,0:T(2,128)S(1)}) custom-call(s32[2,70]{1,0:T(2,128)S(4)} %get-tuple-element.86.cols, ...), custom_call_target="tpu_custom_call", output_to_operand_aliasing={{0}: (5, {}), {1}: (6, {})} | custom-call | flops 1761607680 | bytes 12000000 | tf_op jit(solution)/shard_map/step_7/pallas_call | solution.py:443
  54.4 0.6 collective-permute-done.20.low
  55.0 0.3 ties_7.1
  55.3 0.3 collective-permute-start.22
  55.6 0.9 %collective-permute-start.24 = (f32[2,8960]{1,0:T(2,128)S(1)}, f32[2,8960]{1,0:T(2,128)S(1)}, u32[]{:S(2)}, u32[]{:S(2)}) collective-permute-start(f32[2,8960]{1,0:T(2,128)S(1)} %get-tuple-element.140.refs_2_), channel_id=1, source_target_pairs={{0,1},{1,0},{2,3},{3,2},{4,5},{5,4},{6,7},{7,6},{8,9},{9,8},{10,11... | collective-permute-start | bytes 215048 | tf_op jit(solution)/shard_map/ppermute | solution.py:139
  56.5 1.9 %dispatch.1.refs_6_ = f32[24,4,8960]{2,1,0:T(4,128)} custom-call(f32[70,96,128]{2,1,0:T(8,128)S(1)} %get-tuple-element.137.state), custom_call_target="tpu_custom_call" | custom-call | flops 1000000000 | bytes 1000000 | tf_op jit(solution)/shard_map/dispatch/pallas_call | solution.py:502
  58.4 3.8 %collective-permute-done.22.refs_3_ = f32[2,8960]{1,0:T(2,128)S(1)} collective-permute-done((f32[2,8960]{1,0:T(2,128)S(1)}, f32[2,8960]{1,0:T(2,128)S(1)}, u32[]{:S(2)}, u32[]{:S(2)}) %collective-permute-start.22) | collective-permute-done | bytes 71712 | tf_op jit(solution)/shard_map/ppermute | solution.py:139
  62.2 0.1 collective-permute-start.25
  62.3 0.6 collective-permute-start.26
  62.9 1.8 %multipliers_2.1.refs_4_.refs_1_ = f32[24,4,8960]{2,1,0:T(4,128)} custom-call(f32[70,96,128]{2,1,0:T(8,128)S(1)} %get-tuple-element.137.state, f32[24,4,8960]{2,1,0:T(4,128)S(1)} %copy-done, f32[2,8960]{1,0:T(2,128)S(1)} %get-tuple-element.143.refs_0_), custom_call_target="tpu_custom_call" | custom-call | flops 1000000000 | bytes 1000000 | tf_op jit(solution)/shard_map/multipliers_2/pallas_call | solution.py:484
  64.7 1.9 %collective-permute-done.25.refs_2_ = f32[2,8960]{1,0:T(2,128)S(1)} collective-permute-done((f32[2,8960]{1,0:T(2,128)S(1)}, f32[2,8960]{1,0:T(2,128)S(1)}, u32[]{:S(2)}, u32[]{:S(2)}) %collective-permute-start.25) | collective-permute-done | bytes 71712 | tf_op jit(solution)/shard_map/ppermute | solution.py:139
  66.6 0.3 collective-permute-done.26.refs_3_
  66.9 0.6 collective-permute-start.27
  67.5 0.9 %multipliers_1.1.refs_2_.refs_1_ = f32[24,4,8960]{2,1,0:T(4,128)} custom-call(f32[70,96,128]{2,1,0:T(8,128)S(1)} %get-tuple-element.137.state, f32[24,4,8960]{2,1,0:T(4,128)S(1)} %copy-done, f32[2,8960]{1,0:T(2,128)S(1)} %get-tuple-element.145.refs_0_, f32[24,4,8960]{2,1,0:T(4,128)} %multipliers_2.1.refs_4_.refs_1_), custom_call_target="tpu_custom_call", output_to_operand_aliasing={{}: (3, {})} | custom-call | flops 1000000000 | bytes 1000000 | tf_op jit(solution)/shard_map/multipliers_1/pallas_call | solution.py:484
  68.5 2.8 %collective-permute-done.27.refs_1_ = f32[2,8960]{1,0:T(2,128)S(1)} collective-permute-done((f32[2,8960]{1,0:T(2,128)S(1)}, f32[2,8960]{1,0:T(2,128)S(1)}, u32[]{:S(2)}, u32[]{:S(2)}) %collective-permute-start.27) | collective-permute-done | bytes 71712 | tf_op jit(solution)/shard_map/ppermute | solution.py:139
  71.3 0.9 %multipliers_0.1 = f32[24,4,8960]{2,1,0:T(4,128)} custom-call(f32[70,96,128]{2,1,0:T(8,128)S(1)} %get-tuple-element.137.state, f32[24,4,8960]{2,1,0:T(4,128)S(1)} %copy-done, f32[2,8960]{1,0:T(2,128)S(1)} %node_add_2.3.refs_0_, f32[24,4,8960]{2,1,0:T(4,128)} %multipliers_1.1.refs_2_.refs_1_), custom_call_target="tpu_custom_call", output_to_operand_aliasing={{}: (3, {})} | custom-call | flops 1000000000 | bytes 1000000 | tf_op jit(solution)/shard_map/multipliers_0/pallas_call | solution.py:484
  (36 shorter events, 0.2 us)
Async XLA Ops:
  1.3 16.0 %slice-start = ((s8[9175040]{0:T(1024)(128)(4,1)}), s8[4194304]{0:T(1024)(128)(4,1)S(1)}, s32[]{:S(2)}) async-start(s8[9175040]{0:T(1024)(128)(4,1)} %bitcast.2), calls=%async_computation | async-start | bytes 8388608
  1.3 8.4 %copy-start = (f32[24,4,8960]{2,1,0:T(4,128)S(1)}, f32[24,4,8960]{2,1,0:T(4,128)}, u32[]{:S(2)}) copy-start(f32[24,4,8960]{2,1,0:T(4,128)} %mult.7) | copy-start | bytes 10321924
  1.3 8.4 %copy-start.1 = (f32[24,4,8960]{2,1,0:T(4,128)S(1)}, f32[24,4,8960]{2,1,0:T(4,128)}, u32[]{:S(2)}) copy-start(f32[24,4,8960]{2,1,0:T(4,128)} %start.3) | copy-start | bytes 10321924
  1.3 8.4 %copy-start.2 = (f32[24,8960]{1,0:T(8,128)S(1)}, f32[24,8960]{1,0:T(8,128)}, u32[]{:S(2)}) copy-start(f32[24,8960]{1,0:T(8,128)} %demand.1) | copy-start | bytes 2580484
  1.3 8.4 %copy-start.3 = (f32[4,128,128]{2,1,0:T(8,128)S(1)}, f32[4,128,128]{2,1,0:T(8,128)}, u32[]{:S(2)}) copy-start(f32[4,128,128]{2,1,0:T(8,128)} %tie_weight.1) | copy-start | bytes 786436
  1.3 16.0 %slice-start.1 = ((s8[9175040]{0:T(1024)(128)(4,1)}), s8[4194304]{0:T(1024)(128)(4,1)S(1)}, s32[]{:S(2)}) async-start(s8[9175040]{0:T(1024)(128)(4,1)} %bitcast.2), calls=%async_computation.1 | async-start | bytes 8388608
  1.3 16.0 %slice-start.2 = ((s8[9175040]{0:T(1024)(128)(4,1)}), s8[786432]{0:T(1024)(128)(4,1)S(1)}, s32[]{:S(2)}) async-start(s8[9175040]{0:T(1024)(128)(4,1)} %bitcast.2), calls=%async_computation.2 | async-start | bytes 1572864
  3.1 11.5 %collective-permute-start.2 = (f32[2,8960]{1,0:T(2,128)S(1)}, f32[2,8960]{1,0:T(2,128)S(1)}, u32[]{:S(2)}, u32[]{:S(2)}) collective-permute-start(f32[2,8960]{1,0:T(2,128)S(1)} %get-tuple-element.81.refs_0_), channel_id=1, source_target_pairs={{0,6},{1,7},{2,4},{3,5},{4,2},{5,3},{6,0},{7,1},{8,14},{9,15},{10,... | collective-permute-start | bytes 215048 | tf_op jit(solution)/shard_map/ppermute | solution.py:139
  8.2 6.4 %collective-permute-start.3 = (f32[2,8960]{1,0:T(2,128)S(1)}, f32[2,8960]{1,0:T(2,128)S(1)}, u32[]{:S(2)}, u32[]{:S(2)}) collective-permute-start(f32[2,8960]{1,0:T(2,128)S(1)} %get-tuple-element.82.refs_1_), channel_id=1, source_target_pairs={{0,2},{1,3},{2,0},{3,1},{4,6},{5,7},{6,4},{7,5},{8,10},{9,11},{10,... | collective-permute-start | bytes 215048 | tf_op jit(solution)/shard_map/ppermute | solution.py:139
  8.2 6.4 %collective-permute-start.4 = (f32[2,8960]{1,0:T(2,128)S(1)}, f32[2,8960]{1,0:T(2,128)S(1)}, u32[]{:S(2)}, u32[]{:S(2)}) collective-permute-start(f32[2,8960]{1,0:T(2,128)S(1)} %get-tuple-element.83.refs_2_), channel_id=1, source_target_pairs={{0,1},{1,0},{2,3},{3,2},{4,5},{5,4},{6,7},{7,6},{8,9},{9,8},{10,11... | collective-permute-start | bytes 215048 | tf_op jit(solution)/shard_map/ppermute | solution.py:139
  13.0 12.5 %collective-permute-start = (f32[96,128]{1,0:T(8,128)S(1)}, f32[96,128]{1,0:T(8,128)S(1)}, u32[]{:S(2)}, u32[]{:S(2)}) collective-permute-start(f32[96,128]{1,0:T(8,128)S(1)} %get-tuple-element.79.refs_6_), channel_id=1, source_target_pairs={{0,24},{8,16},{16,8},{24,0},{1,25},{9,17},{17,9},{25,1},{2,26},{10... | collective-permute-start | bytes 147464 | tf_op jit(solution)/shard_map/ppermute | solution.py:149
  13.4 12.2 %collective-permute-start.1 = (f32[96,128]{1,0:T(8,128)S(1)}, f32[96,128]{1,0:T(8,128)S(1)}, u32[]{:S(2)}, u32[]{:S(2)}) collective-permute-start(f32[96,128]{1,0:T(8,128)S(1)} %get-tuple-element.79.refs_6_), channel_id=1, source_target_pairs={{0,8},{8,0},{16,24},{24,16},{1,9},{9,1},{17,25},{25,17},{2,10},{10... | collective-permute-start | bytes 147464 | tf_op jit(solution)/shard_map/ppermute | solution.py:144
  14.7 4.7 %collective-permute-start.5 = (f32[2,8960]{1,0:T(2,128)S(1)}, f32[2,8960]{1,0:T(2,128)S(1)}, u32[]{:S(2)}, u32[]{:S(2)}) collective-permute-start(f32[2,8960]{1,0:T(2,128)S(1)} %get-tuple-element.84.after.refs_0_), channel_id=1, source_target_pairs={{0,2},{1,3},{2,0},{3,1},{4,6},{5,7},{6,4},{7,5},{8,10},{9,11},{10,... | collective-permute-start | bytes 215048 | tf_op jit(solution)/shard_map/ppermute | solution.py:139
  16.8 4.3 %collective-permute-start.6 = (f32[2,8960]{1,0:T(2,128)S(1)}, f32[2,8960]{1,0:T(2,128)S(1)}, u32[]{:S(2)}, u32[]{:S(2)}) collective-permute-start(f32[2,8960]{1,0:T(2,128)S(1)} %get-tuple-element.85.refs_1_), channel_id=1, source_target_pairs={{0,1},{1,0},{2,3},{3,2},{4,5},{5,4},{6,7},{7,6},{8,9},{9,8},{10,11... | collective-permute-start | bytes 215048 | tf_op jit(solution)/shard_map/ppermute | solution.py:139
  21.1 4.4 %collective-permute-start.7 = (f32[2,8960]{1,0:T(2,128)S(1)}, f32[2,8960]{1,0:T(2,128)S(1)}, u32[]{:S(2)}, u32[]{:S(2)}) collective-permute-start(f32[2,8960]{1,0:T(2,128)S(1)} %get-tuple-element.91.refs_0_.after), channel_id=1, source_target_pairs={{0,1},{1,0},{2,3},{3,2},{4,5},{5,4},{6,7},{7,6},{8,9},{9,8},{10,11... | collective-permute-start | bytes 215048 | tf_op jit(solution)/shard_map/ppermute | solution.py:139
  26.5 3.6 %collective-permute-start.8 = (f32[96,128]{1,0:T(8,128)S(1)}, f32[96,128]{1,0:T(8,128)S(1)}, u32[]{:S(2)}, u32[]{:S(2)}) collective-permute-start(f32[96,128]{1,0:T(8,128)S(1)} %get-tuple-element.98), channel_id=1, source_target_pairs={{0,24},{8,16},{16,8},{24,0},{1,25},{9,17},{17,9},{25,1},{2,26},{10... | collective-permute-start | bytes 147464 | tf_op jit(solution)/shard_map/ppermute | solution.py:149
  26.6 3.5 %collective-permute-start.9 = (f32[96,128]{1,0:T(8,128)S(1)}, f32[96,128]{1,0:T(8,128)S(1)}, u32[]{:S(2)}, u32[]{:S(2)}) collective-permute-start(f32[96,128]{1,0:T(8,128)S(1)} %get-tuple-element.98), channel_id=1, source_target_pairs={{0,8},{8,0},{16,24},{24,16},{1,9},{9,1},{17,25},{25,17},{2,10},{10... | collective-permute-start | bytes 147464 | tf_op jit(solution)/shard_map/ppermute | solution.py:144
  30.4 3.6 %collective-permute-start.10 = (f32[96,128]{1,0:T(8,128)S(1)}, f32[96,128]{1,0:T(8,128)S(1)}, u32[]{:S(2)}, u32[]{:S(2)}) collective-permute-start(f32[96,128]{1,0:T(8,128)S(1)} %get-tuple-element.105), channel_id=1, source_target_pairs={{0,24},{8,16},{16,8},{24,0},{1,25},{9,17},{17,9},{25,1},{2,26},{10... | collective-permute-start | bytes 147464 | tf_op jit(solution)/shard_map/ppermute | solution.py:149
  31.1 2.9 %collective-permute-start.11 = (f32[96,128]{1,0:T(8,128)S(1)}, f32[96,128]{1,0:T(8,128)S(1)}, u32[]{:S(2)}, u32[]{:S(2)}) collective-permute-start(f32[96,128]{1,0:T(8,128)S(1)} %get-tuple-element.105), channel_id=1, source_target_pairs={{0,8},{8,0},{16,24},{24,16},{1,9},{9,1},{17,25},{25,17},{2,10},{10... | collective-permute-start | bytes 147464 | tf_op jit(solution)/shard_map/ppermute | solution.py:144
  34.3 4.0 %collective-permute-start.12 = (f32[96,128]{1,0:T(8,128)S(1)}, f32[96,128]{1,0:T(8,128)S(1)}, u32[]{:S(2)}, u32[]{:S(2)}) collective-permute-start(f32[96,128]{1,0:T(8,128)S(1)} %get-tuple-element.110), channel_id=1, source_target_pairs={{0,24},{8,16},{16,8},{24,0},{1,25},{9,17},{17,9},{25,1},{2,26},{10... | collective-permute-start | bytes 147464 | tf_op jit(solution)/shard_map/ppermute | solution.py:149
  35.3 3.1 %collective-permute-start.13 = (f32[96,128]{1,0:T(8,128)S(1)}, f32[96,128]{1,0:T(8,128)S(1)}, u32[]{:S(2)}, u32[]{:S(2)}) collective-permute-start(f32[96,128]{1,0:T(8,128)S(1)} %get-tuple-element.110), channel_id=1, source_target_pairs={{0,8},{8,0},{16,24},{24,16},{1,9},{9,1},{17,25},{25,17},{2,10},{10... | collective-permute-start | bytes 147464 | tf_op jit(solution)/shard_map/ppermute | solution.py:144
  38.7 3.9 %collective-permute-start.14 = (f32[96,128]{1,0:T(8,128)S(1)}, f32[96,128]{1,0:T(8,128)S(1)}, u32[]{:S(2)}, u32[]{:S(2)}) collective-permute-start(f32[96,128]{1,0:T(8,128)S(1)} %get-tuple-element.115), channel_id=1, source_target_pairs={{0,24},{8,16},{16,8},{24,0},{1,25},{9,17},{17,9},{25,1},{2,26},{10... | collective-permute-start | bytes 147464 | tf_op jit(solution)/shard_map/ppermute | solution.py:149
  39.4 3.2 %collective-permute-start.15 = (f32[96,128]{1,0:T(8,128)S(1)}, f32[96,128]{1,0:T(8,128)S(1)}, u32[]{:S(2)}, u32[]{:S(2)}) collective-permute-start(f32[96,128]{1,0:T(8,128)S(1)} %get-tuple-element.115), channel_id=1, source_target_pairs={{0,8},{8,0},{16,24},{24,16},{1,9},{9,1},{17,25},{25,17},{2,10},{10... | collective-permute-start | bytes 147464 | tf_op jit(solution)/shard_map/ppermute | solution.py:144
  42.9 3.8 %collective-permute-start.16 = (f32[96,128]{1,0:T(8,128)S(1)}, f32[96,128]{1,0:T(8,128)S(1)}, u32[]{:S(2)}, u32[]{:S(2)}) collective-permute-start(f32[96,128]{1,0:T(8,128)S(1)} %get-tuple-element.120), channel_id=1, source_target_pairs={{0,24},{8,16},{16,8},{24,0},{1,25},{9,17},{17,9},{25,1},{2,26},{10... | collective-permute-start | bytes 147464 | tf_op jit(solution)/shard_map/ppermute | solution.py:149
  43.5 3.2 %collective-permute-start.17 = (f32[96,128]{1,0:T(8,128)S(1)}, f32[96,128]{1,0:T(8,128)S(1)}, u32[]{:S(2)}, u32[]{:S(2)}) collective-permute-start(f32[96,128]{1,0:T(8,128)S(1)} %get-tuple-element.120), channel_id=1, source_target_pairs={{0,8},{8,0},{16,24},{24,16},{1,9},{9,1},{17,25},{25,17},{2,10},{10... | collective-permute-start | bytes 147464 | tf_op jit(solution)/shard_map/ppermute | solution.py:144
  47.0 3.8 %collective-permute-start.18 = (f32[96,128]{1,0:T(8,128)S(1)}, f32[96,128]{1,0:T(8,128)S(1)}, u32[]{:S(2)}, u32[]{:S(2)}) collective-permute-start(f32[96,128]{1,0:T(8,128)S(1)} %get-tuple-element.125), channel_id=1, source_target_pairs={{0,24},{8,16},{16,8},{24,0},{1,25},{9,17},{17,9},{25,1},{2,26},{10... | collective-permute-start | bytes 147464 | tf_op jit(solution)/shard_map/ppermute | solution.py:149
  47.7 3.2 %collective-permute-start.19 = (f32[96,128]{1,0:T(8,128)S(1)}, f32[96,128]{1,0:T(8,128)S(1)}, u32[]{:S(2)}, u32[]{:S(2)}) collective-permute-start(f32[96,128]{1,0:T(8,128)S(1)} %get-tuple-element.125), channel_id=1, source_target_pairs={{0,8},{8,0},{16,24},{24,16},{1,9},{9,1},{17,25},{25,17},{2,10},{10... | collective-permute-start | bytes 147464 | tf_op jit(solution)/shard_map/ppermute | solution.py:144
  51.2 3.8 %collective-permute-start.20 = (f32[96,128]{1,0:T(8,128)S(1)}, f32[96,128]{1,0:T(8,128)S(1)}, u32[]{:S(2)}, u32[]{:S(2)}) collective-permute-start(f32[96,128]{1,0:T(8,128)S(1)} %get-tuple-element.130), channel_id=1, source_target_pairs={{0,24},{8,16},{16,8},{24,0},{1,25},{9,17},{17,9},{25,1},{2,26},{10... | collective-permute-start | bytes 147464 | tf_op jit(solution)/shard_map/ppermute | solution.py:149
  51.8 3.2 %collective-permute-start.21 = (f32[96,128]{1,0:T(8,128)S(1)}, f32[96,128]{1,0:T(8,128)S(1)}, u32[]{:S(2)}, u32[]{:S(2)}) collective-permute-start(f32[96,128]{1,0:T(8,128)S(1)} %get-tuple-element.130), channel_id=1, source_target_pairs={{0,8},{8,0},{16,24},{24,16},{1,9},{9,1},{17,25},{25,17},{2,10},{10... | collective-permute-start | bytes 147464 | tf_op jit(solution)/shard_map/ppermute | solution.py:144
  55.3 6.9 %collective-permute-start.22 = (f32[2,8960]{1,0:T(2,128)S(1)}, f32[2,8960]{1,0:T(2,128)S(1)}, u32[]{:S(2)}, u32[]{:S(2)}) collective-permute-start(f32[2,8960]{1,0:T(2,128)S(1)} %get-tuple-element.138.refs_0_), channel_id=1, source_target_pairs={{0,6},{1,7},{2,4},{3,5},{4,2},{5,3},{6,0},{7,1},{8,14},{9,15},{10,... | collective-permute-start | bytes 215048 | tf_op jit(solution)/shard_map/ppermute | solution.py:139
  55.6 6.6 %collective-permute-start.23 = (f32[2,8960]{1,0:T(2,128)S(1)}, f32[2,8960]{1,0:T(2,128)S(1)}, u32[]{:S(2)}, u32[]{:S(2)}) collective-permute-start(f32[2,8960]{1,0:T(2,128)S(1)} %get-tuple-element.139.refs_1_), channel_id=1, source_target_pairs={{0,2},{1,3},{2,0},{3,1},{4,6},{5,7},{6,4},{7,5},{8,10},{9,11},{10,... | collective-permute-start | bytes 215048 | tf_op jit(solution)/shard_map/ppermute | solution.py:139
  55.6 6.6 %collective-permute-start.24 = (f32[2,8960]{1,0:T(2,128)S(1)}, f32[2,8960]{1,0:T(2,128)S(1)}, u32[]{:S(2)}, u32[]{:S(2)}) collective-permute-start(f32[2,8960]{1,0:T(2,128)S(1)} %get-tuple-element.140.refs_2_), channel_id=1, source_target_pairs={{0,1},{1,0},{2,3},{3,2},{4,5},{5,4},{6,7},{7,6},{8,9},{9,8},{10,11... | collective-permute-start | bytes 215048 | tf_op jit(solution)/shard_map/ppermute | solution.py:139
  62.2 4.4 %collective-permute-start.25 = (f32[2,8960]{1,0:T(2,128)S(1)}, f32[2,8960]{1,0:T(2,128)S(1)}, u32[]{:S(2)}, u32[]{:S(2)}) collective-permute-start(f32[2,8960]{1,0:T(2,128)S(1)} %get-tuple-element.141.refs_0_), channel_id=1, source_target_pairs={{0,2},{1,3},{2,0},{3,1},{4,6},{5,7},{6,4},{7,5},{8,10},{9,11},{10,... | collective-permute-start | bytes 215048 | tf_op jit(solution)/shard_map/ppermute | solution.py:139
  62.3 4.6 %collective-permute-start.26 = (f32[2,8960]{1,0:T(2,128)S(1)}, f32[2,8960]{1,0:T(2,128)S(1)}, u32[]{:S(2)}, u32[]{:S(2)}) collective-permute-start(f32[2,8960]{1,0:T(2,128)S(1)} %get-tuple-element.142.refs_1_), channel_id=1, source_target_pairs={{0,1},{1,0},{2,3},{3,2},{4,5},{5,4},{6,7},{7,6},{8,9},{9,8},{10,11... | collective-permute-start | bytes 215048 | tf_op jit(solution)/shard_map/ppermute | solution.py:139
  66.9 4.4 %collective-permute-start.27 = (f32[2,8960]{1,0:T(2,128)S(1)}, f32[2,8960]{1,0:T(2,128)S(1)}, u32[]{:S(2)}, u32[]{:S(2)}) collective-permute-start(f32[2,8960]{1,0:T(2,128)S(1)} %get-tuple-element.144.refs_0_), channel_id=1, source_target_pairs={{0,1},{1,0},{2,3},{3,2},{4,5},{5,4},{6,7},{7,6},{8,9},{9,8},{10,11... | collective-permute-start | bytes 215048 | tf_op jit(solution)/shard_map/ppermute | solution.py:139

commit v4 on v3

--- a/solution.py
+++ b/solution.py
@@ -80,10 +80,14 @@
     return total * (1.0 / members)
 
 
-def spread(pair, scenarios):
-    count, width = pair.shape
-    wide = jnp.broadcast_to(pair[:, None, :], (count, scenarios, width))
-    return wide.reshape(count * scenarios, width)
+def spread(ref, first, count, scenarios, block):
+    shape = (count * scenarios, 128)
+    place = lax.broadcasted_iota(jnp.int32, shape, 0)
+    wide = jnp.broadcast_to(ref[first : first + 1, lanes(block)], shape)
+    for t in range(1, count):
+        row = jnp.broadcast_to(ref[first + t : first + t + 1, lanes(block)], shape)
+        wide = jnp.where(place < t * scenarios, wide, row)
+    return wide
 
 
 def copies_of(pairs, sems):
@@ -108,35 +112,51 @@
         copy.wait()
 
 
-def add_kernel(count, *refs):
-    for k in range(count):
-        refs[-count + k][...] = refs[k][...] + refs[count + k][...]
-
-
-def node_totals(sums, beside):
+def add_kernel(counts, *refs):
+    inputs, outputs = iter(refs), refs[-len(counts) :]
+    for count, output in zip(counts, outputs):
+        total = next(inputs)[...]
+        for _ in range(count):
+            total = total + next(inputs)[...]
+        output[...] = total
+
+
+def turns_of(levels, wide):
+    if not wide:
+        return [[1 << level] for level in reversed(range(levels))]
+    if levels < 3:
+        return [[1 << level] for level in range(levels)]
+    low = 1 << (levels - 2)
+    return [[low, 2 * low, 3 * low]] + turns_of(levels - 2, wide)
+
+
+def swap(block, axis, apart):
+    count = lax.axis_size(axis)
+    return lax.ppermute(block, axis, [(i, i ^ apart) for i in range(count)])
+
+
+def node_totals(sums, wide, beside):
     shared = len(sums)
     totals = list(sums)
-    for turn in range(shared):
-        active = [k for k in range(shared) if shared - k - 1 - turn >= 0]
-        received = [swap(totals[k], "scen", shared - k - 1 - turn) for k in active]
-        after = beside(turn, totals)
+    plans = [turns_of(shared - k, wide) for k in range(shared)]
+    for turn in range(max(len(plan) for plan in plans)):
+        active = [k for k in range(shared) if turn < len(plans[k])]
+        operands = []
+        for k in active:
+            operands += [totals[k]] + [swap(totals[k], "scen", apart) for apart in plans[k][turn]]
+        after = beside(turn, totals, [k for k in range(shared) if len(plans[k]) == turn])
+        counts = [len(plans[k][turn]) for k in active]
         added = pl.pallas_call(
-            functools.partial(add_kernel, len(active)),
-            in_specs=[vmem_spec] * (2 * len(active)) + [any_spec] * len(after),
+            functools.partial(add_kernel, counts),
+            in_specs=[vmem_spec] * len(operands) + [any_spec] * len(after),
             out_specs=[vmem_spec] * len(active),
             out_shape=[VMEM(totals[k].shape, f32) for k in active],
             compiler_params=params(2),
             name=f"node_add_{turn}",
-        )(*[in_vmem(totals[k]) for k in active], *[in_vmem(r) for r in received], *after)
+        )(*[in_vmem(a) for a in operands], *after)
         for k, value in zip(active, added):
             totals[k] = value
     return totals
-
-
-def swap(block, axis, level):
-    count = lax.axis_size(axis)
-    apart = 6 if level == 2 else 1 << level
-    return lax.ppermute(block, axis, [(i, i ^ apart) for i in range(count)])
 
 
 def from_pair(value, axis):
@@ -177,7 +197,7 @@
             span = slice(k * per, (k + 1) * per)
             x = start[span, :, lanes(i)].reshape(group, 128)
             m = mult[span, :, lanes(i)].reshape(group, 128)
-            rest = m - spread(demand[span, lanes(i)], scenarios) * load[cut]
+            rest = m - spread(demand, k * per, per, scenarios, i) * load[cut]
             if k >= shared:
                 rest = rest - penalty * local_mean(x, max(scen_all >> k, 1))
             constant[i, cut] = -step_size * rest
@@ -271,7 +291,7 @@
     def one(i, carry):
         for k in range(shared):
             cut = slice(k * group, (k + 1) * group)
-            mean = spread(totals[k][:, lanes(i)], scenarios) * (1.0 / (scen_all >> k))
+            mean = spread(totals[k], 0, group // scenarios, scenarios, i) * (1.0 / (scen_all >> k))
             mean = (step_size * penalty) * mean
             constant[i, cut] = constant[i, cut] + mean
             state[i, cut] = state[i, cut] + mean
@@ -292,46 +312,57 @@
         add_sums(shared, per, scenarios, tie_row[m], value, sums)
 
 
-def write_blocks(pieces, blocks, one, buffer, out, sems):
+def write_blocks(pieces, blocks, one, targets, sems):
     width = blocks // pieces
     copies = []
     for piece in range(pieces):
         lax.fori_loop(piece * width, (piece + 1) * width, one, 0, unroll=largest_divisor(width, 7))
         cut = pl.ds(piece * width * 128, width * 128)
-        copies.append(pltpu.make_async_copy(buffer.at[:, :, cut], out.at[:, :, cut], sems.at[piece]))
-        copies[-1].start()
+        for buffer, out in targets:
+            copies.append(pltpu.make_async_copy(buffer.at[:, :, cut], out.at[:, :, cut], sems.at[len(copies)]))
+            copies[-1].start()
     for copy in copies:
         copy.wait()
 
 
-def dispatch_kernel(pieces, state, dispatch, buffer, sems):
+def put_multipliers(chosen, scen_all, state, mult, totals, buffer, i):
+    per, scenarios = buffer.shape[0] // len(chosen), buffer.shape[1]
+    group = per * scenarios
+    for n, k in enumerate(chosen):
+        value = state[i, k * group : (k + 1) * group]
+        if scen_all >> k > scenarios:
+            mean = spread(totals[k], 0, per, scenarios, i) * (1.0 / (scen_all >> k))
+        else:
+            mean = local_mean(value, max(scen_all >> k, 1))
+        gap = penalty * (value - mean)
+        old = mult[k * per : (k + 1) * per, :, lanes(i)]
+        buffer[n * per : (n + 1) * per, :, lanes(i)] = old + gap.reshape(per, scenarios, 128)
+
+
+def output_kernel(chosen, scen_all, pieces, state, mult, dispatch, new_mult, whole, buffer, sems):
+    periods, scenarios = whole.shape[:2]
+    per = buffer.shape[0] // len(chosen)
+
     def one(i, carry):
-        buffer[:, :, lanes(i)] = state[i].reshape(buffer.shape[0], buffer.shape[1], 128)
+        whole[:, :, lanes(i)] = state[i].reshape(periods, scenarios, 128)
+        put_multipliers(chosen, scen_all, state, mult, {}, buffer, i)
         return carry
 
-    write_blocks(pieces, state.shape[0], one, buffer, dispatch, sems)
-
-
-def multiplier_kernel(sections, scen_all, pieces, state, mult, *refs):
+    rows = pl.ds(chosen[0] * per, len(chosen) * per)
+    write_blocks(pieces, state.shape[0], one, [(whole, dispatch), (buffer, new_mult.at[rows])], sems)
+
+
+def multiplier_kernel(chosen, scen_all, pieces, state, mult, *refs):
     new_mult, buffer, sems = refs[-3:]
-    totals = dict(zip(sections, refs[: -3]))
-    per, scenarios = buffer.shape[0] // len(sections), buffer.shape[1]
-    group = per * scenarios
+    totals = dict(zip(chosen, refs[:-3]))
+    per = buffer.shape[0] // len(chosen)
 
     def one(i, carry):
-        for n, k in enumerate(sections):
-            value = state[i, k * group : (k + 1) * group]
-            if scen_all >> k > scenarios:
-                mean = spread(totals[k][:, lanes(i)], scenarios) * (1.0 / (scen_all >> k))
-            else:
-                mean = local_mean(value, max(scen_all >> k, 1))
-            gap = penalty * (value - mean)
-            old = mult[k * per : (k + 1) * per, :, lanes(i)]
-            buffer[n * per : (n + 1) * per, :, lanes(i)] = old + gap.reshape(per, scenarios, 128)
+        put_multipliers(chosen, scen_all, state, mult, totals, buffer, i)
         return carry
 
-    rows = pl.ds(sections[0] * per, len(sections) * per)
-    write_blocks(pieces, state.shape[0], one, buffer, new_mult.at[rows], sems)
+    rows = pl.ds(chosen[0] * per, len(chosen) * per)
+    write_blocks(pieces, state.shape[0], one, [(buffer, new_mult.at[rows])], sems)
 
 
 def largest_divisor(count, most):
@@ -382,10 +413,10 @@
     parts_shape = VMEM((blocks, 2 * rows, 128), bf16)
 
     weights_shape = VMEM((blocks, 256, 256), bf16)
-    half = blocks // 2
+    half = 2 * blocks // 7
     laid = {}
 
-    def prepare(turn, totals):
+    def prepare(turn, totals, ready):
         after = totals[0]
         if turn == 0:
             laid["start"] = pl.pallas_call(
@@ -399,27 +430,26 @@
                 name="prepare",
             )(in_smem(send), in_smem(source_of_tie), in_smem(labels), in_smem(factors),
               *[in_vmem(a) for a in (start_dispatch, multipliers, demand, tie_weight)])
-            return [in_vmem(laid["start"][5])]
-        if turn > 2:
+        if turn > 1:
             return []
-        first, count = (0, half) if turn == 1 else (half, blocks - half)
+        first, count = (0, half) if turn == 0 else (half, blocks - half)
         held = [in_vmem(a) for a in laid["start"][:3]]
-        made = [] if turn == 1 else [in_vmem(a) for a in laid["made"]]
+        made = [] if turn == 0 else [in_vmem(a) for a in laid["made"]]
         laid["made"] = pl.pallas_call(
-            functools.partial(first_step_begin if turn == 1 else first_step_end, first, count),
+            functools.partial(first_step_begin if turn == 0 else first_step_end, first, count),
             in_specs=[smem_spec] + [vmem_spec] * (5 + len(made)),
             out_specs=[vmem_spec] * 3,
             out_shape=[weights_shape, state_shape, parts_shape],
-            input_output_aliases={} if turn == 1 else {6: 0, 7: 1, 8: 2},
+            input_output_aliases={} if turn == 0 else {6: 0, 7: 1, 8: 2},
             compiler_params=params(2),
             cost_estimate=cost(10**9, 10**6),
             name=f"step_0_{turn}",
         )(in_smem(cols), in_vmem(block_values), *held, in_vmem(after), *made)
-        return [in_vmem(laid["made"][1])] if turn == 1 else []
-
-    totals = node_totals(sums, prepare)
-    for turn in range(shared, 3):
-        prepare(turn, totals)
+        return [in_vmem(laid["made"][1])] if turn == 0 else []
+
+    totals = node_totals(sums, True, prepare)
+    if len(turns_of(shared, True)) < 2:
+        prepare(1, totals, [])
     spare_state, spare_parts, constant, ties, load, boundary = laid["start"]
     weights, state, parts = laid["made"]
     for iteration in range(STEPS):
@@ -475,18 +505,17 @@
             )(in_smem(row_of_tie), in_smem(send), *tie_args, in_vmem(state), in_vmem(parts))
 
     state = in_vmem(state)
-    pieces = largest_divisor(blocks, 7)
+    pieces = largest_divisor(blocks, 5)
     written = {}
 
-    def multiply(chosen, totals, after):
-        old = [in_hbm(written["mult"])] if "mult" in written else []
-        extra = [in_vmem(t) for t in totals] + ([in_vmem(after)] if after is not None else [])
+    def multiply(chosen, totals):
+        extra = [in_vmem(totals[k]) for k in chosen]
         written["mult"] = pl.pallas_call(
             functools.partial(multiplier_kernel, chosen, scen_all, pieces),
-            in_specs=[vmem_spec] * (2 + len(extra)) + [any_spec] * len(old),
+            in_specs=[vmem_spec] * (2 + len(extra)) + [any_spec],
             out_specs=any_spec,
-            out_shape=pltpu.HBM((periods, scenarios, buses), f32),
-            input_output_aliases={2 + len(extra): 0} if old else {},
+            out_shape=whole,
+            input_output_aliases={2 + len(extra): 0},
             scratch_shapes=[
                 VMEM((len(chosen) * per, scenarios, buses), f32),
                 pltpu.SemaphoreType.DMA((pieces,)),
@@ -494,29 +523,39 @@
             compiler_params=params(5),
             cost_estimate=cost(10**9, 10**6),
             name=f"multipliers_{chosen[0]}",
-        )(state, in_vmem(multipliers), *extra, *old)
+        )(state, in_vmem(multipliers), *extra, in_hbm(written["mult"]))
         return [in_hbm(written["mult"])]
 
-    def write(turn, totals):
+    open_sections = list(range(shared))
+    whole = pltpu.HBM((periods, scenarios, buses), f32)
+
+    def write(turn, totals, ready):
         if turn == 0:
-            written["dispatch"] = pl.pallas_call(
-                functools.partial(dispatch_kernel, pieces),
-                in_specs=[vmem_spec],
-                out_specs=any_spec,
-                out_shape=pltpu.HBM((periods, scenarios, buses), f32),
-                scratch_shapes=[VMEM((periods, scenarios, buses), f32), pltpu.SemaphoreType.DMA((pieces,))],
-                compiler_params=params(5),
+            own = list(range(shared, sections))
+            written["dispatch"], written["mult"] = pl.pallas_call(
+                functools.partial(output_kernel, own, scen_all, pieces),
+                in_specs=[vmem_spec] * 2,
+                out_specs=[any_spec] * 2,
+                out_shape=[whole, whole],
+                scratch_shapes=[
+                    VMEM((periods, scenarios, buses), f32),
+                    VMEM((len(own) * per, scenarios, buses), f32),
+                    pltpu.SemaphoreType.DMA((2 * pieces,)),
+                ],
+                compiler_params=params(8),
                 cost_estimate=cost(10**9, 10**6),
-                name="dispatch",
-            )(state)
+                name="outputs",
+            )(state, in_vmem(multipliers))
             return [in_hbm(written["dispatch"])]
-        done = shared - turn
-        chosen = list(range(done, sections if turn == 1 else done + 1))
-        return multiply(chosen, [totals[done]], None)
-
-    totals = node_totals(sums, write)
+        if not ready:
+            return []
+        for k in ready:
+            open_sections.remove(k)
+        return multiply(ready, totals)
+
+    totals = node_totals(sums, False, write)
     dispatch = written["dispatch"]
-    new_mult = multiply([0], [totals[0]], None)[0]
+    new_mult = multiply(open_sections, totals)[0]
     return dispatch, new_mult
 
 

time: 72.6 us -> 70.3 us (0.968)
  waiting for transfers between devices: 16.4 us -> 9.4 us
  starting transfers between devices: 21.3 us -> 26.5 us
    ppermute x12 -> x13, waiting for transfers between devices: 12.2 us -> 7.1 us  [swap(): return lax.ppermute(block, axis, [(i, i ^ apart) for i in range(count)])]
    ppermute x12 -> x13, starting transfers between devices: 12.4 us -> 16.5 us  [swap(): return lax.ppermute(block, axis, [(i, i ^ apart) for i in range(count)])]
    ppermute x8, waiting for transfers between devices: 4.18 us -> 2.27 us  [from_other(): lax.ppermute(value, axis, [(i, (i + 1 if i % 2 else i - 1) % count) for i...]
    ppermute x8, starting transfers between devices: 4.74 us -> 6.36 us  [from_other(): lax.ppermute(value, axis, [(i, (i + 1 if i % 2 else i - 1) % count) for i...]
    pallas_call x9 -> x8, Pallas kernels: 6.19 us -> 7.3 us  [the longest x2 4.28 us: prepare(): pl.pallas_call(functools.partial(first_step_begin if turn == 0 else first...]
    pallas_call x3, Pallas kernels: 3.62 us -> 2.59 us  [multiply(): pl.pallas_call(functools.partial(multiplier_kernel, chosen, scen_all, pie...]
  transfers between devices with their start and end apart: 28 -> 29, of which waited for: 13 -> 10; matrix products, arithmetic and copies ran while one was open for 0% -> 0% of each run, Pallas kernels for 37% -> 38%
where the time goes in v4:
time: 70.3 us; the launch traced here: 70.1 us
  Pallas kernels  32.3 us (46%)
  starting transfers between devices  26.5 us (38%)
  waiting for transfers between devices  9.4 us (13%)
  between operations  1.81 us (3%)
    ppermute x13, starting transfers between devices, swap(): return lax.ppermute(block, axis, [(i, i ^ apart) for i in range(count)])  16.5 us
    pallas_call x7, Pallas kernels, local(): pl.pallas_call(functools.partial(last_step_kernel, shared, per, scenarios...  15 us
    ppermute x13, waiting for transfers between devices, swap(): return lax.ppermute(block, axis, [(i, i ^ apart) for i in range(count)])  7.1 us
    ppermute x8, starting transfers between devices, from_other(): lax.ppermute(value, axis, [(i, (i + 1 if i % 2 else i - 1) % count) for i...  6.36 us
    pallas_call x2, Pallas kernels, prepare(): pl.pallas_call(functools.partial(first_step_begin if turn == 0 else first...  4.28 us
    ppermute x8, starting transfers between devices, from_pair(): return lax.ppermute(value, axis, [(i, i ^ 1) for i in range(count)])  3.66 us
    pallas_call x1, Pallas kernels, write(): pl.pallas_call(functools.partial(output_kernel, own, scen_all, pieces), i...  2.91 us
    pallas_call x1, Pallas kernels, prepare(): pl.pallas_call(functools.partial(prepare_kernel, shared, per, scen_all),...  2.67 us
  transfers between devices with their start and end apart: 29, of which 10 were waited for; matrix products, arithmetic and copies ran while one was open for 0% of the time, Pallas kernels for 38%

profile of v4, /device:TPU:0, one launch (start us, length us, event | category | flops | bytes accessed | tf_op | source)
XLA Modules:
  0.0 70.1 jit_solution(11112425140740181722)
XLA Ops:
  1.3 1.8 %first_sums.1 = (f32[2,8960]{1,0:T(2,128)S(1)}, f32[2,8960]{1,0:T(2,128)S(1)}, f32[2,8960]{1,0:T(2,128)S(1)}, s32[2,70]{1,0:T(2,128)S(4)}, s32[4]{0:T(128)S(4)},...) custom-call(s32[1]{0:T(128)S(6)} %copy.91.send, f32[24,4,8960]{2,1,0:T(4,128)} %start.3, ...), custom_call_target="tpu_custom_call" | custom-call | flops 20000000000 | bytes 1000000 | tf_op jit(solution)/shard_map/first_sums/pallas_call | solution.py:396
  3.1 3.1 %collective-permute-start.2 = (f32[2,8960]{1,0:T(2,128)S(1)}, f32[2,8960]{1,0:T(2,128)S(1)}, u32[]{:S(2)}, u32[]{:S(2)}) collective-permute-start(f32[2,8960]{1,0:T(2,128)S(1)} %get-tuple-element.83.after.refs_0_), channel_id=1, source_target_pairs={{0,2},{1,3},{2,0},{3,1},{4,6},{5,7},{6,4},{7,5},{8,10},{9,11},{10,... | collective-permute-start | bytes 215048 | tf_op jit(solution)/shard_map/ppermute | solution.py:135
  6.2 2.6 %collective-permute-start.3 = (f32[2,8960]{1,0:T(2,128)S(1)}, f32[2,8960]{1,0:T(2,128)S(1)}, u32[]{:S(2)}, u32[]{:S(2)}) collective-permute-start(f32[2,8960]{1,0:T(2,128)S(1)} %get-tuple-element.83.after.refs_0_), channel_id=1, source_target_pairs={{0,4},{1,5},{2,6},{3,7},{4,0},{5,1},{6,2},{7,3},{8,12},{9,13},{10,... | collective-permute-start | bytes 215048 | tf_op jit(solution)/shard_map/ppermute | solution.py:135
  8.8 1.7 %collective-permute-start.5 = (f32[2,8960]{1,0:T(2,128)S(1)}, f32[2,8960]{1,0:T(2,128)S(1)}, u32[]{:S(2)}, u32[]{:S(2)}) collective-permute-start(f32[2,8960]{1,0:T(2,128)S(1)} %get-tuple-element.84.refs_4_), channel_id=1, source_target_pairs={{0,1},{1,0},{2,3},{3,2},{4,5},{5,4},{6,7},{7,6},{8,9},{9,8},{10,11... | collective-permute-start | bytes 215048 | tf_op jit(solution)/shard_map/ppermute | solution.py:135
  10.5 0.3 collective-permute-start.6
  10.8 2.7 %prepare.1 = (f32[70,96,128]{2,1,0:T(8,128)S(1)}, bf16[70,192,128]{2,1,0:T(8,128)(2,1)S(1)}, f32[70,96,128]{2,1,0:T(8,128)S(1)}, bf16[4,256,256]{2,1,0:T(8,128)(...) custom-call(s32[1]{0:T(128)S(4)} %get-tuple-element.77.send, s32[4]{0:T(128)S(4)} %get-tuple-element.78.tie_source, ...), custom_call_target="tpu_custom_call" | custom-call | flops 1000000000 | bytes 1000000 | tf_op jit(solution)/shard_map/prepare/pallas_call | solution.py:422
  13.5 1.2 %step_0_0.1 = (bf16[70,256,256]{2,1,0:T(8,128)(2,1)S(1)}, f32[70,96,128]{2,1,0:T(8,128)S(1)}, bf16[70,192,128]{2,1,0:T(8,128)(2,1)S(1)}) custom-call(s32[2,70]{1,0:T(2,128)S(4)} %get-tuple-element.86.cols, f32[70,2,128,128]{3,2,1,0:T(8,128)S(1)} %copy-done.1, f32[70,96,128]{2,1,0:T(8,128)S(1)} %get-tuple-element.87.state.spare_state, ...), custom_call_target="tpu_custom_call" | custom-call | flops 1000000000 | bytes 1000000 | tf_op jit(solution)/shard_map/step_0_0/pallas_call | solution.py:438
  14.7 0.0 collective-permute-done.2.refs_1_
  14.7 0.1 collective-permute-start
  14.8 0.0 collective-permute-done.3.refs_2_
  14.8 1.8 %collective-permute-start.1 = (f32[96,128]{1,0:T(8,128)S(1)}, f32[96,128]{1,0:T(8,128)S(1)}, u32[]{:S(2)}, u32[]{:S(2)}) collective-permute-start(f32[96,128]{1,0:T(8,128)S(1)} %get-tuple-element.81), channel_id=1, source_target_pairs={{0,8},{8,0},{16,24},{24,16},{1,9},{9,1},{17,25},{25,17},{2,10},{10... | collective-permute-start | bytes 147464 | tf_op jit(solution)/shard_map/ppermute | solution.py:164
  16.7 1.6 %collective-permute-start.7 = (f32[2,8960]{1,0:T(2,128)S(1)}, f32[2,8960]{1,0:T(2,128)S(1)}, u32[]{:S(2)}, u32[]{:S(2)}) collective-permute-start(f32[2,8960]{1,0:T(2,128)S(1)} %get-tuple-element.91.refs_0_.after), channel_id=1, source_target_pairs={{0,1},{1,0},{2,3},{3,2},{4,5},{5,4},{6,7},{7,6},{8,9},{9,8},{10,11... | collective-permute-start | bytes 215048 | tf_op jit(solution)/shard_map/ppermute | solution.py:135
  18.3 0.7 collective-permute-start.8
  18.9 3.1 %step_0_1.1 = (bf16[70,256,256]{2,1,0:T(8,128)(2,1)S(1)}, f32[70,96,128]{2,1,0:T(8,128)S(1)}, bf16[70,192,128]{2,1,0:T(8,128)(2,1)S(1)}) custom-call(s32[2,70]{1,0:T(2,128)S(4)} %get-tuple-element.86.cols, f32[70,2,128,128]{3,2,1,0:T(8,128)S(1)} %copy-done.1, ...), custom_call_target="tpu_custom_call", output_to_operand_aliasing={{0}: (6, {}), {1}: (7, {}), {2}: (8, {})} | custom-call | flops 1000000000 | bytes 1000000 | tf_op jit(solution)/shard_map/step_0_1/pallas_call | solution.py:438
  22.0 0.6 collective-permute-done.8.refs_3_
  22.6 0.8 %anchor.1 = (f32[70,96,128]{2,1,0:T(8,128)S(1)}, bf16[70,192,128]{2,1,0:T(8,128)(2,1)S(1)}, f32[70,96,128]{2,1,0:T(8,128)S(1)}, f32[96,128]{1,0:T(8,128)S(1)}) custom-call(s32[4]{0:T(128)S(4)} %get-tuple-element.76.tie_row, s32[1]{0:T(128)S(4)} %get-tuple-element.77.send, ...), custom_call_target="tpu_custom_call", output_to_operand_aliasing={{0}: (8, {}), {1}: (9, {}), {2}: (10, {})} | custom-call | tf_op jit(solution)/shard_map/anchor/pallas_call | solution.py:460
  23.4 0.1 collective-permute-start.10
  23.5 0.6 collective-permute-start.9
  24.2 2.1 %step_1.1 = (f32[70,96,128]{2,1,0:T(8,128)S(1)}, bf16[70,192,128]{2,1,0:T(8,128)(2,1)S(1)}) custom-call(s32[2,70]{1,0:T(2,128)S(4)} %get-tuple-element.86.cols, bf16[70,256,256]{2,1,0:T(8,128)(2,1)S(1)} %get-tuple-element.101.weights, f32[70,96,128]{2,1,0:T(8,128)S(1)} %get-tuple-element.102.state.spare_state, ...), custom_call_target="tpu_custom_call", output_to_operand_aliasing={{0}: (5, {}), {1}: (6, {})} | custom-call | flops 1761607680 | bytes 12000000 | tf_op jit(solution)/shard_map/step_1/pallas_call | solution.py:473
  26.3 0.8 %collective-permute-done.9.low = f32[96,128]{1,0:T(8,128)S(1)} collective-permute-done((f32[96,128]{1,0:T(8,128)S(1)}, f32[96,128]{1,0:T(8,128)S(1)}, u32[]{:S(2)}, u32[]{:S(2)}) %collective-permute-start.9) | collective-permute-done | bytes 49184 | tf_op jit(solution)/shard_map/ppermute | solution.py:169
  27.1 0.3 ties_1.1
  27.4 0.6 collective-permute-start.11
  28.1 0.2 collective-permute-start.12
  28.3 2.1 %step_2.1 = (f32[70,96,128]{2,1,0:T(8,128)S(1)}, bf16[70,192,128]{2,1,0:T(8,128)(2,1)S(1)}) custom-call(s32[2,70]{1,0:T(2,128)S(4)} %get-tuple-element.86.cols, bf16[70,256,256]{2,1,0:T(8,128)(2,1)S(1)} %get-tuple-element.101.weights, f32[70,96,128]{2,1,0:T(8,128)S(1)} %get-tuple-element.108.state.spare_state, ...), custom_call_target="tpu_custom_call", output_to_operand_aliasing={{0}: (5, {}), {1}: (6, {})} | custom-call | flops 1761607680 | bytes 12000000 | tf_op jit(solution)/shard_map/step_2/pallas_call | solution.py:473
  30.4 0.6 collective-permute-done.11.low
  31.0 0.3 ties_2.1
  31.3 0.9 %collective-permute-start.13 = (f32[96,128]{1,0:T(8,128)S(1)}, f32[96,128]{1,0:T(8,128)S(1)}, u32[]{:S(2)}, u32[]{:S(2)}) collective-permute-start(f32[96,128]{1,0:T(8,128)S(1)} %get-tuple-element.112), channel_id=1, source_target_pairs={{0,24},{8,16},{16,8},{24,0},{1,25},{9,17},{17,9},{25,1},{2,26},{10... | collective-permute-start | bytes 147464 | tf_op jit(solution)/shard_map/ppermute | solution.py:169
  32.2 0.2 collective-permute-start.14
  32.4 2.1 %step_3.1 = (f32[70,96,128]{2,1,0:T(8,128)S(1)}, bf16[70,192,128]{2,1,0:T(8,128)(2,1)S(1)}) custom-call(s32[2,70]{1,0:T(2,128)S(4)} %get-tuple-element.86.cols, bf16[70,256,256]{2,1,0:T(8,128)(2,1)S(1)} %get-tuple-element.101.weights, f32[70,96,128]{2,1,0:T(8,128)S(1)} %get-tuple-element.113.state.spare_state, ...), custom_call_target="tpu_custom_call", output_to_operand_aliasing={{0}: (5, {}), {1}: (6, {})} | custom-call | flops 1761607680 | bytes 12000000 | tf_op jit(solution)/shard_map/step_3/pallas_call | solution.py:473
  34.5 0.4 collective-permute-done.13.low
  34.9 0.3 ties_3.1
  35.2 0.9 %collective-permute-start.15 = (f32[96,128]{1,0:T(8,128)S(1)}, f32[96,128]{1,0:T(8,128)S(1)}, u32[]{:S(2)}, u32[]{:S(2)}) collective-permute-start(f32[96,128]{1,0:T(8,128)S(1)} %get-tuple-element.117), channel_id=1, source_target_pairs={{0,24},{8,16},{16,8},{24,0},{1,25},{9,17},{17,9},{25,1},{2,26},{10... | collective-permute-start | bytes 147464 | tf_op jit(solution)/shard_map/ppermute | solution.py:169
  36.1 0.2 collective-permute-start.16
  36.4 2.1 %step_4.1 = (f32[70,96,128]{2,1,0:T(8,128)S(1)}, bf16[70,192,128]{2,1,0:T(8,128)(2,1)S(1)}) custom-call(s32[2,70]{1,0:T(2,128)S(4)} %get-tuple-element.86.cols, bf16[70,256,256]{2,1,0:T(8,128)(2,1)S(1)} %get-tuple-element.101.weights, f32[70,96,128]{2,1,0:T(8,128)S(1)} %get-tuple-element.118.state.spare_state, ...), custom_call_target="tpu_custom_call", output_to_operand_aliasing={{0}: (5, {}), {1}: (6, {})} | custom-call | flops 1761607680 | bytes 12000000 | tf_op jit(solution)/shard_map/step_4/pallas_call | solution.py:473
  38.5 0.4 collective-permute-done.15.low
  38.8 0.3 ties_4.1
  39.1 0.9 %collective-permute-start.17 = (f32[96,128]{1,0:T(8,128)S(1)}, f32[96,128]{1,0:T(8,128)S(1)}, u32[]{:S(2)}, u32[]{:S(2)}) collective-permute-start(f32[96,128]{1,0:T(8,128)S(1)} %get-tuple-element.122), channel_id=1, source_target_pairs={{0,24},{8,16},{16,8},{24,0},{1,25},{9,17},{17,9},{25,1},{2,26},{10... | collective-permute-start | bytes 147464 | tf_op jit(solution)/shard_map/ppermute | solution.py:169
  40.1 0.3 collective-permute-start.18
  40.4 2.3 %step_5.1 = (f32[70,96,128]{2,1,0:T(8,128)S(1)}, bf16[70,192,128]{2,1,0:T(8,128)(2,1)S(1)}) custom-call(s32[2,70]{1,0:T(2,128)S(4)} %get-tuple-element.86.cols, bf16[70,256,256]{2,1,0:T(8,128)(2,1)S(1)} %get-tuple-element.101.weights, f32[70,96,128]{2,1,0:T(8,128)S(1)} %get-tuple-element.123.state.spare_state, ...), custom_call_target="tpu_custom_call", output_to_operand_aliasing={{0}: (5, {}), {1}: (6, {})} | custom-call | flops 1761607680 | bytes 12000000 | tf_op jit(solution)/shard_map/step_5/pallas_call | solution.py:473
  42.8 0.3 ties_5.1
  43.1 1.1 %collective-permute-start.19 = (f32[96,128]{1,0:T(8,128)S(1)}, f32[96,128]{1,0:T(8,128)S(1)}, u32[]{:S(2)}, u32[]{:S(2)}) collective-permute-start(f32[96,128]{1,0:T(8,128)S(1)} %get-tuple-element.127), channel_id=1, source_target_pairs={{0,24},{8,16},{16,8},{24,0},{1,25},{9,17},{17,9},{25,1},{2,26},{10... | collective-permute-start | bytes 147464 | tf_op jit(solution)/shard_map/ppermute | solution.py:169
  44.2 0.4 collective-permute-start.20
  44.6 2.1 %step_6.1 = (f32[70,96,128]{2,1,0:T(8,128)S(1)}, bf16[70,192,128]{2,1,0:T(8,128)(2,1)S(1)}) custom-call(s32[2,70]{1,0:T(2,128)S(4)} %get-tuple-element.86.cols, bf16[70,256,256]{2,1,0:T(8,128)(2,1)S(1)} %get-tuple-element.101.weights, f32[70,96,128]{2,1,0:T(8,128)S(1)} %get-tuple-element.128.state.spare_state, ...), custom_call_target="tpu_custom_call", output_to_operand_aliasing={{0}: (5, {}), {1}: (6, {})} | custom-call | flops 1761607680 | bytes 12000000 | tf_op jit(solution)/shard_map/step_6/pallas_call | solution.py:473
  46.7 0.0 collective-permute-done.19.low
  46.7 0.3 ties_6.1
  47.0 1.3 %collective-permute-start.21 = (f32[96,128]{1,0:T(8,128)S(1)}, f32[96,128]{1,0:T(8,128)S(1)}, u32[]{:S(2)}, u32[]{:S(2)}) collective-permute-start(f32[96,128]{1,0:T(8,128)S(1)} %get-tuple-element.132), channel_id=1, source_target_pairs={{0,24},{8,16},{16,8},{24,0},{1,25},{9,17},{17,9},{25,1},{2,26},{10... | collective-permute-start | bytes 147464 | tf_op jit(solution)/shard_map/ppermute | solution.py:169
  48.3 0.4 collective-permute-start.22
  48.7 2.2 %step_7.1 = (f32[70,96,128]{2,1,0:T(8,128)S(1)}, bf16[70,192,128]{2,1,0:T(8,128)(2,1)S(1)}, f32[2,8960]{1,0:T(2,128)S(1)}, f32[2,8960]{1,0:T(2,128)S(1)}, f32[2,8960]{1,0:T(2,128)S(1)}) custom-call(s32[2,70]{1,0:T(2,128)S(4)} %get-tuple-element.86.cols, ...), custom_call_target="tpu_custom_call", output_to_operand_aliasing={{0}: (5, {}), {1}: (6, {})} | custom-call | flops 1761607680 | bytes 12000000 | tf_op jit(solution)/shard_map/step_7/pallas_call | solution.py:473
  50.9 0.3 ties_7.1
  51.3 2.6 %collective-permute-start.23 = (f32[2,8960]{1,0:T(2,128)S(1)}, f32[2,8960]{1,0:T(2,128)S(1)}, u32[]{:S(2)}, u32[]{:S(2)}) collective-permute-start(f32[2,8960]{1,0:T(2,128)S(1)} %get-tuple-element.141.refs_0_), channel_id=1, source_target_pairs={{0,4},{1,5},{2,6},{3,7},{4,0},{5,1},{6,2},{7,3},{8,12},{9,13},{10,... | collective-permute-start | bytes 215048 | tf_op jit(solution)/shard_map/ppermute | solution.py:135
  53.8 1.2 %collective-permute-start.24 = (f32[2,8960]{1,0:T(2,128)S(1)}, f32[2,8960]{1,0:T(2,128)S(1)}, u32[]{:S(2)}, u32[]{:S(2)}) collective-permute-start(f32[2,8960]{1,0:T(2,128)S(1)} %get-tuple-element.142.refs_2_), channel_id=1, source_target_pairs={{0,2},{1,3},{2,0},{3,1},{4,6},{5,7},{6,4},{7,5},{8,10},{9,11},{10,... | collective-permute-start | bytes 215048 | tf_op jit(solution)/shard_map/ppermute | solution.py:135
  55.1 0.5 collective-permute-start.25
  55.6 2.9 %outputs.1 = (f32[24,4,8960]{2,1,0:T(4,128)}, f32[24,4,8960]{2,1,0:T(4,128)}) custom-call(f32[70,96,128]{2,1,0:T(8,128)S(1)} %get-tuple-element.139.state, f32[24,4,8960]{2,1,0:T(4,128)S(1)} %copy-done), custom_call_target="tpu_custom_call" | custom-call | flops 1000000000 | bytes 1000000 | tf_op jit(solution)/shard_map/outputs/pallas_call | solution.py:535
  58.6 0.3 collective-permute-done.24.refs_3_
  58.9 0.5 collective-permute-done.25.refs_5_
  59.5 0.8 %collective-permute-start.26 = (f32[2,8960]{1,0:T(2,128)S(1)}, f32[2,8960]{1,0:T(2,128)S(1)}, u32[]{:S(2)}, u32[]{:S(2)}) collective-permute-start(f32[2,8960]{1,0:T(2,128)S(1)} %get-tuple-element.144.refs_0_), channel_id=1, source_target_pairs={{0,2},{1,3},{2,0},{3,1},{4,6},{5,7},{6,4},{7,5},{8,10},{9,11},{10,... | collective-permute-start | bytes 215048 | tf_op jit(solution)/shard_map/ppermute | solution.py:135
  60.3 0.6 collective-permute-start.27
  60.9 0.9 %multipliers_2.1.refs_4_.refs_1_ = f32[24,4,8960]{2,1,0:T(4,128)} custom-call(f32[70,96,128]{2,1,0:T(8,128)S(1)} %get-tuple-element.139.state, f32[24,4,8960]{2,1,0:T(4,128)S(1)} %copy-done, f32[2,8960]{1,0:T(2,128)S(1)} %get-tuple-element.146.refs_0_, f32[24,4,8960]{2,1,0:T(4,128)} %get-tuple-element.147.refs_1_), custom_call_target="tpu_custom_call", output_to_operand_aliasing={{}: (3, {})} | custom-call | flops 1000000000 | bytes 1000000 | tf_op jit(solution)/shard_map/multipliers_2/pallas_call | solution.py:513
  61.8 2.0 %collective-permute-done.26.refs_1_ = f32[2,8960]{1,0:T(2,128)S(1)} collective-permute-done((f32[2,8960]{1,0:T(2,128)S(1)}, f32[2,8960]{1,0:T(2,128)S(1)}, u32[]{:S(2)}, u32[]{:S(2)}) %collective-permute-start.26) | collective-permute-done | bytes 71712 | tf_op jit(solution)/shard_map/ppermute | solution.py:135
  63.9 0.8 %collective-permute-done.27.refs_3_ = f32[2,8960]{1,0:T(2,128)S(1)} collective-permute-done((f32[2,8960]{1,0:T(2,128)S(1)}, f32[2,8960]{1,0:T(2,128)S(1)}, u32[]{:S(2)}, u32[]{:S(2)}) %collective-permute-start.27) | collective-permute-done | bytes 71712 | tf_op jit(solution)/shard_map/ppermute | solution.py:135
  64.7 0.7 %collective-permute-start.28 = (f32[2,8960]{1,0:T(2,128)S(1)}, f32[2,8960]{1,0:T(2,128)S(1)}, u32[]{:S(2)}, u32[]{:S(2)}) collective-permute-start(f32[2,8960]{1,0:T(2,128)S(1)} %get-tuple-element.148.refs_0_), channel_id=1, source_target_pairs={{0,1},{1,0},{2,3},{3,2},{4,5},{5,4},{6,7},{7,6},{8,9},{9,8},{10,11... | collective-permute-start | bytes 215048 | tf_op jit(solution)/shard_map/ppermute | solution.py:135
  65.4 0.9 %multipliers_1.1.refs_2_.refs_1_ = f32[24,4,8960]{2,1,0:T(4,128)} custom-call(f32[70,96,128]{2,1,0:T(8,128)S(1)} %get-tuple-element.139.state, f32[24,4,8960]{2,1,0:T(4,128)S(1)} %copy-done, f32[2,8960]{1,0:T(2,128)S(1)} %get-tuple-element.149.refs_0_, f32[24,4,8960]{2,1,0:T(4,128)} %multipliers_2.1.refs_4_.refs_1_), custom_call_target="tpu_custom_call", output_to_operand_aliasing={{}: (3, {})} | custom-call | flops 1000000000 | bytes 1000000 | tf_op jit(solution)/shard_map/multipliers_1/pallas_call | solution.py:513
  66.2 2.8 %collective-permute-done.28.refs_1_ = f32[2,8960]{1,0:T(2,128)S(1)} collective-permute-done((f32[2,8960]{1,0:T(2,128)S(1)}, f32[2,8960]{1,0:T(2,128)S(1)}, u32[]{:S(2)}, u32[]{:S(2)}) %collective-permute-start.28) | collective-permute-done | bytes 71712 | tf_op jit(solution)/shard_map/ppermute | solution.py:135
  69.1 0.9 %multipliers_0.1 = f32[24,4,8960]{2,1,0:T(4,128)} custom-call(f32[70,96,128]{2,1,0:T(8,128)S(1)} %get-tuple-element.139.state, f32[24,4,8960]{2,1,0:T(4,128)S(1)} %copy-done, f32[2,8960]{1,0:T(2,128)S(1)} %node_add_2.1.refs_0_, f32[24,4,8960]{2,1,0:T(4,128)} %multipliers_1.1.refs_2_.refs_1_), custom_call_target="tpu_custom_call", output_to_operand_aliasing={{}: (3, {})} | custom-call | flops 1000000000 | bytes 1000000 | tf_op jit(solution)/shard_map/multipliers_0/pallas_call | solution.py:513
  (32 shorter events, 0.2 us)
Async XLA Ops:
  1.3 9.5 %copy-start = (f32[24,4,8960]{2,1,0:T(4,128)S(1)}, f32[24,4,8960]{2,1,0:T(4,128)}, u32[]{:S(2)}) copy-start(f32[24,4,8960]{2,1,0:T(4,128)} %mult.9) | copy-start | bytes 10321924
  1.3 9.5 %copy-start.2 = (f32[24,4,8960]{2,1,0:T(4,128)S(1)}, f32[24,4,8960]{2,1,0:T(4,128)}, u32[]{:S(2)}) copy-start(f32[24,4,8960]{2,1,0:T(4,128)} %start.3) | copy-start | bytes 10321924
  1.3 9.5 %copy-start.3 = (f32[24,8960]{1,0:T(8,128)S(1)}, f32[24,8960]{1,0:T(8,128)}, u32[]{:S(2)}) copy-start(f32[24,8960]{1,0:T(8,128)} %demand.1) | copy-start | bytes 2580484
  1.3 9.5 %copy-start.4 = (f32[4,128,128]{2,1,0:T(8,128)S(1)}, f32[4,128,128]{2,1,0:T(8,128)}, u32[]{:S(2)}) copy-start(f32[4,128,128]{2,1,0:T(8,128)} %tie_weight.1) | copy-start | bytes 786436
  1.3 12.2 %copy-start.1 = (f32[70,2,128,128]{3,2,1,0:T(8,128)S(1)}, f32[70,2,128,128]{3,2,1,0:T(8,128)}, u32[]{:S(2)}) copy-start(f32[70,2,128,128]{3,2,1,0:T(8,128)} %values.3) | copy-start | bytes 27525124
  3.1 11.6 %collective-permute-start.2 = (f32[2,8960]{1,0:T(2,128)S(1)}, f32[2,8960]{1,0:T(2,128)S(1)}, u32[]{:S(2)}, u32[]{:S(2)}) collective-permute-start(f32[2,8960]{1,0:T(2,128)S(1)} %get-tuple-element.83.after.refs_0_), channel_id=1, source_target_pairs={{0,2},{1,3},{2,0},{3,1},{4,6},{5,7},{6,4},{7,5},{8,10},{9,11},{10,... | collective-permute-start | bytes 215048 | tf_op jit(solution)/shard_map/ppermute | solution.py:135
  6.2 8.6 %collective-permute-start.3 = (f32[2,8960]{1,0:T(2,128)S(1)}, f32[2,8960]{1,0:T(2,128)S(1)}, u32[]{:S(2)}, u32[]{:S(2)}) collective-permute-start(f32[2,8960]{1,0:T(2,128)S(1)} %get-tuple-element.83.after.refs_0_), channel_id=1, source_target_pairs={{0,4},{1,5},{2,6},{3,7},{4,0},{5,1},{6,2},{7,3},{8,12},{9,13},{10,... | collective-permute-start | bytes 215048 | tf_op jit(solution)/shard_map/ppermute | solution.py:135
  8.8 7.9 %collective-permute-start.4 = (f32[2,8960]{1,0:T(2,128)S(1)}, f32[2,8960]{1,0:T(2,128)S(1)}, u32[]{:S(2)}, u32[]{:S(2)}) collective-permute-start(f32[2,8960]{1,0:T(2,128)S(1)} %get-tuple-element.83.after.refs_0_), channel_id=1, source_target_pairs={{0,6},{1,7},{2,4},{3,5},{4,2},{5,3},{6,0},{7,1},{8,14},{9,15},{10,... | collective-permute-start | bytes 215048 | tf_op jit(solution)/shard_map/ppermute | solution.py:135
  8.8 7.9 %collective-permute-start.5 = (f32[2,8960]{1,0:T(2,128)S(1)}, f32[2,8960]{1,0:T(2,128)S(1)}, u32[]{:S(2)}, u32[]{:S(2)}) collective-permute-start(f32[2,8960]{1,0:T(2,128)S(1)} %get-tuple-element.84.refs_4_), channel_id=1, source_target_pairs={{0,1},{1,0},{2,3},{3,2},{4,5},{5,4},{6,7},{7,6},{8,9},{9,8},{10,11... | collective-permute-start | bytes 215048 | tf_op jit(solution)/shard_map/ppermute | solution.py:135
  10.5 6.2 %collective-permute-start.6 = (f32[2,8960]{1,0:T(2,128)S(1)}, f32[2,8960]{1,0:T(2,128)S(1)}, u32[]{:S(2)}, u32[]{:S(2)}) collective-permute-start(f32[2,8960]{1,0:T(2,128)S(1)} %get-tuple-element.85.refs_6_), channel_id=1, source_target_pairs={{0,1},{1,0},{2,3},{3,2},{4,5},{5,4},{6,7},{7,6},{8,9},{9,8},{10,11... | collective-permute-start | bytes 215048 | tf_op jit(solution)/shard_map/ppermute | solution.py:135
  14.7 7.9 %collective-permute-start = (f32[96,128]{1,0:T(8,128)S(1)}, f32[96,128]{1,0:T(8,128)S(1)}, u32[]{:S(2)}, u32[]{:S(2)}) collective-permute-start(f32[96,128]{1,0:T(8,128)S(1)} %get-tuple-element.81), channel_id=1, source_target_pairs={{0,24},{8,16},{16,8},{24,0},{1,25},{9,17},{17,9},{25,1},{2,26},{10... | collective-permute-start | bytes 147464 | tf_op jit(solution)/shard_map/ppermute | solution.py:169
  14.8 7.8 %collective-permute-start.1 = (f32[96,128]{1,0:T(8,128)S(1)}, f32[96,128]{1,0:T(8,128)S(1)}, u32[]{:S(2)}, u32[]{:S(2)}) collective-permute-start(f32[96,128]{1,0:T(8,128)S(1)} %get-tuple-element.81), channel_id=1, source_target_pairs={{0,8},{8,0},{16,24},{24,16},{1,9},{9,1},{17,25},{25,17},{2,10},{10... | collective-permute-start | bytes 147464 | tf_op jit(solution)/shard_map/ppermute | solution.py:164
  16.7 5.3 %collective-permute-start.7 = (f32[2,8960]{1,0:T(2,128)S(1)}, f32[2,8960]{1,0:T(2,128)S(1)}, u32[]{:S(2)}, u32[]{:S(2)}) collective-permute-start(f32[2,8960]{1,0:T(2,128)S(1)} %get-tuple-element.91.refs_0_.after), channel_id=1, source_target_pairs={{0,1},{1,0},{2,3},{3,2},{4,5},{5,4},{6,7},{7,6},{8,9},{9,8},{10,11... | collective-permute-start | bytes 215048 | tf_op jit(solution)/shard_map/ppermute | solution.py:135
  18.3 4.3 %collective-permute-start.8 = (f32[2,8960]{1,0:T(2,128)S(1)}, f32[2,8960]{1,0:T(2,128)S(1)}, u32[]{:S(2)}, u32[]{:S(2)}) collective-permute-start(f32[2,8960]{1,0:T(2,128)S(1)} %get-tuple-element.92.refs_2_), channel_id=1, source_target_pairs={{0,2},{1,3},{2,0},{3,1},{4,6},{5,7},{6,4},{7,5},{8,10},{9,11},{10,... | collective-permute-start | bytes 215048 | tf_op jit(solution)/shard_map/ppermute | solution.py:135
  23.4 2.8 %collective-permute-start.10 = (f32[96,128]{1,0:T(8,128)S(1)}, f32[96,128]{1,0:T(8,128)S(1)}, u32[]{:S(2)}, u32[]{:S(2)}) collective-permute-start(f32[96,128]{1,0:T(8,128)S(1)} %get-tuple-element.100), channel_id=1, source_target_pairs={{0,8},{8,0},{16,24},{24,16},{1,9},{9,1},{17,25},{25,17},{2,10},{10... | collective-permute-start | bytes 147464 | tf_op jit(solution)/shard_map/ppermute | solution.py:164
  23.5 3.6 %collective-permute-start.9 = (f32[96,128]{1,0:T(8,128)S(1)}, f32[96,128]{1,0:T(8,128)S(1)}, u32[]{:S(2)}, u32[]{:S(2)}) collective-permute-start(f32[96,128]{1,0:T(8,128)S(1)} %get-tuple-element.100), channel_id=1, source_target_pairs={{0,24},{8,16},{16,8},{24,0},{1,25},{9,17},{17,9},{25,1},{2,26},{10... | collective-permute-start | bytes 147464 | tf_op jit(solution)/shard_map/ppermute | solution.py:169
  27.4 3.6 %collective-permute-start.11 = (f32[96,128]{1,0:T(8,128)S(1)}, f32[96,128]{1,0:T(8,128)S(1)}, u32[]{:S(2)}, u32[]{:S(2)}) collective-permute-start(f32[96,128]{1,0:T(8,128)S(1)} %get-tuple-element.107), channel_id=1, source_target_pairs={{0,24},{8,16},{16,8},{24,0},{1,25},{9,17},{17,9},{25,1},{2,26},{10... | collective-permute-start | bytes 147464 | tf_op jit(solution)/shard_map/ppermute | solution.py:169
  28.1 3.0 %collective-permute-start.12 = (f32[96,128]{1,0:T(8,128)S(1)}, f32[96,128]{1,0:T(8,128)S(1)}, u32[]{:S(2)}, u32[]{:S(2)}) collective-permute-start(f32[96,128]{1,0:T(8,128)S(1)} %get-tuple-element.107), channel_id=1, source_target_pairs={{0,8},{8,0},{16,24},{24,16},{1,9},{9,1},{17,25},{25,17},{2,10},{10... | collective-permute-start | bytes 147464 | tf_op jit(solution)/shard_map/ppermute | solution.py:164
  31.3 3.6 %collective-permute-start.13 = (f32[96,128]{1,0:T(8,128)S(1)}, f32[96,128]{1,0:T(8,128)S(1)}, u32[]{:S(2)}, u32[]{:S(2)}) collective-permute-start(f32[96,128]{1,0:T(8,128)S(1)} %get-tuple-element.112), channel_id=1, source_target_pairs={{0,24},{8,16},{16,8},{24,0},{1,25},{9,17},{17,9},{25,1},{2,26},{10... | collective-permute-start | bytes 147464 | tf_op jit(solution)/shard_map/ppermute | solution.py:169
  32.2 2.7 %collective-permute-start.14 = (f32[96,128]{1,0:T(8,128)S(1)}, f32[96,128]{1,0:T(8,128)S(1)}, u32[]{:S(2)}, u32[]{:S(2)}) collective-permute-start(f32[96,128]{1,0:T(8,128)S(1)} %get-tuple-element.112), channel_id=1, source_target_pairs={{0,8},{8,0},{16,24},{24,16},{1,9},{9,1},{17,25},{25,17},{2,10},{10... | collective-permute-start | bytes 147464 | tf_op jit(solution)/shard_map/ppermute | solution.py:164
  35.2 3.6 %collective-permute-start.15 = (f32[96,128]{1,0:T(8,128)S(1)}, f32[96,128]{1,0:T(8,128)S(1)}, u32[]{:S(2)}, u32[]{:S(2)}) collective-permute-start(f32[96,128]{1,0:T(8,128)S(1)} %get-tuple-element.117), channel_id=1, source_target_pairs={{0,24},{8,16},{16,8},{24,0},{1,25},{9,17},{17,9},{25,1},{2,26},{10... | collective-permute-start | bytes 147464 | tf_op jit(solution)/shard_map/ppermute | solution.py:169
  36.1 2.7 %collective-permute-start.16 = (f32[96,128]{1,0:T(8,128)S(1)}, f32[96,128]{1,0:T(8,128)S(1)}, u32[]{:S(2)}, u32[]{:S(2)}) collective-permute-start(f32[96,128]{1,0:T(8,128)S(1)} %get-tuple-element.117), channel_id=1, source_target_pairs={{0,8},{8,0},{16,24},{24,16},{1,9},{9,1},{17,25},{25,17},{2,10},{10... | collective-permute-start | bytes 147464 | tf_op jit(solution)/shard_map/ppermute | solution.py:164
  39.1 3.6 %collective-permute-start.17 = (f32[96,128]{1,0:T(8,128)S(1)}, f32[96,128]{1,0:T(8,128)S(1)}, u32[]{:S(2)}, u32[]{:S(2)}) collective-permute-start(f32[96,128]{1,0:T(8,128)S(1)} %get-tuple-element.122), channel_id=1, source_target_pairs={{0,24},{8,16},{16,8},{24,0},{1,25},{9,17},{17,9},{25,1},{2,26},{10... | collective-permute-start | bytes 147464 | tf_op jit(solution)/shard_map/ppermute | solution.py:169
  40.1 2.7 %collective-permute-start.18 = (f32[96,128]{1,0:T(8,128)S(1)}, f32[96,128]{1,0:T(8,128)S(1)}, u32[]{:S(2)}, u32[]{:S(2)}) collective-permute-start(f32[96,128]{1,0:T(8,128)S(1)} %get-tuple-element.122), channel_id=1, source_target_pairs={{0,8},{8,0},{16,24},{24,16},{1,9},{9,1},{17,25},{25,17},{2,10},{10... | collective-permute-start | bytes 147464 | tf_op jit(solution)/shard_map/ppermute | solution.py:164
  43.1 3.6 %collective-permute-start.19 = (f32[96,128]{1,0:T(8,128)S(1)}, f32[96,128]{1,0:T(8,128)S(1)}, u32[]{:S(2)}, u32[]{:S(2)}) collective-permute-start(f32[96,128]{1,0:T(8,128)S(1)} %get-tuple-element.127), channel_id=1, source_target_pairs={{0,24},{8,16},{16,8},{24,0},{1,25},{9,17},{17,9},{25,1},{2,26},{10... | collective-permute-start | bytes 147464 | tf_op jit(solution)/shard_map/ppermute | solution.py:169
  44.2 2.5 %collective-permute-start.20 = (f32[96,128]{1,0:T(8,128)S(1)}, f32[96,128]{1,0:T(8,128)S(1)}, u32[]{:S(2)}, u32[]{:S(2)}) collective-permute-start(f32[96,128]{1,0:T(8,128)S(1)} %get-tuple-element.127), channel_id=1, source_target_pairs={{0,8},{8,0},{16,24},{24,16},{1,9},{9,1},{17,25},{25,17},{2,10},{10... | collective-permute-start | bytes 147464 | tf_op jit(solution)/shard_map/ppermute | solution.py:164
  47.0 3.9 %collective-permute-start.21 = (f32[96,128]{1,0:T(8,128)S(1)}, f32[96,128]{1,0:T(8,128)S(1)}, u32[]{:S(2)}, u32[]{:S(2)}) collective-permute-start(f32[96,128]{1,0:T(8,128)S(1)} %get-tuple-element.132), channel_id=1, source_target_pairs={{0,24},{8,16},{16,8},{24,0},{1,25},{9,17},{17,9},{25,1},{2,26},{10... | collective-permute-start | bytes 147464 | tf_op jit(solution)/shard_map/ppermute | solution.py:169
  48.3 2.6 %collective-permute-start.22 = (f32[96,128]{1,0:T(8,128)S(1)}, f32[96,128]{1,0:T(8,128)S(1)}, u32[]{:S(2)}, u32[]{:S(2)}) collective-permute-start(f32[96,128]{1,0:T(8,128)S(1)} %get-tuple-element.132), channel_id=1, source_target_pairs={{0,8},{8,0},{16,24},{24,16},{1,9},{9,1},{17,25},{25,17},{2,10},{10... | collective-permute-start | bytes 147464 | tf_op jit(solution)/shard_map/ppermute | solution.py:164
  51.3 7.3 %collective-permute-start.23 = (f32[2,8960]{1,0:T(2,128)S(1)}, f32[2,8960]{1,0:T(2,128)S(1)}, u32[]{:S(2)}, u32[]{:S(2)}) collective-permute-start(f32[2,8960]{1,0:T(2,128)S(1)} %get-tuple-element.141.refs_0_), channel_id=1, source_target_pairs={{0,4},{1,5},{2,6},{3,7},{4,0},{5,1},{6,2},{7,3},{8,12},{9,13},{10,... | collective-permute-start | bytes 215048 | tf_op jit(solution)/shard_map/ppermute | solution.py:135
  53.8 5.0 %collective-permute-start.24 = (f32[2,8960]{1,0:T(2,128)S(1)}, f32[2,8960]{1,0:T(2,128)S(1)}, u32[]{:S(2)}, u32[]{:S(2)}) collective-permute-start(f32[2,8960]{1,0:T(2,128)S(1)} %get-tuple-element.142.refs_2_), channel_id=1, source_target_pairs={{0,2},{1,3},{2,0},{3,1},{4,6},{5,7},{6,4},{7,5},{8,10},{9,11},{10,... | collective-permute-start | bytes 215048 | tf_op jit(solution)/shard_map/ppermute | solution.py:135
  55.1 4.3 %collective-permute-start.25 = (f32[2,8960]{1,0:T(2,128)S(1)}, f32[2,8960]{1,0:T(2,128)S(1)}, u32[]{:S(2)}, u32[]{:S(2)}) collective-permute-start(f32[2,8960]{1,0:T(2,128)S(1)} %get-tuple-element.143.refs_4_), channel_id=1, source_target_pairs={{0,1},{1,0},{2,3},{3,2},{4,5},{5,4},{6,7},{7,6},{8,9},{9,8},{10,11... | collective-permute-start | bytes 215048 | tf_op jit(solution)/shard_map/ppermute | solution.py:135
  59.5 4.4 %collective-permute-start.26 = (f32[2,8960]{1,0:T(2,128)S(1)}, f32[2,8960]{1,0:T(2,128)S(1)}, u32[]{:S(2)}, u32[]{:S(2)}) collective-permute-start(f32[2,8960]{1,0:T(2,128)S(1)} %get-tuple-element.144.refs_0_), channel_id=1, source_target_pairs={{0,2},{1,3},{2,0},{3,1},{4,6},{5,7},{6,4},{7,5},{8,10},{9,11},{10,... | collective-permute-start | bytes 215048 | tf_op jit(solution)/shard_map/ppermute | solution.py:135
  60.3 4.3 %collective-permute-start.27 = (f32[2,8960]{1,0:T(2,128)S(1)}, f32[2,8960]{1,0:T(2,128)S(1)}, u32[]{:S(2)}, u32[]{:S(2)}) collective-permute-start(f32[2,8960]{1,0:T(2,128)S(1)} %get-tuple-element.145.refs_2_), channel_id=1, source_target_pairs={{0,1},{1,0},{2,3},{3,2},{4,5},{5,4},{6,7},{7,6},{8,9},{9,8},{10,11... | collective-permute-start | bytes 215048 | tf_op jit(solution)/shard_map/ppermute | solution.py:135
  64.7 4.4 %collective-permute-start.28 = (f32[2,8960]{1,0:T(2,128)S(1)}, f32[2,8960]{1,0:T(2,128)S(1)}, u32[]{:S(2)}, u32[]{:S(2)}) collective-permute-start(f32[2,8960]{1,0:T(2,128)S(1)} %get-tuple-element.148.refs_0_), channel_id=1, source_target_pairs={{0,1},{1,0},{2,3},{3,2},{4,5},{5,4},{6,7},{7,6},{8,9},{9,8},{10,11... | collective-permute-start | bytes 215048 | tf_op jit(solution)/shard_map/ppermute | solution.py:135

commit v5 on v4

--- a/solution.py
+++ b/solution.py
@@ -99,35 +99,26 @@
 
 def first_kernel(shared, per, small, send, start, *refs):
     sources, refs = refs[:small], refs[small:]
-    sums, targets = refs[:shared], refs[shared : shared + small]
-    send_out, head, sems = refs[shared + small :]
+    places, sizes = places_of(shared, per)
+    sums, targets = refs[: len(sizes)], refs[len(sizes) : len(sizes) + small]
+    send_out, head, sems = refs[len(sizes) + small :]
     cuts = [pl.ds(k * per, per) for k in range(shared)]
     pairs = [(start.at[cut], head.at[cut]) for cut in cuts] + list(zip(sources, targets))
     copies = copies_of(pairs, sems)
     for k in range(shared):
         copies[k].wait()
-        sums[k][...] = jnp.sum(head[k * per : (k + 1) * per], axis=1)
+        array, row = places[k]
+        sums[array][row : row + per, 0 : head.shape[2]] = jnp.sum(head[k * per : (k + 1) * per], axis=1)
     send_out[0] = send[0]
     for copy in copies[shared:]:
         copy.wait()
 
 
-def add_kernel(counts, *refs):
-    inputs, outputs = iter(refs), refs[-len(counts) :]
-    for count, output in zip(counts, outputs):
-        total = next(inputs)[...]
-        for _ in range(count):
-            total = total + next(inputs)[...]
-        output[...] = total
-
-
-def turns_of(levels, wide):
-    if not wide:
-        return [[1 << level] for level in reversed(range(levels))]
+def turns_of(levels):
     if levels < 3:
         return [[1 << level] for level in range(levels)]
     low = 1 << (levels - 2)
-    return [[low, 2 * low, 3 * low]] + turns_of(levels - 2, wide)
+    return [[low, 2 * low, 3 * low]] + turns_of(levels - 2)
 
 
 def swap(block, axis, apart):
@@ -135,22 +126,48 @@
     return lax.ppermute(block, axis, [(i, i ^ apart) for i in range(count)])
 
 
-def node_totals(sums, wide, beside):
-    shared = len(sums)
-    totals = list(sums)
-    plans = [turns_of(shared - k, wide) for k in range(shared)]
+def places_of(shared, per):
+    groups, places, sizes = {}, [], []
+    for k in range(shared):
+        key = tuple(turns_of(shared - k)[0])
+        if key not in groups:
+            groups[key] = len(sizes)
+            sizes.append(0)
+        places.append((groups[key], sizes[groups[key]]))
+        sizes[groups[key]] += per
+    return places, sizes
+
+
+def add_kernel(cuts, counts, *refs):
+    inputs, outputs = iter(refs), refs[-len(counts) :]
+    for cut, count, output in zip(cuts, counts, outputs):
+        wide = slice(0, output.shape[1])
+        total = next(inputs)[cut, wide]
+        for _ in range(count):
+            total = total + next(inputs)[cut, wide]
+        output[...] = total
+
+
+def node_totals(sums, shared, per, buses, beside):
+    places, sizes = places_of(shared, per)
+    totals = [sums[places[k][0]] for k in range(shared)]
+    plans = [turns_of(shared - k) for k in range(shared)]
     for turn in range(max(len(plan) for plan in plans)):
         active = [k for k in range(shared) if turn < len(plans[k])]
-        operands = []
+        operands, cuts, received = [], [], {}
         for k in active:
-            operands += [totals[k]] + [swap(totals[k], "scen", apart) for apart in plans[k][turn]]
+            key = places[k][0] if turn == 0 else shared + k
+            if key not in received:
+                received[key] = [swap(totals[k], "scen", apart) for apart in plans[k][turn]]
+            operands += [totals[k]] + received[key]
+            cuts.append(slice(places[k][1], places[k][1] + per) if turn == 0 else slice(0, per))
         after = beside(turn, totals, [k for k in range(shared) if len(plans[k]) == turn])
         counts = [len(plans[k][turn]) for k in active]
         added = pl.pallas_call(
-            functools.partial(add_kernel, counts),
+            functools.partial(add_kernel, cuts, counts),
             in_specs=[vmem_spec] * len(operands) + [any_spec] * len(after),
             out_specs=[vmem_spec] * len(active),
-            out_shape=[VMEM(totals[k].shape, f32) for k in active],
+            out_shape=[VMEM((per, buses), f32) for k in active],
             compiler_params=params(2),
             name=f"node_add_{turn}",
         )(*[in_vmem(a) for a in operands], *after)
@@ -169,7 +186,7 @@
     return lax.ppermute(value, axis, [(i, (i + 1 if i % 2 else i - 1) % count) for i in range(count)])
 
 
-def prepare_kernel(shared, per, scen_all, send, tie_source, node_ids, load_factor,
+def prepare_kernel(shared, per, scen_all, send, node_ids, load_factor,
                    start, mult, demand, tie_weight, state, parts, constant, ties, load, boundary):
     rows = state.shape[1]
     scenarios = start.shape[1]
@@ -181,15 +198,11 @@
                 at = (k * per + t) * scenarios + s
                 load[at : at + 1] = row
     boundary[...] = start[:, :, lanes(send[0])].reshape(boundary.shape)
-    mine = lax.axis_index("area")
-    zero = jnp.zeros((128, 128), f32)
     for m in range(tie_weight.shape[0]):
         high, low = split(tie_weight[m] * -step_size)
-        from_partner = jnp.full((128, 128), tie_source[m] // send.shape[0], jnp.int32) == (mine ^ 1)
-        for n, part in enumerate((high.astype(f32), low.astype(f32))):
-            cut = slice(n * 128, (n + 1) * 128)
-            ties[m, 0:128, cut] = jnp.where(from_partner, zero, part).astype(bf16)
-            ties[m, 128:256, cut] = jnp.where(from_partner, part, zero).astype(bf16)
+        for half in range(2):
+            ties[m, half * 128 : (half + 1) * 128, 0:128] = high
+            ties[m, half * 128 : (half + 1) * 128, 128:256] = low
 
     def one(i, carry):
         for k in range(rows // group):
@@ -234,56 +247,83 @@
     first_step(first, count, cols, values, state, parts, constant, *refs)
 
 
-def step_kernel(cols, weights, state, parts, constant, spare_state, spare_parts, new_state, new_parts):
+def step_kernel(tie_row, cols, added, weights, constant, a, b, c, d, state, parts, new_state, new_parts):
+    apply_ties(tie_row, added, state, parts)
     for i in range(state.shape[0]):
         advance(i, cols[1, i], weights[i], state, parts, constant, new_state, new_parts)
 
 
 def add_sums(shared, per, scenarios, i, value, sums):
     group = per * scenarios
-    for k in range(shared):
+    for k, (array, row) in enumerate(places_of(shared, per)[0]):
         piece = value[k * group : (k + 1) * group].reshape(per, scenarios, 128)
-        sums[k][:, lanes(i)] = jnp.sum(piece, axis=1)
-
-
-def last_step_kernel(shared, per, scenarios, cols, weights, state, parts, constant, spare_state, spare_parts,
-                     new_state, new_parts, *sums):
+        sums[array][row : row + per, lanes(i)] = jnp.sum(piece, axis=1)
+
+
+def last_step_kernel(shared, per, scenarios, tie_row, cols, added, weights, constant, a, b, c, d,
+                     state, parts, new_state, new_parts, *sums):
+    apply_ties(tie_row, added, state, parts)
     for i in range(state.shape[0]):
         value = advance(i, cols[1, i], weights[i], state, parts, constant, new_state, new_parts)
         add_sums(shared, per, scenarios, i, value, sums)
 
 
-def add_ties(tie_row, low, high, ties, state):
-    rows = state.shape[1]
-    both = jnp.concatenate([low[...], high[...]], axis=1)
-    left = jnp.concatenate(split(both), axis=0)
-    count = ties.shape[0]
-    added = [fold(jnp.dot(left, ties[m], preferred_element_type=f32), rows) for m in range(count)]
-    values = []
-    for m in range(count):
-        total = state[tie_row[m]]
-        for n in range(count):
-            same = jnp.where(tie_row[n] == tie_row[m], 1.0, 0.0)
-            total = total + (added[n] if n == m else same * added[n])
-        values.append(total)
+def tie_products(tie_source, bound_count, other, pair, ties, left):
+    for n, block in enumerate((other, pair)):
+        high, low = split(block[...])
+        left[n, :, 0:128] = high
+        left[n, :, 128:256] = low
+    partner_area = lax.axis_index("area") ^ 1
+    products = []
+    for m in range(ties.shape[0]):
+        source = jnp.where(tie_source[m] // bound_count == partner_area, 1, 0)
+        product = jnp.dot(left[source], ties[m], preferred_element_type=f32)
+        products.append(product[:, :128] + product[:, 128:])
+    return products
+
+
+def meeting(row, tie_row, products):
+    total = None
+    for n, product in enumerate(products):
+        term = jnp.where(tie_row[n] == row, 1.0, 0.0) * product
+        total = term if total is None else total + term
+    return total
+
+
+def apply_ties(tie_row, added, state, parts):
+    count = added.shape[0]
+    products = [added[m] for m in range(count)]
+    values = [state[tie_row[m]] + meeting(tie_row[m], tie_row, products) for m in range(count)]
     for m in range(count):
         state[tie_row[m]] = values[m]
-    return values
-
-
-def put_parts(tie_row, values, parts):
-    for m, value in enumerate(values):
-        store_split(parts, tie_row[m], value)
-
-
-def tie_kernel(tie_row, send, low, high, ties, state_in, parts_in, state, parts, boundary):
-    put_parts(tie_row, add_ties(tie_row, low, high, ties, state), parts)
-    boundary[...] = state[send[0]]
-
-
-def anchor_kernel(shared, scen_all, scenarios, tie_row, send, low, high, ties, *refs):
+        store_split(parts, tie_row[m], values[m])
+
+
+def tie_kernel(tie_row, tie_source, send, pair, other, ties, state, added, boundary, left):
+    products = tie_products(tie_source, send.shape[0], other, pair, ties, left)
+    boundary[...] = state[send[0]] + meeting(send[0], tie_row, products)
+    for m, product in enumerate(products):
+        added[m] = product
+
+
+def anchor_piece(k, scen_all, scenarios, total, i):
+    mean = spread(total, 0, total.shape[0], scenarios, i) * (1.0 / (scen_all >> k))
+    return (step_size * penalty) * mean
+
+
+def first_tie_kernel(shared, scen_all, scenarios, tie_row, tie_source, send, pair, other, ties, state, *refs):
     totals = refs[:shared]
-    state, parts, constant, boundary = refs[shared + 3 :]
+    added, boundary, left = refs[shared:]
+    tie_kernel(tie_row, tie_source, send, pair, other, ties, state, added, boundary, left)
+    group = totals[0].shape[0] * scenarios
+    for k in range(shared):
+        cut = slice(k * group, (k + 1) * group)
+        boundary[cut] = boundary[cut] + anchor_piece(k, scen_all, scenarios, totals[k], send[0])
+
+
+def anchor_kernel(shared, scen_all, scenarios, *refs):
+    totals = refs[:shared]
+    state, parts, constant = refs[shared + 3 :]
     rows = state.shape[1]
     group = totals[0].shape[0] * scenarios
     span = min(-(-shared * group // 16) * 16, rows)
@@ -291,8 +331,7 @@
     def one(i, carry):
         for k in range(shared):
             cut = slice(k * group, (k + 1) * group)
-            mean = spread(totals[k], 0, group // scenarios, scenarios, i) * (1.0 / (scen_all >> k))
-            mean = (step_size * penalty) * mean
+            mean = anchor_piece(k, scen_all, scenarios, totals[k], i)
             constant[i, cut] = constant[i, cut] + mean
             state[i, cut] = state[i, cut] + mean
         high_part, low_part = split(state[i, 0:span])
@@ -301,15 +340,18 @@
         return carry
 
     lax.fori_loop(0, state.shape[0], one, 0, unroll=largest_divisor(state.shape[0], 14))
-    put_parts(tie_row, add_ties(tie_row, low, high, ties, state), parts)
-    boundary[...] = state[send[0]]
-
-
-def last_tie_kernel(shared, per, scenarios, tie_row, low, high, ties, *refs):
-    state, sums = refs[shared + 1], refs[shared + 2 :]
-    values = add_ties(tie_row, low, high, ties, state)
-    for m, value in enumerate(values):
-        add_sums(shared, per, scenarios, tie_row[m], value, sums)
+
+
+def last_tie_kernel(shared, per, scenarios, bound_count, tie_row, tie_source, pair, other, ties, *refs):
+    left = refs[-1]
+    half = (len(refs) - 1) // 2
+    state, sums = refs[half], refs[half + 1 : -1]
+    products = tie_products(tie_source, bound_count, other, pair, ties, left)
+    count = len(products)
+    values = [state[tie_row[m]] + meeting(tie_row[m], tie_row, products) for m in range(count)]
+    for m in range(count):
+        state[tie_row[m]] = values[m]
+        add_sums(shared, per, scenarios, tie_row[m], values[m], sums)
 
 
 def write_blocks(pieces, blocks, one, targets, sems):
@@ -393,11 +435,13 @@
     tie_count = tie_row.shape[0]
 
     small = [block_cols.T, tie_row, tie_source, node_ids.T, load_factor]
+    padded = -(-buses // 1024) * 1024
+    sum_shapes = [VMEM((size, padded if size > per else buses), f32) for size in places_of(shared, per)[1]]
     first = pl.pallas_call(
         functools.partial(first_kernel, shared, per, len(small)),
         in_specs=[smem_spec] + [any_spec] * (1 + len(small)),
-        out_specs=[vmem_spec] * shared + [smem_spec] * (len(small) + 1),
-        out_shape=[VMEM((per, buses), f32)] * shared + [SMEM(a.shape, a.dtype) for a in small + [send_block]],
+        out_specs=[vmem_spec] * len(sum_shapes) + [smem_spec] * (len(small) + 1),
+        out_shape=sum_shapes + [SMEM(a.shape, a.dtype) for a in small + [send_block]],
         scratch_shapes=[
             VMEM((shared * per, scenarios, buses), f32),
             pltpu.SemaphoreType.DMA((shared + len(small),)),
@@ -406,8 +450,8 @@
         cost_estimate=cost(2 * 10**10, 10**6),
         name="first_sums",
     )(send_block, in_hbm(start_dispatch), *[in_hbm(a) for a in small])
-    sums = list(first[:shared])
-    cols, row_of_tie, source_of_tie, labels, factors, send = first[shared:]
+    sums = list(first[: len(sum_shapes)])
+    cols, row_of_tie, source_of_tie, labels, factors, send = first[len(sum_shapes) :]
 
     state_shape = VMEM((blocks, rows, 128), f32)
     parts_shape = VMEM((blocks, 2 * rows, 128), bf16)
@@ -421,14 +465,14 @@
         if turn == 0:
             laid["start"] = pl.pallas_call(
                 functools.partial(prepare_kernel, shared, per, scen_all),
-                in_specs=[smem_spec] * 4 + [vmem_spec] * 4,
+                in_specs=[smem_spec] * 3 + [vmem_spec] * 4,
                 out_specs=[vmem_spec] * 6,
                 out_shape=[state_shape, parts_shape, state_shape]
                 + [VMEM((tie_count, 256, 256), bf16), VMEM((rows, 128), f32), VMEM((rows, 128), f32)],
                 compiler_params=params(2),
                 cost_estimate=cost(10**9, 10**6),
                 name="prepare",
-            )(in_smem(send), in_smem(source_of_tie), in_smem(labels), in_smem(factors),
+            )(in_smem(send), in_smem(labels), in_smem(factors),
               *[in_vmem(a) for a in (start_dispatch, multipliers, demand, tie_weight)])
         if turn > 1:
             return []
@@ -447,62 +491,67 @@
         )(in_smem(cols), in_vmem(block_values), *held, in_vmem(after), *made)
         return [in_vmem(laid["made"][1])] if turn == 0 else []
 
-    totals = node_totals(sums, True, prepare)
-    if len(turns_of(shared, True)) < 2:
+    totals = node_totals(sums, shared, per, buses, prepare)
+    if len(turns_of(shared)) < 2:
         prepare(1, totals, [])
     spare_state, spare_parts, constant, ties, load, boundary = laid["start"]
     weights, state, parts = laid["made"]
+    added_shape = VMEM((tie_count, rows, 128), f32)
+    left_shape = VMEM((2, rows, 256), bf16)
+    tie_scalars = [in_smem(row_of_tie), in_smem(source_of_tie)]
     for iteration in range(STEPS):
-        low = from_other(boundary, "area")
-        high = from_pair(boundary, "area")
-        tie_args = [in_vmem(low), in_vmem(high), in_vmem(ties)]
-        if iteration == 0:
-            state, parts, constant, boundary = pl.pallas_call(
-                functools.partial(anchor_kernel, shared, scen_all, scenarios),
-                in_specs=[smem_spec] * 2 + [vmem_spec] * (6 + shared),
-                out_specs=[vmem_spec] * 4,
-                out_shape=[state_shape, parts_shape, state_shape, VMEM((rows, 128), f32)],
-                input_output_aliases={5 + shared: 0, 6 + shared: 1, 7 + shared: 2},
+        other = from_other(boundary, "area")
+        pair = from_pair(boundary, "area")
+        if iteration > 0:
+            last = iteration == STEPS - 1
+            made = pl.pallas_call(
+                functools.partial(last_step_kernel, shared, per, scenarios) if last else step_kernel,
+                in_specs=[smem_spec] * 2 + [vmem_spec] * 7,
+                out_specs=[vmem_spec] * (4 + len(sum_shapes) * last),
+                out_shape=[state_shape, parts_shape] * 2 + sum_shapes * last,
+                input_output_aliases={5: 0, 6: 1, 7: 2, 8: 3},
                 compiler_params=params(2),
-                name="anchor",
-            )(in_smem(row_of_tie), in_smem(send), *tie_args, *[in_vmem(t) for t in totals],
-              in_vmem(state), in_vmem(parts), in_vmem(constant))
-            continue
-        last = iteration == STEPS - 1
-        used = (state, parts)
-        made = pl.pallas_call(
-            functools.partial(last_step_kernel, shared, per, scenarios) if last else step_kernel,
-            in_specs=[smem_spec] + [vmem_spec] * 6,
-            out_specs=[vmem_spec] * (2 + shared * last),
-            out_shape=[state_shape, parts_shape] + [VMEM((per, buses), f32)] * (shared * last),
-            input_output_aliases={5: 0, 6: 1},
-            compiler_params=params(2),
-            cost_estimate=cost(blocks * 2 * rows * 256 * 256 * 2, 12 * 10**6),
-            name=f"step_{iteration}",
-        )(in_smem(cols), *[in_vmem(a) for a in (weights, state, parts, constant, spare_state, spare_parts)])
-        state, parts = made[:2]
-        spare_state, spare_parts = used
-        if last:
-            made = pl.pallas_call(
-                functools.partial(last_tie_kernel, shared, per, scenarios),
-                in_specs=[smem_spec] + [vmem_spec] * (4 + shared),
-                out_specs=[vmem_spec] * (1 + shared),
-                out_shape=[state_shape] + [VMEM((per, buses), f32)] * shared,
-                input_output_aliases={4 + k: k for k in range(1 + shared)},
+                cost_estimate=cost(blocks * 2 * rows * 256 * 256 * 2, 12 * 10**6),
+                name=f"step_{iteration}",
+            )(tie_scalars[0], in_smem(cols),
+              *[in_vmem(a) for a in (added, weights, constant, state, parts, spare_state, spare_parts)])
+            spare_state, spare_parts, state, parts = made[:4]
+            sums = list(made[4:])
+        blocks_in = [in_vmem(pair), in_vmem(other), in_vmem(ties), in_vmem(state)]
+        if iteration < STEPS - 1:
+            nodes = [in_vmem(t) for t in totals] if iteration == 0 else []
+            added, boundary = pl.pallas_call(
+                functools.partial(first_tie_kernel, shared, scen_all, scenarios) if iteration == 0 else tie_kernel,
+                in_specs=[smem_spec] * 3 + [vmem_spec] * (4 + len(nodes)),
+                out_specs=[vmem_spec] * 2,
+                out_shape=[added_shape, VMEM((rows, 128), f32)],
+                scratch_shapes=[left_shape],
                 compiler_params=params(2),
                 name=f"ties_{iteration}",
-            )(in_smem(row_of_tie), *tie_args, in_vmem(state), *[in_vmem(a) for a in made[2:]])
-            state, sums = made[0], list(made[1:])
+            )(*tie_scalars, in_smem(send), *blocks_in, *nodes)
+            if iteration == 0:
+                state, parts, constant = pl.pallas_call(
+                    functools.partial(anchor_kernel, shared, scen_all, scenarios),
+                    in_specs=[vmem_spec] * (3 + shared),
+                    out_specs=[vmem_spec] * 3,
+                    out_shape=[state_shape, parts_shape, state_shape],
+                    input_output_aliases={shared: 0, shared + 1: 1, shared + 2: 2},
+                    compiler_params=params(2),
+                    cost_estimate=cost(10**9, 10**6),
+                    name="anchor",
+                )(*nodes, in_vmem(state), in_vmem(parts), in_vmem(constant))
         else:
-            state, parts, boundary = pl.pallas_call(
-                tie_kernel,
-                in_specs=[smem_spec] * 2 + [vmem_spec] * 5,
-                out_specs=[vmem_spec] * 3,
-                out_shape=[state_shape, parts_shape, VMEM((rows, 128), f32)],
-                input_output_aliases={5: 0, 6: 1},
+            made = pl.pallas_call(
+                functools.partial(last_tie_kernel, shared, per, scenarios, send_block.shape[0]),
+                in_specs=[smem_spec] * 2 + [vmem_spec] * (4 + len(sum_shapes)),
+                out_specs=[vmem_spec] * (1 + len(sum_shapes)),
+                out_shape=[state_shape] + sum_shapes,
+                input_output_aliases={5 + k: k for k in range(1 + len(sum_shapes))},
+                scratch_shapes=[left_shape],
                 compiler_params=params(2),
                 name=f"ties_{iteration}",
-            )(in_smem(row_of_tie), in_smem(send), *tie_args, in_vmem(state), in_vmem(parts))
+            )(*tie_scalars, *blocks_in, *[in_vmem(a) for a in sums])
+            state, sums = made[0], list(made[1:])
 
     state = in_vmem(state)
     pieces = largest_divisor(blocks, 5)
@@ -553,7 +602,7 @@
             open_sections.remove(k)
         return multiply(ready, totals)
 
-    totals = node_totals(sums, False, write)
+    totals = node_totals(sums, shared, per, buses, write)
     dispatch = written["dispatch"]
     new_mult = multiply(open_sections, totals)[0]
     return dispatch, new_mult

time: 70.3 us -> 68.1 us (0.969)
  Pallas kernels: 32.3 us -> 31.3 us
    ppermute x8, starting transfers between devices: 3.66 us -> 4.8 us  [from_pair(): return lax.ppermute(value, axis, [(i, i ^ 1) for i in range(count)])]
    ppermute x8, starting transfers between devices: 6.36 us -> 5.55 us  [from_other(): lax.ppermute(value, axis, [(i, (i + 1 if i % 2 else i - 1) % count) for i...]
    ppermute x13 -> x12, starting transfers between devices: 16.5 us -> 15.7 us  [swap(): return lax.ppermute(block, axis, [(i, i ^ apart) for i in range(count)])]
    pallas_call x3 -> x2, Pallas kernels: 2.59 us -> 1.81 us  [multiply(): pl.pallas_call(functools.partial(multiplier_kernel, chosen, scen_all, pie...]
    ppermute x13 -> x12, waiting for transfers between devices: 7.1 us -> 6.7 us  [swap(): return lax.ppermute(block, axis, [(i, i ^ apart) for i in range(count)])]
  transfers between devices with their start and end apart: 29 -> 28, of which waited for: 10 -> 11; matrix products, arithmetic and copies ran while one was open for 0% -> 0% of each run, Pallas kernels for 38% -> 39%
where the time goes in v5:
time: 68.1 us; the launch traced here: 68 us
  Pallas kernels  31.3 us (46%)
  starting transfers between devices  26.1 us (38%)
  waiting for transfers between devices  8.88 us (13%)
  between operations  1.71 us (3%)
    ppermute x12, starting transfers between devices, swap(): return lax.ppermute(block, axis, [(i, i ^ apart) for i in range(count)])  15.7 us
    pallas_call x7, Pallas kernels, local(): pl.pallas_call(functools.partial(last_step_kernel, shared, per, scenarios...  15.4 us
    ppermute x12, waiting for transfers between devices, swap(): return lax.ppermute(block, axis, [(i, i ^ apart) for i in range(count)])  6.7 us
    ppermute x8, starting transfers between devices, from_other(): lax.ppermute(value, axis, [(i, (i + 1 if i % 2 else i - 1) % count) for i...  5.55 us
    ppermute x8, starting transfers between devices, from_pair(): return lax.ppermute(value, axis, [(i, i ^ 1) for i in range(count)])  4.8 us
    pallas_call x2, Pallas kernels, prepare(): pl.pallas_call(functools.partial(first_step_begin if turn == 0 else first...  4.26 us
    pallas_call x1, Pallas kernels, write(): pl.pallas_call(functools.partial(output_kernel, own, scen_all, pieces), i...  2.91 us
    pallas_call x1, Pallas kernels, prepare(): pl.pallas_call(functools.partial(prepare_kernel, shared, per, scen_all),...  2.63 us
  transfers between devices with their start and end apart: 28, of which 11 were waited for; matrix products, arithmetic and copies ran while one was open for 0% of the time, Pallas kernels for 39%

profile of v5, /device:TPU:0, one launch (start us, length us, event | category | flops | bytes accessed | tf_op | source)
XLA Modules:
  0.0 68.0 jit_solution(9189284642817622949)
XLA Ops:
  1.3 1.7 %first_sums.1 = (f32[2,8960]{1,0:T(2,128)S(1)}, f32[4,9216]{1,0:T(4,128)S(1)}, s32[2,70]{1,0:T(2,128)S(4)}, s32[4]{0:T(128)S(4)}, s32[4]{0:T(128)S(4)}, /*index=...) custom-call(s32[1]{0:T(128)S(6)} %copy.91.send, f32[24,4,8960]{2,1,0:T(4,128)} %start.3, s32[2,70]{1,0:T(2,128)} %bitcast.3, ...), custom_call_target="tpu_custom_call" | custom-call | flops 20000000000 | bytes 1000000 | tf_op jit(solution)/shard_map/first_sums/pallas_call | solution.py:440
  3.1 5.1 %collective-permute-start.4 = (f32[2,8960]{1,0:T(2,128)S(1)}, f32[2,8960]{1,0:T(2,128)S(1)}, u32[]{:S(2)}, u32[]{:S(2)}) collective-permute-start(f32[2,8960]{1,0:T(2,128)S(1)} %get-tuple-element.91.after.refs_0_), channel_id=1, source_target_pairs={{0,6},{1,7},{2,4},{3,5},{4,2},{5,3},{6,0},{7,1},{8,14},{9,15},{10,... | collective-permute-start | bytes 215048 | tf_op jit(solution)/shard_map/ppermute | solution.py:126
  8.2 0.0 collective-permute-start.3
  8.2 0.6 collective-permute-start.2
  8.8 1.6 %collective-permute-start.5 = (f32[4,9216]{1,0:T(4,128)S(1)}, f32[4,9216]{1,0:T(4,128)S(1)}, u32[]{:S(2)}, u32[]{:S(2)}) collective-permute-start(f32[4,9216]{1,0:T(4,128)S(1)} %get-tuple-element.92.refs_4_.refs_6_), channel_id=1, source_target_pairs={{0,1},{1,0},{2,3},{3,2},{4,5},{5,4},{6,7},{7,6},{8,9},{9,8},{10,11... | collective-permute-start | bytes 442376 | tf_op jit(solution)/shard_map/ppermute | solution.py:126
  10.5 2.6 %prepare.1 = (f32[70,96,128]{2,1,0:T(8,128)S(1)}, bf16[70,192,128]{2,1,0:T(8,128)(2,1)S(1)}, f32[70,96,128]{2,1,0:T(8,128)S(1)}, bf16[4,256,256]{2,1,0:T(8,128)(...) custom-call(s32[1]{0:T(128)S(4)} %get-tuple-element.82.send, s32[4,12]{1,0:T(4,128)S(4)} %get-tuple-element.83.node_ids, ...), custom_call_target="tpu_custom_call" | custom-call | flops 1000000000 | bytes 1000000 | tf_op jit(solution)/shard_map/prepare/pallas_call | solution.py:466
  13.1 1.2 %step_0_0.1 = (bf16[70,256,256]{2,1,0:T(8,128)(2,1)S(1)}, f32[70,96,128]{2,1,0:T(8,128)S(1)}, bf16[70,192,128]{2,1,0:T(8,128)(2,1)S(1)}) custom-call(s32[2,70]{1,0:T(2,128)S(4)} %get-tuple-element.87.cols, f32[70,2,128,128]{3,2,1,0:T(8,128)S(1)} %copy-done.1, f32[70,96,128]{2,1,0:T(8,128)S(1)} %get-tuple-element.88.state.c, ...), custom_call_target="tpu_custom_call" | custom-call | flops 1000000000 | bytes 1000000 | tf_op jit(solution)/shard_map/step_0_0/pallas_call | solution.py:482
  14.4 0.0 collective-permute-done.4.refs_3_
  14.4 1.7 %collective-permute-start = (f32[96,128]{1,0:T(8,128)S(1)}, f32[96,128]{1,0:T(8,128)S(1)}, u32[]{:S(2)}, u32[]{:S(2)}) collective-permute-start(f32[96,128]{1,0:T(8,128)S(1)} %get-tuple-element.85), channel_id=1, source_target_pairs={{0,8},{8,0},{16,24},{24,16},{1,9},{9,1},{17,25},{25,17},{2,10},{10... | collective-permute-start | bytes 147464 | tf_op jit(solution)/shard_map/ppermute | solution.py:181
  16.1 0.1 node_add_0.2
  16.1 1.3 %collective-permute-start.7 = (f32[2,8960]{1,0:T(2,128)S(1)}, f32[2,8960]{1,0:T(2,128)S(1)}, u32[]{:S(2)}, u32[]{:S(2)}) collective-permute-start(f32[2,8960]{1,0:T(2,128)S(1)} %get-tuple-element.98.refs_2_), channel_id=1, source_target_pairs={{0,2},{1,3},{2,0},{3,1},{4,6},{5,7},{6,4},{7,5},{8,10},{9,11},{10,... | collective-permute-start | bytes 215048 | tf_op jit(solution)/shard_map/ppermute | solution.py:126
  17.4 0.5 collective-permute-start.6
  18.0 3.0 %step_0_1.1 = (bf16[70,256,256]{2,1,0:T(8,128)(2,1)S(1)}, f32[70,96,128]{2,1,0:T(8,128)S(1)}, bf16[70,192,128]{2,1,0:T(8,128)(2,1)S(1)}) custom-call(s32[2,70]{1,0:T(2,128)S(4)} %get-tuple-element.87.cols, f32[70,2,128,128]{3,2,1,0:T(8,128)S(1)} %copy-done.1, ...), custom_call_target="tpu_custom_call", output_to_operand_aliasing={{0}: (6, {}), {1}: (7, {}), {2}: (8, {})} | custom-call | flops 1000000000 | bytes 1000000 | tf_op jit(solution)/shard_map/step_0_1/pallas_call | solution.py:482
  21.0 0.0 collective-permute-done.7.refs_3_
  21.0 0.7 %collective-permute-done.6.refs_1_ = f32[2,8960]{1,0:T(2,128)S(1)} collective-permute-done((f32[2,8960]{1,0:T(2,128)S(1)}, f32[2,8960]{1,0:T(2,128)S(1)}, u32[]{:S(2)}, u32[]{:S(2)}) %collective-permute-start.6) | collective-permute-done | bytes 71712 | tf_op jit(solution)/shard_map/ppermute | solution.py:126
  21.8 0.2 ties_0.1
  22.1 0.1 collective-permute-start.9
  22.1 0.6 collective-permute-start.8
  22.7 0.5 anchor.1
  23.2 2.1 %step_1.1 = (f32[70,96,128]{2,1,0:T(8,128)S(1)}, bf16[70,192,128]{2,1,0:T(8,128)(2,1)S(1)}, f32[70,96,128]{2,1,0:T(8,128)S(1)}, bf16[70,192,128]{2,1,0:T(8,128)(2,1)S(1)}) custom-call(s32[4]{0:T(128)S(4)} %get-tuple-element.80.tie_row, s32[2,70]{1,0:T(2,128)S(4)} %get-tuple-element.87.cols, ...), custom_call_target="tpu_custom_call", output_to_operand_aliasing={{0}: (5, {}), {1}: (6, {}), {2}: (7, {}), {3}: (8, {})} | custom-call | flops 1761607680 | bytes 12000000 | tf_op jit(solution)/shard_map/step_1/pallas_call | solution.py:507
  25.4 0.2 collective-permute-done.9.other
  25.6 0.2 ties_1.1
  25.9 1.0 %collective-permute-start.11 = (f32[96,128]{1,0:T(8,128)S(1)}, f32[96,128]{1,0:T(8,128)S(1)}, u32[]{:S(2)}, u32[]{:S(2)}) collective-permute-start(f32[96,128]{1,0:T(8,128)S(1)} %get-tuple-element.110), channel_id=1, source_target_pairs={{0,24},{8,16},{16,8},{24,0},{1,25},{9,17},{17,9},{25,1},{2,26},{10... | collective-permute-start | bytes 147464 | tf_op jit(solution)/shard_map/ppermute | solution.py:186
  26.8 0.5 collective-permute-start.10
  27.4 2.1 %step_2.1 = (f32[70,96,128]{2,1,0:T(8,128)S(1)}, bf16[70,192,128]{2,1,0:T(8,128)(2,1)S(1)}, f32[70,96,128]{2,1,0:T(8,128)S(1)}, bf16[70,192,128]{2,1,0:T(8,128)(2,1)S(1)}) custom-call(s32[4]{0:T(128)S(4)} %get-tuple-element.80.tie_row, s32[2,70]{1,0:T(2,128)S(4)} %get-tuple-element.87.cols, ...), custom_call_target="tpu_custom_call", output_to_operand_aliasing={{0}: (5, {}), {1}: (6, {}), {2}: (7, {}), {3}: (8, {})} | custom-call | flops 1761607680 | bytes 12000000 | tf_op jit(solution)/shard_map/step_2/pallas_call | solution.py:507
  29.5 0.4 collective-permute-done.11.other
  29.9 0.2 ties_2.1
  30.2 0.9 %collective-permute-start.13 = (f32[96,128]{1,0:T(8,128)S(1)}, f32[96,128]{1,0:T(8,128)S(1)}, u32[]{:S(2)}, u32[]{:S(2)}) collective-permute-start(f32[96,128]{1,0:T(8,128)S(1)} %get-tuple-element.116), channel_id=1, source_target_pairs={{0,24},{8,16},{16,8},{24,0},{1,25},{9,17},{17,9},{25,1},{2,26},{10... | collective-permute-start | bytes 147464 | tf_op jit(solution)/shard_map/ppermute | solution.py:186
  31.1 0.4 collective-permute-start.12
  31.5 2.1 %step_3.1 = (f32[70,96,128]{2,1,0:T(8,128)S(1)}, bf16[70,192,128]{2,1,0:T(8,128)(2,1)S(1)}, f32[70,96,128]{2,1,0:T(8,128)S(1)}, bf16[70,192,128]{2,1,0:T(8,128)(2,1)S(1)}) custom-call(s32[4]{0:T(128)S(4)} %get-tuple-element.80.tie_row, s32[2,70]{1,0:T(2,128)S(4)} %get-tuple-element.87.cols, ...), custom_call_target="tpu_custom_call", output_to_operand_aliasing={{0}: (5, {}), {1}: (6, {}), {2}: (7, {}), {3}: (8, {})} | custom-call | flops 1761607680 | bytes 12000000 | tf_op jit(solution)/shard_map/step_3/pallas_call | solution.py:507
  33.7 0.4 collective-permute-done.13.other
  34.0 0.2 ties_3.1
  34.3 0.9 %collective-permute-start.15 = (f32[96,128]{1,0:T(8,128)S(1)}, f32[96,128]{1,0:T(8,128)S(1)}, u32[]{:S(2)}, u32[]{:S(2)}) collective-permute-start(f32[96,128]{1,0:T(8,128)S(1)} %get-tuple-element.122), channel_id=1, source_target_pairs={{0,24},{8,16},{16,8},{24,0},{1,25},{9,17},{17,9},{25,1},{2,26},{10... | collective-permute-start | bytes 147464 | tf_op jit(solution)/shard_map/ppermute | solution.py:186
  35.2 0.4 collective-permute-start.14
  35.6 2.1 %step_4.1 = (f32[70,96,128]{2,1,0:T(8,128)S(1)}, bf16[70,192,128]{2,1,0:T(8,128)(2,1)S(1)}, f32[70,96,128]{2,1,0:T(8,128)S(1)}, bf16[70,192,128]{2,1,0:T(8,128)(2,1)S(1)}) custom-call(s32[4]{0:T(128)S(4)} %get-tuple-element.80.tie_row, s32[2,70]{1,0:T(2,128)S(4)} %get-tuple-element.87.cols, ...), custom_call_target="tpu_custom_call", output_to_operand_aliasing={{0}: (5, {}), {1}: (6, {}), {2}: (7, {}), {3}: (8, {})} | custom-call | flops 1761607680 | bytes 12000000 | tf_op jit(solution)/shard_map/step_4/pallas_call | solution.py:507
  37.7 0.4 collective-permute-done.15.other
  38.1 0.2 ties_4.1
  38.3 0.9 %collective-permute-start.17 = (f32[96,128]{1,0:T(8,128)S(1)}, f32[96,128]{1,0:T(8,128)S(1)}, u32[]{:S(2)}, u32[]{:S(2)}) collective-permute-start(f32[96,128]{1,0:T(8,128)S(1)} %get-tuple-element.128), channel_id=1, source_target_pairs={{0,24},{8,16},{16,8},{24,0},{1,25},{9,17},{17,9},{25,1},{2,26},{10... | collective-permute-start | bytes 147464 | tf_op jit(solution)/shard_map/ppermute | solution.py:186
  39.2 0.4 collective-permute-start.16
  39.6 2.4 %step_5.1 = (f32[70,96,128]{2,1,0:T(8,128)S(1)}, bf16[70,192,128]{2,1,0:T(8,128)(2,1)S(1)}, f32[70,96,128]{2,1,0:T(8,128)S(1)}, bf16[70,192,128]{2,1,0:T(8,128)(2,1)S(1)}) custom-call(s32[4]{0:T(128)S(4)} %get-tuple-element.80.tie_row, s32[2,70]{1,0:T(2,128)S(4)} %get-tuple-element.87.cols, ...), custom_call_target="tpu_custom_call", output_to_operand_aliasing={{0}: (5, {}), {1}: (6, {}), {2}: (7, {}), {3}: (8, {})} | custom-call | flops 1761607680 | bytes 12000000 | tf_op jit(solution)/shard_map/step_5/pallas_call | solution.py:507
  42.0 0.1 collective-permute-done.17.other
  42.1 0.2 ties_5.1
  42.4 0.9 %collective-permute-start.19 = (f32[96,128]{1,0:T(8,128)S(1)}, f32[96,128]{1,0:T(8,128)S(1)}, u32[]{:S(2)}, u32[]{:S(2)}) collective-permute-start(f32[96,128]{1,0:T(8,128)S(1)} %get-tuple-element.134), channel_id=1, source_target_pairs={{0,24},{8,16},{16,8},{24,0},{1,25},{9,17},{17,9},{25,1},{2,26},{10... | collective-permute-start | bytes 147464 | tf_op jit(solution)/shard_map/ppermute | solution.py:186
  43.3 0.4 collective-permute-start.18
  43.7 2.1 %step_6.1 = (f32[70,96,128]{2,1,0:T(8,128)S(1)}, bf16[70,192,128]{2,1,0:T(8,128)(2,1)S(1)}, f32[70,96,128]{2,1,0:T(8,128)S(1)}, bf16[70,192,128]{2,1,0:T(8,128)(2,1)S(1)}) custom-call(s32[4]{0:T(128)S(4)} %get-tuple-element.80.tie_row, s32[2,70]{1,0:T(2,128)S(4)} %get-tuple-element.87.cols, ...), custom_call_target="tpu_custom_call", output_to_operand_aliasing={{0}: (5, {}), {1}: (6, {}), {2}: (7, {}), {3}: (8, {})} | custom-call | flops 1761607680 | bytes 12000000 | tf_op jit(solution)/shard_map/step_6/pallas_call | solution.py:507
  45.8 0.4 collective-permute-done.19.other
  46.2 0.2 ties_6.1
  46.4 0.9 %collective-permute-start.21 = (f32[96,128]{1,0:T(8,128)S(1)}, f32[96,128]{1,0:T(8,128)S(1)}, u32[]{:S(2)}, u32[]{:S(2)}) collective-permute-start(f32[96,128]{1,0:T(8,128)S(1)} %get-tuple-element.140), channel_id=1, source_target_pairs={{0,24},{8,16},{16,8},{24,0},{1,25},{9,17},{17,9},{25,1},{2,26},{10... | collective-permute-start | bytes 147464 | tf_op jit(solution)/shard_map/ppermute | solution.py:186
  47.3 0.4 collective-permute-start.20
  47.7 2.3 %step_7.1 = (f32[70,96,128]{2,1,0:T(8,128)S(1)}, bf16[70,192,128]{2,1,0:T(8,128)(2,1)S(1)}, f32[70,96,128]{2,1,0:T(8,128)S(1)}, bf16[70,192,128]{2,1,0:T(8,128)(...) custom-call(s32[4]{0:T(128)S(4)} %get-tuple-element.80.tie_row, ...), custom_call_target="tpu_custom_call", output_to_operand_aliasing={{0}: (5, {}), {1}: (6, {}), {2}: (7, {}), {3}: (8, {})} | custom-call | flops 1761607680 | bytes 12000000 | tf_op jit(solution)/shard_map/step_7/pallas_call | solution.py:507
  50.0 0.2 collective-permute-done.21.other
  50.3 0.3 ties_7.1
  50.5 1.0 %collective-permute-start.25 = (f32[4,9216]{1,0:T(4,128)S(1)}, f32[4,9216]{1,0:T(4,128)S(1)}, u32[]{:S(2)}, u32[]{:S(2)}) collective-permute-start(f32[4,9216]{1,0:T(4,128)S(1)} %get-tuple-element.151.refs_4_.refs_6_), channel_id=1, source_target_pairs={{0,1},{1,0},{2,3},{3,2},{4,5},{5,4},{6,7},{7,6},{8,9},{9,8},{10,11... | collective-permute-start | bytes 442376 | tf_op jit(solution)/shard_map/ppermute | solution.py:126
  51.5 2.5 %collective-permute-start.24 = (f32[2,8960]{1,0:T(2,128)S(1)}, f32[2,8960]{1,0:T(2,128)S(1)}, u32[]{:S(2)}, u32[]{:S(2)}) collective-permute-start(f32[2,8960]{1,0:T(2,128)S(1)} %get-tuple-element.150.refs_0_), channel_id=1, source_target_pairs={{0,6},{1,7},{2,4},{3,5},{4,2},{5,3},{6,0},{7,1},{8,14},{9,15},{10,... | collective-permute-start | bytes 215048 | tf_op jit(solution)/shard_map/ppermute | solution.py:126
  54.0 0.5 collective-permute-start.23
  54.5 1.4 %collective-permute-start.22 = (f32[2,8960]{1,0:T(2,128)S(1)}, f32[2,8960]{1,0:T(2,128)S(1)}, u32[]{:S(2)}, u32[]{:S(2)}) collective-permute-start(f32[2,8960]{1,0:T(2,128)S(1)} %get-tuple-element.150.refs_0_), channel_id=1, source_target_pairs={{0,2},{1,3},{2,0},{3,1},{4,6},{5,7},{6,4},{7,5},{8,10},{9,11},{10,... | collective-permute-start | bytes 215048 | tf_op jit(solution)/shard_map/ppermute | solution.py:126
  55.9 2.9 %outputs.1 = (f32[24,4,8960]{2,1,0:T(4,128)}, f32[24,4,8960]{2,1,0:T(4,128)}) custom-call(f32[70,96,128]{2,1,0:T(8,128)S(1)} %get-tuple-element.148.state, f32[24,4,8960]{2,1,0:T(4,128)S(1)} %copy-done), custom_call_target="tpu_custom_call" | custom-call | flops 1000000000 | bytes 1000000 | tf_op jit(solution)/shard_map/outputs/pallas_call | solution.py:584
  58.8 2.5 %collective-permute-done.23.refs_2_ = f32[2,8960]{1,0:T(2,128)S(1)} collective-permute-done((f32[2,8960]{1,0:T(2,128)S(1)}, f32[2,8960]{1,0:T(2,128)S(1)}, u32[]{:S(2)}, u32[]{:S(2)}) %collective-permute-start.23) | collective-permute-done | bytes 71712 | tf_op jit(solution)/shard_map/ppermute | solution.py:126
  61.3 0.1 node_add_0.3
  61.4 1.1 %collective-permute-start.26 = (f32[2,8960]{1,0:T(2,128)S(1)}, f32[2,8960]{1,0:T(2,128)S(1)}, u32[]{:S(2)}, u32[]{:S(2)}) collective-permute-start(f32[2,8960]{1,0:T(2,128)S(1)} %get-tuple-element.152.refs_0_), channel_id=1, source_target_pairs={{0,1},{1,0},{2,3},{3,2},{4,5},{5,4},{6,7},{7,6},{8,9},{9,8},{10,11... | collective-permute-start | bytes 215048 | tf_op jit(solution)/shard_map/ppermute | solution.py:126
  62.5 0.9 %multipliers_2.1.refs_4_.refs_2_ = f32[24,4,8960]{2,1,0:T(4,128)} custom-call(f32[70,96,128]{2,1,0:T(8,128)S(1)} %get-tuple-element.148.state, f32[24,4,8960]{2,1,0:T(4,128)S(1)} %copy-done, f32[2,8960]{1,0:T(2,128)S(1)} %get-tuple-element.154.refs_0_, f32[24,4,8960]{2,1,0:T(4,128)} %get-tuple-element.155.refs_1_), custom_call_target="tpu_custom_call", output_to_operand_aliasing={{}: (3, {})} | custom-call | flops 1000000000 | bytes 1000000 | tf_op jit(solution)/shard_map/multipliers_2/pallas_call | solution.py:562
  63.4 2.4 %collective-permute-done.26.refs_1_ = f32[2,8960]{1,0:T(2,128)S(1)} collective-permute-done((f32[2,8960]{1,0:T(2,128)S(1)}, f32[2,8960]{1,0:T(2,128)S(1)}, u32[]{:S(2)}, u32[]{:S(2)}) %collective-permute-start.26) | collective-permute-done | bytes 71712 | tf_op jit(solution)/shard_map/ppermute | solution.py:126
  65.8 1.1 %collective-permute-done.27.refs_3_ = f32[2,8960]{1,0:T(2,128)S(1)} collective-permute-done((f32[2,8960]{1,0:T(2,128)S(1)}, f32[2,8960]{1,0:T(2,128)S(1)}, u32[]{:S(2)}, u32[]{:S(2)}) %collective-permute-start.27) | collective-permute-done | bytes 71712 | tf_op jit(solution)/shard_map/ppermute | solution.py:126
  66.8 0.9 %multipliers_0.1 = f32[24,4,8960]{2,1,0:T(4,128)} custom-call(f32[70,96,128]{2,1,0:T(8,128)S(1)} %get-tuple-element.148.state, f32[24,4,8960]{2,1,0:T(4,128)S(1)} %copy-done, f32[2,8960]{1,0:T(2,128)S(1)} %get-tuple-element.156.refs_0_, f32[2,8960]{1,0:T(2,128)S(1)} %get-tuple-element.157.refs_1_, ...), custom_call_target="tpu_custom_call", output_to_operand_aliasing={{}: (4, {})} | custom-call | flops 1000000000 | bytes 1000000 | tf_op jit(solution)/shard_map/multipliers_0/pallas_call | solution.py:562
  (29 shorter events, 0.1 us)
Async XLA Ops:
  1.3 9.2 %copy-start = (f32[24,4,8960]{2,1,0:T(4,128)S(1)}, f32[24,4,8960]{2,1,0:T(4,128)}, u32[]{:S(2)}) copy-start(f32[24,4,8960]{2,1,0:T(4,128)} %mult.7) | copy-start | bytes 10321924
  1.3 9.2 %copy-start.2 = (f32[24,4,8960]{2,1,0:T(4,128)S(1)}, f32[24,4,8960]{2,1,0:T(4,128)}, u32[]{:S(2)}) copy-start(f32[24,4,8960]{2,1,0:T(4,128)} %start.3) | copy-start | bytes 10321924
  1.3 9.2 %copy-start.3 = (f32[24,8960]{1,0:T(8,128)S(1)}, f32[24,8960]{1,0:T(8,128)}, u32[]{:S(2)}) copy-start(f32[24,8960]{1,0:T(8,128)} %demand.1) | copy-start | bytes 2580484
  1.3 9.2 %copy-start.4 = (f32[4,128,128]{2,1,0:T(8,128)S(1)}, f32[4,128,128]{2,1,0:T(8,128)}, u32[]{:S(2)}) copy-start(f32[4,128,128]{2,1,0:T(8,128)} %tie_weight.1) | copy-start | bytes 786436
  1.3 11.8 %copy-start.1 = (f32[70,2,128,128]{3,2,1,0:T(8,128)S(1)}, f32[70,2,128,128]{3,2,1,0:T(8,128)}, u32[]{:S(2)}) copy-start(f32[70,2,128,128]{3,2,1,0:T(8,128)} %values.3) | copy-start | bytes 27525124
  3.1 11.3 %collective-permute-start.4 = (f32[2,8960]{1,0:T(2,128)S(1)}, f32[2,8960]{1,0:T(2,128)S(1)}, u32[]{:S(2)}, u32[]{:S(2)}) collective-permute-start(f32[2,8960]{1,0:T(2,128)S(1)} %get-tuple-element.91.after.refs_0_), channel_id=1, source_target_pairs={{0,6},{1,7},{2,4},{3,5},{4,2},{5,3},{6,0},{7,1},{8,14},{9,15},{10,... | collective-permute-start | bytes 215048 | tf_op jit(solution)/shard_map/ppermute | solution.py:126
  8.2 7.9 %collective-permute-start.3 = (f32[2,8960]{1,0:T(2,128)S(1)}, f32[2,8960]{1,0:T(2,128)S(1)}, u32[]{:S(2)}, u32[]{:S(2)}) collective-permute-start(f32[2,8960]{1,0:T(2,128)S(1)} %get-tuple-element.91.after.refs_0_), channel_id=1, source_target_pairs={{0,4},{1,5},{2,6},{3,7},{4,0},{5,1},{6,2},{7,3},{8,12},{9,13},{10,... | collective-permute-start | bytes 215048 | tf_op jit(solution)/shard_map/ppermute | solution.py:126
  8.2 7.9 %collective-permute-start.2 = (f32[2,8960]{1,0:T(2,128)S(1)}, f32[2,8960]{1,0:T(2,128)S(1)}, u32[]{:S(2)}, u32[]{:S(2)}) collective-permute-start(f32[2,8960]{1,0:T(2,128)S(1)} %get-tuple-element.91.after.refs_0_), channel_id=1, source_target_pairs={{0,2},{1,3},{2,0},{3,1},{4,6},{5,7},{6,4},{7,5},{8,10},{9,11},{10,... | collective-permute-start | bytes 215048 | tf_op jit(solution)/shard_map/ppermute | solution.py:126
  8.8 7.2 %collective-permute-start.5 = (f32[4,9216]{1,0:T(4,128)S(1)}, f32[4,9216]{1,0:T(4,128)S(1)}, u32[]{:S(2)}, u32[]{:S(2)}) collective-permute-start(f32[4,9216]{1,0:T(4,128)S(1)} %get-tuple-element.92.refs_4_.refs_6_), channel_id=1, source_target_pairs={{0,1},{1,0},{2,3},{3,2},{4,5},{5,4},{6,7},{7,6},{8,9},{9,8},{10,11... | collective-permute-start | bytes 442376 | tf_op jit(solution)/shard_map/ppermute | solution.py:126
  13.1 8.7 %collective-permute-start.1 = (f32[96,128]{1,0:T(8,128)S(1)}, f32[96,128]{1,0:T(8,128)S(1)}, u32[]{:S(2)}, u32[]{:S(2)}) collective-permute-start(f32[96,128]{1,0:T(8,128)S(1)} %get-tuple-element.85), channel_id=1, source_target_pairs={{0,24},{8,16},{16,8},{24,0},{1,25},{9,17},{17,9},{25,1},{2,26},{10... | collective-permute-start | bytes 147464 | tf_op jit(solution)/shard_map/ppermute | solution.py:186
  14.4 7.4 %collective-permute-start = (f32[96,128]{1,0:T(8,128)S(1)}, f32[96,128]{1,0:T(8,128)S(1)}, u32[]{:S(2)}, u32[]{:S(2)}) collective-permute-start(f32[96,128]{1,0:T(8,128)S(1)} %get-tuple-element.85), channel_id=1, source_target_pairs={{0,8},{8,0},{16,24},{24,16},{1,9},{9,1},{17,25},{25,17},{2,10},{10... | collective-permute-start | bytes 147464 | tf_op jit(solution)/shard_map/ppermute | solution.py:181
  16.1 4.9 %collective-permute-start.7 = (f32[2,8960]{1,0:T(2,128)S(1)}, f32[2,8960]{1,0:T(2,128)S(1)}, u32[]{:S(2)}, u32[]{:S(2)}) collective-permute-start(f32[2,8960]{1,0:T(2,128)S(1)} %get-tuple-element.98.refs_2_), channel_id=1, source_target_pairs={{0,2},{1,3},{2,0},{3,1},{4,6},{5,7},{6,4},{7,5},{8,10},{9,11},{10,... | collective-permute-start | bytes 215048 | tf_op jit(solution)/shard_map/ppermute | solution.py:126
  17.4 4.3 %collective-permute-start.6 = (f32[2,8960]{1,0:T(2,128)S(1)}, f32[2,8960]{1,0:T(2,128)S(1)}, u32[]{:S(2)}, u32[]{:S(2)}) collective-permute-start(f32[2,8960]{1,0:T(2,128)S(1)} %get-tuple-element.94.after.refs_0_), channel_id=1, source_target_pairs={{0,1},{1,0},{2,3},{3,2},{4,5},{5,4},{6,7},{7,6},{8,9},{9,8},{10,11... | collective-permute-start | bytes 215048 | tf_op jit(solution)/shard_map/ppermute | solution.py:126
  22.1 3.6 %collective-permute-start.9 = (f32[96,128]{1,0:T(8,128)S(1)}, f32[96,128]{1,0:T(8,128)S(1)}, u32[]{:S(2)}, u32[]{:S(2)}) collective-permute-start(f32[96,128]{1,0:T(8,128)S(1)} %get-tuple-element.102), channel_id=1, source_target_pairs={{0,24},{8,16},{16,8},{24,0},{1,25},{9,17},{17,9},{25,1},{2,26},{10... | collective-permute-start | bytes 147464 | tf_op jit(solution)/shard_map/ppermute | solution.py:186
  22.1 3.5 %collective-permute-start.8 = (f32[96,128]{1,0:T(8,128)S(1)}, f32[96,128]{1,0:T(8,128)S(1)}, u32[]{:S(2)}, u32[]{:S(2)}) collective-permute-start(f32[96,128]{1,0:T(8,128)S(1)} %get-tuple-element.102), channel_id=1, source_target_pairs={{0,8},{8,0},{16,24},{24,16},{1,9},{9,1},{17,25},{25,17},{2,10},{10... | collective-permute-start | bytes 147464 | tf_op jit(solution)/shard_map/ppermute | solution.py:181
  25.9 4.1 %collective-permute-start.11 = (f32[96,128]{1,0:T(8,128)S(1)}, f32[96,128]{1,0:T(8,128)S(1)}, u32[]{:S(2)}, u32[]{:S(2)}) collective-permute-start(f32[96,128]{1,0:T(8,128)S(1)} %get-tuple-element.110), channel_id=1, source_target_pairs={{0,24},{8,16},{16,8},{24,0},{1,25},{9,17},{17,9},{25,1},{2,26},{10... | collective-permute-start | bytes 147464 | tf_op jit(solution)/shard_map/ppermute | solution.py:186
  26.8 3.1 %collective-permute-start.10 = (f32[96,128]{1,0:T(8,128)S(1)}, f32[96,128]{1,0:T(8,128)S(1)}, u32[]{:S(2)}, u32[]{:S(2)}) collective-permute-start(f32[96,128]{1,0:T(8,128)S(1)} %get-tuple-element.110), channel_id=1, source_target_pairs={{0,8},{8,0},{16,24},{24,16},{1,9},{9,1},{17,25},{25,17},{2,10},{10... | collective-permute-start | bytes 147464 | tf_op jit(solution)/shard_map/ppermute | solution.py:181
  30.2 3.9 %collective-permute-start.13 = (f32[96,128]{1,0:T(8,128)S(1)}, f32[96,128]{1,0:T(8,128)S(1)}, u32[]{:S(2)}, u32[]{:S(2)}) collective-permute-start(f32[96,128]{1,0:T(8,128)S(1)} %get-tuple-element.116), channel_id=1, source_target_pairs={{0,24},{8,16},{16,8},{24,0},{1,25},{9,17},{17,9},{25,1},{2,26},{10... | collective-permute-start | bytes 147464 | tf_op jit(solution)/shard_map/ppermute | solution.py:186
  31.1 2.9 %collective-permute-start.12 = (f32[96,128]{1,0:T(8,128)S(1)}, f32[96,128]{1,0:T(8,128)S(1)}, u32[]{:S(2)}, u32[]{:S(2)}) collective-permute-start(f32[96,128]{1,0:T(8,128)S(1)} %get-tuple-element.116), channel_id=1, source_target_pairs={{0,8},{8,0},{16,24},{24,16},{1,9},{9,1},{17,25},{25,17},{2,10},{10... | collective-permute-start | bytes 147464 | tf_op jit(solution)/shard_map/ppermute | solution.py:181
  34.3 3.8 %collective-permute-start.15 = (f32[96,128]{1,0:T(8,128)S(1)}, f32[96,128]{1,0:T(8,128)S(1)}, u32[]{:S(2)}, u32[]{:S(2)}) collective-permute-start(f32[96,128]{1,0:T(8,128)S(1)} %get-tuple-element.122), channel_id=1, source_target_pairs={{0,24},{8,16},{16,8},{24,0},{1,25},{9,17},{17,9},{25,1},{2,26},{10... | collective-permute-start | bytes 147464 | tf_op jit(solution)/shard_map/ppermute | solution.py:186
  35.2 2.9 %collective-permute-start.14 = (f32[96,128]{1,0:T(8,128)S(1)}, f32[96,128]{1,0:T(8,128)S(1)}, u32[]{:S(2)}, u32[]{:S(2)}) collective-permute-start(f32[96,128]{1,0:T(8,128)S(1)} %get-tuple-element.122), channel_id=1, source_target_pairs={{0,8},{8,0},{16,24},{24,16},{1,9},{9,1},{17,25},{25,17},{2,10},{10... | collective-permute-start | bytes 147464 | tf_op jit(solution)/shard_map/ppermute | solution.py:181
  38.3 3.8 %collective-permute-start.17 = (f32[96,128]{1,0:T(8,128)S(1)}, f32[96,128]{1,0:T(8,128)S(1)}, u32[]{:S(2)}, u32[]{:S(2)}) collective-permute-start(f32[96,128]{1,0:T(8,128)S(1)} %get-tuple-element.128), channel_id=1, source_target_pairs={{0,24},{8,16},{16,8},{24,0},{1,25},{9,17},{17,9},{25,1},{2,26},{10... | collective-permute-start | bytes 147464 | tf_op jit(solution)/shard_map/ppermute | solution.py:186
  39.2 2.9 %collective-permute-start.16 = (f32[96,128]{1,0:T(8,128)S(1)}, f32[96,128]{1,0:T(8,128)S(1)}, u32[]{:S(2)}, u32[]{:S(2)}) collective-permute-start(f32[96,128]{1,0:T(8,128)S(1)} %get-tuple-element.128), channel_id=1, source_target_pairs={{0,8},{8,0},{16,24},{24,16},{1,9},{9,1},{17,25},{25,17},{2,10},{10... | collective-permute-start | bytes 147464 | tf_op jit(solution)/shard_map/ppermute | solution.py:181
  42.4 3.8 %collective-permute-start.19 = (f32[96,128]{1,0:T(8,128)S(1)}, f32[96,128]{1,0:T(8,128)S(1)}, u32[]{:S(2)}, u32[]{:S(2)}) collective-permute-start(f32[96,128]{1,0:T(8,128)S(1)} %get-tuple-element.134), channel_id=1, source_target_pairs={{0,24},{8,16},{16,8},{24,0},{1,25},{9,17},{17,9},{25,1},{2,26},{10... | collective-permute-start | bytes 147464 | tf_op jit(solution)/shard_map/ppermute | solution.py:186
  43.3 2.9 %collective-permute-start.18 = (f32[96,128]{1,0:T(8,128)S(1)}, f32[96,128]{1,0:T(8,128)S(1)}, u32[]{:S(2)}, u32[]{:S(2)}) collective-permute-start(f32[96,128]{1,0:T(8,128)S(1)} %get-tuple-element.134), channel_id=1, source_target_pairs={{0,8},{8,0},{16,24},{24,16},{1,9},{9,1},{17,25},{25,17},{2,10},{10... | collective-permute-start | bytes 147464 | tf_op jit(solution)/shard_map/ppermute | solution.py:181
  46.4 3.8 %collective-permute-start.21 = (f32[96,128]{1,0:T(8,128)S(1)}, f32[96,128]{1,0:T(8,128)S(1)}, u32[]{:S(2)}, u32[]{:S(2)}) collective-permute-start(f32[96,128]{1,0:T(8,128)S(1)} %get-tuple-element.140), channel_id=1, source_target_pairs={{0,24},{8,16},{16,8},{24,0},{1,25},{9,17},{17,9},{25,1},{2,26},{10... | collective-permute-start | bytes 147464 | tf_op jit(solution)/shard_map/ppermute | solution.py:186
  47.3 2.9 %collective-permute-start.20 = (f32[96,128]{1,0:T(8,128)S(1)}, f32[96,128]{1,0:T(8,128)S(1)}, u32[]{:S(2)}, u32[]{:S(2)}) collective-permute-start(f32[96,128]{1,0:T(8,128)S(1)} %get-tuple-element.140), channel_id=1, source_target_pairs={{0,8},{8,0},{16,24},{24,16},{1,9},{9,1},{17,25},{25,17},{2,10},{10... | collective-permute-start | bytes 147464 | tf_op jit(solution)/shard_map/ppermute | solution.py:181
  50.5 10.8 %collective-permute-start.25 = (f32[4,9216]{1,0:T(4,128)S(1)}, f32[4,9216]{1,0:T(4,128)S(1)}, u32[]{:S(2)}, u32[]{:S(2)}) collective-permute-start(f32[4,9216]{1,0:T(4,128)S(1)} %get-tuple-element.151.refs_4_.refs_6_), channel_id=1, source_target_pairs={{0,1},{1,0},{2,3},{3,2},{4,5},{5,4},{6,7},{7,6},{8,9},{9,8},{10,11... | collective-permute-start | bytes 442376 | tf_op jit(solution)/shard_map/ppermute | solution.py:126
  51.5 7.3 %collective-permute-start.24 = (f32[2,8960]{1,0:T(2,128)S(1)}, f32[2,8960]{1,0:T(2,128)S(1)}, u32[]{:S(2)}, u32[]{:S(2)}) collective-permute-start(f32[2,8960]{1,0:T(2,128)S(1)} %get-tuple-element.150.refs_0_), channel_id=1, source_target_pairs={{0,6},{1,7},{2,4},{3,5},{4,2},{5,3},{6,0},{7,1},{8,14},{9,15},{10,... | collective-permute-start | bytes 215048 | tf_op jit(solution)/shard_map/ppermute | solution.py:126
  54.0 7.3 %collective-permute-start.23 = (f32[2,8960]{1,0:T(2,128)S(1)}, f32[2,8960]{1,0:T(2,128)S(1)}, u32[]{:S(2)}, u32[]{:S(2)}) collective-permute-start(f32[2,8960]{1,0:T(2,128)S(1)} %get-tuple-element.150.refs_0_), channel_id=1, source_target_pairs={{0,4},{1,5},{2,6},{3,7},{4,0},{5,1},{6,2},{7,3},{8,12},{9,13},{10,... | collective-permute-start | bytes 215048 | tf_op jit(solution)/shard_map/ppermute | solution.py:126
  54.5 6.8 %collective-permute-start.22 = (f32[2,8960]{1,0:T(2,128)S(1)}, f32[2,8960]{1,0:T(2,128)S(1)}, u32[]{:S(2)}, u32[]{:S(2)}) collective-permute-start(f32[2,8960]{1,0:T(2,128)S(1)} %get-tuple-element.150.refs_0_), channel_id=1, source_target_pairs={{0,2},{1,3},{2,0},{3,1},{4,6},{5,7},{6,4},{7,5},{8,10},{9,11},{10,... | collective-permute-start | bytes 215048 | tf_op jit(solution)/shard_map/ppermute | solution.py:126
  61.4 4.4 %collective-permute-start.26 = (f32[2,8960]{1,0:T(2,128)S(1)}, f32[2,8960]{1,0:T(2,128)S(1)}, u32[]{:S(2)}, u32[]{:S(2)}) collective-permute-start(f32[2,8960]{1,0:T(2,128)S(1)} %get-tuple-element.152.refs_0_), channel_id=1, source_target_pairs={{0,1},{1,0},{2,3},{3,2},{4,5},{5,4},{6,7},{7,6},{8,9},{9,8},{10,11... | collective-permute-start | bytes 215048 | tf_op jit(solution)/shard_map/ppermute | solution.py:126
  62.5 4.3 %collective-permute-start.27 = (f32[2,8960]{1,0:T(2,128)S(1)}, f32[2,8960]{1,0:T(2,128)S(1)}, u32[]{:S(2)}, u32[]{:S(2)}) collective-permute-start(f32[2,8960]{1,0:T(2,128)S(1)} %get-tuple-element.153.refs_2_), channel_id=1, source_target_pairs={{0,2},{1,3},{2,0},{3,1},{4,6},{5,7},{6,4},{7,5},{8,10},{9,11},{10,... | collective-permute-start | bytes 215048 | tf_op jit(solution)/shard_map/ppermute | solution.py:126

commit v6 on v5

--- a/solution.py
+++ b/solution.py
@@ -51,7 +51,7 @@
 
 def store_split(ref, index, value):
     rows = value.shape[0]
-    high, low = split(value)
+    high, low = split(value * -step_size)
     ref[index, 0:rows] = high
     ref[index, rows : 2 * rows] = low
 
@@ -186,8 +186,8 @@
     return lax.ppermute(value, axis, [(i, (i + 1 if i % 2 else i - 1) % count) for i in range(count)])
 
 
-def prepare_kernel(shared, per, scen_all, send, node_ids, load_factor,
-                   start, mult, demand, tie_weight, state, parts, constant, ties, load, boundary):
+def prepare_kernel(shared, per, scen_all, send, tie_row, tie_source, node_ids, load_factor,
+                   start, mult, demand, tie_weight, state, parts, constant, ties, loops, load, boundary):
     rows = state.shape[1]
     scenarios = start.shape[1]
     group = per * scenarios
@@ -198,11 +198,23 @@
                 at = (k * per + t) * scenarios + s
                 load[at : at + 1] = row
     boundary[...] = start[:, :, lanes(send[0])].reshape(boundary.shape)
+    def put_matrix(ref, n, value):
+        high, low = split(value)
+        for half in range(2):
+            ref[n, half * 128 : (half + 1) * 128, 0:128] = high
+            ref[n, half * 128 : (half + 1) * 128, 128:256] = low
+
+    partner_area = lax.axis_index("area") ^ 1
+    ending = [jnp.zeros((128, 128), f32)] * 2
     for m in range(tie_weight.shape[0]):
-        high, low = split(tie_weight[m] * -step_size)
-        for half in range(2):
-            ties[m, half * 128 : (half + 1) * 128, 0:128] = high
-            ties[m, half * 128 : (half + 1) * 128, 128:256] = low
+        value = tie_weight[m] * -step_size
+        put_matrix(ties, m, value)
+        ends = tie_row[m] == send[0]
+        paired = tie_source[m] // send.shape[0] == partner_area
+        ending[0] = ending[0] + jnp.where(jnp.logical_and(ends, jnp.logical_not(paired)), 1.0, 0.0) * value
+        ending[1] = ending[1] + jnp.where(jnp.logical_and(ends, paired), 1.0, 0.0) * value
+    for n in range(2):
+        put_matrix(loops, n, ending[n])
 
     def one(i, carry):
         for k in range(rows // group):
@@ -233,7 +245,7 @@
 def first_step(first, count, cols, values, state, parts, constant, weights, new_state, new_parts):
     for i in range(first, first + count):
         for j in range(2):
-            high, low = split(values[i, j] * -step_size)
+            high, low = split(values[i, j])
             weights[i, j * 128 : (j + 1) * 128, 0:128] = high
             weights[i, j * 128 : (j + 1) * 128, 128:256] = low
         advance(i, cols[1, i], weights[i], state, parts, constant, new_state, new_parts)
@@ -247,8 +259,10 @@
     first_step(first, count, cols, values, state, parts, constant, *refs)
 
 
-def step_kernel(tie_row, cols, added, weights, constant, a, b, c, d, state, parts, new_state, new_parts):
-    apply_ties(tie_row, added, state, parts)
+def step_kernel(tie_row, tie_source, cols, bound_count, other, pair, ties, weights, constant, a, b, c, d,
+                state, parts, new_state, new_parts, left):
+    products = tie_products(tie_source, bound_count, other, pair, ties, left)
+    apply_ties(tie_row, products, state, parts)
     for i in range(state.shape[0]):
         advance(i, cols[1, i], weights[i], state, parts, constant, new_state, new_parts)
 
@@ -260,9 +274,11 @@
         sums[array][row : row + per, lanes(i)] = jnp.sum(piece, axis=1)
 
 
-def last_step_kernel(shared, per, scenarios, tie_row, cols, added, weights, constant, a, b, c, d,
-                     state, parts, new_state, new_parts, *sums):
-    apply_ties(tie_row, added, state, parts)
+def last_step_kernel(shared, per, scenarios, tie_row, tie_source, cols, bound_count, other, pair, ties,
+                     weights, constant, a, b, c, d, state, parts, new_state, new_parts, *refs):
+    sums, left = refs[:-1], refs[-1]
+    products = tie_products(tie_source, bound_count, other, pair, ties, left)
+    apply_ties(tie_row, products, state, parts)
     for i in range(state.shape[0]):
         value = advance(i, cols[1, i], weights[i], state, parts, constant, new_state, new_parts)
         add_sums(shared, per, scenarios, i, value, sums)
@@ -276,7 +292,7 @@
     partner_area = lax.axis_index("area") ^ 1
     products = []
     for m in range(ties.shape[0]):
-        source = jnp.where(tie_source[m] // bound_count == partner_area, 1, 0)
+        source = jnp.where(tie_source[m] // bound_count[0] == partner_area, 1, 0)
         product = jnp.dot(left[source], ties[m], preferred_element_type=f32)
         products.append(product[:, :128] + product[:, 128:])
     return products
@@ -290,20 +306,25 @@
     return total
 
 
-def apply_ties(tie_row, added, state, parts):
-    count = added.shape[0]
-    products = [added[m] for m in range(count)]
+def apply_ties(tie_row, products, state, parts):
+    count = len(products)
     values = [state[tie_row[m]] + meeting(tie_row[m], tie_row, products) for m in range(count)]
     for m in range(count):
         state[tie_row[m]] = values[m]
         store_split(parts, tie_row[m], values[m])
 
 
-def tie_kernel(tie_row, tie_source, send, pair, other, ties, state, added, boundary, left):
-    products = tie_products(tie_source, send.shape[0], other, pair, ties, left)
-    boundary[...] = state[send[0]] + meeting(send[0], tie_row, products)
-    for m, product in enumerate(products):
-        added[m] = product
+def boundary_after(send, other, pair, loops, state):
+    value = state[send[0]]
+    for n, block in enumerate((other, pair)):
+        left = jnp.concatenate(split(block[...]), axis=1)
+        product = jnp.dot(left, loops[n], preferred_element_type=f32)
+        value = value + (product[:, :128] + product[:, 128:])
+    return value
+
+
+def tie_kernel(send, pair, other, loops, state, boundary):
+    boundary[...] = boundary_after(send, other, pair, loops, state)
 
 
 def anchor_piece(k, scen_all, scenarios, total, i):
@@ -311,10 +332,9 @@
     return (step_size * penalty) * mean
 
 
-def first_tie_kernel(shared, scen_all, scenarios, tie_row, tie_source, send, pair, other, ties, state, *refs):
-    totals = refs[:shared]
-    added, boundary, left = refs[shared:]
-    tie_kernel(tie_row, tie_source, send, pair, other, ties, state, added, boundary, left)
+def first_tie_kernel(shared, scen_all, scenarios, send, pair, other, loops, state, *refs):
+    totals, boundary = refs[:shared], refs[shared]
+    boundary[...] = boundary_after(send, other, pair, loops, state)
     group = totals[0].shape[0] * scenarios
     for k in range(shared):
         cut = slice(k * group, (k + 1) * group)
@@ -334,7 +354,7 @@
             mean = anchor_piece(k, scen_all, scenarios, totals[k], i)
             constant[i, cut] = constant[i, cut] + mean
             state[i, cut] = state[i, cut] + mean
-        high_part, low_part = split(state[i, 0:span])
+        high_part, low_part = split(state[i, 0:span] * -step_size)
         parts[i, 0:span] = high_part
         parts[i, rows : rows + span] = low_part
         return carry
@@ -457,7 +477,7 @@
     parts_shape = VMEM((blocks, 2 * rows, 128), bf16)
 
     weights_shape = VMEM((blocks, 256, 256), bf16)
-    half = 2 * blocks // 7
+    half = blocks // 7
     laid = {}
 
     def prepare(turn, totals, ready):
@@ -465,14 +485,15 @@
         if turn == 0:
             laid["start"] = pl.pallas_call(
                 functools.partial(prepare_kernel, shared, per, scen_all),
-                in_specs=[smem_spec] * 3 + [vmem_spec] * 4,
-                out_specs=[vmem_spec] * 6,
+                in_specs=[smem_spec] * 5 + [vmem_spec] * 4,
+                out_specs=[vmem_spec] * 7,
                 out_shape=[state_shape, parts_shape, state_shape]
-                + [VMEM((tie_count, 256, 256), bf16), VMEM((rows, 128), f32), VMEM((rows, 128), f32)],
+                + [VMEM((tie_count, 256, 256), bf16), VMEM((2, 256, 256), bf16)]
+                + [VMEM((rows, 128), f32), VMEM((rows, 128), f32)],
                 compiler_params=params(2),
                 cost_estimate=cost(10**9, 10**6),
                 name="prepare",
-            )(in_smem(send), in_smem(labels), in_smem(factors),
+            )(in_smem(send), in_smem(row_of_tie), in_smem(source_of_tie), in_smem(labels), in_smem(factors),
               *[in_vmem(a) for a in (start_dispatch, multipliers, demand, tie_weight)])
         if turn > 1:
             return []
@@ -494,41 +515,47 @@
     totals = node_totals(sums, shared, per, buses, prepare)
     if len(turns_of(shared)) < 2:
         prepare(1, totals, [])
-    spare_state, spare_parts, constant, ties, load, boundary = laid["start"]
+    spare_state, spare_parts, constant, ties, loops, load, boundary = laid["start"]
     weights, state, parts = laid["made"]
-    added_shape = VMEM((tie_count, rows, 128), f32)
     left_shape = VMEM((2, rows, 256), bf16)
     tie_scalars = [in_smem(row_of_tie), in_smem(source_of_tie)]
+    bound_count = send_block.shape[0]
     for iteration in range(STEPS):
+        previous = (other, pair) if iteration > 0 else None
         other = from_other(boundary, "area")
         pair = from_pair(boundary, "area")
         if iteration > 0:
             last = iteration == STEPS - 1
+            body = functools.partial(last_step_kernel, shared, per, scenarios) if last else step_kernel
+
+            def kernel(tie_row, tie_source, cols, *refs, body=body):
+                body(tie_row, tie_source, cols, (bound_count,), *refs)
+
             made = pl.pallas_call(
-                functools.partial(last_step_kernel, shared, per, scenarios) if last else step_kernel,
-                in_specs=[smem_spec] * 2 + [vmem_spec] * 7,
+                kernel,
+                in_specs=[smem_spec] * 3 + [vmem_spec] * 9,
                 out_specs=[vmem_spec] * (4 + len(sum_shapes) * last),
                 out_shape=[state_shape, parts_shape] * 2 + sum_shapes * last,
-                input_output_aliases={5: 0, 6: 1, 7: 2, 8: 3},
+                input_output_aliases={8: 0, 9: 1, 10: 2, 11: 3},
+                scratch_shapes=[left_shape],
                 compiler_params=params(2),
                 cost_estimate=cost(blocks * 2 * rows * 256 * 256 * 2, 12 * 10**6),
                 name=f"step_{iteration}",
-            )(tie_scalars[0], in_smem(cols),
-              *[in_vmem(a) for a in (added, weights, constant, state, parts, spare_state, spare_parts)])
+            )(*tie_scalars, in_smem(cols), *[in_vmem(a) for a in previous],
+              *[in_vmem(a) for a in (ties, weights, constant, state, parts, spare_state, spare_parts)])
             spare_state, spare_parts, state, parts = made[:4]
             sums = list(made[4:])
-        blocks_in = [in_vmem(pair), in_vmem(other), in_vmem(ties), in_vmem(state)]
+        arrived = [in_vmem(pair), in_vmem(other)]
         if iteration < STEPS - 1:
             nodes = [in_vmem(t) for t in totals] if iteration == 0 else []
-            added, boundary = pl.pallas_call(
+            (boundary,) = pl.pallas_call(
                 functools.partial(first_tie_kernel, shared, scen_all, scenarios) if iteration == 0 else tie_kernel,
-                in_specs=[smem_spec] * 3 + [vmem_spec] * (4 + len(nodes)),
-                out_specs=[vmem_spec] * 2,
-                out_shape=[added_shape, VMEM((rows, 128), f32)],
-                scratch_shapes=[left_shape],
+                in_specs=[smem_spec] + [vmem_spec] * (4 + len(nodes)),
+                out_specs=[vmem_spec],
+                out_shape=[VMEM((rows, 128), f32)],
                 compiler_params=params(2),
                 name=f"ties_{iteration}",
-            )(*tie_scalars, in_smem(send), *blocks_in, *nodes)
+            )(in_smem(send), *arrived, in_vmem(loops), in_vmem(state), *nodes)
             if iteration == 0:
                 state, parts, constant = pl.pallas_call(
                     functools.partial(anchor_kernel, shared, scen_all, scenarios),
@@ -542,7 +569,7 @@
                 )(*nodes, in_vmem(state), in_vmem(parts), in_vmem(constant))
         else:
             made = pl.pallas_call(
-                functools.partial(last_tie_kernel, shared, per, scenarios, send_block.shape[0]),
+                functools.partial(last_tie_kernel, shared, per, scenarios, (bound_count,)),
                 in_specs=[smem_spec] * 2 + [vmem_spec] * (4 + len(sum_shapes)),
                 out_specs=[vmem_spec] * (1 + len(sum_shapes)),
                 out_shape=[state_shape] + sum_shapes,
@@ -550,7 +577,7 @@
                 scratch_shapes=[left_shape],
                 compiler_params=params(2),
                 name=f"ties_{iteration}",
-            )(*tie_scalars, *blocks_in, *[in_vmem(a) for a in sums])
+            )(*tie_scalars, *arrived, in_vmem(ties), in_vmem(state), *[in_vmem(a) for a in sums])
             state, sums = made[0], list(made[1:])
 
     state = in_vmem(state)

time: 68.1 us -> 67.6 us (level)
  waiting for transfers between devices: 8.88 us -> 6.7 us
  Pallas kernels: 31.3 us -> 32.1 us
  starting transfers between devices: 26.1 us -> 26.8 us
    ppermute x8, waiting for transfers between devices: 2.16 us -> 0.39 us  [from_other(): lax.ppermute(value, axis, [(i, (i + 1 if i % 2 else i - 1) % count) for i...]
    pallas_call x7, Pallas kernels: 15.4 us -> 16.6 us  [local(): pl.pallas_call(kernel, in_specs=[smem_spec] * 3 + [vmem_spec] * 9, out_sp...]
  transfers between devices with their start and end apart: 28 -> 28, of which waited for: 11 -> 6; matrix products, arithmetic and copies ran while one was open for 0% -> 0% of each run, Pallas kernels for 39% -> 41%
where the time goes in v6:
time: 67.6 us; the launch traced here: 67.5 us
  Pallas kernels  32.1 us (47%)
  starting transfers between devices  26.8 us (40%)
  waiting for transfers between devices  6.7 us (10%)
  between operations  1.82 us (3%)
    pallas_call x7, Pallas kernels, local(): pl.pallas_call(kernel, in_specs=[smem_spec] * 3 + [vmem_spec] * 9, out_sp...  16.6 us
    ppermute x12, starting transfers between devices, swap(): return lax.ppermute(block, axis, [(i, i ^ apart) for i in range(count)])  15.7 us
    ppermute x12, waiting for transfers between devices, swap(): return lax.ppermute(block, axis, [(i, i ^ apart) for i in range(count)])  6.3 us
    ppermute x8, starting transfers between devices, from_other(): lax.ppermute(value, axis, [(i, (i + 1 if i % 2 else i - 1) % count) for i...  6.19 us
    ppermute x8, starting transfers between devices, from_pair(): return lax.ppermute(value, axis, [(i, i ^ 1) for i in range(count)])  4.86 us
    pallas_call x2, Pallas kernels, prepare(): pl.pallas_call(functools.partial(first_step_begin if turn == 0 else first...  4.03 us
    pallas_call x1, Pallas kernels, write(): pl.pallas_call(functools.partial(output_kernel, own, scen_all, pieces), i...  2.91 us
    pallas_call x1, Pallas kernels, prepare(): pl.pallas_call(functools.partial(prepare_kernel, shared, per, scen_all),...  2.83 us
  transfers between devices with their start and end apart: 28, of which 6 were waited for; matrix products, arithmetic and copies ran while one was open for 0% of the time, Pallas kernels for 41%

profile of v6, /device:TPU:0, one launch (start us, length us, event | category | flops | bytes accessed | tf_op | source)
XLA Modules:
  0.0 67.5 jit_solution(13856167002235759803)
XLA Ops:
  1.3 1.7 %first_sums.1 = (f32[2,8960]{1,0:T(2,128)S(1)}, f32[4,9216]{1,0:T(4,128)S(1)}, s32[2,70]{1,0:T(2,128)S(4)}, s32[4]{0:T(128)S(4)}, s32[4]{0:T(128)S(4)}, /*index=...) custom-call(s32[1]{0:T(128)S(6)} %copy.91.send, f32[24,4,8960]{2,1,0:T(4,128)} %start.3, s32[2,70]{1,0:T(2,128)} %bitcast.3, ...), custom_call_target="tpu_custom_call" | custom-call | flops 20000000000 | bytes 1000000 | tf_op jit(solution)/shard_map/first_sums/pallas_call | solution.py:460
  3.1 5.1 %collective-permute-start.4 = (f32[2,8960]{1,0:T(2,128)S(1)}, f32[2,8960]{1,0:T(2,128)S(1)}, u32[]{:S(2)}, u32[]{:S(2)}) collective-permute-start(f32[2,8960]{1,0:T(2,128)S(1)} %get-tuple-element.78.after.refs_0_), channel_id=1, source_target_pairs={{0,6},{1,7},{2,4},{3,5},{4,2},{5,3},{6,0},{7,1},{8,14},{9,15},{10,... | collective-permute-start | bytes 215048 | tf_op jit(solution)/shard_map/ppermute | solution.py:126
  8.2 0.6 collective-permute-start.2
  8.8 1.6 %collective-permute-start.5 = (f32[4,9216]{1,0:T(4,128)S(1)}, f32[4,9216]{1,0:T(4,128)S(1)}, u32[]{:S(2)}, u32[]{:S(2)}) collective-permute-start(f32[4,9216]{1,0:T(4,128)S(1)} %get-tuple-element.79.refs_4_.refs_6_), channel_id=1, source_target_pairs={{0,1},{1,0},{2,3},{3,2},{4,5},{5,4},{6,7},{7,6},{8,9},{9,8},{10,11... | collective-permute-start | bytes 442376 | tf_op jit(solution)/shard_map/ppermute | solution.py:126
  10.5 2.8 %prepare.1 = (f32[70,96,128]{2,1,0:T(8,128)S(1)}, bf16[70,192,128]{2,1,0:T(8,128)(2,1)S(1)}, f32[70,96,128]{2,1,0:T(8,128)S(1)}, bf16[4,256,256]{2,1,0:T(8,128)(...) custom-call(s32[1]{0:T(128)S(4)} %get-tuple-element.69.send, ...), custom_call_target="tpu_custom_call" | custom-call | flops 1000000000 | bytes 1000000 | tf_op jit(solution)/shard_map/prepare/pallas_call | solution.py:486
  13.3 0.0 collective-permute-start.1
  13.3 0.6 step_0_0.1
  13.9 0.0 collective-permute-done.4.refs_3_
  14.0 1.7 %collective-permute-start = (f32[96,128]{1,0:T(8,128)S(1)}, f32[96,128]{1,0:T(8,128)S(1)}, u32[]{:S(2)}, u32[]{:S(2)}) collective-permute-start(f32[96,128]{1,0:T(8,128)S(1)} %get-tuple-element.72), channel_id=1, source_target_pairs={{0,8},{8,0},{16,24},{24,16},{1,9},{9,1},{17,25},{25,17},{2,10},{10... | collective-permute-start | bytes 147464 | tf_op jit(solution)/shard_map/ppermute | solution.py:181
  15.6 0.0 collective-permute-done.3.refs_2_
  15.7 0.0 collective-permute-done.2.refs_1_
  15.7 0.0 collective-permute-done.5.refs_5_.refs_7_
  15.7 0.1 node_add_0.2
  15.7 1.3 %collective-permute-start.7 = (f32[2,8960]{1,0:T(2,128)S(1)}, f32[2,8960]{1,0:T(2,128)S(1)}, u32[]{:S(2)}, u32[]{:S(2)}) collective-permute-start(f32[2,8960]{1,0:T(2,128)S(1)} %get-tuple-element.85.refs_2_), channel_id=1, source_target_pairs={{0,2},{1,3},{2,0},{3,1},{4,6},{5,7},{6,4},{7,5},{8,10},{9,11},{10,... | collective-permute-start | bytes 215048 | tf_op jit(solution)/shard_map/ppermute | solution.py:126
  17.0 0.5 collective-permute-start.6
  17.6 3.4 %step_0_1.1 = (bf16[70,256,256]{2,1,0:T(8,128)(2,1)S(1)}, f32[70,96,128]{2,1,0:T(8,128)S(1)}, bf16[70,192,128]{2,1,0:T(8,128)(2,1)S(1)}) custom-call(s32[2,70]{1,0:T(2,128)S(4)} %get-tuple-element.74.cols, f32[70,2,128,128]{3,2,1,0:T(8,128)S(1)} %copy-done.1, ...), custom_call_target="tpu_custom_call", output_to_operand_aliasing={{0}: (6, {}), {1}: (7, {}), {2}: (8, {})} | custom-call | flops 1000000000 | bytes 1000000 | tf_op jit(solution)/shard_map/step_0_1/pallas_call | solution.py:503
  21.0 0.0 collective-permute-done.7.refs_3_
  21.0 0.4 collective-permute-done.6.refs_1_
  21.4 0.0 collective-permute-done.1.other.refs_0_
  21.4 0.2 ties_0.1
  21.6 0.1 collective-permute-start.9
  21.7 0.7 %collective-permute-start.8 = (f32[96,128]{1,0:T(8,128)S(1)}, f32[96,128]{1,0:T(8,128)S(1)}, u32[]{:S(2)}, u32[]{:S(2)}) collective-permute-start(f32[96,128]{1,0:T(8,128)S(1)} %ties_0.1), channel_id=1, source_target_pairs={{0,8},{8,0},{16,24},{24,16},{1,9},{9,1},{17,25},{25,17},{2,10},{10... | collective-permute-start | bytes 147464 | tf_op jit(solution)/shard_map/ppermute | solution.py:181
  22.4 0.5 anchor.1
  22.9 2.3 %step_1.1 = (f32[70,96,128]{2,1,0:T(8,128)S(1)}, bf16[70,192,128]{2,1,0:T(8,128)(2,1)S(1)}, f32[70,96,128]{2,1,0:T(8,128)S(1)}, bf16[70,192,128]{2,1,0:T(8,128)(2,1)S(1)}) custom-call(s32[4]{0:T(128)S(4)} %get-tuple-element.67.tie_row, s32[4]{0:T(128)S(4)} %get-tuple-element.68.tie_source, ...), custom_call_target="tpu_custom_call", output_to_operand_aliasing={{0}: (8, {}), {1}: (9, {}), {2}: (10, {}), {3}: (11, {})} | custom-call | flops 1761607680 | bytes 12000000 | tf_op jit(solution)/shard_map/step_1/pallas_call | solution.py:534
  25.3 0.2 ties_1.1
  25.4 1.1 %collective-permute-start.11 = (f32[96,128]{1,0:T(8,128)S(1)}, f32[96,128]{1,0:T(8,128)S(1)}, u32[]{:S(2)}, u32[]{:S(2)}) collective-permute-start(f32[96,128]{1,0:T(8,128)S(1)} %ties_1.1), channel_id=1, source_target_pairs={{0,24},{8,16},{16,8},{24,0},{1,25},{9,17},{17,9},{25,1},{2,26},{10... | collective-permute-start | bytes 147464 | tf_op jit(solution)/shard_map/ppermute | solution.py:186
  26.5 0.5 collective-permute-start.10
  27.0 2.3 %step_2.1 = (f32[70,96,128]{2,1,0:T(8,128)S(1)}, bf16[70,192,128]{2,1,0:T(8,128)(2,1)S(1)}, f32[70,96,128]{2,1,0:T(8,128)S(1)}, bf16[70,192,128]{2,1,0:T(8,128)(2,1)S(1)}) custom-call(s32[4]{0:T(128)S(4)} %get-tuple-element.67.tie_row, s32[4]{0:T(128)S(4)} %get-tuple-element.68.tie_source, ...), custom_call_target="tpu_custom_call", output_to_operand_aliasing={{0}: (8, {}), {1}: (9, {}), {2}: (10, {}), {3}: (11, {})} | custom-call | flops 1761607680 | bytes 12000000 | tf_op jit(solution)/shard_map/step_2/pallas_call | solution.py:534
  29.4 0.2 ties_2.1
  29.6 1.2 %collective-permute-start.13 = (f32[96,128]{1,0:T(8,128)S(1)}, f32[96,128]{1,0:T(8,128)S(1)}, u32[]{:S(2)}, u32[]{:S(2)}) collective-permute-start(f32[96,128]{1,0:T(8,128)S(1)} %ties_2.1), channel_id=1, source_target_pairs={{0,24},{8,16},{16,8},{24,0},{1,25},{9,17},{17,9},{25,1},{2,26},{10... | collective-permute-start | bytes 147464 | tf_op jit(solution)/shard_map/ppermute | solution.py:186
  30.8 0.4 collective-permute-start.12
  31.2 2.3 %step_3.1 = (f32[70,96,128]{2,1,0:T(8,128)S(1)}, bf16[70,192,128]{2,1,0:T(8,128)(2,1)S(1)}, f32[70,96,128]{2,1,0:T(8,128)S(1)}, bf16[70,192,128]{2,1,0:T(8,128)(2,1)S(1)}) custom-call(s32[4]{0:T(128)S(4)} %get-tuple-element.67.tie_row, s32[4]{0:T(128)S(4)} %get-tuple-element.68.tie_source, ...), custom_call_target="tpu_custom_call", output_to_operand_aliasing={{0}: (8, {}), {1}: (9, {}), {2}: (10, {}), {3}: (11, {})} | custom-call | flops 1761607680 | bytes 12000000 | tf_op jit(solution)/shard_map/step_3/pallas_call | solution.py:534
  33.5 0.2 ties_3.1
  33.7 1.1 %collective-permute-start.15 = (f32[96,128]{1,0:T(8,128)S(1)}, f32[96,128]{1,0:T(8,128)S(1)}, u32[]{:S(2)}, u32[]{:S(2)}) collective-permute-start(f32[96,128]{1,0:T(8,128)S(1)} %ties_3.1), channel_id=1, source_target_pairs={{0,24},{8,16},{16,8},{24,0},{1,25},{9,17},{17,9},{25,1},{2,26},{10... | collective-permute-start | bytes 147464 | tf_op jit(solution)/shard_map/ppermute | solution.py:186
  34.8 0.4 collective-permute-start.14
  35.2 2.3 %step_4.1 = (f32[70,96,128]{2,1,0:T(8,128)S(1)}, bf16[70,192,128]{2,1,0:T(8,128)(2,1)S(1)}, f32[70,96,128]{2,1,0:T(8,128)S(1)}, bf16[70,192,128]{2,1,0:T(8,128)(2,1)S(1)}) custom-call(s32[4]{0:T(128)S(4)} %get-tuple-element.67.tie_row, s32[4]{0:T(128)S(4)} %get-tuple-element.68.tie_source, ...), custom_call_target="tpu_custom_call", output_to_operand_aliasing={{0}: (8, {}), {1}: (9, {}), {2}: (10, {}), {3}: (11, {})} | custom-call | flops 1761607680 | bytes 12000000 | tf_op jit(solution)/shard_map/step_4/pallas_call | solution.py:534
  37.5 0.0 collective-permute-done.15.other.refs_0_
  37.5 0.2 ties_4.1
  37.7 1.1 %collective-permute-start.17 = (f32[96,128]{1,0:T(8,128)S(1)}, f32[96,128]{1,0:T(8,128)S(1)}, u32[]{:S(2)}, u32[]{:S(2)}) collective-permute-start(f32[96,128]{1,0:T(8,128)S(1)} %ties_4.1), channel_id=1, source_target_pairs={{0,24},{8,16},{16,8},{24,0},{1,25},{9,17},{17,9},{25,1},{2,26},{10... | collective-permute-start | bytes 147464 | tf_op jit(solution)/shard_map/ppermute | solution.py:186
  38.8 0.4 collective-permute-start.16
  39.2 2.5 %step_5.1 = (f32[70,96,128]{2,1,0:T(8,128)S(1)}, bf16[70,192,128]{2,1,0:T(8,128)(2,1)S(1)}, f32[70,96,128]{2,1,0:T(8,128)S(1)}, bf16[70,192,128]{2,1,0:T(8,128)(2,1)S(1)}) custom-call(s32[4]{0:T(128)S(4)} %get-tuple-element.67.tie_row, s32[4]{0:T(128)S(4)} %get-tuple-element.68.tie_source, ...), custom_call_target="tpu_custom_call", output_to_operand_aliasing={{0}: (8, {}), {1}: (9, {}), {2}: (10, {}), {3}: (11, {})} | custom-call | flops 1761607680 | bytes 12000000 | tf_op jit(solution)/shard_map/step_5/pallas_call | solution.py:534
  41.7 0.2 ties_5.1
  41.9 0.8 %collective-permute-start.19 = (f32[96,128]{1,0:T(8,128)S(1)}, f32[96,128]{1,0:T(8,128)S(1)}, u32[]{:S(2)}, u32[]{:S(2)}) collective-permute-start(f32[96,128]{1,0:T(8,128)S(1)} %ties_5.1), channel_id=1, source_target_pairs={{0,24},{8,16},{16,8},{24,0},{1,25},{9,17},{17,9},{25,1},{2,26},{10... | collective-permute-start | bytes 147464 | tf_op jit(solution)/shard_map/ppermute | solution.py:186
  42.8 0.4 collective-permute-start.18
  43.2 2.3 %step_6.1 = (f32[70,96,128]{2,1,0:T(8,128)S(1)}, bf16[70,192,128]{2,1,0:T(8,128)(2,1)S(1)}, f32[70,96,128]{2,1,0:T(8,128)S(1)}, bf16[70,192,128]{2,1,0:T(8,128)(2,1)S(1)}) custom-call(s32[4]{0:T(128)S(4)} %get-tuple-element.67.tie_row, s32[4]{0:T(128)S(4)} %get-tuple-element.68.tie_source, ...), custom_call_target="tpu_custom_call", output_to_operand_aliasing={{0}: (8, {}), {1}: (9, {}), {2}: (10, {}), {3}: (11, {})} | custom-call | flops 1761607680 | bytes 12000000 | tf_op jit(solution)/shard_map/step_6/pallas_call | solution.py:534
  45.5 0.3 collective-permute-done.19.other.refs_0_
  45.8 0.2 ties_6.1
  45.9 0.8 %collective-permute-start.21 = (f32[96,128]{1,0:T(8,128)S(1)}, f32[96,128]{1,0:T(8,128)S(1)}, u32[]{:S(2)}, u32[]{:S(2)}) collective-permute-start(f32[96,128]{1,0:T(8,128)S(1)} %ties_6.1), channel_id=1, source_target_pairs={{0,24},{8,16},{16,8},{24,0},{1,25},{9,17},{17,9},{25,1},{2,26},{10... | collective-permute-start | bytes 147464 | tf_op jit(solution)/shard_map/ppermute | solution.py:186
  46.8 0.4 collective-permute-start.20
  47.2 2.5 %step_7.1 = (f32[70,96,128]{2,1,0:T(8,128)S(1)}, bf16[70,192,128]{2,1,0:T(8,128)(2,1)S(1)}, f32[70,96,128]{2,1,0:T(8,128)S(1)}, bf16[70,192,128]{2,1,0:T(8,128)(...) custom-call(s32[4]{0:T(128)S(4)} %get-tuple-element.67.tie_row, ...), custom_call_target="tpu_custom_call", output_to_operand_aliasing={{0}: (8, {}), {1}: (9, {}), {2}: (10, {}), {3}: (11, {})} | custom-call | flops 1761607680 | bytes 12000000 | tf_op jit(solution)/shard_map/step_7/pallas_call | solution.py:534
  49.7 0.1 collective-permute-done.21.other
  49.8 0.3 ties_7.1
  50.0 1.2 %collective-permute-start.25 = (f32[4,9216]{1,0:T(4,128)S(1)}, f32[4,9216]{1,0:T(4,128)S(1)}, u32[]{:S(2)}, u32[]{:S(2)}) collective-permute-start(f32[4,9216]{1,0:T(4,128)S(1)} %get-tuple-element.125.refs_4_.refs_6_), channel_id=1, source_target_pairs={{0,1},{1,0},{2,3},{3,2},{4,5},{5,4},{6,7},{7,6},{8,9},{9,8},{10,11... | collective-permute-start | bytes 442376 | tf_op jit(solution)/shard_map/ppermute | solution.py:126
  51.2 2.4 %collective-permute-start.24 = (f32[2,8960]{1,0:T(2,128)S(1)}, f32[2,8960]{1,0:T(2,128)S(1)}, u32[]{:S(2)}, u32[]{:S(2)}) collective-permute-start(f32[2,8960]{1,0:T(2,128)S(1)} %get-tuple-element.124.refs_0_), channel_id=1, source_target_pairs={{0,6},{1,7},{2,4},{3,5},{4,2},{5,3},{6,0},{7,1},{8,14},{9,15},{10,... | collective-permute-start | bytes 215048 | tf_op jit(solution)/shard_map/ppermute | solution.py:126
  53.7 0.5 collective-permute-start.23
  54.2 1.5 %collective-permute-start.22 = (f32[2,8960]{1,0:T(2,128)S(1)}, f32[2,8960]{1,0:T(2,128)S(1)}, u32[]{:S(2)}, u32[]{:S(2)}) collective-permute-start(f32[2,8960]{1,0:T(2,128)S(1)} %get-tuple-element.124.refs_0_), channel_id=1, source_target_pairs={{0,2},{1,3},{2,0},{3,1},{4,6},{5,7},{6,4},{7,5},{8,10},{9,11},{10,... | collective-permute-start | bytes 215048 | tf_op jit(solution)/shard_map/ppermute | solution.py:126
  55.6 2.9 %outputs.1 = (f32[24,4,8960]{2,1,0:T(4,128)}, f32[24,4,8960]{2,1,0:T(4,128)}) custom-call(f32[70,96,128]{2,1,0:T(8,128)S(1)} %get-tuple-element.122.state, f32[24,4,8960]{2,1,0:T(4,128)S(1)} %copy-done), custom_call_target="tpu_custom_call" | custom-call | flops 1000000000 | bytes 1000000 | tf_op jit(solution)/shard_map/outputs/pallas_call | solution.py:611
  58.5 2.5 %collective-permute-done.23.refs_2_ = f32[2,8960]{1,0:T(2,128)S(1)} collective-permute-done((f32[2,8960]{1,0:T(2,128)S(1)}, f32[2,8960]{1,0:T(2,128)S(1)}, u32[]{:S(2)}, u32[]{:S(2)}) %collective-permute-start.23) | collective-permute-done | bytes 71712 | tf_op jit(solution)/shard_map/ppermute | solution.py:126
  61.0 0.1 node_add_0.3
  61.1 0.9 %collective-permute-start.26 = (f32[2,8960]{1,0:T(2,128)S(1)}, f32[2,8960]{1,0:T(2,128)S(1)}, u32[]{:S(2)}, u32[]{:S(2)}) collective-permute-start(f32[2,8960]{1,0:T(2,128)S(1)} %get-tuple-element.126.refs_0_), channel_id=1, source_target_pairs={{0,1},{1,0},{2,3},{3,2},{4,5},{5,4},{6,7},{7,6},{8,9},{9,8},{10,11... | collective-permute-start | bytes 215048 | tf_op jit(solution)/shard_map/ppermute | solution.py:126
  62.0 0.9 %multipliers_2.1.refs_4_.refs_2_ = f32[24,4,8960]{2,1,0:T(4,128)} custom-call(f32[70,96,128]{2,1,0:T(8,128)S(1)} %get-tuple-element.122.state, f32[24,4,8960]{2,1,0:T(4,128)S(1)} %copy-done, f32[2,8960]{1,0:T(2,128)S(1)} %get-tuple-element.128.refs_0_, f32[24,4,8960]{2,1,0:T(4,128)} %get-tuple-element.129.refs_1_), custom_call_target="tpu_custom_call", output_to_operand_aliasing={{}: (3, {})} | custom-call | flops 1000000000 | bytes 1000000 | tf_op jit(solution)/shard_map/multipliers_2/pallas_call | solution.py:589
  62.9 2.6 %collective-permute-done.26.refs_1_ = f32[2,8960]{1,0:T(2,128)S(1)} collective-permute-done((f32[2,8960]{1,0:T(2,128)S(1)}, f32[2,8960]{1,0:T(2,128)S(1)}, u32[]{:S(2)}, u32[]{:S(2)}) %collective-permute-start.26) | collective-permute-done | bytes 71712 | tf_op jit(solution)/shard_map/ppermute | solution.py:126
  65.5 0.9 %collective-permute-done.27.refs_3_ = f32[2,8960]{1,0:T(2,128)S(1)} collective-permute-done((f32[2,8960]{1,0:T(2,128)S(1)}, f32[2,8960]{1,0:T(2,128)S(1)}, u32[]{:S(2)}, u32[]{:S(2)}) %collective-permute-start.27) | collective-permute-done | bytes 71712 | tf_op jit(solution)/shard_map/ppermute | solution.py:126
  66.3 0.9 %multipliers_0.1 = f32[24,4,8960]{2,1,0:T(4,128)} custom-call(f32[70,96,128]{2,1,0:T(8,128)S(1)} %get-tuple-element.122.state, f32[24,4,8960]{2,1,0:T(4,128)S(1)} %copy-done, f32[2,8960]{1,0:T(2,128)S(1)} %get-tuple-element.130.refs_0_, f32[2,8960]{1,0:T(2,128)S(1)} %get-tuple-element.131.refs_1_, ...), custom_call_target="tpu_custom_call", output_to_operand_aliasing={{}: (4, {})} | custom-call | flops 1000000000 | bytes 1000000 | tf_op jit(solution)/shard_map/multipliers_0/pallas_call | solution.py:589
  (29 shorter events, 0.1 us)
Async XLA Ops:
  1.3 9.2 %copy-start = (f32[24,4,8960]{2,1,0:T(4,128)S(1)}, f32[24,4,8960]{2,1,0:T(4,128)}, u32[]{:S(2)}) copy-start(f32[24,4,8960]{2,1,0:T(4,128)} %mult.7) | copy-start | bytes 10321924
  1.3 9.2 %copy-start.2 = (f32[24,4,8960]{2,1,0:T(4,128)S(1)}, f32[24,4,8960]{2,1,0:T(4,128)}, u32[]{:S(2)}) copy-start(f32[24,4,8960]{2,1,0:T(4,128)} %start.3) | copy-start | bytes 10321924
  1.3 9.2 %copy-start.3 = (f32[24,8960]{1,0:T(8,128)S(1)}, f32[24,8960]{1,0:T(8,128)}, u32[]{:S(2)}) copy-start(f32[24,8960]{1,0:T(8,128)} %demand.1) | copy-start | bytes 2580484
  1.3 9.2 %copy-start.4 = (f32[4,128,128]{2,1,0:T(8,128)S(1)}, f32[4,128,128]{2,1,0:T(8,128)}, u32[]{:S(2)}) copy-start(f32[4,128,128]{2,1,0:T(8,128)} %tie_weight.1) | copy-start | bytes 786436
  1.3 12.0 %copy-start.1 = (f32[70,2,128,128]{3,2,1,0:T(8,128)S(1)}, f32[70,2,128,128]{3,2,1,0:T(8,128)}, u32[]{:S(2)}) copy-start(f32[70,2,128,128]{3,2,1,0:T(8,128)} %values.3) | copy-start | bytes 27525124
  3.1 10.9 %collective-permute-start.4 = (f32[2,8960]{1,0:T(2,128)S(1)}, f32[2,8960]{1,0:T(2,128)S(1)}, u32[]{:S(2)}, u32[]{:S(2)}) collective-permute-start(f32[2,8960]{1,0:T(2,128)S(1)} %get-tuple-element.78.after.refs_0_), channel_id=1, source_target_pairs={{0,6},{1,7},{2,4},{3,5},{4,2},{5,3},{6,0},{7,1},{8,14},{9,15},{10,... | collective-permute-start | bytes 215048 | tf_op jit(solution)/shard_map/ppermute | solution.py:126
  8.2 7.5 %collective-permute-start.3 = (f32[2,8960]{1,0:T(2,128)S(1)}, f32[2,8960]{1,0:T(2,128)S(1)}, u32[]{:S(2)}, u32[]{:S(2)}) collective-permute-start(f32[2,8960]{1,0:T(2,128)S(1)} %get-tuple-element.78.after.refs_0_), channel_id=1, source_target_pairs={{0,4},{1,5},{2,6},{3,7},{4,0},{5,1},{6,2},{7,3},{8,12},{9,13},{10,... | collective-permute-start | bytes 215048 | tf_op jit(solution)/shard_map/ppermute | solution.py:126
  8.2 7.5 %collective-permute-start.2 = (f32[2,8960]{1,0:T(2,128)S(1)}, f32[2,8960]{1,0:T(2,128)S(1)}, u32[]{:S(2)}, u32[]{:S(2)}) collective-permute-start(f32[2,8960]{1,0:T(2,128)S(1)} %get-tuple-element.78.after.refs_0_), channel_id=1, source_target_pairs={{0,2},{1,3},{2,0},{3,1},{4,6},{5,7},{6,4},{7,5},{8,10},{9,11},{10,... | collective-permute-start | bytes 215048 | tf_op jit(solution)/shard_map/ppermute | solution.py:126
  8.8 6.8 %collective-permute-start.5 = (f32[4,9216]{1,0:T(4,128)S(1)}, f32[4,9216]{1,0:T(4,128)S(1)}, u32[]{:S(2)}, u32[]{:S(2)}) collective-permute-start(f32[4,9216]{1,0:T(4,128)S(1)} %get-tuple-element.79.refs_4_.refs_6_), channel_id=1, source_target_pairs={{0,1},{1,0},{2,3},{3,2},{4,5},{5,4},{6,7},{7,6},{8,9},{9,8},{10,11... | collective-permute-start | bytes 442376 | tf_op jit(solution)/shard_map/ppermute | solution.py:126
  13.3 8.1 %collective-permute-start.1 = (f32[96,128]{1,0:T(8,128)S(1)}, f32[96,128]{1,0:T(8,128)S(1)}, u32[]{:S(2)}, u32[]{:S(2)}) collective-permute-start(f32[96,128]{1,0:T(8,128)S(1)} %get-tuple-element.72), channel_id=1, source_target_pairs={{0,24},{8,16},{16,8},{24,0},{1,25},{9,17},{17,9},{25,1},{2,26},{10... | collective-permute-start | bytes 147464 | tf_op jit(solution)/shard_map/ppermute | solution.py:186
  14.0 7.4 %collective-permute-start = (f32[96,128]{1,0:T(8,128)S(1)}, f32[96,128]{1,0:T(8,128)S(1)}, u32[]{:S(2)}, u32[]{:S(2)}) collective-permute-start(f32[96,128]{1,0:T(8,128)S(1)} %get-tuple-element.72), channel_id=1, source_target_pairs={{0,8},{8,0},{16,24},{24,16},{1,9},{9,1},{17,25},{25,17},{2,10},{10... | collective-permute-start | bytes 147464 | tf_op jit(solution)/shard_map/ppermute | solution.py:181
  15.7 5.3 %collective-permute-start.7 = (f32[2,8960]{1,0:T(2,128)S(1)}, f32[2,8960]{1,0:T(2,128)S(1)}, u32[]{:S(2)}, u32[]{:S(2)}) collective-permute-start(f32[2,8960]{1,0:T(2,128)S(1)} %get-tuple-element.85.refs_2_), channel_id=1, source_target_pairs={{0,2},{1,3},{2,0},{3,1},{4,6},{5,7},{6,4},{7,5},{8,10},{9,11},{10,... | collective-permute-start | bytes 215048 | tf_op jit(solution)/shard_map/ppermute | solution.py:126
  17.0 4.3 %collective-permute-start.6 = (f32[2,8960]{1,0:T(2,128)S(1)}, f32[2,8960]{1,0:T(2,128)S(1)}, u32[]{:S(2)}, u32[]{:S(2)}) collective-permute-start(f32[2,8960]{1,0:T(2,128)S(1)} %get-tuple-element.81.after.refs_0_), channel_id=1, source_target_pairs={{0,1},{1,0},{2,3},{3,2},{4,5},{5,4},{6,7},{7,6},{8,9},{9,8},{10,11... | collective-permute-start | bytes 215048 | tf_op jit(solution)/shard_map/ppermute | solution.py:126
  21.6 3.6 %collective-permute-start.9 = (f32[96,128]{1,0:T(8,128)S(1)}, f32[96,128]{1,0:T(8,128)S(1)}, u32[]{:S(2)}, u32[]{:S(2)}) collective-permute-start(f32[96,128]{1,0:T(8,128)S(1)} %ties_0.1), channel_id=1, source_target_pairs={{0,24},{8,16},{16,8},{24,0},{1,25},{9,17},{17,9},{25,1},{2,26},{10... | collective-permute-start | bytes 147464 | tf_op jit(solution)/shard_map/ppermute | solution.py:186
  21.7 3.6 %collective-permute-start.8 = (f32[96,128]{1,0:T(8,128)S(1)}, f32[96,128]{1,0:T(8,128)S(1)}, u32[]{:S(2)}, u32[]{:S(2)}) collective-permute-start(f32[96,128]{1,0:T(8,128)S(1)} %ties_0.1), channel_id=1, source_target_pairs={{0,8},{8,0},{16,24},{24,16},{1,9},{9,1},{17,25},{25,17},{2,10},{10... | collective-permute-start | bytes 147464 | tf_op jit(solution)/shard_map/ppermute | solution.py:181
  25.4 3.9 %collective-permute-start.11 = (f32[96,128]{1,0:T(8,128)S(1)}, f32[96,128]{1,0:T(8,128)S(1)}, u32[]{:S(2)}, u32[]{:S(2)}) collective-permute-start(f32[96,128]{1,0:T(8,128)S(1)} %ties_1.1), channel_id=1, source_target_pairs={{0,24},{8,16},{16,8},{24,0},{1,25},{9,17},{17,9},{25,1},{2,26},{10... | collective-permute-start | bytes 147464 | tf_op jit(solution)/shard_map/ppermute | solution.py:186
  26.5 2.8 %collective-permute-start.10 = (f32[96,128]{1,0:T(8,128)S(1)}, f32[96,128]{1,0:T(8,128)S(1)}, u32[]{:S(2)}, u32[]{:S(2)}) collective-permute-start(f32[96,128]{1,0:T(8,128)S(1)} %ties_1.1), channel_id=1, source_target_pairs={{0,8},{8,0},{16,24},{24,16},{1,9},{9,1},{17,25},{25,17},{2,10},{10... | collective-permute-start | bytes 147464 | tf_op jit(solution)/shard_map/ppermute | solution.py:181
  29.6 3.9 %collective-permute-start.13 = (f32[96,128]{1,0:T(8,128)S(1)}, f32[96,128]{1,0:T(8,128)S(1)}, u32[]{:S(2)}, u32[]{:S(2)}) collective-permute-start(f32[96,128]{1,0:T(8,128)S(1)} %ties_2.1), channel_id=1, source_target_pairs={{0,24},{8,16},{16,8},{24,0},{1,25},{9,17},{17,9},{25,1},{2,26},{10... | collective-permute-start | bytes 147464 | tf_op jit(solution)/shard_map/ppermute | solution.py:186
  30.8 2.7 %collective-permute-start.12 = (f32[96,128]{1,0:T(8,128)S(1)}, f32[96,128]{1,0:T(8,128)S(1)}, u32[]{:S(2)}, u32[]{:S(2)}) collective-permute-start(f32[96,128]{1,0:T(8,128)S(1)} %ties_2.1), channel_id=1, source_target_pairs={{0,8},{8,0},{16,24},{24,16},{1,9},{9,1},{17,25},{25,17},{2,10},{10... | collective-permute-start | bytes 147464 | tf_op jit(solution)/shard_map/ppermute | solution.py:181
  33.7 3.8 %collective-permute-start.15 = (f32[96,128]{1,0:T(8,128)S(1)}, f32[96,128]{1,0:T(8,128)S(1)}, u32[]{:S(2)}, u32[]{:S(2)}) collective-permute-start(f32[96,128]{1,0:T(8,128)S(1)} %ties_3.1), channel_id=1, source_target_pairs={{0,24},{8,16},{16,8},{24,0},{1,25},{9,17},{17,9},{25,1},{2,26},{10... | collective-permute-start | bytes 147464 | tf_op jit(solution)/shard_map/ppermute | solution.py:186
  34.8 2.7 %collective-permute-start.14 = (f32[96,128]{1,0:T(8,128)S(1)}, f32[96,128]{1,0:T(8,128)S(1)}, u32[]{:S(2)}, u32[]{:S(2)}) collective-permute-start(f32[96,128]{1,0:T(8,128)S(1)} %ties_3.1), channel_id=1, source_target_pairs={{0,8},{8,0},{16,24},{24,16},{1,9},{9,1},{17,25},{25,17},{2,10},{10... | collective-permute-start | bytes 147464 | tf_op jit(solution)/shard_map/ppermute | solution.py:181
  37.7 4.0 %collective-permute-start.17 = (f32[96,128]{1,0:T(8,128)S(1)}, f32[96,128]{1,0:T(8,128)S(1)}, u32[]{:S(2)}, u32[]{:S(2)}) collective-permute-start(f32[96,128]{1,0:T(8,128)S(1)} %ties_4.1), channel_id=1, source_target_pairs={{0,24},{8,16},{16,8},{24,0},{1,25},{9,17},{17,9},{25,1},{2,26},{10... | collective-permute-start | bytes 147464 | tf_op jit(solution)/shard_map/ppermute | solution.py:186
  38.8 3.0 %collective-permute-start.16 = (f32[96,128]{1,0:T(8,128)S(1)}, f32[96,128]{1,0:T(8,128)S(1)}, u32[]{:S(2)}, u32[]{:S(2)}) collective-permute-start(f32[96,128]{1,0:T(8,128)S(1)} %ties_4.1), channel_id=1, source_target_pairs={{0,8},{8,0},{16,24},{24,16},{1,9},{9,1},{17,25},{25,17},{2,10},{10... | collective-permute-start | bytes 147464 | tf_op jit(solution)/shard_map/ppermute | solution.py:181
  41.9 3.8 %collective-permute-start.19 = (f32[96,128]{1,0:T(8,128)S(1)}, f32[96,128]{1,0:T(8,128)S(1)}, u32[]{:S(2)}, u32[]{:S(2)}) collective-permute-start(f32[96,128]{1,0:T(8,128)S(1)} %ties_5.1), channel_id=1, source_target_pairs={{0,24},{8,16},{16,8},{24,0},{1,25},{9,17},{17,9},{25,1},{2,26},{10... | collective-permute-start | bytes 147464 | tf_op jit(solution)/shard_map/ppermute | solution.py:186
  42.8 3.0 %collective-permute-start.18 = (f32[96,128]{1,0:T(8,128)S(1)}, f32[96,128]{1,0:T(8,128)S(1)}, u32[]{:S(2)}, u32[]{:S(2)}) collective-permute-start(f32[96,128]{1,0:T(8,128)S(1)} %ties_5.1), channel_id=1, source_target_pairs={{0,8},{8,0},{16,24},{24,16},{1,9},{9,1},{17,25},{25,17},{2,10},{10... | collective-permute-start | bytes 147464 | tf_op jit(solution)/shard_map/ppermute | solution.py:181
  45.9 3.8 %collective-permute-start.21 = (f32[96,128]{1,0:T(8,128)S(1)}, f32[96,128]{1,0:T(8,128)S(1)}, u32[]{:S(2)}, u32[]{:S(2)}) collective-permute-start(f32[96,128]{1,0:T(8,128)S(1)} %ties_6.1), channel_id=1, source_target_pairs={{0,24},{8,16},{16,8},{24,0},{1,25},{9,17},{17,9},{25,1},{2,26},{10... | collective-permute-start | bytes 147464 | tf_op jit(solution)/shard_map/ppermute | solution.py:186
  46.8 3.0 %collective-permute-start.20 = (f32[96,128]{1,0:T(8,128)S(1)}, f32[96,128]{1,0:T(8,128)S(1)}, u32[]{:S(2)}, u32[]{:S(2)}) collective-permute-start(f32[96,128]{1,0:T(8,128)S(1)} %ties_6.1), channel_id=1, source_target_pairs={{0,8},{8,0},{16,24},{24,16},{1,9},{9,1},{17,25},{25,17},{2,10},{10... | collective-permute-start | bytes 147464 | tf_op jit(solution)/shard_map/ppermute | solution.py:181
  50.0 11.0 %collective-permute-start.25 = (f32[4,9216]{1,0:T(4,128)S(1)}, f32[4,9216]{1,0:T(4,128)S(1)}, u32[]{:S(2)}, u32[]{:S(2)}) collective-permute-start(f32[4,9216]{1,0:T(4,128)S(1)} %get-tuple-element.125.refs_4_.refs_6_), channel_id=1, source_target_pairs={{0,1},{1,0},{2,3},{3,2},{4,5},{5,4},{6,7},{7,6},{8,9},{9,8},{10,11... | collective-permute-start | bytes 442376 | tf_op jit(solution)/shard_map/ppermute | solution.py:126
  51.2 7.3 %collective-permute-start.24 = (f32[2,8960]{1,0:T(2,128)S(1)}, f32[2,8960]{1,0:T(2,128)S(1)}, u32[]{:S(2)}, u32[]{:S(2)}) collective-permute-start(f32[2,8960]{1,0:T(2,128)S(1)} %get-tuple-element.124.refs_0_), channel_id=1, source_target_pairs={{0,6},{1,7},{2,4},{3,5},{4,2},{5,3},{6,0},{7,1},{8,14},{9,15},{10,... | collective-permute-start | bytes 215048 | tf_op jit(solution)/shard_map/ppermute | solution.py:126
  53.7 7.3 %collective-permute-start.23 = (f32[2,8960]{1,0:T(2,128)S(1)}, f32[2,8960]{1,0:T(2,128)S(1)}, u32[]{:S(2)}, u32[]{:S(2)}) collective-permute-start(f32[2,8960]{1,0:T(2,128)S(1)} %get-tuple-element.124.refs_0_), channel_id=1, source_target_pairs={{0,4},{1,5},{2,6},{3,7},{4,0},{5,1},{6,2},{7,3},{8,12},{9,13},{10,... | collective-permute-start | bytes 215048 | tf_op jit(solution)/shard_map/ppermute | solution.py:126
  54.2 6.8 %collective-permute-start.22 = (f32[2,8960]{1,0:T(2,128)S(1)}, f32[2,8960]{1,0:T(2,128)S(1)}, u32[]{:S(2)}, u32[]{:S(2)}) collective-permute-start(f32[2,8960]{1,0:T(2,128)S(1)} %get-tuple-element.124.refs_0_), channel_id=1, source_target_pairs={{0,2},{1,3},{2,0},{3,1},{4,6},{5,7},{6,4},{7,5},{8,10},{9,11},{10,... | collective-permute-start | bytes 215048 | tf_op jit(solution)/shard_map/ppermute | solution.py:126
  61.1 4.4 %collective-permute-start.26 = (f32[2,8960]{1,0:T(2,128)S(1)}, f32[2,8960]{1,0:T(2,128)S(1)}, u32[]{:S(2)}, u32[]{:S(2)}) collective-permute-start(f32[2,8960]{1,0:T(2,128)S(1)} %get-tuple-element.126.refs_0_), channel_id=1, source_target_pairs={{0,1},{1,0},{2,3},{3,2},{4,5},{5,4},{6,7},{7,6},{8,9},{9,8},{10,11... | collective-permute-start | bytes 215048 | tf_op jit(solution)/shard_map/ppermute | solution.py:126
  62.0 4.3 %collective-permute-start.27 = (f32[2,8960]{1,0:T(2,128)S(1)}, f32[2,8960]{1,0:T(2,128)S(1)}, u32[]{:S(2)}, u32[]{:S(2)}) collective-permute-start(f32[2,8960]{1,0:T(2,128)S(1)} %get-tuple-element.127.refs_2_), channel_id=1, source_target_pairs={{0,2},{1,3},{2,0},{3,1},{4,6},{5,7},{6,4},{7,5},{8,10},{9,11},{10,... | collective-permute-start | bytes 215048 | tf_op jit(solution)/shard_map/ppermute | solution.py:126

commit v7 on v6

--- a/solution.py
+++ b/solution.py
@@ -242,21 +242,11 @@
     return value
 
 
-def first_step(first, count, cols, values, state, parts, constant, weights, new_state, new_parts):
-    for i in range(first, first + count):
-        for j in range(2):
-            high, low = split(values[i, j])
-            weights[i, j * 128 : (j + 1) * 128, 0:128] = high
-            weights[i, j * 128 : (j + 1) * 128, 128:256] = low
-        advance(i, cols[1, i], weights[i], state, parts, constant, new_state, new_parts)
-
-
-def first_step_begin(first, count, cols, values, state, parts, constant, after, *refs):
-    first_step(first, count, cols, values, state, parts, constant, *refs)
-
-
-def first_step_end(first, count, cols, values, state, parts, constant, after, w_in, s_in, p_in, *refs):
-    first_step(first, count, cols, values, state, parts, constant, *refs)
+def first_step_kernel(cols, values, state, parts, constant, after, weights, new_state, new_parts):
+    for i in range(state.shape[0]):
+        weight = jnp.concatenate([jnp.concatenate(split(values[i, j]), axis=1) for j in range(2)], axis=0)
+        weights[i] = weight
+        advance(i, cols[1, i], weight, state, parts, constant, new_state, new_parts)
 
 
 def step_kernel(tie_row, tie_source, cols, bound_count, other, pair, ties, weights, constant, a, b, c, d,
@@ -477,7 +467,6 @@
     parts_shape = VMEM((blocks, 2 * rows, 128), bf16)
 
     weights_shape = VMEM((blocks, 256, 256), bf16)
-    half = blocks // 7
     laid = {}
 
     def prepare(turn, totals, ready):
@@ -491,26 +480,24 @@
                 + [VMEM((tie_count, 256, 256), bf16), VMEM((2, 256, 256), bf16)]
                 + [VMEM((rows, 128), f32), VMEM((rows, 128), f32)],
                 compiler_params=params(2),
-                cost_estimate=cost(10**9, 10**6),
+                cost_estimate=cost(4 * 10**9, 10**6),
                 name="prepare",
             )(in_smem(send), in_smem(row_of_tie), in_smem(source_of_tie), in_smem(labels), in_smem(factors),
               *[in_vmem(a) for a in (start_dispatch, multipliers, demand, tie_weight)])
+            return [in_vmem(laid["start"][0])]
         if turn > 1:
             return []
-        first, count = (0, half) if turn == 0 else (half, blocks - half)
         held = [in_vmem(a) for a in laid["start"][:3]]
-        made = [] if turn == 0 else [in_vmem(a) for a in laid["made"]]
         laid["made"] = pl.pallas_call(
-            functools.partial(first_step_begin if turn == 0 else first_step_end, first, count),
-            in_specs=[smem_spec] + [vmem_spec] * (5 + len(made)),
+            first_step_kernel,
+            in_specs=[smem_spec] + [vmem_spec] * 5,
             out_specs=[vmem_spec] * 3,
             out_shape=[weights_shape, state_shape, parts_shape],
-            input_output_aliases={} if turn == 0 else {6: 0, 7: 1, 8: 2},
             compiler_params=params(2),
             cost_estimate=cost(10**9, 10**6),
-            name=f"step_0_{turn}",
-        )(in_smem(cols), in_vmem(block_values), *held, in_vmem(after), *made)
-        return [in_vmem(laid["made"][1])] if turn == 0 else []
+            name="step_0",
+        )(in_smem(cols), in_vmem(block_values), *held, in_vmem(after))
+        return []
 
     totals = node_totals(sums, shared, per, buses, prepare)
     if len(turns_of(shared)) < 2:
@@ -619,7 +606,7 @@
                     pltpu.SemaphoreType.DMA((2 * pieces,)),
                 ],
                 compiler_params=params(8),
-                cost_estimate=cost(10**9, 10**6),
+                cost_estimate=cost(4 * 10**9, 10**6),
                 name="outputs",
             )(state, in_vmem(multipliers))
             return [in_hbm(written["dispatch"])]

time: 67.6 us -> 66.4 us (0.982)
  Pallas kernels: 32.1 us -> 31.1 us
    pallas_call x2 -> x1, Pallas kernels: 4.03 us -> 3 us  [prepare(): pl.pallas_call(first_step_kernel, in_specs=[smem_spec] + [vmem_spec] * 5,...]
    ppermute x12, waiting for transfers between devices: 6.3 us -> 5.48 us  [swap(): return lax.ppermute(block, axis, [(i, i ^ apart) for i in range(count)])]
    ppermute x8, starting transfers between devices: 6.19 us -> 5.47 us  [from_other(): lax.ppermute(value, axis, [(i, (i + 1 if i % 2 else i - 1) % count) for i...]
    ppermute x12, starting transfers between devices: 15.7 us -> 16.4 us  [swap(): return lax.ppermute(block, axis, [(i, i ^ apart) for i in range(count)])]
  transfers between devices with their start and end apart: 28 -> 28, of which waited for: 6 -> 9; matrix products, arithmetic and copies ran while one was open for 0% -> 0% of each run, Pallas kernels for 41% -> 41%
where the time goes in v7:
time: 66.4 us; the launch traced here: 66.2 us
  Pallas kernels  31.1 us (47%)
  starting transfers between devices  26.9 us (41%)
  waiting for transfers between devices  6.37 us (10%)
  between operations  1.79 us (3%)
    pallas_call x7, Pallas kernels, local(): pl.pallas_call(kernel, in_specs=[smem_spec] * 3 + [vmem_spec] * 9, out_sp...  16.6 us
    ppermute x12, starting transfers between devices, swap(): return lax.ppermute(block, axis, [(i, i ^ apart) for i in range(count)])  16.4 us
    ppermute x12, waiting for transfers between devices, swap(): return lax.ppermute(block, axis, [(i, i ^ apart) for i in range(count)])  5.48 us
    ppermute x8, starting transfers between devices, from_other(): lax.ppermute(value, axis, [(i, (i + 1 if i % 2 else i - 1) % count) for i...  5.47 us
    ppermute x8, starting transfers between devices, from_pair(): return lax.ppermute(value, axis, [(i, i ^ 1) for i in range(count)])  5.04 us
    pallas_call x1, Pallas kernels, prepare(): pl.pallas_call(first_step_kernel, in_specs=[smem_spec] + [vmem_spec] * 5,...  3 us
    pallas_call x1, Pallas kernels, write(): pl.pallas_call(functools.partial(output_kernel, own, scen_all, pieces), i...  2.91 us
    pallas_call x1, Pallas kernels, prepare(): pl.pallas_call(functools.partial(prepare_kernel, shared, per, scen_all),...  2.82 us
  transfers between devices with their start and end apart: 28, of which 9 were waited for; matrix products, arithmetic and copies ran while one was open for 0% of the time, Pallas kernels for 41%

profile of v7, /device:TPU:0, one launch (start us, length us, event | category | flops | bytes accessed | tf_op | source)
XLA Modules:
  0.0 66.2 jit_solution(6020096534873700516)
XLA Ops:
  1.3 1.7 %first_sums.1 = (f32[2,8960]{1,0:T(2,128)S(1)}, f32[4,9216]{1,0:T(4,128)S(1)}, s32[2,70]{1,0:T(2,128)S(4)}, s32[4]{0:T(128)S(4)}, s32[4]{0:T(128)S(4)}, /*index=...) custom-call(s32[1]{0:T(128)S(6)} %copy.85.send, f32[24,4,8960]{2,1,0:T(4,128)} %start.3, s32[2,70]{1,0:T(2,128)} %bitcast.5, ...), custom_call_target="tpu_custom_call" | custom-call | flops 20000000000 | bytes 1000000 | tf_op jit(solution)/shard_map/first_sums/pallas_call | solution.py:450
  3.1 5.1 %collective-permute-start.4 = (f32[2,8960]{1,0:T(2,128)S(1)}, f32[2,8960]{1,0:T(2,128)S(1)}, u32[]{:S(2)}, u32[]{:S(2)}) collective-permute-start(f32[2,8960]{1,0:T(2,128)S(1)} %get-tuple-element.75.refs_0_), channel_id=1, source_target_pairs={{0,6},{1,7},{2,4},{3,5},{4,2},{5,3},{6,0},{7,1},{8,14},{9,15},{10,... | collective-permute-start | bytes 215048 | tf_op jit(solution)/shard_map/ppermute | solution.py:126
  8.2 0.6 collective-permute-start.2
  8.8 1.6 %collective-permute-start.5 = (f32[4,9216]{1,0:T(4,128)S(1)}, f32[4,9216]{1,0:T(4,128)S(1)}, u32[]{:S(2)}, u32[]{:S(2)}) collective-permute-start(f32[4,9216]{1,0:T(4,128)S(1)} %get-tuple-element.76.refs_4_.refs_6_), channel_id=1, source_target_pairs={{0,1},{1,0},{2,3},{3,2},{4,5},{5,4},{6,7},{7,6},{8,9},{9,8},{10,11... | collective-permute-start | bytes 442376 | tf_op jit(solution)/shard_map/ppermute | solution.py:126
  10.5 0.0 slice-start.1
  10.5 2.8 %prepare.1 = (f32[70,96,128]{2,1,0:T(8,128)S(1)}, bf16[70,192,128]{2,1,0:T(8,128)(2,1)S(1)}, f32[70,96,128]{2,1,0:T(8,128)S(1)}, bf16[4,256,256]{2,1,0:T(8,128)(...) custom-call(s32[1]{0:T(128)S(4)} %get-tuple-element.66.send, ...), custom_call_target="tpu_custom_call" | custom-call | flops 4000000000 | bytes 1000000 | tf_op jit(solution)/shard_map/prepare/pallas_call | solution.py:475
  13.3 1.6 %collective-permute-start = (f32[96,128]{1,0:T(8,128)S(1)}, f32[96,128]{1,0:T(8,128)S(1)}, u32[]{:S(2)}, u32[]{:S(2)}) collective-permute-start(f32[96,128]{1,0:T(8,128)S(1)} %get-tuple-element.69), channel_id=1, source_target_pairs={{0,8},{8,0},{16,24},{24,16},{1,9},{9,1},{17,25},{25,17},{2,10},{10... | collective-permute-start | bytes 147464 | tf_op jit(solution)/shard_map/ppermute | solution.py:181
  15.0 0.0 collective-permute-done.3.refs_2_
  15.0 0.0 collective-permute-done.2.refs_1_
  15.0 0.0 collective-permute-done.5.refs_5_.refs_7_
  15.0 0.1 node_add_0.2
  15.1 1.3 %collective-permute-start.7 = (f32[2,8960]{1,0:T(2,128)S(1)}, f32[2,8960]{1,0:T(2,128)S(1)}, u32[]{:S(2)}, u32[]{:S(2)}) collective-permute-start(f32[2,8960]{1,0:T(2,128)S(1)} %get-tuple-element.79.refs_2_), channel_id=1, source_target_pairs={{0,2},{1,3},{2,0},{3,1},{4,6},{5,7},{6,4},{7,5},{8,10},{9,11},{10,... | collective-permute-start | bytes 215048 | tf_op jit(solution)/shard_map/ppermute | solution.py:126
  16.4 0.6 collective-permute-start.6
  17.0 3.0 %step_0.1 = (bf16[70,256,256]{2,1,0:T(8,128)(2,1)S(1)}, f32[70,96,128]{2,1,0:T(8,128)S(1)}, bf16[70,192,128]{2,1,0:T(8,128)(2,1)S(1)}) custom-call(s32[2,70]{1,0:T(2,128)S(4)} %get-tuple-element.71.cols, f32[70,2,128,128]{3,2,1,0:T(8,128)S(1)} %bitcast.3, f32[70,96,128]{2,1,0:T(8,128)S(1)} %get-tuple-element.72.refs_8_.state.refs_7_, ...), custom_call_target="tpu_custom_call" | custom-call | flops 1000000000 | bytes 1000000 | tf_op jit(solution)/shard_map/step_0/pallas_call | solution.py:491
  20.0 0.7 %collective-permute-done.6.refs_1_ = f32[2,8960]{1,0:T(2,128)S(1)} collective-permute-done((f32[2,8960]{1,0:T(2,128)S(1)}, f32[2,8960]{1,0:T(2,128)S(1)}, u32[]{:S(2)}, u32[]{:S(2)}) %collective-permute-start.6) | collective-permute-done | bytes 71712 | tf_op jit(solution)/shard_map/ppermute | solution.py:126
  20.7 0.2 ties_0.1
  20.9 0.1 collective-permute-start.9
  21.0 1.0 %collective-permute-start.8 = (f32[96,128]{1,0:T(8,128)S(1)}, f32[96,128]{1,0:T(8,128)S(1)}, u32[]{:S(2)}, u32[]{:S(2)}) collective-permute-start(f32[96,128]{1,0:T(8,128)S(1)} %ties_0.1), channel_id=1, source_target_pairs={{0,8},{8,0},{16,24},{24,16},{1,9},{9,1},{17,25},{25,17},{2,10},{10... | collective-permute-start | bytes 147464 | tf_op jit(solution)/shard_map/ppermute | solution.py:181
  22.0 0.5 anchor.1
  22.5 2.3 %step_1.1 = (f32[70,96,128]{2,1,0:T(8,128)S(1)}, bf16[70,192,128]{2,1,0:T(8,128)(2,1)S(1)}, f32[70,96,128]{2,1,0:T(8,128)S(1)}, bf16[70,192,128]{2,1,0:T(8,128)(2,1)S(1)}) custom-call(s32[4]{0:T(128)S(4)} %get-tuple-element.64.tie_row, s32[4]{0:T(128)S(4)} %get-tuple-element.65.tie_source, ...), custom_call_target="tpu_custom_call", output_to_operand_aliasing={{0}: (8, {}), {1}: (9, {}), {2}: (10, {}), {3}: (11, {})} | custom-call | flops 1761607680 | bytes 12000000 | tf_op jit(solution)/shard_map/step_1/pallas_call | solution.py:521
  24.8 0.0 collective-permute-done.9.other.refs_0_
  24.8 0.2 ties_1.1
  25.0 0.8 %collective-permute-start.11 = (f32[96,128]{1,0:T(8,128)S(1)}, f32[96,128]{1,0:T(8,128)S(1)}, u32[]{:S(2)}, u32[]{:S(2)}) collective-permute-start(f32[96,128]{1,0:T(8,128)S(1)} %ties_1.1), channel_id=1, source_target_pairs={{0,24},{8,16},{16,8},{24,0},{1,25},{9,17},{17,9},{25,1},{2,26},{10... | collective-permute-start | bytes 147464 | tf_op jit(solution)/shard_map/ppermute | solution.py:186
  25.9 0.5 collective-permute-start.10
  26.4 2.3 %step_2.1 = (f32[70,96,128]{2,1,0:T(8,128)S(1)}, bf16[70,192,128]{2,1,0:T(8,128)(2,1)S(1)}, f32[70,96,128]{2,1,0:T(8,128)S(1)}, bf16[70,192,128]{2,1,0:T(8,128)(2,1)S(1)}) custom-call(s32[4]{0:T(128)S(4)} %get-tuple-element.64.tie_row, s32[4]{0:T(128)S(4)} %get-tuple-element.65.tie_source, ...), custom_call_target="tpu_custom_call", output_to_operand_aliasing={{0}: (8, {}), {1}: (9, {}), {2}: (10, {}), {3}: (11, {})} | custom-call | flops 1761607680 | bytes 12000000 | tf_op jit(solution)/shard_map/step_2/pallas_call | solution.py:521
  28.7 0.2 collective-permute-done.11.other.refs_0_
  29.0 0.2 ties_2.1
  29.1 1.0 %collective-permute-start.13 = (f32[96,128]{1,0:T(8,128)S(1)}, f32[96,128]{1,0:T(8,128)S(1)}, u32[]{:S(2)}, u32[]{:S(2)}) collective-permute-start(f32[96,128]{1,0:T(8,128)S(1)} %ties_2.1), channel_id=1, source_target_pairs={{0,24},{8,16},{16,8},{24,0},{1,25},{9,17},{17,9},{25,1},{2,26},{10... | collective-permute-start | bytes 147464 | tf_op jit(solution)/shard_map/ppermute | solution.py:186
  30.1 0.4 collective-permute-start.12
  30.5 2.3 %step_3.1 = (f32[70,96,128]{2,1,0:T(8,128)S(1)}, bf16[70,192,128]{2,1,0:T(8,128)(2,1)S(1)}, f32[70,96,128]{2,1,0:T(8,128)S(1)}, bf16[70,192,128]{2,1,0:T(8,128)(2,1)S(1)}) custom-call(s32[4]{0:T(128)S(4)} %get-tuple-element.64.tie_row, s32[4]{0:T(128)S(4)} %get-tuple-element.65.tie_source, ...), custom_call_target="tpu_custom_call", output_to_operand_aliasing={{0}: (8, {}), {1}: (9, {}), {2}: (10, {}), {3}: (11, {})} | custom-call | flops 1761607680 | bytes 12000000 | tf_op jit(solution)/shard_map/step_3/pallas_call | solution.py:521
  32.8 0.1 collective-permute-done.13.other.refs_0_
  33.0 0.2 ties_3.1
  33.2 1.0 %collective-permute-start.15 = (f32[96,128]{1,0:T(8,128)S(1)}, f32[96,128]{1,0:T(8,128)S(1)}, u32[]{:S(2)}, u32[]{:S(2)}) collective-permute-start(f32[96,128]{1,0:T(8,128)S(1)} %ties_3.1), channel_id=1, source_target_pairs={{0,24},{8,16},{16,8},{24,0},{1,25},{9,17},{17,9},{25,1},{2,26},{10... | collective-permute-start | bytes 147464 | tf_op jit(solution)/shard_map/ppermute | solution.py:186
  34.1 0.4 collective-permute-start.14
  34.5 2.3 %step_4.1 = (f32[70,96,128]{2,1,0:T(8,128)S(1)}, bf16[70,192,128]{2,1,0:T(8,128)(2,1)S(1)}, f32[70,96,128]{2,1,0:T(8,128)S(1)}, bf16[70,192,128]{2,1,0:T(8,128)(2,1)S(1)}) custom-call(s32[4]{0:T(128)S(4)} %get-tuple-element.64.tie_row, s32[4]{0:T(128)S(4)} %get-tuple-element.65.tie_source, ...), custom_call_target="tpu_custom_call", output_to_operand_aliasing={{0}: (8, {}), {1}: (9, {}), {2}: (10, {}), {3}: (11, {})} | custom-call | flops 1761607680 | bytes 12000000 | tf_op jit(solution)/shard_map/step_4/pallas_call | solution.py:521
  36.8 0.1 collective-permute-done.15.other.refs_0_
  37.0 0.2 ties_4.1
  37.1 1.0 %collective-permute-start.17 = (f32[96,128]{1,0:T(8,128)S(1)}, f32[96,128]{1,0:T(8,128)S(1)}, u32[]{:S(2)}, u32[]{:S(2)}) collective-permute-start(f32[96,128]{1,0:T(8,128)S(1)} %ties_4.1), channel_id=1, source_target_pairs={{0,24},{8,16},{16,8},{24,0},{1,25},{9,17},{17,9},{25,1},{2,26},{10... | collective-permute-start | bytes 147464 | tf_op jit(solution)/shard_map/ppermute | solution.py:186
  38.1 0.4 collective-permute-start.16
  38.5 2.6 %step_5.1 = (f32[70,96,128]{2,1,0:T(8,128)S(1)}, bf16[70,192,128]{2,1,0:T(8,128)(2,1)S(1)}, f32[70,96,128]{2,1,0:T(8,128)S(1)}, bf16[70,192,128]{2,1,0:T(8,128)(2,1)S(1)}) custom-call(s32[4]{0:T(128)S(4)} %get-tuple-element.64.tie_row, s32[4]{0:T(128)S(4)} %get-tuple-element.65.tie_source, ...), custom_call_target="tpu_custom_call", output_to_operand_aliasing={{0}: (8, {}), {1}: (9, {}), {2}: (10, {}), {3}: (11, {})} | custom-call | flops 1761607680 | bytes 12000000 | tf_op jit(solution)/shard_map/step_5/pallas_call | solution.py:521
  41.1 0.2 ties_5.1
  41.3 0.8 %collective-permute-start.19 = (f32[96,128]{1,0:T(8,128)S(1)}, f32[96,128]{1,0:T(8,128)S(1)}, u32[]{:S(2)}, u32[]{:S(2)}) collective-permute-start(f32[96,128]{1,0:T(8,128)S(1)} %ties_5.1), channel_id=1, source_target_pairs={{0,24},{8,16},{16,8},{24,0},{1,25},{9,17},{17,9},{25,1},{2,26},{10... | collective-permute-start | bytes 147464 | tf_op jit(solution)/shard_map/ppermute | solution.py:186
  42.1 0.4 collective-permute-start.18
  42.5 2.3 %step_6.1 = (f32[70,96,128]{2,1,0:T(8,128)S(1)}, bf16[70,192,128]{2,1,0:T(8,128)(2,1)S(1)}, f32[70,96,128]{2,1,0:T(8,128)S(1)}, bf16[70,192,128]{2,1,0:T(8,128)(2,1)S(1)}) custom-call(s32[4]{0:T(128)S(4)} %get-tuple-element.64.tie_row, s32[4]{0:T(128)S(4)} %get-tuple-element.65.tie_source, ...), custom_call_target="tpu_custom_call", output_to_operand_aliasing={{0}: (8, {}), {1}: (9, {}), {2}: (10, {}), {3}: (11, {})} | custom-call | flops 1761607680 | bytes 12000000 | tf_op jit(solution)/shard_map/step_6/pallas_call | solution.py:521
  44.8 0.3 collective-permute-done.19.other.refs_0_
  45.1 0.2 ties_6.1
  45.3 0.8 %collective-permute-start.21 = (f32[96,128]{1,0:T(8,128)S(1)}, f32[96,128]{1,0:T(8,128)S(1)}, u32[]{:S(2)}, u32[]{:S(2)}) collective-permute-start(f32[96,128]{1,0:T(8,128)S(1)} %ties_6.1), channel_id=1, source_target_pairs={{0,24},{8,16},{16,8},{24,0},{1,25},{9,17},{17,9},{25,1},{2,26},{10... | collective-permute-start | bytes 147464 | tf_op jit(solution)/shard_map/ppermute | solution.py:186
  46.1 0.4 collective-permute-start.20
  46.5 2.5 %step_7.1 = (f32[70,96,128]{2,1,0:T(8,128)S(1)}, bf16[70,192,128]{2,1,0:T(8,128)(2,1)S(1)}, f32[70,96,128]{2,1,0:T(8,128)S(1)}, bf16[70,192,128]{2,1,0:T(8,128)(...) custom-call(s32[4]{0:T(128)S(4)} %get-tuple-element.64.tie_row, ...), custom_call_target="tpu_custom_call", output_to_operand_aliasing={{0}: (8, {}), {1}: (9, {}), {2}: (10, {}), {3}: (11, {})} | custom-call | flops 1761607680 | bytes 12000000 | tf_op jit(solution)/shard_map/step_7/pallas_call | solution.py:521
  49.0 0.1 collective-permute-done.21.other
  49.1 0.3 ties_7.1
  49.4 2.5 %collective-permute-start.24 = (f32[2,8960]{1,0:T(2,128)S(1)}, f32[2,8960]{1,0:T(2,128)S(1)}, u32[]{:S(2)}, u32[]{:S(2)}) collective-permute-start(f32[2,8960]{1,0:T(2,128)S(1)} %get-tuple-element.118.refs_0_), channel_id=1, source_target_pairs={{0,6},{1,7},{2,4},{3,5},{4,2},{5,3},{6,0},{7,1},{8,14},{9,15},{10,... | collective-permute-start | bytes 215048 | tf_op jit(solution)/shard_map/ppermute | solution.py:126
  51.9 0.6 collective-permute-start.23
  52.4 1.4 %collective-permute-start.22 = (f32[2,8960]{1,0:T(2,128)S(1)}, f32[2,8960]{1,0:T(2,128)S(1)}, u32[]{:S(2)}, u32[]{:S(2)}) collective-permute-start(f32[2,8960]{1,0:T(2,128)S(1)} %get-tuple-element.118.refs_0_), channel_id=1, source_target_pairs={{0,2},{1,3},{2,0},{3,1},{4,6},{5,7},{6,4},{7,5},{8,10},{9,11},{10,... | collective-permute-start | bytes 215048 | tf_op jit(solution)/shard_map/ppermute | solution.py:126
  53.8 1.1 %collective-permute-start.25 = (f32[4,9216]{1,0:T(4,128)S(1)}, f32[4,9216]{1,0:T(4,128)S(1)}, u32[]{:S(2)}, u32[]{:S(2)}) collective-permute-start(f32[4,9216]{1,0:T(4,128)S(1)} %get-tuple-element.119.refs_4_.refs_6_), channel_id=1, source_target_pairs={{0,1},{1,0},{2,3},{3,2},{4,5},{5,4},{6,7},{7,6},{8,9},{9,8},{10,11... | collective-permute-start | bytes 442376 | tf_op jit(solution)/shard_map/ppermute | solution.py:126
  54.9 2.9 %outputs.1 = (f32[24,4,8960]{2,1,0:T(4,128)}, f32[24,4,8960]{2,1,0:T(4,128)}) custom-call(f32[70,96,128]{2,1,0:T(8,128)S(1)} %get-tuple-element.116.state, f32[24,4,8960]{2,1,0:T(4,128)S(1)} %copy-done), custom_call_target="tpu_custom_call" | custom-call | flops 4000000000 | bytes 1000000 | tf_op jit(solution)/shard_map/outputs/pallas_call | solution.py:598
  57.9 1.6 %collective-permute-done.23.refs_2_ = f32[2,8960]{1,0:T(2,128)S(1)} collective-permute-done((f32[2,8960]{1,0:T(2,128)S(1)}, f32[2,8960]{1,0:T(2,128)S(1)}, u32[]{:S(2)}, u32[]{:S(2)}) %collective-permute-start.23) | collective-permute-done | bytes 71712 | tf_op jit(solution)/shard_map/ppermute | solution.py:126
  59.5 0.1 node_add_0.3
  59.5 1.2 %collective-permute-start.26 = (f32[2,8960]{1,0:T(2,128)S(1)}, f32[2,8960]{1,0:T(2,128)S(1)}, u32[]{:S(2)}, u32[]{:S(2)}) collective-permute-start(f32[2,8960]{1,0:T(2,128)S(1)} %get-tuple-element.120.refs_0_), channel_id=1, source_target_pairs={{0,1},{1,0},{2,3},{3,2},{4,5},{5,4},{6,7},{7,6},{8,9},{9,8},{10,11... | collective-permute-start | bytes 215048 | tf_op jit(solution)/shard_map/ppermute | solution.py:126
  60.8 0.3 collective-permute-start.27
  61.1 0.9 %multipliers_2.1.refs_4_.refs_2_ = f32[24,4,8960]{2,1,0:T(4,128)} custom-call(f32[70,96,128]{2,1,0:T(8,128)S(1)} %get-tuple-element.116.state, f32[24,4,8960]{2,1,0:T(4,128)S(1)} %copy-done, f32[2,8960]{1,0:T(2,128)S(1)} %get-tuple-element.122.refs_0_, f32[24,4,8960]{2,1,0:T(4,128)} %get-tuple-element.123.refs_1_), custom_call_target="tpu_custom_call", output_to_operand_aliasing={{}: (3, {})} | custom-call | flops 1000000000 | bytes 1000000 | tf_op jit(solution)/shard_map/multipliers_2/pallas_call | solution.py:576
  61.9 2.0 %collective-permute-done.26.refs_1_ = f32[2,8960]{1,0:T(2,128)S(1)} collective-permute-done((f32[2,8960]{1,0:T(2,128)S(1)}, f32[2,8960]{1,0:T(2,128)S(1)}, u32[]{:S(2)}, u32[]{:S(2)}) %collective-permute-start.26) | collective-permute-done | bytes 71712 | tf_op jit(solution)/shard_map/ppermute | solution.py:126
  63.9 1.2 %collective-permute-done.27.refs_3_ = f32[2,8960]{1,0:T(2,128)S(1)} collective-permute-done((f32[2,8960]{1,0:T(2,128)S(1)}, f32[2,8960]{1,0:T(2,128)S(1)}, u32[]{:S(2)}, u32[]{:S(2)}) %collective-permute-start.27) | collective-permute-done | bytes 71712 | tf_op jit(solution)/shard_map/ppermute | solution.py:126
  65.1 0.9 %multipliers_0.1 = f32[24,4,8960]{2,1,0:T(4,128)} custom-call(f32[70,96,128]{2,1,0:T(8,128)S(1)} %get-tuple-element.116.state, f32[24,4,8960]{2,1,0:T(4,128)S(1)} %copy-done, f32[2,8960]{1,0:T(2,128)S(1)} %get-tuple-element.124.refs_0_, f32[2,8960]{1,0:T(2,128)S(1)} %get-tuple-element.125.refs_1_, ...), custom_call_target="tpu_custom_call", output_to_operand_aliasing={{}: (4, {})} | custom-call | flops 1000000000 | bytes 1000000 | tf_op jit(solution)/shard_map/multipliers_0/pallas_call | solution.py:576
  (33 shorter events, 0.1 us)
Async XLA Ops:
  1.3 9.2 %copy-start = (f32[24,4,8960]{2,1,0:T(4,128)S(1)}, f32[24,4,8960]{2,1,0:T(4,128)}, u32[]{:S(2)}) copy-start(f32[24,4,8960]{2,1,0:T(4,128)} %mult.7) | copy-start | bytes 10321924
  1.3 9.2 %copy-start.1 = (f32[24,4,8960]{2,1,0:T(4,128)S(1)}, f32[24,4,8960]{2,1,0:T(4,128)}, u32[]{:S(2)}) copy-start(f32[24,4,8960]{2,1,0:T(4,128)} %start.3) | copy-start | bytes 10321924
  1.3 9.2 %copy-start.2 = (f32[24,8960]{1,0:T(8,128)S(1)}, f32[24,8960]{1,0:T(8,128)}, u32[]{:S(2)}) copy-start(f32[24,8960]{1,0:T(8,128)} %demand.1) | copy-start | bytes 2580484
  1.3 9.2 %copy-start.3 = (f32[4,128,128]{2,1,0:T(8,128)S(1)}, f32[4,128,128]{2,1,0:T(8,128)}, u32[]{:S(2)}) copy-start(f32[4,128,128]{2,1,0:T(8,128)} %tie_weight.1) | copy-start | bytes 786436
  3.1 10.3 %collective-permute-start.4 = (f32[2,8960]{1,0:T(2,128)S(1)}, f32[2,8960]{1,0:T(2,128)S(1)}, u32[]{:S(2)}, u32[]{:S(2)}) collective-permute-start(f32[2,8960]{1,0:T(2,128)S(1)} %get-tuple-element.75.refs_0_), channel_id=1, source_target_pairs={{0,6},{1,7},{2,4},{3,5},{4,2},{5,3},{6,0},{7,1},{8,14},{9,15},{10,... | collective-permute-start | bytes 215048 | tf_op jit(solution)/shard_map/ppermute | solution.py:126
  8.2 6.8 %collective-permute-start.3 = (f32[2,8960]{1,0:T(2,128)S(1)}, f32[2,8960]{1,0:T(2,128)S(1)}, u32[]{:S(2)}, u32[]{:S(2)}) collective-permute-start(f32[2,8960]{1,0:T(2,128)S(1)} %get-tuple-element.75.refs_0_), channel_id=1, source_target_pairs={{0,4},{1,5},{2,6},{3,7},{4,0},{5,1},{6,2},{7,3},{8,12},{9,13},{10,... | collective-permute-start | bytes 215048 | tf_op jit(solution)/shard_map/ppermute | solution.py:126
  8.2 6.8 %collective-permute-start.2 = (f32[2,8960]{1,0:T(2,128)S(1)}, f32[2,8960]{1,0:T(2,128)S(1)}, u32[]{:S(2)}, u32[]{:S(2)}) collective-permute-start(f32[2,8960]{1,0:T(2,128)S(1)} %get-tuple-element.75.refs_0_), channel_id=1, source_target_pairs={{0,2},{1,3},{2,0},{3,1},{4,6},{5,7},{6,4},{7,5},{8,10},{9,11},{10,... | collective-permute-start | bytes 215048 | tf_op jit(solution)/shard_map/ppermute | solution.py:126
  8.8 6.2 %collective-permute-start.5 = (f32[4,9216]{1,0:T(4,128)S(1)}, f32[4,9216]{1,0:T(4,128)S(1)}, u32[]{:S(2)}, u32[]{:S(2)}) collective-permute-start(f32[4,9216]{1,0:T(4,128)S(1)} %get-tuple-element.76.refs_4_.refs_6_), channel_id=1, source_target_pairs={{0,1},{1,0},{2,3},{3,2},{4,5},{5,4},{6,7},{7,6},{8,9},{9,8},{10,11... | collective-permute-start | bytes 442376 | tf_op jit(solution)/shard_map/ppermute | solution.py:126
  10.5 6.5 %slice-start = ((s8[9175040]{0:T(1024)(128)(4,1)}), s8[4194304]{0:T(1024)(128)(4,1)S(1)}, s32[]{:S(2)}) async-start(s8[9175040]{0:T(1024)(128)(4,1)} %bitcast.2), calls=%async_computation | async-start | bytes 8388608
  10.5 6.5 %slice-start.1 = ((s8[9175040]{0:T(1024)(128)(4,1)}), s8[4194304]{0:T(1024)(128)(4,1)S(1)}, s32[]{:S(2)}) async-start(s8[9175040]{0:T(1024)(128)(4,1)} %bitcast.2), calls=%async_computation.1 | async-start | bytes 8388608
  10.5 6.5 %slice-start.2 = ((s8[9175040]{0:T(1024)(128)(4,1)}), s8[786432]{0:T(1024)(128)(4,1)S(1)}, s32[]{:S(2)}) async-start(s8[9175040]{0:T(1024)(128)(4,1)} %bitcast.2), calls=%async_computation.2 | async-start | bytes 1572864
  13.3 7.4 %collective-permute-start.1 = (f32[96,128]{1,0:T(8,128)S(1)}, f32[96,128]{1,0:T(8,128)S(1)}, u32[]{:S(2)}, u32[]{:S(2)}) collective-permute-start(f32[96,128]{1,0:T(8,128)S(1)} %get-tuple-element.69), channel_id=1, source_target_pairs={{0,24},{8,16},{16,8},{24,0},{1,25},{9,17},{17,9},{25,1},{2,26},{10... | collective-permute-start | bytes 147464 | tf_op jit(solution)/shard_map/ppermute | solution.py:186
  13.3 7.4 %collective-permute-start = (f32[96,128]{1,0:T(8,128)S(1)}, f32[96,128]{1,0:T(8,128)S(1)}, u32[]{:S(2)}, u32[]{:S(2)}) collective-permute-start(f32[96,128]{1,0:T(8,128)S(1)} %get-tuple-element.69), channel_id=1, source_target_pairs={{0,8},{8,0},{16,24},{24,16},{1,9},{9,1},{17,25},{25,17},{2,10},{10... | collective-permute-start | bytes 147464 | tf_op jit(solution)/shard_map/ppermute | solution.py:181
  15.1 4.9 %collective-permute-start.7 = (f32[2,8960]{1,0:T(2,128)S(1)}, f32[2,8960]{1,0:T(2,128)S(1)}, u32[]{:S(2)}, u32[]{:S(2)}) collective-permute-start(f32[2,8960]{1,0:T(2,128)S(1)} %get-tuple-element.79.refs_2_), channel_id=1, source_target_pairs={{0,2},{1,3},{2,0},{3,1},{4,6},{5,7},{6,4},{7,5},{8,10},{9,11},{10,... | collective-permute-start | bytes 215048 | tf_op jit(solution)/shard_map/ppermute | solution.py:126
  16.4 4.3 %collective-permute-start.6 = (f32[2,8960]{1,0:T(2,128)S(1)}, f32[2,8960]{1,0:T(2,128)S(1)}, u32[]{:S(2)}, u32[]{:S(2)}) collective-permute-start(f32[2,8960]{1,0:T(2,128)S(1)} %get-tuple-element.77.after.refs_0_), channel_id=1, source_target_pairs={{0,1},{1,0},{2,3},{3,2},{4,5},{5,4},{6,7},{7,6},{8,9},{9,8},{10,11... | collective-permute-start | bytes 215048 | tf_op jit(solution)/shard_map/ppermute | solution.py:126
  20.9 3.9 %collective-permute-start.9 = (f32[96,128]{1,0:T(8,128)S(1)}, f32[96,128]{1,0:T(8,128)S(1)}, u32[]{:S(2)}, u32[]{:S(2)}) collective-permute-start(f32[96,128]{1,0:T(8,128)S(1)} %ties_0.1), channel_id=1, source_target_pairs={{0,24},{8,16},{16,8},{24,0},{1,25},{9,17},{17,9},{25,1},{2,26},{10... | collective-permute-start | bytes 147464 | tf_op jit(solution)/shard_map/ppermute | solution.py:186
  21.0 3.8 %collective-permute-start.8 = (f32[96,128]{1,0:T(8,128)S(1)}, f32[96,128]{1,0:T(8,128)S(1)}, u32[]{:S(2)}, u32[]{:S(2)}) collective-permute-start(f32[96,128]{1,0:T(8,128)S(1)} %ties_0.1), channel_id=1, source_target_pairs={{0,8},{8,0},{16,24},{24,16},{1,9},{9,1},{17,25},{25,17},{2,10},{10... | collective-permute-start | bytes 147464 | tf_op jit(solution)/shard_map/ppermute | solution.py:181
  25.0 3.9 %collective-permute-start.11 = (f32[96,128]{1,0:T(8,128)S(1)}, f32[96,128]{1,0:T(8,128)S(1)}, u32[]{:S(2)}, u32[]{:S(2)}) collective-permute-start(f32[96,128]{1,0:T(8,128)S(1)} %ties_1.1), channel_id=1, source_target_pairs={{0,24},{8,16},{16,8},{24,0},{1,25},{9,17},{17,9},{25,1},{2,26},{10... | collective-permute-start | bytes 147464 | tf_op jit(solution)/shard_map/ppermute | solution.py:186
  25.9 3.1 %collective-permute-start.10 = (f32[96,128]{1,0:T(8,128)S(1)}, f32[96,128]{1,0:T(8,128)S(1)}, u32[]{:S(2)}, u32[]{:S(2)}) collective-permute-start(f32[96,128]{1,0:T(8,128)S(1)} %ties_1.1), channel_id=1, source_target_pairs={{0,8},{8,0},{16,24},{24,16},{1,9},{9,1},{17,25},{25,17},{2,10},{10... | collective-permute-start | bytes 147464 | tf_op jit(solution)/shard_map/ppermute | solution.py:181
  29.1 3.8 %collective-permute-start.13 = (f32[96,128]{1,0:T(8,128)S(1)}, f32[96,128]{1,0:T(8,128)S(1)}, u32[]{:S(2)}, u32[]{:S(2)}) collective-permute-start(f32[96,128]{1,0:T(8,128)S(1)} %ties_2.1), channel_id=1, source_target_pairs={{0,24},{8,16},{16,8},{24,0},{1,25},{9,17},{17,9},{25,1},{2,26},{10... | collective-permute-start | bytes 147464 | tf_op jit(solution)/shard_map/ppermute | solution.py:186
  30.1 2.9 %collective-permute-start.12 = (f32[96,128]{1,0:T(8,128)S(1)}, f32[96,128]{1,0:T(8,128)S(1)}, u32[]{:S(2)}, u32[]{:S(2)}) collective-permute-start(f32[96,128]{1,0:T(8,128)S(1)} %ties_2.1), channel_id=1, source_target_pairs={{0,8},{8,0},{16,24},{24,16},{1,9},{9,1},{17,25},{25,17},{2,10},{10... | collective-permute-start | bytes 147464 | tf_op jit(solution)/shard_map/ppermute | solution.py:181
  33.2 3.8 %collective-permute-start.15 = (f32[96,128]{1,0:T(8,128)S(1)}, f32[96,128]{1,0:T(8,128)S(1)}, u32[]{:S(2)}, u32[]{:S(2)}) collective-permute-start(f32[96,128]{1,0:T(8,128)S(1)} %ties_3.1), channel_id=1, source_target_pairs={{0,24},{8,16},{16,8},{24,0},{1,25},{9,17},{17,9},{25,1},{2,26},{10... | collective-permute-start | bytes 147464 | tf_op jit(solution)/shard_map/ppermute | solution.py:186
  34.1 2.8 %collective-permute-start.14 = (f32[96,128]{1,0:T(8,128)S(1)}, f32[96,128]{1,0:T(8,128)S(1)}, u32[]{:S(2)}, u32[]{:S(2)}) collective-permute-start(f32[96,128]{1,0:T(8,128)S(1)} %ties_3.1), channel_id=1, source_target_pairs={{0,8},{8,0},{16,24},{24,16},{1,9},{9,1},{17,25},{25,17},{2,10},{10... | collective-permute-start | bytes 147464 | tf_op jit(solution)/shard_map/ppermute | solution.py:181
  37.1 3.9 %collective-permute-start.17 = (f32[96,128]{1,0:T(8,128)S(1)}, f32[96,128]{1,0:T(8,128)S(1)}, u32[]{:S(2)}, u32[]{:S(2)}) collective-permute-start(f32[96,128]{1,0:T(8,128)S(1)} %ties_4.1), channel_id=1, source_target_pairs={{0,24},{8,16},{16,8},{24,0},{1,25},{9,17},{17,9},{25,1},{2,26},{10... | collective-permute-start | bytes 147464 | tf_op jit(solution)/shard_map/ppermute | solution.py:186
  38.1 3.0 %collective-permute-start.16 = (f32[96,128]{1,0:T(8,128)S(1)}, f32[96,128]{1,0:T(8,128)S(1)}, u32[]{:S(2)}, u32[]{:S(2)}) collective-permute-start(f32[96,128]{1,0:T(8,128)S(1)} %ties_4.1), channel_id=1, source_target_pairs={{0,8},{8,0},{16,24},{24,16},{1,9},{9,1},{17,25},{25,17},{2,10},{10... | collective-permute-start | bytes 147464 | tf_op jit(solution)/shard_map/ppermute | solution.py:181
  41.3 3.8 %collective-permute-start.19 = (f32[96,128]{1,0:T(8,128)S(1)}, f32[96,128]{1,0:T(8,128)S(1)}, u32[]{:S(2)}, u32[]{:S(2)}) collective-permute-start(f32[96,128]{1,0:T(8,128)S(1)} %ties_5.1), channel_id=1, source_target_pairs={{0,24},{8,16},{16,8},{24,0},{1,25},{9,17},{17,9},{25,1},{2,26},{10... | collective-permute-start | bytes 147464 | tf_op jit(solution)/shard_map/ppermute | solution.py:186
  42.1 3.0 %collective-permute-start.18 = (f32[96,128]{1,0:T(8,128)S(1)}, f32[96,128]{1,0:T(8,128)S(1)}, u32[]{:S(2)}, u32[]{:S(2)}) collective-permute-start(f32[96,128]{1,0:T(8,128)S(1)} %ties_5.1), channel_id=1, source_target_pairs={{0,8},{8,0},{16,24},{24,16},{1,9},{9,1},{17,25},{25,17},{2,10},{10... | collective-permute-start | bytes 147464 | tf_op jit(solution)/shard_map/ppermute | solution.py:181
  45.3 3.8 %collective-permute-start.21 = (f32[96,128]{1,0:T(8,128)S(1)}, f32[96,128]{1,0:T(8,128)S(1)}, u32[]{:S(2)}, u32[]{:S(2)}) collective-permute-start(f32[96,128]{1,0:T(8,128)S(1)} %ties_6.1), channel_id=1, source_target_pairs={{0,24},{8,16},{16,8},{24,0},{1,25},{9,17},{17,9},{25,1},{2,26},{10... | collective-permute-start | bytes 147464 | tf_op jit(solution)/shard_map/ppermute | solution.py:186
  46.1 3.0 %collective-permute-start.20 = (f32[96,128]{1,0:T(8,128)S(1)}, f32[96,128]{1,0:T(8,128)S(1)}, u32[]{:S(2)}, u32[]{:S(2)}) collective-permute-start(f32[96,128]{1,0:T(8,128)S(1)} %ties_6.1), channel_id=1, source_target_pairs={{0,8},{8,0},{16,24},{24,16},{1,9},{9,1},{17,25},{25,17},{2,10},{10... | collective-permute-start | bytes 147464 | tf_op jit(solution)/shard_map/ppermute | solution.py:181
  49.4 8.5 %collective-permute-start.24 = (f32[2,8960]{1,0:T(2,128)S(1)}, f32[2,8960]{1,0:T(2,128)S(1)}, u32[]{:S(2)}, u32[]{:S(2)}) collective-permute-start(f32[2,8960]{1,0:T(2,128)S(1)} %get-tuple-element.118.refs_0_), channel_id=1, source_target_pairs={{0,6},{1,7},{2,4},{3,5},{4,2},{5,3},{6,0},{7,1},{8,14},{9,15},{10,... | collective-permute-start | bytes 215048 | tf_op jit(solution)/shard_map/ppermute | solution.py:126
  51.9 7.6 %collective-permute-start.23 = (f32[2,8960]{1,0:T(2,128)S(1)}, f32[2,8960]{1,0:T(2,128)S(1)}, u32[]{:S(2)}, u32[]{:S(2)}) collective-permute-start(f32[2,8960]{1,0:T(2,128)S(1)} %get-tuple-element.118.refs_0_), channel_id=1, source_target_pairs={{0,4},{1,5},{2,6},{3,7},{4,0},{5,1},{6,2},{7,3},{8,12},{9,13},{10,... | collective-permute-start | bytes 215048 | tf_op jit(solution)/shard_map/ppermute | solution.py:126
  52.4 7.1 %collective-permute-start.22 = (f32[2,8960]{1,0:T(2,128)S(1)}, f32[2,8960]{1,0:T(2,128)S(1)}, u32[]{:S(2)}, u32[]{:S(2)}) collective-permute-start(f32[2,8960]{1,0:T(2,128)S(1)} %get-tuple-element.118.refs_0_), channel_id=1, source_target_pairs={{0,2},{1,3},{2,0},{3,1},{4,6},{5,7},{6,4},{7,5},{8,10},{9,11},{10,... | collective-permute-start | bytes 215048 | tf_op jit(solution)/shard_map/ppermute | solution.py:126
  53.8 5.7 %collective-permute-start.25 = (f32[4,9216]{1,0:T(4,128)S(1)}, f32[4,9216]{1,0:T(4,128)S(1)}, u32[]{:S(2)}, u32[]{:S(2)}) collective-permute-start(f32[4,9216]{1,0:T(4,128)S(1)} %get-tuple-element.119.refs_4_.refs_6_), channel_id=1, source_target_pairs={{0,1},{1,0},{2,3},{3,2},{4,5},{5,4},{6,7},{7,6},{8,9},{9,8},{10,11... | collective-permute-start | bytes 442376 | tf_op jit(solution)/shard_map/ppermute | solution.py:126
  59.5 4.4 %collective-permute-start.26 = (f32[2,8960]{1,0:T(2,128)S(1)}, f32[2,8960]{1,0:T(2,128)S(1)}, u32[]{:S(2)}, u32[]{:S(2)}) collective-permute-start(f32[2,8960]{1,0:T(2,128)S(1)} %get-tuple-element.120.refs_0_), channel_id=1, source_target_pairs={{0,1},{1,0},{2,3},{3,2},{4,5},{5,4},{6,7},{7,6},{8,9},{9,8},{10,11... | collective-permute-start | bytes 215048 | tf_op jit(solution)/shard_map/ppermute | solution.py:126
  60.8 4.3 %collective-permute-start.27 = (f32[2,8960]{1,0:T(2,128)S(1)}, f32[2,8960]{1,0:T(2,128)S(1)}, u32[]{:S(2)}, u32[]{:S(2)}) collective-permute-start(f32[2,8960]{1,0:T(2,128)S(1)} %get-tuple-element.121.refs_2_), channel_id=1, source_target_pairs={{0,2},{1,3},{2,0},{3,1},{4,6},{5,7},{6,4},{7,5},{8,10},{9,11},{10,... | collective-permute-start | bytes 215048 | tf_op jit(solution)/shard_map/ppermute | solution.py:126

commit v8 on v7

--- a/solution.py
+++ b/solution.py
@@ -51,7 +51,7 @@
 
 def store_split(ref, index, value):
     rows = value.shape[0]
-    high, low = split(value * -step_size)
+    high, low = split(value)
     ref[index, 0:rows] = high
     ref[index, rows : 2 * rows] = low
 
@@ -244,7 +244,7 @@
 
 def first_step_kernel(cols, values, state, parts, constant, after, weights, new_state, new_parts):
     for i in range(state.shape[0]):
-        weight = jnp.concatenate([jnp.concatenate(split(values[i, j]), axis=1) for j in range(2)], axis=0)
+        weight = jnp.concatenate([jnp.concatenate(split(values[i, j] * -step_size), axis=1) for j in range(2)], axis=0)
         weights[i] = weight
         advance(i, cols[1, i], weight, state, parts, constant, new_state, new_parts)
 
@@ -344,7 +344,7 @@
             mean = anchor_piece(k, scen_all, scenarios, totals[k], i)
             constant[i, cut] = constant[i, cut] + mean
             state[i, cut] = state[i, cut] + mean
-        high_part, low_part = split(state[i, 0:span] * -step_size)
+        high_part, low_part = split(state[i, 0:span])
         parts[i, 0:span] = high_part
         parts[i, rows : rows + span] = low_part
         return carry
@@ -527,7 +527,7 @@
                 scratch_shapes=[left_shape],
                 compiler_params=params(2),
                 cost_estimate=cost(blocks * 2 * rows * 256 * 256 * 2, 12 * 10**6),
-                name=f"step_{iteration}",
+                name="last_step" if last else "step",
             )(*tie_scalars, in_smem(cols), *[in_vmem(a) for a in previous],
               *[in_vmem(a) for a in (ties, weights, constant, state, parts, spare_state, spare_parts)])
             spare_state, spare_parts, state, parts = made[:4]
@@ -541,7 +541,7 @@
                 out_specs=[vmem_spec],
                 out_shape=[VMEM((rows, 128), f32)],
                 compiler_params=params(2),
-                name=f"ties_{iteration}",
+                name="first_ties" if iteration == 0 else "ties",
             )(in_smem(send), *arrived, in_vmem(loops), in_vmem(state), *nodes)
             if iteration == 0:
                 state, parts, constant = pl.pallas_call(
@@ -563,7 +563,7 @@
                 input_output_aliases={5 + k: k for k in range(1 + len(sum_shapes))},
                 scratch_shapes=[left_shape],
                 compiler_params=params(2),
-                name=f"ties_{iteration}",
+                name="last_ties",
             )(*tie_scalars, *arrived, in_vmem(ties), in_vmem(state), *[in_vmem(a) for a in sums])
             state, sums = made[0], list(made[1:])
 

time: 66.4 us -> 66.4 us (level)
  starting transfers between devices: 26.9 us -> 24.6 us
  waiting for transfers between devices: 6.37 us -> 8.34 us
    ppermute x8, starting transfers between devices: 5.47 us -> 3.14 us  [from_other(): lax.ppermute(value, axis, [(i, (i + 1 if i % 2 else i - 1) % count) for i...]
    ppermute x8, waiting for transfers between devices: 0.87 us -> 3.12 us  [from_other(): lax.ppermute(value, axis, [(i, (i + 1 if i % 2 else i - 1) % count) for i...]
    ppermute x8, starting transfers between devices: 5.04 us -> 5.79 us  [from_pair(): return lax.ppermute(value, axis, [(i, i ^ 1) for i in range(count)])]
    ppermute x12, starting transfers between devices: 16.4 us -> 15.7 us  [swap(): return lax.ppermute(block, axis, [(i, i ^ apart) for i in range(count)])]
where the time goes in v8:
time: 66.4 us; the launch traced here: 66.2 us
  Pallas kernels  31.5 us (47%)
  starting transfers between devices  24.6 us (37%)
  waiting for transfers between devices  8.34 us (13%)
  between operations  1.79 us (3%)
    pallas_call x7, Pallas kernels, local(): pl.pallas_call(kernel, in_specs=[smem_spec] * 3 + [vmem_spec] * 9, out_sp...  16.5 us
    ppermute x12, starting transfers between devices, swap(): return lax.ppermute(block, axis, [(i, i ^ apart) for i in range(count)])  15.7 us
    ppermute x8, starting transfers between devices, from_pair(): return lax.ppermute(value, axis, [(i, i ^ 1) for i in range(count)])  5.79 us
    ppermute x12, waiting for transfers between devices, swap(): return lax.ppermute(block, axis, [(i, i ^ apart) for i in range(count)])  5.2 us
    pallas_call x1, Pallas kernels, prepare(): pl.pallas_call(first_step_kernel, in_specs=[smem_spec] + [vmem_spec] * 5,...  3.57 us
    ppermute x8, starting transfers between devices, from_other(): lax.ppermute(value, axis, [(i, (i + 1 if i % 2 else i - 1) % count) for i...  3.14 us
    ppermute x8, waiting for transfers between devices, from_other(): lax.ppermute(value, axis, [(i, (i + 1 if i % 2 else i - 1) % count) for i...  3.12 us
    pallas_call x1, Pallas kernels, write(): pl.pallas_call(functools.partial(output_kernel, own, scen_all, pieces), i...  2.91 us
  transfers between devices with their start and end apart: 28, of which 9 were waited for; matrix products, arithmetic and copies ran while one was open for 0% of the time, Pallas kernels for 41%

profile of v8, /device:TPU:0, one launch (start us, length us, event | category | flops | bytes accessed | tf_op | source)
XLA Modules:
  0.0 66.2 jit_solution(4031471683669872314)
XLA Ops:
  1.3 1.7 %first_sums.1 = (f32[2,8960]{1,0:T(2,128)S(1)}, f32[4,9216]{1,0:T(4,128)S(1)}, s32[2,70]{1,0:T(2,128)S(4)}, s32[4]{0:T(128)S(4)}, s32[4]{0:T(128)S(4)}, /*index=...) custom-call(s32[1]{0:T(128)S(6)} %copy.85.send, f32[24,4,8960]{2,1,0:T(4,128)} %start.3, s32[2,70]{1,0:T(2,128)} %bitcast.5, ...), custom_call_target="tpu_custom_call" | custom-call | flops 20000000000 | bytes 1000000 | tf_op jit(solution)/shard_map/first_sums/pallas_call | solution.py:450
  3.1 5.1 %collective-permute-start.4 = (f32[2,8960]{1,0:T(2,128)S(1)}, f32[2,8960]{1,0:T(2,128)S(1)}, u32[]{:S(2)}, u32[]{:S(2)}) collective-permute-start(f32[2,8960]{1,0:T(2,128)S(1)} %get-tuple-element.75.refs_0_), channel_id=1, source_target_pairs={{0,6},{1,7},{2,4},{3,5},{4,2},{5,3},{6,0},{7,1},{8,14},{9,15},{10,... | collective-permute-start | bytes 215048 | tf_op jit(solution)/shard_map/ppermute | solution.py:126
  8.2 0.6 collective-permute-start.2
  8.8 1.6 %collective-permute-start.5 = (f32[4,9216]{1,0:T(4,128)S(1)}, f32[4,9216]{1,0:T(4,128)S(1)}, u32[]{:S(2)}, u32[]{:S(2)}) collective-permute-start(f32[4,9216]{1,0:T(4,128)S(1)} %get-tuple-element.76.refs_4_.refs_6_), channel_id=1, source_target_pairs={{0,1},{1,0},{2,3},{3,2},{4,5},{5,4},{6,7},{7,6},{8,9},{9,8},{10,11... | collective-permute-start | bytes 442376 | tf_op jit(solution)/shard_map/ppermute | solution.py:126
  10.5 0.0 slice-start.1
  10.5 2.7 %prepare.1 = (f32[70,96,128]{2,1,0:T(8,128)S(1)}, bf16[70,192,128]{2,1,0:T(8,128)(2,1)S(1)}, f32[70,96,128]{2,1,0:T(8,128)S(1)}, bf16[4,256,256]{2,1,0:T(8,128)(...) custom-call(s32[1]{0:T(128)S(4)} %get-tuple-element.66.send, ...), custom_call_target="tpu_custom_call" | custom-call | flops 4000000000 | bytes 1000000 | tf_op jit(solution)/shard_map/prepare/pallas_call | solution.py:475
  13.2 0.0 collective-permute-start.1
  13.2 0.0 collective-permute-done.4.refs_3_
  13.2 1.6 %collective-permute-start = (f32[96,128]{1,0:T(8,128)S(1)}, f32[96,128]{1,0:T(8,128)S(1)}, u32[]{:S(2)}, u32[]{:S(2)}) collective-permute-start(f32[96,128]{1,0:T(8,128)S(1)} %get-tuple-element.69), channel_id=1, source_target_pairs={{0,8},{8,0},{16,24},{24,16},{1,9},{9,1},{17,25},{25,17},{2,10},{10... | collective-permute-start | bytes 147464 | tf_op jit(solution)/shard_map/ppermute | solution.py:181
  14.9 0.1 node_add_0.2
  15.0 1.3 %collective-permute-start.7 = (f32[2,8960]{1,0:T(2,128)S(1)}, f32[2,8960]{1,0:T(2,128)S(1)}, u32[]{:S(2)}, u32[]{:S(2)}) collective-permute-start(f32[2,8960]{1,0:T(2,128)S(1)} %get-tuple-element.79.refs_2_), channel_id=1, source_target_pairs={{0,2},{1,3},{2,0},{3,1},{4,6},{5,7},{6,4},{7,5},{8,10},{9,11},{10,... | collective-permute-start | bytes 215048 | tf_op jit(solution)/shard_map/ppermute | solution.py:126
  16.3 0.7 %collective-permute-start.6 = (f32[2,8960]{1,0:T(2,128)S(1)}, f32[2,8960]{1,0:T(2,128)S(1)}, u32[]{:S(2)}, u32[]{:S(2)}) collective-permute-start(f32[2,8960]{1,0:T(2,128)S(1)} %get-tuple-element.77.after.refs_0_), channel_id=1, source_target_pairs={{0,1},{1,0},{2,3},{3,2},{4,5},{5,4},{6,7},{7,6},{8,9},{9,8},{10,11... | collective-permute-start | bytes 215048 | tf_op jit(solution)/shard_map/ppermute | solution.py:126
  17.0 3.6 %step_0.1 = (bf16[70,256,256]{2,1,0:T(8,128)(2,1)S(1)}, f32[70,96,128]{2,1,0:T(8,128)S(1)}, bf16[70,192,128]{2,1,0:T(8,128)(2,1)S(1)}) custom-call(s32[2,70]{1,0:T(2,128)S(4)} %get-tuple-element.71.cols, f32[70,2,128,128]{3,2,1,0:T(8,128)S(1)} %bitcast.3, f32[70,96,128]{2,1,0:T(8,128)S(1)} %get-tuple-element.72.refs_8_.state.refs_7_, ...), custom_call_target="tpu_custom_call" | custom-call | flops 1000000000 | bytes 1000000 | tf_op jit(solution)/shard_map/step_0/pallas_call | solution.py:491
  20.6 0.0 collective-permute-done.7.refs_3_
  20.6 0.0 collective-permute-done.6.refs_1_
  20.6 0.2 first_ties.1
  20.8 0.1 collective-permute-start.9
  20.9 1.6 %collective-permute-start.8 = (f32[96,128]{1,0:T(8,128)S(1)}, f32[96,128]{1,0:T(8,128)S(1)}, u32[]{:S(2)}, u32[]{:S(2)}) collective-permute-start(f32[96,128]{1,0:T(8,128)S(1)} %first_ties.1), channel_id=1, source_target_pairs={{0,8},{8,0},{16,24},{24,16},{1,9},{9,1},{17,25},{25,17},{2,10},{10... | collective-permute-start | bytes 147464 | tf_op jit(solution)/shard_map/ppermute | solution.py:181
  22.5 0.5 anchor.1
  23.0 2.3 %step.6 = (f32[70,96,128]{2,1,0:T(8,128)S(1)}, bf16[70,192,128]{2,1,0:T(8,128)(2,1)S(1)}, f32[70,96,128]{2,1,0:T(8,128)S(1)}, bf16[70,192,128]{2,1,0:T(8,128)(2,1)S(1)}) custom-call(s32[4]{0:T(128)S(4)} %get-tuple-element.64.tie_row, s32[4]{0:T(128)S(4)} %get-tuple-element.65.tie_source, ...), custom_call_target="tpu_custom_call", output_to_operand_aliasing={{0}: (8, {}), {1}: (9, {}), {2}: (10, {}), {3}: (11, {})} | custom-call | flops 1761607680 | bytes 12000000 | tf_op jit(solution)/shard_map/step/pallas_call | solution.py:521
  25.4 0.2 ties.6
  25.6 0.2 collective-permute-start.11
  25.7 0.6 collective-permute-start.10
  26.3 2.3 %step.7 = (f32[70,96,128]{2,1,0:T(8,128)S(1)}, bf16[70,192,128]{2,1,0:T(8,128)(2,1)S(1)}, f32[70,96,128]{2,1,0:T(8,128)S(1)}, bf16[70,192,128]{2,1,0:T(8,128)(2,1)S(1)}) custom-call(s32[4]{0:T(128)S(4)} %get-tuple-element.64.tie_row, s32[4]{0:T(128)S(4)} %get-tuple-element.65.tie_source, ...), custom_call_target="tpu_custom_call", output_to_operand_aliasing={{0}: (8, {}), {1}: (9, {}), {2}: (10, {}), {3}: (11, {})} | custom-call | flops 1761607680 | bytes 12000000 | tf_op jit(solution)/shard_map/step/pallas_call | solution.py:521
  28.6 0.9 %collective-permute-done.11.other.refs_0_ = f32[96,128]{1,0:T(8,128)S(1)} collective-permute-done((f32[96,128]{1,0:T(8,128)S(1)}, f32[96,128]{1,0:T(8,128)S(1)}, u32[]{:S(2)}, u32[]{:S(2)}) %collective-permute-start.11) | collective-permute-done | bytes 49184 | tf_op jit(solution)/shard_map/ppermute | solution.py:186
  29.5 0.2 ties.7
  29.7 0.4 collective-permute-start.13
  30.1 0.4 collective-permute-start.12
  30.5 2.3 %step.8 = (f32[70,96,128]{2,1,0:T(8,128)S(1)}, bf16[70,192,128]{2,1,0:T(8,128)(2,1)S(1)}, f32[70,96,128]{2,1,0:T(8,128)S(1)}, bf16[70,192,128]{2,1,0:T(8,128)(2,1)S(1)}) custom-call(s32[4]{0:T(128)S(4)} %get-tuple-element.64.tie_row, s32[4]{0:T(128)S(4)} %get-tuple-element.65.tie_source, ...), custom_call_target="tpu_custom_call", output_to_operand_aliasing={{0}: (8, {}), {1}: (9, {}), {2}: (10, {}), {3}: (11, {})} | custom-call | flops 1761607680 | bytes 12000000 | tf_op jit(solution)/shard_map/step/pallas_call | solution.py:521
  32.8 0.7 %collective-permute-done.13.other.refs_0_ = f32[96,128]{1,0:T(8,128)S(1)} collective-permute-done((f32[96,128]{1,0:T(8,128)S(1)}, f32[96,128]{1,0:T(8,128)S(1)}, u32[]{:S(2)}, u32[]{:S(2)}) %collective-permute-start.13) | collective-permute-done | bytes 49184 | tf_op jit(solution)/shard_map/ppermute | solution.py:186
  33.5 0.2 ties.8
  33.7 0.5 collective-permute-start.15
  34.2 0.4 collective-permute-start.14
  34.6 2.3 %step.9 = (f32[70,96,128]{2,1,0:T(8,128)S(1)}, bf16[70,192,128]{2,1,0:T(8,128)(2,1)S(1)}, f32[70,96,128]{2,1,0:T(8,128)S(1)}, bf16[70,192,128]{2,1,0:T(8,128)(2,1)S(1)}) custom-call(s32[4]{0:T(128)S(4)} %get-tuple-element.64.tie_row, s32[4]{0:T(128)S(4)} %get-tuple-element.65.tie_source, ...), custom_call_target="tpu_custom_call", output_to_operand_aliasing={{0}: (8, {}), {1}: (9, {}), {2}: (10, {}), {3}: (11, {})} | custom-call | flops 1761607680 | bytes 12000000 | tf_op jit(solution)/shard_map/step/pallas_call | solution.py:521
  36.9 0.6 collective-permute-done.15.other.refs_0_
  37.5 0.2 ties.9
  37.7 0.5 collective-permute-start.17
  38.2 0.4 collective-permute-start.16
  38.6 2.5 %step.10 = (f32[70,96,128]{2,1,0:T(8,128)S(1)}, bf16[70,192,128]{2,1,0:T(8,128)(2,1)S(1)}, f32[70,96,128]{2,1,0:T(8,128)S(1)}, bf16[70,192,128]{2,1,0:T(8,128)(2,1)S(1)}) custom-call(s32[4]{0:T(128)S(4)} %get-tuple-element.64.tie_row, s32[4]{0:T(128)S(4)} %get-tuple-element.65.tie_source, ...), custom_call_target="tpu_custom_call", output_to_operand_aliasing={{0}: (8, {}), {1}: (9, {}), {2}: (10, {}), {3}: (11, {})} | custom-call | flops 1761607680 | bytes 12000000 | tf_op jit(solution)/shard_map/step/pallas_call | solution.py:521
  41.1 0.4 collective-permute-done.17.other.refs_0_
  41.5 0.2 ties.10
  41.7 0.7 %collective-permute-start.19 = (f32[96,128]{1,0:T(8,128)S(1)}, f32[96,128]{1,0:T(8,128)S(1)}, u32[]{:S(2)}, u32[]{:S(2)}) collective-permute-start(f32[96,128]{1,0:T(8,128)S(1)} %ties.10), channel_id=1, source_target_pairs={{0,24},{8,16},{16,8},{24,0},{1,25},{9,17},{17,9},{25,1},{2,26},{10... | collective-permute-start | bytes 147464 | tf_op jit(solution)/shard_map/ppermute | solution.py:186
  42.4 0.4 collective-permute-start.18
  42.8 2.3 %step.11 = (f32[70,96,128]{2,1,0:T(8,128)S(1)}, bf16[70,192,128]{2,1,0:T(8,128)(2,1)S(1)}, f32[70,96,128]{2,1,0:T(8,128)S(1)}, bf16[70,192,128]{2,1,0:T(8,128)(2,1)S(1)}) custom-call(s32[4]{0:T(128)S(4)} %get-tuple-element.64.tie_row, s32[4]{0:T(128)S(4)} %get-tuple-element.65.tie_source, ...), custom_call_target="tpu_custom_call", output_to_operand_aliasing={{0}: (8, {}), {1}: (9, {}), {2}: (10, {}), {3}: (11, {})} | custom-call | flops 1761607680 | bytes 12000000 | tf_op jit(solution)/shard_map/step/pallas_call | solution.py:521
  45.1 0.4 collective-permute-done.19.other.refs_0_
  45.5 0.2 ties.11
  45.7 0.7 %collective-permute-start.21 = (f32[96,128]{1,0:T(8,128)S(1)}, f32[96,128]{1,0:T(8,128)S(1)}, u32[]{:S(2)}, u32[]{:S(2)}) collective-permute-start(f32[96,128]{1,0:T(8,128)S(1)} %ties.11), channel_id=1, source_target_pairs={{0,24},{8,16},{16,8},{24,0},{1,25},{9,17},{17,9},{25,1},{2,26},{10... | collective-permute-start | bytes 147464 | tf_op jit(solution)/shard_map/ppermute | solution.py:186
  46.4 0.4 collective-permute-start.20
  46.8 2.5 %last_step.1 = (f32[70,96,128]{2,1,0:T(8,128)S(1)}, bf16[70,192,128]{2,1,0:T(8,128)(2,1)S(1)}, f32[70,96,128]{2,1,0:T(8,128)S(1)}, bf16[70,192,128]{2,1,0:T(8,12...) custom-call(s32[4]{0:T(128)S(4)} %get-tuple-element.64.tie_row, ...), custom_call_target="tpu_custom_call", output_to_operand_aliasing={{0}: (8, {}), {1}: (9, {}), {2}: (10, {}), {3}: (11, {})} | custom-call | flops 1761607680 | bytes 12000000 | tf_op jit(solution)/shard_map/last_step/pallas_call | solution.py:521
  49.3 0.2 collective-permute-done.21.other
  49.5 0.3 last_ties.1
  49.8 2.5 %collective-permute-start.24 = (f32[2,8960]{1,0:T(2,128)S(1)}, f32[2,8960]{1,0:T(2,128)S(1)}, u32[]{:S(2)}, u32[]{:S(2)}) collective-permute-start(f32[2,8960]{1,0:T(2,128)S(1)} %get-tuple-element.118.refs_0_), channel_id=1, source_target_pairs={{0,6},{1,7},{2,4},{3,5},{4,2},{5,3},{6,0},{7,1},{8,14},{9,15},{10,... | collective-permute-start | bytes 215048 | tf_op jit(solution)/shard_map/ppermute | solution.py:126
  52.3 0.6 collective-permute-start.23
  52.8 1.4 %collective-permute-start.22 = (f32[2,8960]{1,0:T(2,128)S(1)}, f32[2,8960]{1,0:T(2,128)S(1)}, u32[]{:S(2)}, u32[]{:S(2)}) collective-permute-start(f32[2,8960]{1,0:T(2,128)S(1)} %get-tuple-element.118.refs_0_), channel_id=1, source_target_pairs={{0,2},{1,3},{2,0},{3,1},{4,6},{5,7},{6,4},{7,5},{8,10},{9,11},{10,... | collective-permute-start | bytes 215048 | tf_op jit(solution)/shard_map/ppermute | solution.py:126
  54.2 0.7 %collective-permute-start.25 = (f32[4,9216]{1,0:T(4,128)S(1)}, f32[4,9216]{1,0:T(4,128)S(1)}, u32[]{:S(2)}, u32[]{:S(2)}) collective-permute-start(f32[4,9216]{1,0:T(4,128)S(1)} %get-tuple-element.119.refs_4_.refs_6_), channel_id=1, source_target_pairs={{0,1},{1,0},{2,3},{3,2},{4,5},{5,4},{6,7},{7,6},{8,9},{9,8},{10,11... | collective-permute-start | bytes 442376 | tf_op jit(solution)/shard_map/ppermute | solution.py:126
  54.9 2.9 %outputs.1 = (f32[24,4,8960]{2,1,0:T(4,128)}, f32[24,4,8960]{2,1,0:T(4,128)}) custom-call(f32[70,96,128]{2,1,0:T(8,128)S(1)} %get-tuple-element.116.state, f32[24,4,8960]{2,1,0:T(4,128)S(1)} %copy-done), custom_call_target="tpu_custom_call" | custom-call | flops 4000000000 | bytes 1000000 | tf_op jit(solution)/shard_map/outputs/pallas_call | solution.py:598
  57.9 2.0 %collective-permute-done.23.refs_2_ = f32[2,8960]{1,0:T(2,128)S(1)} collective-permute-done((f32[2,8960]{1,0:T(2,128)S(1)}, f32[2,8960]{1,0:T(2,128)S(1)}, u32[]{:S(2)}, u32[]{:S(2)}) %collective-permute-start.23) | collective-permute-done | bytes 71712 | tf_op jit(solution)/shard_map/ppermute | solution.py:126
  59.9 0.1 node_add_0.3
  59.9 0.8 %collective-permute-start.26 = (f32[2,8960]{1,0:T(2,128)S(1)}, f32[2,8960]{1,0:T(2,128)S(1)}, u32[]{:S(2)}, u32[]{:S(2)}) collective-permute-start(f32[2,8960]{1,0:T(2,128)S(1)} %get-tuple-element.120.refs_0_), channel_id=1, source_target_pairs={{0,1},{1,0},{2,3},{3,2},{4,5},{5,4},{6,7},{7,6},{8,9},{9,8},{10,11... | collective-permute-start | bytes 215048 | tf_op jit(solution)/shard_map/ppermute | solution.py:126
  60.7 0.3 collective-permute-start.27
  61.0 0.9 %multipliers_2.1.refs_4_.refs_2_ = f32[24,4,8960]{2,1,0:T(4,128)} custom-call(f32[70,96,128]{2,1,0:T(8,128)S(1)} %get-tuple-element.116.state, f32[24,4,8960]{2,1,0:T(4,128)S(1)} %copy-done, f32[2,8960]{1,0:T(2,128)S(1)} %get-tuple-element.122.refs_0_, f32[24,4,8960]{2,1,0:T(4,128)} %get-tuple-element.123.refs_1_), custom_call_target="tpu_custom_call", output_to_operand_aliasing={{}: (3, {})} | custom-call | flops 1000000000 | bytes 1000000 | tf_op jit(solution)/shard_map/multipliers_2/pallas_call | solution.py:576
  61.9 2.4 %collective-permute-done.26.refs_1_ = f32[2,8960]{1,0:T(2,128)S(1)} collective-permute-done((f32[2,8960]{1,0:T(2,128)S(1)}, f32[2,8960]{1,0:T(2,128)S(1)}, u32[]{:S(2)}, u32[]{:S(2)}) %collective-permute-start.26) | collective-permute-done | bytes 71712 | tf_op jit(solution)/shard_map/ppermute | solution.py:126
  64.3 0.7 %collective-permute-done.27.refs_3_ = f32[2,8960]{1,0:T(2,128)S(1)} collective-permute-done((f32[2,8960]{1,0:T(2,128)S(1)}, f32[2,8960]{1,0:T(2,128)S(1)}, u32[]{:S(2)}, u32[]{:S(2)}) %collective-permute-start.27) | collective-permute-done | bytes 71712 | tf_op jit(solution)/shard_map/ppermute | solution.py:126
  65.1 0.9 %multipliers_0.1 = f32[24,4,8960]{2,1,0:T(4,128)} custom-call(f32[70,96,128]{2,1,0:T(8,128)S(1)} %get-tuple-element.116.state, f32[24,4,8960]{2,1,0:T(4,128)S(1)} %copy-done, f32[2,8960]{1,0:T(2,128)S(1)} %get-tuple-element.124.refs_0_, f32[2,8960]{1,0:T(2,128)S(1)} %get-tuple-element.125.refs_1_, ...), custom_call_target="tpu_custom_call", output_to_operand_aliasing={{}: (4, {})} | custom-call | flops 1000000000 | bytes 1000000 | tf_op jit(solution)/shard_map/multipliers_0/pallas_call | solution.py:576
  (33 shorter events, 0.1 us)
Async XLA Ops:
  1.3 9.2 %copy-start = (f32[24,4,8960]{2,1,0:T(4,128)S(1)}, f32[24,4,8960]{2,1,0:T(4,128)}, u32[]{:S(2)}) copy-start(f32[24,4,8960]{2,1,0:T(4,128)} %mult.7) | copy-start | bytes 10321924
  1.3 9.2 %copy-start.1 = (f32[24,4,8960]{2,1,0:T(4,128)S(1)}, f32[24,4,8960]{2,1,0:T(4,128)}, u32[]{:S(2)}) copy-start(f32[24,4,8960]{2,1,0:T(4,128)} %start.3) | copy-start | bytes 10321924
  1.3 9.2 %copy-start.2 = (f32[24,8960]{1,0:T(8,128)S(1)}, f32[24,8960]{1,0:T(8,128)}, u32[]{:S(2)}) copy-start(f32[24,8960]{1,0:T(8,128)} %demand.1) | copy-start | bytes 2580484
  1.3 9.2 %copy-start.3 = (f32[4,128,128]{2,1,0:T(8,128)S(1)}, f32[4,128,128]{2,1,0:T(8,128)}, u32[]{:S(2)}) copy-start(f32[4,128,128]{2,1,0:T(8,128)} %tie_weight.1) | copy-start | bytes 786436
  3.1 10.2 %collective-permute-start.4 = (f32[2,8960]{1,0:T(2,128)S(1)}, f32[2,8960]{1,0:T(2,128)S(1)}, u32[]{:S(2)}, u32[]{:S(2)}) collective-permute-start(f32[2,8960]{1,0:T(2,128)S(1)} %get-tuple-element.75.refs_0_), channel_id=1, source_target_pairs={{0,6},{1,7},{2,4},{3,5},{4,2},{5,3},{6,0},{7,1},{8,14},{9,15},{10,... | collective-permute-start | bytes 215048 | tf_op jit(solution)/shard_map/ppermute | solution.py:126
  8.2 6.7 %collective-permute-start.3 = (f32[2,8960]{1,0:T(2,128)S(1)}, f32[2,8960]{1,0:T(2,128)S(1)}, u32[]{:S(2)}, u32[]{:S(2)}) collective-permute-start(f32[2,8960]{1,0:T(2,128)S(1)} %get-tuple-element.75.refs_0_), channel_id=1, source_target_pairs={{0,4},{1,5},{2,6},{3,7},{4,0},{5,1},{6,2},{7,3},{8,12},{9,13},{10,... | collective-permute-start | bytes 215048 | tf_op jit(solution)/shard_map/ppermute | solution.py:126
  8.2 6.7 %collective-permute-start.2 = (f32[2,8960]{1,0:T(2,128)S(1)}, f32[2,8960]{1,0:T(2,128)S(1)}, u32[]{:S(2)}, u32[]{:S(2)}) collective-permute-start(f32[2,8960]{1,0:T(2,128)S(1)} %get-tuple-element.75.refs_0_), channel_id=1, source_target_pairs={{0,2},{1,3},{2,0},{3,1},{4,6},{5,7},{6,4},{7,5},{8,10},{9,11},{10,... | collective-permute-start | bytes 215048 | tf_op jit(solution)/shard_map/ppermute | solution.py:126
  8.8 6.0 %collective-permute-start.5 = (f32[4,9216]{1,0:T(4,128)S(1)}, f32[4,9216]{1,0:T(4,128)S(1)}, u32[]{:S(2)}, u32[]{:S(2)}) collective-permute-start(f32[4,9216]{1,0:T(4,128)S(1)} %get-tuple-element.76.refs_4_.refs_6_), channel_id=1, source_target_pairs={{0,1},{1,0},{2,3},{3,2},{4,5},{5,4},{6,7},{7,6},{8,9},{9,8},{10,11... | collective-permute-start | bytes 442376 | tf_op jit(solution)/shard_map/ppermute | solution.py:126
  10.5 6.5 %slice-start = ((s8[9175040]{0:T(1024)(128)(4,1)}), s8[4194304]{0:T(1024)(128)(4,1)S(1)}, s32[]{:S(2)}) async-start(s8[9175040]{0:T(1024)(128)(4,1)} %bitcast.2), calls=%async_computation | async-start | bytes 8388608
  10.5 6.5 %slice-start.1 = ((s8[9175040]{0:T(1024)(128)(4,1)}), s8[4194304]{0:T(1024)(128)(4,1)S(1)}, s32[]{:S(2)}) async-start(s8[9175040]{0:T(1024)(128)(4,1)} %bitcast.2), calls=%async_computation.1 | async-start | bytes 8388608
  10.5 6.5 %slice-start.2 = ((s8[9175040]{0:T(1024)(128)(4,1)}), s8[786432]{0:T(1024)(128)(4,1)S(1)}, s32[]{:S(2)}) async-start(s8[9175040]{0:T(1024)(128)(4,1)} %bitcast.2), calls=%async_computation.2 | async-start | bytes 1572864
  13.2 7.4 %collective-permute-start.1 = (f32[96,128]{1,0:T(8,128)S(1)}, f32[96,128]{1,0:T(8,128)S(1)}, u32[]{:S(2)}, u32[]{:S(2)}) collective-permute-start(f32[96,128]{1,0:T(8,128)S(1)} %get-tuple-element.69), channel_id=1, source_target_pairs={{0,24},{8,16},{16,8},{24,0},{1,25},{9,17},{17,9},{25,1},{2,26},{10... | collective-permute-start | bytes 147464 | tf_op jit(solution)/shard_map/ppermute | solution.py:186
  13.2 7.4 %collective-permute-start = (f32[96,128]{1,0:T(8,128)S(1)}, f32[96,128]{1,0:T(8,128)S(1)}, u32[]{:S(2)}, u32[]{:S(2)}) collective-permute-start(f32[96,128]{1,0:T(8,128)S(1)} %get-tuple-element.69), channel_id=1, source_target_pairs={{0,8},{8,0},{16,24},{24,16},{1,9},{9,1},{17,25},{25,17},{2,10},{10... | collective-permute-start | bytes 147464 | tf_op jit(solution)/shard_map/ppermute | solution.py:181
  15.0 5.6 %collective-permute-start.7 = (f32[2,8960]{1,0:T(2,128)S(1)}, f32[2,8960]{1,0:T(2,128)S(1)}, u32[]{:S(2)}, u32[]{:S(2)}) collective-permute-start(f32[2,8960]{1,0:T(2,128)S(1)} %get-tuple-element.79.refs_2_), channel_id=1, source_target_pairs={{0,2},{1,3},{2,0},{3,1},{4,6},{5,7},{6,4},{7,5},{8,10},{9,11},{10,... | collective-permute-start | bytes 215048 | tf_op jit(solution)/shard_map/ppermute | solution.py:126
  16.3 4.3 %collective-permute-start.6 = (f32[2,8960]{1,0:T(2,128)S(1)}, f32[2,8960]{1,0:T(2,128)S(1)}, u32[]{:S(2)}, u32[]{:S(2)}) collective-permute-start(f32[2,8960]{1,0:T(2,128)S(1)} %get-tuple-element.77.after.refs_0_), channel_id=1, source_target_pairs={{0,1},{1,0},{2,3},{3,2},{4,5},{5,4},{6,7},{7,6},{8,9},{9,8},{10,11... | collective-permute-start | bytes 215048 | tf_op jit(solution)/shard_map/ppermute | solution.py:126
  20.8 4.5 %collective-permute-start.9 = (f32[96,128]{1,0:T(8,128)S(1)}, f32[96,128]{1,0:T(8,128)S(1)}, u32[]{:S(2)}, u32[]{:S(2)}) collective-permute-start(f32[96,128]{1,0:T(8,128)S(1)} %first_ties.1), channel_id=1, source_target_pairs={{0,24},{8,16},{16,8},{24,0},{1,25},{9,17},{17,9},{25,1},{2,26},{10... | collective-permute-start | bytes 147464 | tf_op jit(solution)/shard_map/ppermute | solution.py:186
  20.9 4.5 %collective-permute-start.8 = (f32[96,128]{1,0:T(8,128)S(1)}, f32[96,128]{1,0:T(8,128)S(1)}, u32[]{:S(2)}, u32[]{:S(2)}) collective-permute-start(f32[96,128]{1,0:T(8,128)S(1)} %first_ties.1), channel_id=1, source_target_pairs={{0,8},{8,0},{16,24},{24,16},{1,9},{9,1},{17,25},{25,17},{2,10},{10... | collective-permute-start | bytes 147464 | tf_op jit(solution)/shard_map/ppermute | solution.py:181
  25.6 3.9 %collective-permute-start.11 = (f32[96,128]{1,0:T(8,128)S(1)}, f32[96,128]{1,0:T(8,128)S(1)}, u32[]{:S(2)}, u32[]{:S(2)}) collective-permute-start(f32[96,128]{1,0:T(8,128)S(1)} %ties.6), channel_id=1, source_target_pairs={{0,24},{8,16},{16,8},{24,0},{1,25},{9,17},{17,9},{25,1},{2,26},{10... | collective-permute-start | bytes 147464 | tf_op jit(solution)/shard_map/ppermute | solution.py:186
  25.7 3.8 %collective-permute-start.10 = (f32[96,128]{1,0:T(8,128)S(1)}, f32[96,128]{1,0:T(8,128)S(1)}, u32[]{:S(2)}, u32[]{:S(2)}) collective-permute-start(f32[96,128]{1,0:T(8,128)S(1)} %ties.6), channel_id=1, source_target_pairs={{0,8},{8,0},{16,24},{24,16},{1,9},{9,1},{17,25},{25,17},{2,10},{10... | collective-permute-start | bytes 147464 | tf_op jit(solution)/shard_map/ppermute | solution.py:181
  29.7 3.8 %collective-permute-start.13 = (f32[96,128]{1,0:T(8,128)S(1)}, f32[96,128]{1,0:T(8,128)S(1)}, u32[]{:S(2)}, u32[]{:S(2)}) collective-permute-start(f32[96,128]{1,0:T(8,128)S(1)} %ties.7), channel_id=1, source_target_pairs={{0,24},{8,16},{16,8},{24,0},{1,25},{9,17},{17,9},{25,1},{2,26},{10... | collective-permute-start | bytes 147464 | tf_op jit(solution)/shard_map/ppermute | solution.py:186
  30.1 3.4 %collective-permute-start.12 = (f32[96,128]{1,0:T(8,128)S(1)}, f32[96,128]{1,0:T(8,128)S(1)}, u32[]{:S(2)}, u32[]{:S(2)}) collective-permute-start(f32[96,128]{1,0:T(8,128)S(1)} %ties.7), channel_id=1, source_target_pairs={{0,8},{8,0},{16,24},{24,16},{1,9},{9,1},{17,25},{25,17},{2,10},{10... | collective-permute-start | bytes 147464 | tf_op jit(solution)/shard_map/ppermute | solution.py:181
  33.7 3.8 %collective-permute-start.15 = (f32[96,128]{1,0:T(8,128)S(1)}, f32[96,128]{1,0:T(8,128)S(1)}, u32[]{:S(2)}, u32[]{:S(2)}) collective-permute-start(f32[96,128]{1,0:T(8,128)S(1)} %ties.8), channel_id=1, source_target_pairs={{0,24},{8,16},{16,8},{24,0},{1,25},{9,17},{17,9},{25,1},{2,26},{10... | collective-permute-start | bytes 147464 | tf_op jit(solution)/shard_map/ppermute | solution.py:186
  34.2 3.3 %collective-permute-start.14 = (f32[96,128]{1,0:T(8,128)S(1)}, f32[96,128]{1,0:T(8,128)S(1)}, u32[]{:S(2)}, u32[]{:S(2)}) collective-permute-start(f32[96,128]{1,0:T(8,128)S(1)} %ties.8), channel_id=1, source_target_pairs={{0,8},{8,0},{16,24},{24,16},{1,9},{9,1},{17,25},{25,17},{2,10},{10... | collective-permute-start | bytes 147464 | tf_op jit(solution)/shard_map/ppermute | solution.py:181
  37.7 3.8 %collective-permute-start.17 = (f32[96,128]{1,0:T(8,128)S(1)}, f32[96,128]{1,0:T(8,128)S(1)}, u32[]{:S(2)}, u32[]{:S(2)}) collective-permute-start(f32[96,128]{1,0:T(8,128)S(1)} %ties.9), channel_id=1, source_target_pairs={{0,24},{8,16},{16,8},{24,0},{1,25},{9,17},{17,9},{25,1},{2,26},{10... | collective-permute-start | bytes 147464 | tf_op jit(solution)/shard_map/ppermute | solution.py:186
  38.2 3.3 %collective-permute-start.16 = (f32[96,128]{1,0:T(8,128)S(1)}, f32[96,128]{1,0:T(8,128)S(1)}, u32[]{:S(2)}, u32[]{:S(2)}) collective-permute-start(f32[96,128]{1,0:T(8,128)S(1)} %ties.9), channel_id=1, source_target_pairs={{0,8},{8,0},{16,24},{24,16},{1,9},{9,1},{17,25},{25,17},{2,10},{10... | collective-permute-start | bytes 147464 | tf_op jit(solution)/shard_map/ppermute | solution.py:181
  41.7 3.8 %collective-permute-start.19 = (f32[96,128]{1,0:T(8,128)S(1)}, f32[96,128]{1,0:T(8,128)S(1)}, u32[]{:S(2)}, u32[]{:S(2)}) collective-permute-start(f32[96,128]{1,0:T(8,128)S(1)} %ties.10), channel_id=1, source_target_pairs={{0,24},{8,16},{16,8},{24,0},{1,25},{9,17},{17,9},{25,1},{2,26},{10... | collective-permute-start | bytes 147464 | tf_op jit(solution)/shard_map/ppermute | solution.py:186
  42.4 3.1 %collective-permute-start.18 = (f32[96,128]{1,0:T(8,128)S(1)}, f32[96,128]{1,0:T(8,128)S(1)}, u32[]{:S(2)}, u32[]{:S(2)}) collective-permute-start(f32[96,128]{1,0:T(8,128)S(1)} %ties.10), channel_id=1, source_target_pairs={{0,8},{8,0},{16,24},{24,16},{1,9},{9,1},{17,25},{25,17},{2,10},{10... | collective-permute-start | bytes 147464 | tf_op jit(solution)/shard_map/ppermute | solution.py:181
  45.7 3.8 %collective-permute-start.21 = (f32[96,128]{1,0:T(8,128)S(1)}, f32[96,128]{1,0:T(8,128)S(1)}, u32[]{:S(2)}, u32[]{:S(2)}) collective-permute-start(f32[96,128]{1,0:T(8,128)S(1)} %ties.11), channel_id=1, source_target_pairs={{0,24},{8,16},{16,8},{24,0},{1,25},{9,17},{17,9},{25,1},{2,26},{10... | collective-permute-start | bytes 147464 | tf_op jit(solution)/shard_map/ppermute | solution.py:186
  46.4 3.1 %collective-permute-start.20 = (f32[96,128]{1,0:T(8,128)S(1)}, f32[96,128]{1,0:T(8,128)S(1)}, u32[]{:S(2)}, u32[]{:S(2)}) collective-permute-start(f32[96,128]{1,0:T(8,128)S(1)} %ties.11), channel_id=1, source_target_pairs={{0,8},{8,0},{16,24},{24,16},{1,9},{9,1},{17,25},{25,17},{2,10},{10... | collective-permute-start | bytes 147464 | tf_op jit(solution)/shard_map/ppermute | solution.py:181
  49.8 8.1 %collective-permute-start.24 = (f32[2,8960]{1,0:T(2,128)S(1)}, f32[2,8960]{1,0:T(2,128)S(1)}, u32[]{:S(2)}, u32[]{:S(2)}) collective-permute-start(f32[2,8960]{1,0:T(2,128)S(1)} %get-tuple-element.118.refs_0_), channel_id=1, source_target_pairs={{0,6},{1,7},{2,4},{3,5},{4,2},{5,3},{6,0},{7,1},{8,14},{9,15},{10,... | collective-permute-start | bytes 215048 | tf_op jit(solution)/shard_map/ppermute | solution.py:126
  52.3 7.6 %collective-permute-start.23 = (f32[2,8960]{1,0:T(2,128)S(1)}, f32[2,8960]{1,0:T(2,128)S(1)}, u32[]{:S(2)}, u32[]{:S(2)}) collective-permute-start(f32[2,8960]{1,0:T(2,128)S(1)} %get-tuple-element.118.refs_0_), channel_id=1, source_target_pairs={{0,4},{1,5},{2,6},{3,7},{4,0},{5,1},{6,2},{7,3},{8,12},{9,13},{10,... | collective-permute-start | bytes 215048 | tf_op jit(solution)/shard_map/ppermute | solution.py:126
  52.8 7.0 %collective-permute-start.22 = (f32[2,8960]{1,0:T(2,128)S(1)}, f32[2,8960]{1,0:T(2,128)S(1)}, u32[]{:S(2)}, u32[]{:S(2)}) collective-permute-start(f32[2,8960]{1,0:T(2,128)S(1)} %get-tuple-element.118.refs_0_), channel_id=1, source_target_pairs={{0,2},{1,3},{2,0},{3,1},{4,6},{5,7},{6,4},{7,5},{8,10},{9,11},{10,... | collective-permute-start | bytes 215048 | tf_op jit(solution)/shard_map/ppermute | solution.py:126
  54.2 5.6 %collective-permute-start.25 = (f32[4,9216]{1,0:T(4,128)S(1)}, f32[4,9216]{1,0:T(4,128)S(1)}, u32[]{:S(2)}, u32[]{:S(2)}) collective-permute-start(f32[4,9216]{1,0:T(4,128)S(1)} %get-tuple-element.119.refs_4_.refs_6_), channel_id=1, source_target_pairs={{0,1},{1,0},{2,3},{3,2},{4,5},{5,4},{6,7},{7,6},{8,9},{9,8},{10,11... | collective-permute-start | bytes 442376 | tf_op jit(solution)/shard_map/ppermute | solution.py:126
  59.9 4.4 %collective-permute-start.26 = (f32[2,8960]{1,0:T(2,128)S(1)}, f32[2,8960]{1,0:T(2,128)S(1)}, u32[]{:S(2)}, u32[]{:S(2)}) collective-permute-start(f32[2,8960]{1,0:T(2,128)S(1)} %get-tuple-element.120.refs_0_), channel_id=1, source_target_pairs={{0,1},{1,0},{2,3},{3,2},{4,5},{5,4},{6,7},{7,6},{8,9},{9,8},{10,11... | collective-permute-start | bytes 215048 | tf_op jit(solution)/shard_map/ppermute | solution.py:126
  60.7 4.3 %collective-permute-start.27 = (f32[2,8960]{1,0:T(2,128)S(1)}, f32[2,8960]{1,0:T(2,128)S(1)}, u32[]{:S(2)}, u32[]{:S(2)}) collective-permute-start(f32[2,8960]{1,0:T(2,128)S(1)} %get-tuple-element.121.refs_2_), channel_id=1, source_target_pairs={{0,2},{1,3},{2,0},{3,1},{4,6},{5,7},{6,4},{7,5},{8,10},{9,11},{10,... | collective-permute-start | bytes 215048 | tf_op jit(solution)/shard_map/ppermute | solution.py:126
